TPU v7x, 32 devices: a whole 2x2x4 slice. The times are simulated.
32 devices in a mesh: gx: 8 (over z, core), gy: 4 (over y, x).
Axes of the slice: x: 2, y: 2, z: 4, core: 2. Of those that a mesh axis runs over, the one named last changes fastest.
Arguments:
- feature: bfloat16 [6, 64, 192, 512], P(None, None, 'gx', 'gy'), may hold values from -6 to 6
- widths: int32 [8], replicated, may hold values from 8 to 24, as said below
- dw_weight: float32 [27, 64], replicated, may hold values from -1.25 to 1.25
- dw_bias: float32 [64], replicated, may hold values from -3 to 3
- pw_weight: bfloat16 [64, 64], replicated, may hold values from -0.75 to 0.75
- pw_bias: float32 [64], replicated, may hold values from -3 to 3
- lift_weight: float32 [64, 3], replicated, may hold values from -3 to 3
- coarse: float32 [3, 8, 32], P(None, 'gy'), may hold values from -6 to 6
Outputs:
- block_out: bfloat16 [2, 64, 192, 512], P(None, None, 'gx', 'gy')
Inputs may be any that keep to these rules, and one draw needn't show every extreme that they name: The widths sum to 128; some slab has width exactly 24 and some exactly 8.
All inputs are finite; a program needn't handle non-finite values.
Results may differ from a plain program's by a relative error of at most 0.0031.
Values may be sent and summed in bfloat16 or wider, within the bound.
No kernel may reach another device: no remote copies, remote signals or barrier semaphores. Data moves between devices by JAX's collectives and lax.ppermute only.
A program may use at most 64 MiB of HBM per device.

v0:
```python
import jax
import jax.numpy as jnp
from jax import lax
from jax.sharding import PartitionSpec as P

XW = 16
ZOUT = 2
CF = 16


def with_halo(cells, sides, width):
    for axis, dim in sides:
        count = lax.axis_size(axis)
        head = lax.slice_in_dim(cells, 0, width, axis=dim)
        tail = lax.slice_in_dim(cells, cells.shape[dim] - width, cells.shape[dim], axis=dim)
        cells = jnp.concatenate(
            [
                lax.ppermute(tail, axis, [(i, (i + 1) % count) for i in range(count)]),
                cells,
                lax.ppermute(head, axis, [((i + 1) % count, i) for i in range(count)]),
            ],
            axis=dim,
        )
    return cells


def passed_along(shard, axis, by):
    length = lax.axis_size(axis)
    return lax.ppermute(shard, axis, [(i, (i + by) % length) for i in range(length)])


def attach_rows(block, width, from_lower, from_upper):
    rim_shape = list(block.shape)
    rim_shape[2] = 2
    joined = jnp.concatenate([from_lower, block, jnp.zeros(rim_shape, block.dtype)], axis=2)
    return lax.dynamic_update_slice_in_dim(joined, from_upper, width + 2, axis=2)


def shards(feature, widths, dw_weight, dw_bias, pw_weight, pw_bias, lift_weight, coarse):
    slab_index = lax.axis_index("gx")
    width = widths[slab_index]
    starts = jnp.cumsum(widths) - widths
    start = starts[slab_index]
    slots = feature.shape[2]
    tile = feature.shape[3]
    total = XW * lax.axis_size("gx")
    widened = with_halo(feature, (("gy", 3),), 2)
    last_two = lax.dynamic_slice_in_dim(widened, width - 2, 2, axis=2)
    from_lower = passed_along(last_two, "gx", 1)
    from_upper = passed_along(widened[:, :, :2, :], "gx", -1)
    padded = attach_rows(widened, width, from_lower, from_upper)
    depth = (
        jnp.zeros((ZOUT, feature.shape[1], slots, tile), jnp.float32) + dw_bias[None, :, None, None]
    )
    for dz in (-1, 0, 1):
        for dx in (-1, 0, 1):
            for dy in (-1, 0, 1):
                tap = 9 * (dz + 1) + 3 * (dx + 1) + (dy + 1)
                window = padded[
                    2 + 2 * dz : 2 + 2 * dz + ZOUT,
                    :,
                    2 + 2 * dx : 2 + 2 * dx + slots,
                    2 + 2 * dy : 2 + 2 * dy + tile,
                ]
                depth = depth + dw_weight[tap][None, :, None, None] * window.astype(jnp.float32)
    depth = depth.astype(jnp.bfloat16)
    mixed = jnp.einsum("oc,zcxy->zoxy", pw_weight, depth, preferred_element_type=jnp.float32)
    mixed = mixed + pw_bias[None, :, None, None]
    active = jnp.where(mixed > 0, mixed, 0.2 * mixed)
    local = lax.all_to_all(coarse, "gy", split_axis=2, concat_axis=1, tiled=True)
    rows = start + jnp.arange(slots, dtype=jnp.int32)
    cells = rows % total // CF
    onehot = (cells[:, None] == jnp.arange(local.shape[1], dtype=jnp.int32)[None, :]).astype(
        jnp.float32
    )
    along_x = jnp.einsum("xn,knv->kxv", onehot, local, precision=lax.Precision.HIGHEST)
    upsampled = jnp.repeat(along_x, CF, axis=2)
    lifted = jnp.einsum("ck,kxy->cxy", lift_weight, upsampled, precision=lax.Precision.HIGHEST)
    value = feature[2 : 2 + ZOUT].astype(jnp.float32) + active + lifted[None]
    valid = jnp.arange(slots, dtype=jnp.int32) < width
    return jnp.where(valid[None, None, :, None], value, 0.0).astype(jnp.bfloat16)


def solution(mesh):
    placed = (P(None, None, "gx", "gy"), P(), P(), P(), P(), P(), P(), P(None, "gy", None))
    return jax.shard_map(
        shards, mesh=mesh, in_specs=placed, out_specs=P(None, None, "gx", "gy"), check_vma=False
    )
```

profile of v0, /device:TPU:18, one launch (start us, length us, event | category | flops | bytes accessed | tf_op | source)
XLA Modules:
  0.0 59.3 jit_solution(17691703370667424272)
XLA Ops:
  0.0 0.0 copy-start
  0.0 4.9 %fusion.11 = (bf16[6,64,24,2]{3,2,1,0:T(8,128)(2,1)S(1)}, bf16[6,64,24,2]{3,2,1,0:T(8,128)(2,1)}) fusion(bf16[6,64,24,128]{3,2,1,0:T(8,128)(2,1)} %param.8), kind=kLoop, calls=%fused_computation.56 | loop fusion | bytes 147456 | tf_op jit(solution)/shard_map/slice | solution.py:15
  4.9 1.4 %copy.46 = bf16[6,64,24,2]{1,2,3,0:T(8,128)(2,1)S(1)} copy(bf16[6,64,24,2]{3,2,1,0:T(8,128)(2,1)S(1)} %get-tuple-element.7) | data formatting | bytes 73728
  6.3 0.0 copy-start.6
  6.3 0.0 copy-start.1
  6.3 1.5 %collective-permute-start = (bf16[6,64,24,2]{1,2,3,0:T(8,128)(2,1)S(1)}, bf16[6,64,24,2]{1,2,3,0:T(8,128)(2,1)S(1)}, u32[]{:S(2)}, u32[]{:S(2)}) collective-permute-start(bf16[6,64,24,2]{1,2,3,0:T(8,128)(2,1)S(1)} %copy.46), channel_id=1, source_target_pairs={{0,1},{1,2},{2,3},{3,0},{4,5},{5,6},{6,7},{7,4},{8,9},{9,10},{10,1... | collective-permute-start | bytes 110600 | tf_op jit(solution)/shard_map/ppermute | solution.py:18
  7.9 2.9 %copy.47 = bf16[6,64,24,2]{1,2,3,0:T(8,128)(2,1)S(1)} copy(bf16[6,64,24,2]{3,2,1,0:T(8,128)(2,1)} %get-tuple-element.8) | data formatting | bytes 73728
  10.8 0.6 collective-permute-start.1
  11.3 0.0 copy-done.6
  11.4 0.7 %copy.39 = f32[3,2,32]{0,1,2:T(2,128)} copy(f32[3,2,32]{2,1,0:T(2,128)S(1)} %copy-done.6) | data formatting | bytes 1536 | tf_op args[7]
  12.1 4.8 %all-to-all-start = ((f32[3,2,32]{0,1,2:T(2,128)}), f32[3,2,32]{0,1,2:T(2,128)S(1)}, u32[]{:S(2)}, u32[]{:S(2)}) async-start(f32[3,2,32]{0,1,2:T(2,128)} %copy.39), calls=%async_computation | async-start | bytes 65536 | tf_op jit(solution)/shard_map/all_to_all | solution.py:70
  16.9 0.0 copy-done.1
  16.9 2.1 %copy.33 = bf16[6,64,24,128]{3,1,2,0:T(8,128)(2,1)} copy(bf16[6,64,24,128]{3,2,1,0:T(8,128)(2,1)S(1)} %copy-done.1) | data formatting | bytes 4718592 | tf_op args[0]
  19.0 0.0 copy-done.5
  19.0 0.0 copy-done.8
  19.0 0.7 %dynamic_slice.9 = s32[1]{0:T(128)} dynamic-slice(s32[8]{0:T(128)S(1)} %copy-done.8, s32[]{:T(128)S(6)} %select_n.38), dynamic_slice_sizes={1} | dynamic-slice | bytes 12 | tf_op jit(solution)/shard_map/dynamic_slice | solution.py:41
  19.7 0.7 %iota_compare_fusion.2 = pred[24]{0:T(512)(128)(4,1)S(1)} fusion(s32[]{:T(128)} %bitcast), kind=kLoop, calls=%fused_computation.54 | loop fusion | flops 24 | bytes 28 | tf_op jit(solution)/shard_map/lt | solution.py:80
  21.7 0.2 reduce-window.9
  21.9 0.7 %dynamic_slice.11 = s32[1]{0:T(128)} dynamic-slice(s32[8]{0:T(128)S(1)} %bitcast_subtract_fusion, s32[]{:T(128)S(6)} %select_n.38), dynamic_slice_sizes={1} | dynamic-slice | bytes 12 | tf_op jit(solution)/shard_map/dynamic_slice | solution.py:43
  22.5 0.7 %and_select_fusion = s32[24]{0:T(128)S(1)} fusion(s32[]{:T(128)} %bitcast.33), kind=kLoop, calls=%fused_computation.18 | loop fusion | flops 648 | bytes 100 | tf_op jit(solution)/shard_map/jit(floor_divide)/jit(_where)/select_n | solution.py:72
  24.6 0.1 pad.4.clone
  24.7 0.0 all-to-all-done
  24.7 0.1 copy.40
  24.8 0.1 copy.41
  24.9 0.1 convolution_bitcast_fusion.1
  25.0 0.1 copy.42
  25.1 0.1 broadcast_in_dim.24
  25.3 0.1 reshape.95
  25.4 0.0 collective-permute-done
  25.4 2.1 %copy.36 = bf16[6,64,24,2]{3,1,2,0:T(8,128)(2,1)} copy(bf16[6,64,24,2]{1,2,3,0:T(8,128)(2,1)S(1)} %collective-permute-done) | data formatting | bytes 73728 | tf_op jit(solution)/shard_map/ppermute | solution.py:18
  27.5 0.0 collective-permute-done.1
  27.5 2.1 %copy.38 = bf16[6,64,24,2]{3,1,2,0:T(8,128)(2,1)} copy(bf16[6,64,24,2]{1,2,3,0:T(8,128)(2,1)S(1)} %collective-permute-done.1) | data formatting | bytes 73728 | tf_op jit(solution)/shard_map/ppermute | solution.py:20
  29.7 0.0 copy-done.2
  29.7 4.8 %pad_maximum_fusion = bf16[6,64,24,132]{3,1,2,0:T(8,128)(2,1)S(1)} fusion(bf16[6,64,24,2]{3,1,2,0:T(8,128)(2,1)} %copy.38, bf16[6,64,24,128]{3,1,2,0:T(8,128)(2,1)S(1)} %copy-done.2, bf16[6,64,24,2]{3,1,2,0:T(8,128)(2,1)} %copy.36), kind=kLoop, calls=%fused_computation.1 | loop fusion | flops 7299072 | bytes 4866048 | tf_op jit(solution)/shard_map/concatenate | solution.py:16
  34.5 0.0 copy-start.3
  34.5 0.1 fusion.10
  34.6 0.1 collective-permute-start.2
  34.6 0.0 copy-done.7
  34.6 0.8 %convolution_bitcast_fusion = f32[64,24,128]{2,0,1:T(8,128)S(1)} fusion(f32[3,24,128]{2,1,0:T(8,128)S(1)} %reshape.95, f32[64,3]{0,1:T(4,128)S(1)} %copy-done.7), kind=kOutput, calls=%fused_computation.8 | convolution fusion | flops 7077888 | bytes 824064 | tf_op jit(solution)/shard_map/ck,kxy->cxy/dot_general | solution.py:78
  35.5 0.0 copy-start.9
  35.5 0.0 copy-start.10
  35.5 2.0 %collective-permute-start.3 = (bf16[6,64,2,132]{3,1,2,0:T(8,128)(2,1)S(1)}, bf16[6,64,2,132]{3,1,2,0:T(8,128)(2,1)S(1)}, u32[]{:S(2)}, u32[]{:S(2)}) collective-permute-start(bf16[6,64,2,132]{3,1,2,0:T(8,128)(2,1)S(1)} %get-tuple-element.5), channel_id=1, source_target_pairs={{0,28},{4,0},{8,4},{12,8},{16,12},{20,16},{24,20},{28,24},{1,29},{... | collective-permute-start | bytes 608264 | tf_op jit(solution)/shard_map/ppermute | solution.py:29
  37.4 8.6 %collective-permute-done.2 = bf16[6,64,2,132]{3,1,2,0:T(8,128)(2,1)S(1)} collective-permute-done((bf16[6,64,2,132]{3,1,2,0:T(8,128)(2,1)S(1)}, bf16[6,64,2,132]{3,1,2,0:T(8,128)(2,1)S(1)}, u32[]{:S(2)}, u32[]{:S(2)}) %collective-permute-start.2) | collective-permute-done | bytes 202784 | tf_op jit(solution)/shard_map/ppermute | solution.py:29
  46.0 0.0 copy-done.4
  46.0 4.1 %maximum_maximum_fusion = bf16[6,64,28,132]{3,1,2,0:T(8,128)(2,1)S(1)} fusion(bf16[6,64,24,2]{3,1,2,0:T(8,128)(2,1)S(1)} %copy-done.4, bf16[6,64,24,128]{3,1,2,0:T(8,128)(2,1)S(1)} %copy-done.2, bf16[6,64,24,2]{3,1,2,0:T(8,128)(2,1)S(1)} %copy-done.3, bf16[6,64,2,132]{3,1,2,0:T(8,128)(2,1)S(1)} %collective-permute-done.2, bf16[28]{0:T(256)(128)(2,1)S(1)} %pad.4.clone), kind=kLoop, calls=%fused_computation | loop fusion | flops 14192640 | bytes 5474360 | tf_op jit(solution)/shard_map/concatenate | solution.py:35
  50.1 0.0 collective-permute-done.3
  50.2 7.7 %fusion.3 = bf16[2,64,24,128]{3,1,2,0:T(8,128)(2,1)S(1)} fusion(bf16[6,64,24,128]{3,1,2,0:T(8,128)(2,1)S(1)} %copy-done.2, f32[64,24,128]{2,0,1:T(8,128)S(1)} %convolution_bitcast_fusion, f32[64]{0:T(128)S(1)} %copy-done.9, pred[24]{0:T(512)(128)(4,1)S(1)} %iota_compare_fusion.2, bf16[6,64,28,132]{3,1,2,0:T(8,128)(2,1)S(1)} %constant_dynamic-update-slice_fusion, ...), kind=kOutput, calls=%fused_computation.6 | convolution fusion | flops 86114304 | bytes 23624704 | tf_op jit(solution)/shard_map/oc,zcxy->zoxy/dot_general | solution.py:67
  57.9 1.4 %copy.44 = bf16[2,64,24,128]{3,2,1,0:T(8,128)(2,1)} copy(bf16[2,64,24,128]{3,1,2,0:T(8,128)(2,1)S(1)} %fusion.3) | data formatting | bytes 1572864 | tf_op jit(solution)/shard_map/convert_element_type | solution.py:81
  (14 shorter events, 0.1 us)
Async XLA Ops:
  0.0 50.2 %copy-start = (bf16[64,64]{1,0:T(8,128)(2,1)S(1)}, bf16[64,64]{1,0:T(8,128)(2,1)}, u32[]{:S(2)}) copy-start(bf16[64,64]{1,0:T(8,128)(2,1)} %param.12) | copy-start | bytes 24580
  6.3 5.0 %copy-start.6 = (f32[3,2,32]{2,1,0:T(2,128)S(1)}, f32[3,2,32]{2,1,0:T(2,128)}, u32[]{:S(2)}) copy-start(f32[3,2,32]{2,1,0:T(2,128)} %param.15) | copy-start | bytes 2308
  6.3 10.6 %copy-start.1 = (bf16[6,64,24,128]{3,2,1,0:T(8,128)(2,1)S(1)}, bf16[6,64,24,128]{3,2,1,0:T(8,128)(2,1)}, u32[]{:S(2)}) copy-start(bf16[6,64,24,128]{3,2,1,0:T(8,128)(2,1)} %param.8) | copy-start | bytes 7077892
  6.3 19.1 %collective-permute-start = (bf16[6,64,24,2]{1,2,3,0:T(8,128)(2,1)S(1)}, bf16[6,64,24,2]{1,2,3,0:T(8,128)(2,1)S(1)}, u32[]{:S(2)}, u32[]{:S(2)}) collective-permute-start(bf16[6,64,24,2]{1,2,3,0:T(8,128)(2,1)S(1)} %copy.46), channel_id=1, source_target_pairs={{0,1},{1,2},{2,3},{3,0},{4,5},{5,6},{6,7},{7,4},{8,9},{9,10},{10,1... | collective-permute-start | bytes 110600 | tf_op jit(solution)/shard_map/ppermute | solution.py:18
  10.8 16.8 %collective-permute-start.1 = (bf16[6,64,24,2]{1,2,3,0:T(8,128)(2,1)S(1)}, bf16[6,64,24,2]{1,2,3,0:T(8,128)(2,1)S(1)}, u32[]{:S(2)}, u32[]{:S(2)}) collective-permute-start(bf16[6,64,24,2]{1,2,3,0:T(8,128)(2,1)S(1)} %copy.47), channel_id=1, source_target_pairs={{1,0},{2,1},{3,2},{0,3},{5,4},{6,5},{7,6},{4,7},{9,8},{10,9},{11,1... | collective-permute-start | bytes 110600 | tf_op jit(solution)/shard_map/ppermute | solution.py:20
  12.1 12.6 %all-to-all-start = ((f32[3,2,32]{0,1,2:T(2,128)}), f32[3,2,32]{0,1,2:T(2,128)S(1)}, u32[]{:S(2)}, u32[]{:S(2)}) async-start(f32[3,2,32]{0,1,2:T(2,128)} %copy.39), calls=%async_computation | async-start | bytes 65536 | tf_op jit(solution)/shard_map/all_to_all | solution.py:70
  16.9 2.1 %copy-start.5 = (f32[27,64]{1,0:T(8,128)S(1)}, f32[27,64]{1,0:T(8,128)}, u32[]{:S(2)}) copy-start(f32[27,64]{1,0:T(8,128)} %param.10) | copy-start | bytes 20740
  16.9 2.1 %copy-start.8 = (s32[8]{0:T(128)S(1)}, s32[8]{0:T(128)}, u32[]{:S(2)}) copy-start(s32[8]{0:T(128)} %param.9) | copy-start | bytes 100
  27.5 2.1 %copy-start.2 = (bf16[6,64,24,128]{3,1,2,0:T(8,128)(2,1)S(1)}, bf16[6,64,24,128]{3,1,2,0:T(8,128)(2,1)}, u32[]{:S(2)}) copy-start(bf16[6,64,24,128]{3,1,2,0:T(8,128)(2,1)} %copy.33) | copy-start | bytes 7077892
  29.7 5.0 %copy-start.7 = (f32[64,3]{0,1:T(4,128)S(1)}, f32[64,3]{0,1:T(4,128)}, u32[]{:S(2)}) copy-start(f32[64,3]{0,1:T(4,128)} %param.14) | copy-start | bytes 2308
  29.7 16.4 %copy-start.4 = (bf16[6,64,24,2]{3,1,2,0:T(8,128)(2,1)S(1)}, bf16[6,64,24,2]{3,1,2,0:T(8,128)(2,1)}, u32[]{:S(2)}) copy-start(bf16[6,64,24,2]{3,1,2,0:T(8,128)(2,1)} %copy.38) | copy-start | bytes 110596
  34.5 11.6 %copy-start.3 = (bf16[6,64,24,2]{3,1,2,0:T(8,128)(2,1)S(1)}, bf16[6,64,24,2]{3,1,2,0:T(8,128)(2,1)}, u32[]{:S(2)}) copy-start(bf16[6,64,24,2]{3,1,2,0:T(8,128)(2,1)} %copy.36) | copy-start | bytes 110596
  34.6 11.5 %collective-permute-start.2 = (bf16[6,64,2,132]{3,1,2,0:T(8,128)(2,1)S(1)}, bf16[6,64,2,132]{3,1,2,0:T(8,128)(2,1)S(1)}, u32[]{:S(2)}, u32[]{:S(2)}) collective-permute-start(bf16[6,64,2,132]{3,1,2,0:T(8,128)(2,1)S(1)} %get-tuple-element.6), channel_id=1, source_target_pairs={{0,4},{4,8},{8,12},{12,16},{16,20},{20,24},{24,28},{28,0},{1,5},{5... | collective-permute-start | bytes 608264 | tf_op jit(solution)/shard_map/ppermute | solution.py:29
  35.5 14.8 %copy-start.9 = (f32[64]{0:T(128)S(1)}, f32[64]{0:T(128)}, u32[]{:S(2)}) copy-start(f32[64]{0:T(128)} %param.13) | copy-start | bytes 772
  35.5 14.7 %copy-start.10 = (f32[64]{0:T(128)S(1)}, f32[64]{0:T(128)}, u32[]{:S(2)}) copy-start(f32[64]{0:T(128)} %param.11) | copy-start | bytes 772
  35.5 14.7 %collective-permute-start.3 = (bf16[6,64,2,132]{3,1,2,0:T(8,128)(2,1)S(1)}, bf16[6,64,2,132]{3,1,2,0:T(8,128)(2,1)S(1)}, u32[]{:S(2)}, u32[]{:S(2)}) collective-permute-start(bf16[6,64,2,132]{3,1,2,0:T(8,128)(2,1)S(1)} %get-tuple-element.5), channel_id=1, source_target_pairs={{0,28},{4,0},{8,4},{12,8},{16,12},{20,16},{24,20},{28,24},{1,29},{... | collective-permute-start | bytes 608264 | tf_op jit(solution)/shard_map/ppermute | solution.py:29
where the time goes:
time: 59.6 us; the launch traced here: 59.3 us
  local copies, waits for them, and re-layouts  19.7 us (33%)
  other arithmetic  10.5 us (18%)
  starting transfers between devices  8.98 us (15%)
  matrix products  8.65 us (15%)
  waiting for transfers between devices  8.6 us (14%)
  between operations  2.92 us (5%)
    ppermute x2, waiting for transfers between devices, passed_along(): lax.ppermute(shard, axis, [(i, (i + by) % length) for i in range(length)])  8.59 us
    dot_general x1, matrix products, shards(): jnp.einsum('oc,zcxy->zoxy', pw_weight, depth, preferred_element_type=jnp....  7.71 us
    unnamed x26, local copies, waits for them, and re-layouts  7.15 us
    slice x1, local copies, waits for them, and re-layouts, with_halo(): lax.slice_in_dim(cells, cells.shape[dim] - width, cells.shape[dim], axis=...  4.87 us
    all_to_all x1, starting transfers between devices, shards(): lax.all_to_all(coarse, 'gy', split_axis=2, concat_axis=1, tiled=True)  4.84 us
    concatenate x1, other arithmetic, with_halo(): jnp.concatenate([lax.ppermute(tail, axis, [(i, (i + 1) % count) for i in...  4.81 us
    concatenate x1, other arithmetic, attach_rows(): jnp.concatenate([from_lower, block, jnp.zeros(rim_shape, block.dtype)], a...  4.1 us
    ppermute x1, local copies, waits for them, and re-layouts, with_halo(): lax.ppermute(tail, axis, [(i, (i + 1) % count) for i in range(count)])  2.12 us
  transfers between devices with their start and end apart: 5, of which 1 were waited for; matrix products, arithmetic and copies ran while one was open for 28% of the time, Pallas kernels for 0%

commit v1 on v0

v1 whole, which is shorter than its diff:
```python
import functools

import jax
import jax.numpy as jnp
from jax import lax
from jax.experimental import pallas as pl
from jax.experimental.pallas import tpu as pltpu
from jax.sharding import PartitionSpec as P

XW = 16
ZOUT = 2
CF = 16
ROWS = 8
PAD = 8
F32 = jnp.float32
BF16 = jnp.bfloat16
VMEM_BYTES = 48 * 1024 * 1024


def lane_iota(shape):
    return lax.broadcasted_iota(jnp.int32, shape, len(shape) - 1)


def row_iota(shape):
    return lax.broadcasted_iota(jnp.int32, shape, len(shape) - 2)


def pack_kernel(
    widths, feature, planes, top, bottom, left, right, left_top, left_bottom, right_top, right_bottom,
    cells, pairs, edges, corners, sems,
):
    width = widths[lax.axis_index("gx")]
    count, channels, slots, tile = feature.shape

    def copy_of(z):
        return pltpu.make_async_copy(feature.at[z], planes.at[z], sems.at[z])

    for z in range(count):
        copy_of(z).start()
    corners[...] = jnp.zeros_like(corners)
    half = lane_iota((slots, tile)) // 2
    for z in range(count):
        copy_of(z).wait()
        cells[...] = planes[z].astype(F32).reshape(channels * slots, tile)
        for side, begin in ((0, 0), (1, width - 2)):
            for r in range(2):
                picked = cells[pl.ds(begin + r, channels, stride=slots), :]
                place = (z // ZOUT) * channels * 4 + (z % ZOUT) * 2 + r
                pairs[side, pl.ds(place, channels, stride=4), :] = picked
        low = jnp.zeros((slots, tile), F32)
        high = jnp.zeros((slots, tile), F32)
        for c in range(channels):
            moved = cells[c * slots : (c + 1) * slots, :]
            if c:
                moved = pltpu.roll(moved, 2 * c, 1)
            low = jnp.where(half == c, moved, low)
            high = jnp.where(half == (c - 1) % channels, moved, high)
        high = pltpu.roll(high, 2, 1)
        left[z] = low.astype(BF16)
        right[z] = high.astype(BF16)
        edges[0] = low
        edges[1] = high
        for side in range(2):
            corners[side, 0, 2 * z : 2 * z + 2, :] = edges[side, 0:2, :]
            corners[side, 1, 2 * z : 2 * z + 2, :] = edges[side, pl.ds(width - 2, 2), :]
    top[...] = pairs[0].astype(BF16)
    bottom[...] = pairs[1].astype(BF16)
    left_top[...] = corners[0, 0].astype(BF16)
    left_bottom[...] = corners[0, 1].astype(BF16)
    right_top[...] = corners[1, 0].astype(BF16)
    right_bottom[...] = corners[1, 1].astype(BF16)


def tap_of(m, dx, dy):
    return 9 * m + 3 * (dx + 1) + (dy + 1)


def shifted_sum(centre, before, after):
    lane = lane_iota(centre.shape)
    tile = centre.shape[-1]
    before = jnp.where(lane < 2, 0.0, pltpu.roll(before, 2, 1))
    after = jnp.where(lane >= tile - 2, 0.0, pltpu.roll(after, tile - 2, 1))
    return centre + before + after


def inner_kernel(widths, taps, bias, planes, mix, depth, spread, lane_taps, padded):
    width = widths[lax.axis_index("gx")]
    count, channels, slots, tile = planes.shape
    valid = row_iota((slots, tile)) < width

    def widen(c, carry):
        for z in range(count):
            padded[z, c, 0:PAD, :] = jnp.zeros((PAD, tile), F32)
            padded[z, c, PAD : PAD + slots, :] = jnp.where(valid, planes[z, c].astype(F32), 0.0)
            padded[z, c, PAD + slots : 2 * PAD + slots, :] = jnp.zeros((PAD, tile), F32)
        return carry

    lax.fori_loop(0, channels, widen, 0)

    def convolve(c, carry):
        for out in range(ZOUT):
            for b in range(slots // ROWS):
                sums = [None, None, None]
                for m in range(3):
                    for dx in (-1, 0, 1):
                        rows = padded[out + 2 * m, c, pl.ds(PAD + 2 * dx + ROWS * b, ROWS), :]
                        for dy in (-1, 0, 1):
                            term = taps[tap_of(m, dx, dy), c] * rows
                            held = sums[dy + 1]
                            sums[dy + 1] = term if held is None else held + term
                total = shifted_sum(sums[1], sums[0], sums[2]) + bias[c]
                depth[out, c, ROWS * b : ROWS * (b + 1), :] = total
        return carry

    lax.fori_loop(0, channels, convolve, 0)
    size = channels * ROWS
    tall = (size, channels)
    wide = (channels, size)
    column = lane_iota(tall) * ROWS
    row = row_iota(tall)
    grow = ((row >= column) & (row < column + ROWS)).astype(BF16)
    row = row_iota(wide) * ROWS
    column = lane_iota(wide)
    stretch = ((column >= row) & (column < row + ROWS)).astype(BF16)
    repeated = jnp.dot(grow, mix[...], preferred_element_type=F32).astype(BF16)
    repeated = jnp.dot(repeated, stretch, preferred_element_type=F32)
    square = (size, size)
    same = (row_iota(square) & (ROWS - 1)) == (lane_iota(square) & (ROWS - 1))
    spread[...] = jnp.where(same, repeated, 0.0).astype(BF16)


def finish_kernel(
    widths, taps, pw_bias, lift, planes, spread, lane_taps, lower, upper, from_left, from_right,
    lower_left, upper_left, lower_right, upper_right, coarse, depth_in,
    out, depth,
    rims, rows8, halo, sides, mixed_in, block, sems,
):
    slab = lax.axis_index("gx")
    count, channels, slots, tile = planes.shape
    width = widths[slab]
    slabs = widths.shape[0]
    total = XW * slabs
    start = jnp.int32(0)
    for d in range(slabs):
        start = start + jnp.where(d < slab, widths[d], 0)
    valid = row_iota((slots, tile)) < width

    for side, strip, low, high in (
        (0, from_left, lower_left, upper_left),
        (1, from_right, lower_right, upper_right),
    ):
        rims[0:16, :] = low[...].astype(F32)
        rims[16:32, :] = high[...].astype(F32)
        for z in range(count):
            halo[z, PAD : PAD + slots, :] = jnp.where(valid, strip[z].astype(F32), 0.0)
            halo[z, PAD + slots : 2 * PAD + slots, :] = jnp.zeros((PAD, tile), F32)
            halo[z, PAD - 2 : PAD, :] = rims[2 * z : 2 * z + 2, :]
            halo[z, pl.ds(PAD + width, 2), :] = rims[16 + 2 * z : 18 + 2 * z, :]
        dy = 2 * side - 1
        for o in range(ZOUT):
            held = jnp.zeros((slots, tile), F32)
            for m in range(3):
                for dx in (-1, 0, 1):
                    tap = tap_of(m, dx, dy)
                    held = held + lane_taps[tap : tap + 1, :] * halo[o + 2 * m, PAD + 2 * dx : PAD + 2 * dx + slots, :]
            sides[side, o] = held

    groups = lower.shape[0] // 4
    for side, strip in ((0, lower), (1, upper)):
        rims[...] = strip[...].astype(F32)
        for q in range(4):
            rows8[pl.ds(4 * side + q, groups, stride=8), :] = rims[pl.ds(q, groups, stride=4), :]
    first = row_iota((8, tile)) < 4

    def attach(c, carry):
        sums = [None, None, None]
        for m in range(3):
            rows = rows8[pl.ds(pl.multiple_of((m * channels + c) * 8, 8), 8), :]
            for dy in (-1, 0, 1):
                weight = jnp.where(first, taps[tap_of(m, -1, dy), c], taps[tap_of(m, 1, dy), c])
                held = sums[dy + 1]
                sums[dy + 1] = weight * rows if held is None else held + weight * rows
        added = shifted_sum(sums[1], sums[0], sums[2])
        for o in range(ZOUT):
            depth[o, c, 0:2, :] = depth_in[o, c, 0:2, :] + added[2 * o : 2 * o + 2, :]
            depth[o, c, pl.ds(width - 2, 2), :] = depth_in[o, c, pl.ds(width - 2, 2), :] + added[4 + 2 * o : 6 + 2 * o, :]
        return carry

    lax.fori_loop(0, channels, attach, 0)

    lane = lane_iota((ROWS, tile))

    def gather(pair, carry):
        for o in range(ZOUT):
            for b in range(slots // ROWS):
                both = []
                for k in range(2):
                    c = 2 * pair + k
                    at = slice(ROWS * b, ROWS * (b + 1))
                    before = pltpu.roll(sides[0, o, at, :], tile - 2 * c, 1)
                    after = pltpu.roll(sides[1, o, at, :], tile - 2 - 2 * c, 1)
                    edge = jnp.where(lane < 2, before, jnp.where(lane >= tile - 2, after, 0.0))
                    both.append(depth[o, c, at, :] + edge)
                both = jnp.concatenate(both, axis=0).astype(BF16)
                at = pl.ds(pl.multiple_of(pair * 2 * ROWS, 2 * ROWS), 2 * ROWS)
                mixed_in[b, at, o * tile : (o + 1) * tile] = both
        return carry

    lax.fori_loop(0, channels // 2, gather, 0)

    _, ncx, ncy = coarse.shape
    shape = (ncy, tile)
    cell = row_iota(shape) * CF
    place = lane_iota(shape) + lax.axis_index("gy") * tile
    along_y = ((place >= cell) & (place < cell + CF)).astype(F32)
    shape = (slots, ncx)
    cell = lane_iota(shape) * CF
    place = row_iota(shape) + start
    place = jnp.where(place >= total, place - total, place)
    along_x = ((place >= cell) & (place < cell + CF)).astype(F32)
    lifted = []
    for k in range(coarse.shape[0]):
        wide = jnp.dot(coarse[k], along_y, precision=lax.Precision.HIGHEST, preferred_element_type=F32)
        lifted.append(jnp.dot(along_x, wide, precision=lax.Precision.HIGHEST, preferred_element_type=F32))

    chunk = 16
    copies = []
    for part in range(channels // chunk):
        rows = slice(part * chunk * ROWS, (part + 1) * chunk * ROWS)
        mixed = [
            jnp.dot(spread[rows, :], mixed_in[b], preferred_element_type=F32) for b in range(slots // ROWS)
        ]
        for k in range(chunk):
            o = part * chunk + k
            lift_o = lift[o, 0] * lifted[0] + lift[o, 1] * lifted[1] + lift[o, 2] * lifted[2]
            for z in range(ZOUT):
                value = jnp.concatenate(
                    [m[k * ROWS : (k + 1) * ROWS, z * tile : (z + 1) * tile] for m in mixed], axis=0
                )
                value = value + pw_bias[o]
                value = jnp.where(value > 0, value, 0.2 * value) + lift_o
                value = value + planes[2 + z, o].astype(F32)
                block[z, o] = jnp.where(valid, value, 0.0).astype(BF16)
        for z in range(ZOUT):
            part_of = pl.ds(part * chunk, chunk)
            copy = pltpu.make_async_copy(block.at[z, part_of], out.at[z, part_of], sems.at[part, z])
            copy.start()
            copies.append(copy)
    for copy in copies:
        copy.wait()


def shards(feature, widths, dw_weight, dw_bias, pw_weight, pw_bias, lift_weight, coarse):
    planes, channels, slots, tile = feature.shape
    nx, ny = lax.axis_size("gx"), lax.axis_size("gy")
    smem = pl.BlockSpec(memory_space=pltpu.SMEM)
    vmem = pl.BlockSpec(memory_space=pltpu.VMEM)
    anywhere = pl.BlockSpec(memory_space=pl.ANY)
    params = pltpu.CompilerParams(vmem_limit_bytes=VMEM_BYTES)
    shape = jax.ShapeDtypeStruct
    message = planes // ZOUT * channels * 4
    strip = shape((planes, slots, tile), BF16)
    corner = shape((16, tile), BF16)
    held, top, bottom, left, right, left_top, left_bottom, right_top, right_bottom = pl.pallas_call(
        pack_kernel,
        out_shape=(
            pltpu.VMEM(feature.shape, BF16),
            shape((message, tile), BF16),
            shape((message, tile), BF16),
            strip,
            strip,
            corner,
            corner,
            corner,
            corner,
        ),
        in_specs=[smem, anywhere],
        out_specs=(vmem,) * 9,
        scratch_shapes=[
            pltpu.VMEM((channels * slots, tile), F32),
            pltpu.VMEM((2, message, tile), F32),
            pltpu.VMEM((2, slots, tile), F32),
            pltpu.VMEM((2, 2, 16, tile), F32),
            pltpu.SemaphoreType.DMA((planes,)),
        ],
        compiler_params=params,
    )(widths, feature)

    def sent(array, by_x, by_y):
        route = [
            (x * ny + y, (x + by_x) % nx * ny + (y + by_y) % ny) for x in range(nx) for y in range(ny)
        ]
        return lax.ppermute(array, ("gx", "gy"), route)

    lower = sent(bottom, 1, 0)
    upper = sent(top, -1, 0)
    from_left = sent(right, 0, 1)
    from_right = sent(left, 0, -1)
    lower_left = sent(right_bottom, 1, 1)
    upper_left = sent(right_top, -1, 1)
    lower_right = sent(left_bottom, 1, -1)
    upper_right = sent(left_top, -1, -1)
    every = lax.all_gather(coarse, "gy", axis=1, tiled=True)
    lane_taps = jnp.repeat(dw_weight, 2, axis=1)
    size = channels * ROWS
    depth, spread = pl.pallas_call(
        lambda w, t, b, f, m, d, s, p: inner_kernel(w, t, b, f, m, d, s, None, p),
        out_shape=(pltpu.VMEM((ZOUT, channels, slots, tile), F32), pltpu.VMEM((size, size), BF16)),
        in_specs=[smem, smem, smem, vmem, vmem],
        out_specs=(vmem, vmem),
        scratch_shapes=[pltpu.VMEM((planes, channels, slots + 2 * PAD, tile), F32)],
        compiler_params=params,
        cost_estimate=pl.CostEstimate(flops=10**9, bytes_accessed=3 * 10**6, transcendentals=0),
    )(widths, dw_weight, dw_bias, held, pw_weight)
    out, _ = pl.pallas_call(
        finish_kernel,
        out_shape=(
            shape((ZOUT, channels, slots, tile), BF16),
            pltpu.VMEM((ZOUT, channels, slots, tile), F32),
        ),
        in_specs=[smem, smem, smem, smem] + [vmem] * 13,
        out_specs=(anywhere, vmem),
        scratch_shapes=[
            pltpu.VMEM((message, tile), F32),
            pltpu.VMEM((2 * message, tile), F32),
            pltpu.VMEM((planes, slots + 2 * PAD, tile), F32),
            pltpu.VMEM((2, ZOUT, slots, tile), F32),
            pltpu.VMEM((slots // ROWS, size, ZOUT * tile), BF16),
            pltpu.VMEM((ZOUT, channels, slots, tile), BF16),
            pltpu.SemaphoreType.DMA((channels // 16, ZOUT)),
        ],
        input_output_aliases={16: 1},
        compiler_params=params,
    )(
        widths, dw_weight, pw_bias, lift_weight, held, spread, lane_taps, lower, upper, from_left, from_right,
        lower_left, upper_left, lower_right, upper_right, every, depth,
    )
    return out


def solution(mesh):
    placed = (P(None, None, "gx", "gy"), P(), P(), P(), P(), P(), P(), P(None, "gy", None))
    return jax.shard_map(
        shards, mesh=mesh, in_specs=placed, out_specs=P(None, None, "gx", "gy"), check_vma=False
    )
```

time: 59.6 us -> 62.9 us (1.055)
  the two profiles are of different devices: /device:TPU:18 before, /device:TPU:0 now
where the time goes in v1:
time: 62.9 us; the launch traced here: 62.6 us
  Pallas kernels  27.7 us (44%)
  starting transfers between devices  17.6 us (28%)
  blocking collectives  8.15 us (13%)
  local copies, waits for them, and re-layouts  8.01 us (13%)
  waiting for transfers between devices  0.91 us (1%)
    ppermute x8, starting transfers between devices, sent(): return lax.ppermute(array, ('gx', 'gy'), route)  17.6 us
    pallas_call x1, Pallas kernels, shards(): pl.pallas_call(finish_kernel, out_shape=(shape((ZOUT, channels, slots, ti...  12.4 us
    pallas_call x1, Pallas kernels, shards(): pl.pallas_call(lambda w, t, b, f, m, d, s, p: inner_kernel(w, t, b, f, m,...  10.5 us
    all_gather x1, blocking collectives, shards(): every = lax.all_gather(coarse, 'gy', axis=1, tiled=True)  8.15 us
    unnamed x25, local copies, waits for them, and re-layouts  5.7 us
    pallas_call x1, Pallas kernels, shards(): pl.pallas_call(pack_kernel, out_shape=(pltpu.VMEM(feature.shape, BF16), s...  4.8 us
    broadcast_in_dim x1, local copies, waits for them, and re-layouts, shards(): lane_taps = jnp.repeat(dw_weight, 2, axis=1)  1.41 us
  transfers between devices with their start and end apart: 8, of which 1 were waited for; matrix products, arithmetic and copies ran while one was open for 5% of the time, Pallas kernels for 17%

profile of v1, /device:TPU:0, one launch (start us, length us, event | category | flops | bytes accessed | tf_op | source)
XLA Modules:
  0.0 62.6 jit_solution(12985934116679841981)
XLA Ops:
  0.0 0.0 copy-start
  0.0 1.7 %copy-done = bf16[6,64,24,128]{3,2,1,0:T(8,128)(2,1)S(1)} copy-done((bf16[6,64,24,128]{3,2,1,0:T(8,128)(2,1)S(1)}, bf16[6,64,24,128]{3,2,1,0:T(8,128)(2,1)}, u32[]{:S(2)}) %copy-start) | copy-done | bytes 2359320
  1.7 0.0 copy-start.4
  1.7 0.7 %copy-done.4 = s32[8]{0:T(128)S(1)} copy-done((s32[8]{0:T(128)S(1)}, s32[8]{0:T(128)}, u32[]{:S(2)}) %copy-start.4) | copy-done | bytes 56
  2.3 0.0 copy-start.3
  2.3 0.0 copy-start.7
  2.3 0.0 copy-start.8
  2.3 4.8 %shard_map.82 = (bf16[6,64,24,128]{3,2,1,0:T(8,128)(2,1)S(1)}, bf16[768,128]{1,0:T(8,128)(2,1)}, bf16[768,128]{1,0:T(8,128)(2,1)}, bf16[6,24,128]{2,1,0:T(8,128)...) custom-call(s32[8]{0:T(128)S(1)} %copy-done.4, ...), custom_call_target="tpu_custom_call" | custom-call | tf_op jit(solution)/shard_map/pallas_call | solution.py:264
  7.1 0.0 copy-start.9
  7.1 0.0 copy-start.10
  7.2 0.0 copy-start.5
  7.2 0.0 copy-start.6
  7.2 0.5 collective-permute-start
  7.7 4.1 %collective-permute-start.1 = (bf16[768,128]{1,0:T(8,128)(2,1)}, bf16[768,128]{1,0:T(8,128)(2,1)S(1)}, u32[]{:S(2)}, u32[]{:S(2)}) collective-permute-start(bf16[768,128]{1,0:T(8,128)(2,1)} %get-tuple-element.20), channel_id=1, source_target_pairs={{0,28},{1,29},{2,30},{3,31},{4,0},{5,1},{6,2},{7,3},{8,4},{9,5},{1... | collective-permute-start | bytes 589832 | tf_op jit(solution)/shard_map/ppermute | solution.py:293
  11.8 0.0 collective-permute-start.4
  11.8 5.8 %collective-permute-start.5 = (bf16[16,128]{1,0:T(8,128)(2,1)S(1)}, bf16[16,128]{1,0:T(8,128)(2,1)S(1)}, u32[]{:S(2)}, u32[]{:S(2)}) collective-permute-start(bf16[16,128]{1,0:T(8,128)(2,1)S(1)} %get-tuple-element.24), channel_id=1, source_target_pairs={{0,29},{1,30},{2,31},{3,28},{4,1},{5,2},{6,3},{7,0},{8,5},{9,6},{1... | collective-permute-start | bytes 12296 | tf_op jit(solution)/shard_map/ppermute | solution.py:293
  17.6 0.0 collective-permute-start.6
  17.6 0.9 %collective-permute-done.4.lower_left = bf16[16,128]{1,0:T(8,128)(2,1)S(1)} collective-permute-done((bf16[16,128]{1,0:T(8,128)(2,1)S(1)}, bf16[16,128]{1,0:T(8,128)(2,1)S(1)}, u32[]{:S(2)}, u32[]{:S(2)}) %collective-permute-start.4) | collective-permute-done | bytes 4128 | tf_op jit(solution)/shard_map/ppermute | solution.py:293
  18.5 3.1 %collective-permute-start.7 = (bf16[16,128]{1,0:T(8,128)(2,1)S(1)}, bf16[16,128]{1,0:T(8,128)(2,1)S(1)}, u32[]{:S(2)}, u32[]{:S(2)}) collective-permute-start(bf16[16,128]{1,0:T(8,128)(2,1)S(1)} %get-tuple-element.26), channel_id=1, source_target_pairs={{0,31},{1,28},{2,29},{3,30},{4,3},{5,0},{6,1},{7,2},{8,7},{9,4},{1... | collective-permute-start | bytes 12296 | tf_op jit(solution)/shard_map/ppermute | solution.py:293
  21.6 0.0 collective-permute-done.5.upper_left
  21.6 1.9 %collective-permute-start.2 = (bf16[6,24,128]{2,1,0:T(8,128)(2,1)S(1)}, bf16[6,24,128]{2,1,0:T(8,128)(2,1)S(1)}, u32[]{:S(2)}, u32[]{:S(2)}) collective-permute-start(bf16[6,24,128]{2,1,0:T(8,128)(2,1)S(1)} %get-tuple-element.21), channel_id=1, source_target_pairs={{0,1},{1,2},{2,3},{3,0},{4,5},{5,6},{6,7},{7,4},{8,9},{9,10},{10,1... | collective-permute-start | bytes 110600 | tf_op jit(solution)/shard_map/ppermute | solution.py:293
  23.5 0.0 collective-permute-done.6.lower_right
  23.5 2.2 %collective-permute-start.3 = (bf16[6,24,128]{2,1,0:T(8,128)(2,1)S(1)}, bf16[6,24,128]{2,1,0:T(8,128)(2,1)S(1)}, u32[]{:S(2)}, u32[]{:S(2)}) collective-permute-start(bf16[6,24,128]{2,1,0:T(8,128)(2,1)S(1)} %get-tuple-element.22), channel_id=1, source_target_pairs={{0,3},{1,0},{2,1},{3,2},{4,7},{5,4},{6,5},{7,6},{8,11},{9,8},{10,9... | collective-permute-start | bytes 110600 | tf_op jit(solution)/shard_map/ppermute | solution.py:293
  25.7 0.0 copy-done.3
  25.7 0.0 copy-done.7
  25.7 0.0 copy-done.8
  25.7 10.5 %shard_map.83 = (f32[2,64,24,128]{3,2,1,0:T(8,128)S(1)}, bf16[512,512]{1,0:T(8,128)(2,1)S(1)}) custom-call(s32[8]{0:T(128)S(1)} %copy-done.4, f32[27,64]{1,0:T(8,128)S(1)} %copy-done.3, f32[64]{0:T(128)S(1)} %copy-done.8, bf16[6,64,24,128]{3,2,1,0:T(8,128)(2,1)S(1)} %get-tuple-element.17.f.planes, bf16[64,64]{1,0:T(8,128)(2,1)S(1)} %copy-done.7), custom_call_target="tpu_custom_call" | custom-call | flops 1000000000 | bytes 3000000 | tf_op jit(solution)/shard_map/pallas_call | solution.py:306
  36.2 0.0 copy-start.1
  36.2 1.2 %copy-done.1 = f32[2,64,24,128]{3,2,1,0:T(8,128)} copy-done((f32[2,64,24,128]{3,2,1,0:T(8,128)}, f32[2,64,24,128]{3,2,1,0:T(8,128)S(1)}, u32[]{:S(2)}) %copy-start.1) | copy-done | bytes 1572888
  37.4 0.7 %copy.14 = f32[27,64]{0,1:T(8,128)} copy(f32[27,64]{1,0:T(8,128)S(1)} %copy-done.3) | data formatting | bytes 13824 | tf_op args[2]
  38.1 0.0 copy-done.9
  38.1 8.2 %all_gather.3 = f32[3,8,32]{2,0,1:T(4,128)S(1)} all-gather(f32[3,2,32]{2,0,1:T(4,128)S(1)} %copy.15), channel_id=1, replica_groups=mesh['gx'=8,'gy'=4] {'gy'}, dimensions={1}, use_global_device_ids=true | all-gather | bytes 3840 | tf_op jit(solution)/shard_map/all_gather | solution.py:303
  46.3 0.0 copy-done.10
  46.3 0.1 copy.16.lift
  46.4 1.4 %broadcast_in_dim.3 = f32[27,64,2]{0,2,1:T(2,128)} broadcast(f32[27,64]{0,1:T(8,128)} %copy.14), dimensions={0,1} | broadcast | bytes 20736 | tf_op jit(solution)/shard_map/broadcast_in_dim | solution.py:304
  47.8 0.9 %copy.17.lane_taps = f32[27,128]{1,0:T(8,128)S(1)} copy(f32[27,128]{0,1:T(8,128)} %bitcast.1) | data formatting | bytes 27648 | tf_op jit(solution)/shard_map/reshape | solution.py:304
  48.7 0.0 collective-permute-done.7.upper_right
  48.7 0.0 collective-permute-done.2.from_left
  48.7 0.0 collective-permute-done.3.from_right
  48.7 0.0 collective-permute-done.lower
  48.7 0.0 collective-permute-done.1.upper
  48.7 0.0 copy-done.5
  48.7 0.0 copy-done.6
  48.7 0.0 copy-start.2
  48.8 1.4 %copy-done.2 = f32[2,64,24,128]{3,2,1,0:T(8,128)S(1)} copy-done((f32[2,64,24,128]{3,2,1,0:T(8,128)S(1)}, f32[2,64,24,128]{3,2,1,0:T(8,128)}, u32[]{:S(2)}) %copy-start.2) | copy-done | bytes 1572888
  50.2 12.4 %shard_map.84 = (bf16[2,64,24,128]{3,2,1,0:T(8,128)(2,1)}, f32[2,64,24,128]{3,2,1,0:T(8,128)S(1)}) custom-call(s32[8]{0:T(128)S(1)} %copy-done.5, f32[27,64]{1,0:T(8,128)S(1)} %copy-done.3, f32[64]{0:T(128)S(1)} %copy-done.6, f32[64,3]{1,0:T(8,128)S(1)} %copy.16.lift, ...), custom_call_target="tpu_custom_call", output_to_operand_aliasing={{1}: (16, {})} | custom-call | tf_op jit(solution)/shard_map/pallas_call | solution.py:315
  (2 shorter events, 0.0 us)
Async XLA Ops:
  0.0 1.7 %copy-start = (bf16[6,64,24,128]{3,2,1,0:T(8,128)(2,1)S(1)}, bf16[6,64,24,128]{3,2,1,0:T(8,128)(2,1)}, u32[]{:S(2)}) copy-start(bf16[6,64,24,128]{3,2,1,0:T(8,128)(2,1)} %feature.1) | copy-start | bytes 7077892
  1.7 0.7 %copy-start.4 = (s32[8]{0:T(128)S(1)}, s32[8]{0:T(128)}, u32[]{:S(2)}) copy-start(s32[8]{0:T(128)} %widths.3) | copy-start | bytes 100
  2.3 23.4 %copy-start.3 = (f32[27,64]{1,0:T(8,128)S(1)}, f32[27,64]{1,0:T(8,128)}, u32[]{:S(2)}) copy-start(f32[27,64]{1,0:T(8,128)} %taps.1) | copy-start | bytes 20740
  2.3 23.4 %copy-start.7 = (bf16[64,64]{1,0:T(8,128)(2,1)S(1)}, bf16[64,64]{1,0:T(8,128)(2,1)}, u32[]{:S(2)}) copy-start(bf16[64,64]{1,0:T(8,128)(2,1)} %m.1) | copy-start | bytes 24580
  2.3 23.4 %copy-start.8 = (f32[64]{0:T(128)S(1)}, f32[64]{0:T(128)}, u32[]{:S(2)}) copy-start(f32[64]{0:T(128)} %b.1) | copy-start | bytes 772
  7.1 31.0 %copy-start.9 = (f32[3,2,32]{2,1,0:T(2,128)S(1)}, f32[3,2,32]{2,1,0:T(2,128)}, u32[]{:S(2)}) copy-start(f32[3,2,32]{2,1,0:T(2,128)} %param.15) | copy-start | bytes 2308
  7.1 39.1 %copy-start.10 = (f32[64,3]{0,1:T(4,128)S(1)}, f32[64,3]{0,1:T(4,128)}, u32[]{:S(2)}) copy-start(f32[64,3]{0,1:T(4,128)} %param.14) | copy-start | bytes 2308
  7.2 41.6 %copy-start.5 = (s32[8]{0:T(128)S(1)}, s32[8]{0:T(128)}, u32[]{:S(2)}) copy-start(s32[8]{0:T(128)} %widths.3) | copy-start | bytes 100
  7.2 41.6 %copy-start.6 = (f32[64]{0:T(128)S(1)}, f32[64]{0:T(128)}, u32[]{:S(2)}) copy-start(f32[64]{0:T(128)} %pw_bias.1) | copy-start | bytes 772
  7.2 41.5 %collective-permute-start = (bf16[768,128]{1,0:T(8,128)(2,1)}, bf16[768,128]{1,0:T(8,128)(2,1)S(1)}, u32[]{:S(2)}, u32[]{:S(2)}) collective-permute-start(bf16[768,128]{1,0:T(8,128)(2,1)} %get-tuple-element.19), channel_id=1, source_target_pairs={{0,4},{1,5},{2,6},{3,7},{4,8},{5,9},{6,10},{7,11},{8,12},{9,13},{1... | collective-permute-start | bytes 589832 | tf_op jit(solution)/shard_map/ppermute | solution.py:293
  7.7 41.0 %collective-permute-start.1 = (bf16[768,128]{1,0:T(8,128)(2,1)}, bf16[768,128]{1,0:T(8,128)(2,1)S(1)}, u32[]{:S(2)}, u32[]{:S(2)}) collective-permute-start(bf16[768,128]{1,0:T(8,128)(2,1)} %get-tuple-element.20), channel_id=1, source_target_pairs={{0,28},{1,29},{2,30},{3,31},{4,0},{5,1},{6,2},{7,3},{8,4},{9,5},{1... | collective-permute-start | bytes 589832 | tf_op jit(solution)/shard_map/ppermute | solution.py:293
  11.8 6.7 %collective-permute-start.4 = (bf16[16,128]{1,0:T(8,128)(2,1)S(1)}, bf16[16,128]{1,0:T(8,128)(2,1)S(1)}, u32[]{:S(2)}, u32[]{:S(2)}) collective-permute-start(bf16[16,128]{1,0:T(8,128)(2,1)S(1)} %get-tuple-element.23), channel_id=1, source_target_pairs={{0,5},{1,6},{2,7},{3,4},{4,9},{5,10},{6,11},{7,8},{8,13},{9,14},{1... | collective-permute-start | bytes 12296 | tf_op jit(solution)/shard_map/ppermute | solution.py:293
  11.8 9.8 %collective-permute-start.5 = (bf16[16,128]{1,0:T(8,128)(2,1)S(1)}, bf16[16,128]{1,0:T(8,128)(2,1)S(1)}, u32[]{:S(2)}, u32[]{:S(2)}) collective-permute-start(bf16[16,128]{1,0:T(8,128)(2,1)S(1)} %get-tuple-element.24), channel_id=1, source_target_pairs={{0,29},{1,30},{2,31},{3,28},{4,1},{5,2},{6,3},{7,0},{8,5},{9,6},{1... | collective-permute-start | bytes 12296 | tf_op jit(solution)/shard_map/ppermute | solution.py:293
  17.6 5.9 %collective-permute-start.6 = (bf16[16,128]{1,0:T(8,128)(2,1)S(1)}, bf16[16,128]{1,0:T(8,128)(2,1)S(1)}, u32[]{:S(2)}, u32[]{:S(2)}) collective-permute-start(bf16[16,128]{1,0:T(8,128)(2,1)S(1)} %get-tuple-element.25), channel_id=1, source_target_pairs={{0,7},{1,4},{2,5},{3,6},{4,11},{5,8},{6,9},{7,10},{8,15},{9,12},{1... | collective-permute-start | bytes 12296 | tf_op jit(solution)/shard_map/ppermute | solution.py:293
  18.5 30.2 %collective-permute-start.7 = (bf16[16,128]{1,0:T(8,128)(2,1)S(1)}, bf16[16,128]{1,0:T(8,128)(2,1)S(1)}, u32[]{:S(2)}, u32[]{:S(2)}) collective-permute-start(bf16[16,128]{1,0:T(8,128)(2,1)S(1)} %get-tuple-element.26), channel_id=1, source_target_pairs={{0,31},{1,28},{2,29},{3,30},{4,3},{5,0},{6,1},{7,2},{8,7},{9,4},{1... | collective-permute-start | bytes 12296 | tf_op jit(solution)/shard_map/ppermute | solution.py:293
  21.6 27.1 %collective-permute-start.2 = (bf16[6,24,128]{2,1,0:T(8,128)(2,1)S(1)}, bf16[6,24,128]{2,1,0:T(8,128)(2,1)S(1)}, u32[]{:S(2)}, u32[]{:S(2)}) collective-permute-start(bf16[6,24,128]{2,1,0:T(8,128)(2,1)S(1)} %get-tuple-element.21), channel_id=1, source_target_pairs={{0,1},{1,2},{2,3},{3,0},{4,5},{5,6},{6,7},{7,4},{8,9},{9,10},{10,1... | collective-permute-start | bytes 110600 | tf_op jit(solution)/shard_map/ppermute | solution.py:293
  23.5 25.2 %collective-permute-start.3 = (bf16[6,24,128]{2,1,0:T(8,128)(2,1)S(1)}, bf16[6,24,128]{2,1,0:T(8,128)(2,1)S(1)}, u32[]{:S(2)}, u32[]{:S(2)}) collective-permute-start(bf16[6,24,128]{2,1,0:T(8,128)(2,1)S(1)} %get-tuple-element.22), channel_id=1, source_target_pairs={{0,3},{1,0},{2,1},{3,2},{4,7},{5,4},{6,5},{7,6},{8,11},{9,8},{10,9... | collective-permute-start | bytes 110600 | tf_op jit(solution)/shard_map/ppermute | solution.py:293
  36.2 1.2 %copy-start.1 = (f32[2,64,24,128]{3,2,1,0:T(8,128)}, f32[2,64,24,128]{3,2,1,0:T(8,128)S(1)}, u32[]{:S(2)}) copy-start(f32[2,64,24,128]{3,2,1,0:T(8,128)S(1)} %get-tuple-element.27.depth_in) | copy-start | bytes 4718596
  48.7 1.4 %copy-start.2 = (f32[2,64,24,128]{3,2,1,0:T(8,128)S(1)}, f32[2,64,24,128]{3,2,1,0:T(8,128)}, u32[]{:S(2)}) copy-start(f32[2,64,24,128]{3,2,1,0:T(8,128)} %copy-done.1) | copy-start | bytes 4718596

commit v2 on v0

v2 whole, which is shorter than its diff:
```python
import jax
import jax.numpy as jnp
from jax import lax
from jax.experimental import pallas as pl
from jax.experimental.pallas import tpu as pltpu
from jax.sharding import PartitionSpec as P

XW = 16
ZOUT = 2
CF = 16
ROWS = 8
OUTER = 32
F32 = jnp.float32
BF16 = jnp.bfloat16
VMEM_BYTES = 48 * 1024 * 1024


def lane_iota(shape):
    return lax.broadcasted_iota(jnp.int32, shape, len(shape) - 1)


def row_iota(shape):
    return lax.broadcasted_iota(jnp.int32, shape, len(shape) - 2)


def tap_of(m, dx, dy):
    return 9 * m + 3 * (dx + 1) + (dy + 1)


def is_even(axis):
    return lax.rem(lax.axis_index(axis), 2) == 0


def pack_kernel(widths, feature, taps, planes, band, first, second, tap_rows, masks, sems):
    width = widths[lax.axis_index("gx")]
    count, channels, slots, tile = feature.shape
    depth = 3 * slots
    lanes = band.shape[2]

    def copy_of(z):
        return pltpu.make_async_copy(feature.at[z], planes.at[z], sems.at[z])

    for z in range(count):
        copy_of(z).start()

    shape = (taps.shape[0], lanes)
    lane = lane_iota(shape)
    segment = sum((lane >= slots * i).astype(jnp.int32) for i in range(1, 6))
    high = taps[...].astype(BF16)
    low = (taps[...] - high.astype(F32)).astype(BF16)
    over_taps = (((0,), (0,)), ((), ()))
    for k in range(9):
        row = row_iota(shape)
        in_high = ((row == 9 * segment + k) & (lane < depth)).astype(BF16)
        in_low = ((row == 9 * (segment - 3) + k) & (lane >= depth) & (lane < 2 * depth)).astype(BF16)
        tap_rows[k] = lax.dot_general(high, in_high, over_taps, preferred_element_type=F32) + lax.dot_general(
            low, in_low, over_taps, preferred_element_type=F32
        )
    shape = (OUTER, lanes)
    lane = lane_iota(shape)
    segment = sum((lane >= slots * i).astype(jnp.int32) for i in range(1, 6))
    source = lane - slots * segment
    row = row_iota(shape)
    target = jnp.where(row < slots, row, jnp.where(row < slots + 2, row - slots - 2, row - slots - 2 + width))
    target = jnp.where(row < slots + 4, target, 4 * OUTER)
    known = (lane < 2 * depth) & (source < width)
    for dx in (-1, 0, 1):
        masks[dx + 1] = ((source == target + 2 * dx) & known).astype(F32)

    def build(c, carry):
        for dy in (-1, 0, 1):
            total = None
            for dx in (-1, 0, 1):
                term = masks[dx + 1] * tap_rows[3 * (dx + 1) + dy + 1, pl.ds(c, 1), :]
                total = term if total is None else total + term
            band[c, OUTER * (dy + 1) : OUTER * (dy + 2), :] = total.astype(BF16)
        return carry

    lax.fori_loop(0, channels, build, 0, unroll=2)

    lane = lane_iota((slots, tile))
    even = is_even("gy")

    def merged(z, level, c):
        if level == 0:
            return planes[z, c].astype(F32)
        step = tile >> level
        one = merged(z, level - 1, c)
        other = pltpu.roll(merged(z, level - 1, c + step // 2), step, 1)
        if step > 2:
            return jnp.where(((lane + step // 2) & step) != 0, other, one)
        return jnp.where((lane & 2) != 0, other, one), jnp.where((lane & 2) != 0, one, other)

    for z in range(count):
        copy_of(z).wait()
        left, right = merged(z, channels.bit_length() - 1, 0)
        right = pltpu.roll(right, 2, 1)
        first[z] = jnp.where(even, right, left).astype(BF16)
        second[z] = jnp.where(even, left, right).astype(BF16)


def shifted_sum(centre, before, after):
    lane = lane_iota(centre.shape)
    tile = centre.shape[-1]
    before = jnp.where(lane < 2, 0.0, pltpu.roll(before, 2, 1))
    after = jnp.where(lane >= tile - 2, 0.0, pltpu.roll(after, tile - 2, 1))
    return centre + before + after


def conv_kernel(bias, planes, band, depth):
    count, channels, slots, tile = planes.shape
    inside = row_iota((OUTER, tile)) < slots

    def convolve(c, carry):
        cells = jnp.concatenate(
            [
                jnp.concatenate([planes[z + ZOUT * m, c] for m in range(3)] * 2, axis=0)
                for z in range(ZOUT)
            ],
            axis=1,
        )
        sums = jnp.dot(band[c][:, : cells.shape[0]], cells, preferred_element_type=F32)
        for z in range(ZOUT):
            part = [sums[OUTER * k : OUTER * (k + 1), z * tile : (z + 1) * tile] for k in range(3)]
            total = shifted_sum(part[1], part[0], part[2])
            at = pl.ds(pl.multiple_of(c * OUTER, OUTER), OUTER)
            depth[z, at, :] = total + jnp.where(inside, bias[c], 0.0)
        return carry

    lax.fori_loop(0, channels, convolve, 0, unroll=4)


def rim_kernel(widths, taps, first, second, depth, edge, near, far, strips, held, beyond, tail):
    width = widths[lax.axis_index("gx")]
    count, slots, tile = first.shape
    channels = taps.shape[1]
    pad = 8
    wide = 2 * tile

    shape = (wide, wide)
    row = row_iota(shape)
    own = row & (tile - 1)
    from_right = (row < tile) == is_even("gy")
    target = ((own >> 1) << 2) + (own & 1) + jnp.where(from_right, 0, 2)
    spread = (lane_iota(shape) == target).astype(BF16)
    both = jnp.concatenate(
        [first[...].reshape(count * slots, tile), second[...].reshape(count * slots, tile)], axis=1
    )
    both = jnp.dot(both, spread, preferred_element_type=F32)
    valid = row_iota((slots, wide)) < width
    for z in range(count):
        strips[z, 0:pad, :] = jnp.zeros((pad, wide), F32)
        strips[z, pad : pad + slots, :] = jnp.where(valid, both[z * slots : (z + 1) * slots, :], 0.0)
        strips[z, pad + slots : 2 * pad + slots, :] = jnp.zeros((pad, wide), F32)
    shape = (channels, wide)
    spread = ((lane_iota(shape) >> 2) == row_iota(shape)).astype(F32)
    along = jnp.dot(taps[...], spread, precision=lax.Precision.HIGHEST, preferred_element_type=F32)
    on_left = (lane_iota((1, wide)) & 2) != 0
    size = slots + 4
    for z in range(ZOUT):
        total = None
        for m in range(3):
            for dx in (-1, 0, 1):
                before, after = tap_of(m, dx, -1), tap_of(m, dx, 1)
                weight = jnp.where(on_left, along[before : before + 1, :], along[after : after + 1, :])
                begin = pad - 4 + 2 * dx
                term = weight * strips[z + ZOUT * m, begin : begin + slots + 8, :]
                total = term if total is None else total + term
        for h in range(2):
            held[h] = total[:, h * tile : (h + 1) * tile]
            edge[z, h] = held[h, 4 : 4 + slots, :]
            beyond[z, h, 0:2, :] = held[h, 2:4, :]
            beyond[z, h, 2:4, :] = held[h, pl.ds(4 + width, 2), :]
            beyond[z, h, 4:8, :] = jnp.zeros((4, tile), F32)

    lane = lane_iota((ROWS, tile))
    per_tile = tile // 4
    for z in range(ZOUT):
        for c in range(channels):
            cells = pltpu.roll(beyond[z, c // per_tile], (tile - 2 - 4 * (c % per_tile)) % tile, 1)
            cells = jnp.where((lane < 2) | (lane >= tile - 2), cells, 0.0)
            at = slice(c * OUTER + slots, (c + 1) * OUTER)
            row = (z * channels + c) * ROWS
            tail[row : row + ROWS, :] = depth[z, at, :] + cells
    even = is_even("gx")
    rows = ZOUT * channels
    for r in range(2):
        to_lower = tail[pl.ds(r, rows, stride=ROWS), :]
        to_upper = tail[pl.ds(2 + r, rows, stride=ROWS), :]
        at = slice(r * rows, (r + 1) * rows)
        near[at, :] = jnp.where(even, to_upper, to_lower).astype(BF16)
        far[at, :] = jnp.where(even, to_lower, to_upper).astype(BF16)


def settle_kernel(widths, mix, coarse, edge, depth_in, depth, spread, lifted):
    slab = lax.axis_index("gx")
    slabs = widths.shape[0]
    channels = mix.shape[0]
    _, _, slots, tile = edge.shape
    lane = lane_iota((slots, tile))
    per_tile = tile // 4
    for z in range(ZOUT):
        for c in range(channels):
            cells = pltpu.roll(edge[z, c // per_tile], (tile - 2 - 4 * (c % per_tile)) % tile, 1)
            cells = jnp.where((lane < 2) | (lane >= tile - 2), cells, 0.0)
            at = slice(c * OUTER, c * OUTER + slots)
            depth[z, at, :] = depth_in[z, at, :] + cells

    size = channels * ROWS
    tall = (size, channels)
    flat = (channels, size)
    grow = ((row_iota(tall) >> 3) == lane_iota(tall)).astype(BF16)
    stretch = ((lane_iota(flat) >> 3) == row_iota(flat)).astype(BF16)
    repeated = jnp.dot(grow, mix[...], preferred_element_type=F32).astype(BF16)
    repeated = jnp.dot(repeated, stretch, preferred_element_type=F32)
    square = (size, size)
    same = (row_iota(square) & (ROWS - 1)) == (lane_iota(square) & (ROWS - 1))
    spread[...] = jnp.where(same, repeated, 0.0).astype(BF16)

    total = XW * slabs
    start = jnp.int32(0)
    for d in range(slabs):
        start = start + jnp.where(d < slab, widths[d], 0)
    parts, ncx, own = coarse.shape
    shape = (own, tile)
    cell = row_iota(shape) * CF
    place = lane_iota(shape)
    along_y = ((place >= cell) & (place < cell + CF)).astype(F32)
    shape = (slots, ncx)
    cell = lane_iota(shape) * CF
    place = row_iota(shape) + start
    place = jnp.where(place >= total, place - total, place)
    along_x = ((place >= cell) & (place < cell + CF)).astype(F32)
    for k in range(parts):
        across = jnp.dot(coarse[k], along_y, precision=lax.Precision.HIGHEST, preferred_element_type=F32)
        lifted[k] = jnp.dot(along_x, across, precision=lax.Precision.HIGHEST, preferred_element_type=F32)


def finish_kernel(widths, pw_bias, lift, planes, spread, lifted, near, far, depth_in, out, depth, mixed_in, block, sems):
    slab = lax.axis_index("gx")
    width = widths[slab]
    count, channels, slots, tile = planes.shape
    even = is_even("gx")
    rows = ZOUT * channels
    for arrived, at_top in ((near, jnp.logical_not(even)), (far, even)):
        begin = jnp.where(at_top, 0, width - 2)
        for r in range(2):
            for z in range(ZOUT):
                at = pl.ds(begin + r, channels, stride=OUTER)
                begin_row = r * rows + z * channels
                depth[z, at, :] = depth_in[z, at, :] + arrived[begin_row : begin_row + channels, :].astype(F32)
    for c in range(0, channels, 2):
        for z in range(ZOUT):
            for b in range(slots // ROWS):
                both = [depth[z, (c + k) * OUTER + ROWS * b : (c + k) * OUTER + ROWS * (b + 1), :] for k in range(2)]
                both = jnp.concatenate(both, axis=0).astype(BF16)
                mixed_in[b, c * ROWS : (c + 2) * ROWS, z * tile : (z + 1) * tile] = both

    valid = row_iota((slots, tile)) < width
    chunk = 16
    copies = []
    for part in range(channels // chunk):
        picked = slice(part * chunk * ROWS, (part + 1) * chunk * ROWS)
        mixed = [
            jnp.dot(spread[picked, :], mixed_in[b], preferred_element_type=F32) for b in range(slots // ROWS)
        ]
        for k in range(chunk):
            o = part * chunk + k
            lift_o = lift[o, 0] * lifted[0] + lift[o, 1] * lifted[1] + lift[o, 2] * lifted[2]
            for z in range(ZOUT):
                value = jnp.concatenate(
                    [m[k * ROWS : (k + 1) * ROWS, z * tile : (z + 1) * tile] for m in mixed], axis=0
                )
                value = value + pw_bias[o]
                value = jnp.maximum(value, 0.2 * value) + lift_o
                value = value + planes[2 + z, o].astype(F32)
                block[z, o] = jnp.where(valid, value, 0.0).astype(BF16)
        for z in range(ZOUT):
            part_of = pl.ds(part * chunk, chunk)
            copy = pltpu.make_async_copy(block.at[z, part_of], out.at[z, part_of], sems.at[part, z])
            copy.start()
            copies.append(copy)
    for copy in copies:
        copy.wait()


def shards(feature, widths, dw_weight, dw_bias, pw_weight, pw_bias, lift_weight, coarse):
    planes, channels, slots, tile = feature.shape
    smem = pl.BlockSpec(memory_space=pltpu.SMEM)
    vmem = pl.BlockSpec(memory_space=pltpu.VMEM)
    hbm = pl.BlockSpec(memory_space=pltpu.HBM)
    params = pltpu.CompilerParams(vmem_limit_bytes=VMEM_BYTES)
    shape = jax.ShapeDtypeStruct
    strip = shape((planes, slots, tile), BF16)
    depth_shape = pltpu.VMEM((ZOUT, channels * OUTER, tile), F32)
    message = shape((2 * ZOUT * channels, tile), BF16)
    size = channels * ROWS

    def swapped(array, axis, first):
        count = lax.axis_size(axis)
        pairs = []
        for i in range(first, count + first, 2):
            a, b = i % count, (i + 1) % count
            pairs += [(a, b), (b, a)]
        return lax.ppermute(array, axis, pairs)

    local = lax.all_to_all(coarse, "gy", split_axis=2, concat_axis=1, tiled=True)
    held, band, first, second = pl.pallas_call(
        pack_kernel,
        out_shape=(
            pltpu.VMEM(feature.shape, BF16),
            pltpu.VMEM((channels, 3 * OUTER, 2 * tile), BF16),
            strip,
            strip,
        ),
        in_specs=[smem, hbm, vmem],
        out_specs=(vmem,) * 4,
        scratch_shapes=[
            pltpu.VMEM((9, channels, 2 * tile), F32),
            pltpu.VMEM((3, OUTER, 2 * tile), F32),
            pltpu.SemaphoreType.DMA((planes,)),
        ],
        compiler_params=params,
    )(widths, feature, dw_weight)
    first = swapped(first, "gy", 0)
    second = swapped(second, "gy", 1)
    depth = pl.pallas_call(
        conv_kernel,
        out_shape=depth_shape,
        in_specs=[smem, vmem, vmem],
        out_specs=vmem,
        compiler_params=params,
        cost_estimate=pl.CostEstimate(flops=10**9, bytes_accessed=10**6, transcendentals=0),
    )(dw_bias, held, band)
    edge, near, far = pl.pallas_call(
        rim_kernel,
        out_shape=(pltpu.VMEM((ZOUT, 2, slots, tile), F32), message, message),
        in_specs=[smem] + [vmem] * 4,
        out_specs=(vmem,) * 3,
        scratch_shapes=[
            pltpu.VMEM((planes, slots + 16, 2 * tile), F32),
            pltpu.VMEM((2, slots + 8, tile), F32),
            pltpu.VMEM((ZOUT, 2, ROWS, tile), F32),
            pltpu.VMEM((ZOUT * channels * ROWS, tile), F32),
        ],
        compiler_params=params,
    )(widths, dw_weight, first, second, depth)
    near = swapped(near, "gx", 0)
    far = swapped(far, "gx", 1)
    depth, spread, lifted = pl.pallas_call(
        settle_kernel,
        out_shape=(depth_shape, pltpu.VMEM((size, size), BF16), pltpu.VMEM((3, slots, tile), F32)),
        in_specs=[smem] + [vmem] * 4,
        out_specs=(vmem,) * 3,
        input_output_aliases={4: 0},
        compiler_params=params,
        cost_estimate=pl.CostEstimate(flops=10**9, bytes_accessed=10**6, transcendentals=0),
    )(widths, pw_weight, local, edge, depth)
    out, _ = pl.pallas_call(
        finish_kernel,
        out_shape=(shape((ZOUT, channels, slots, tile), BF16), depth_shape),
        in_specs=[smem, smem, smem] + [vmem] * 6,
        out_specs=(hbm, vmem),
        scratch_shapes=[
            pltpu.VMEM((slots // ROWS, size, ZOUT * tile), BF16),
            pltpu.VMEM((ZOUT, channels, slots, tile), BF16),
            pltpu.SemaphoreType.DMA((channels // 16, ZOUT)),
        ],
        input_output_aliases={8: 1},
        compiler_params=params,
    )(widths, pw_bias, lift_weight, held, spread, lifted, near, far, depth)
    return out


def solution(mesh):
    placed = (P(None, None, "gx", "gy"), P(), P(), P(), P(), P(), P(), P(None, "gy", None))
    return jax.shard_map(
        shards, mesh=mesh, in_specs=placed, out_specs=P(None, None, "gx", "gy"), check_vma=False
    )
```

time: 59.6 us -> 37.2 us (0.62)
  the two profiles are of different devices: /device:TPU:18 before, /device:TPU:0 now
where the time goes in v2:
time: 37.2 us; the launch traced here: 36.8 us
  Pallas kernels  17.7 us (48%)
  starting transfers between devices  12.4 us (33%)
  local copies, waits for them, and re-layouts  6.09 us (16%)
  waiting for transfers between devices  0.49 us (1%)
    ppermute x4, starting transfers between devices, swapped(): return lax.ppermute(array, axis, pairs)  7.26 us
    pallas_call x1, Pallas kernels, shards(): pl.pallas_call(conv_kernel, out_shape=depth_shape, in_specs=[smem, vmem,...  6.59 us
    unnamed x24, local copies, waits for them, and re-layouts  5.96 us
    pallas_call x1, Pallas kernels, shards(): pl.pallas_call(pack_kernel, out_shape=(pltpu.VMEM(feature.shape, BF16), p...  5.24 us
    all_to_all x1, starting transfers between devices, shards(): lax.all_to_all(coarse, 'gy', split_axis=2, concat_axis=1, tiled=True)  5.16 us
    pallas_call x1, Pallas kernels, shards(): pl.pallas_call(finish_kernel, out_shape=(shape((ZOUT, channels, slots, ti...  3.29 us
    pallas_call x1, Pallas kernels, shards(): pl.pallas_call(settle_kernel, out_shape=(depth_shape, pltpu.VMEM((size, s...  1.55 us
    pallas_call x1, Pallas kernels, shards(): pl.pallas_call(rim_kernel, out_shape=(pltpu.VMEM((ZOUT, 2, slots, tile),...  1.06 us
  transfers between devices with their start and end apart: 5, of which 1 were waited for; matrix products, arithmetic and copies ran while one was open for 1% of the time, Pallas kernels for 36%

profile of v2, /device:TPU:0, one launch (start us, length us, event | category | flops | bytes accessed | tf_op | source)
XLA Modules:
  0.0 36.8 jit_solution(6008961531351771473)
XLA Ops:
  0.0 0.0 copy-start.7
  0.0 1.4 %copy.16 = f32[3,2,32]{0,1,2:T(2,128)} copy(f32[3,2,32]{2,1,0:T(2,128)} %param.15) | data formatting | bytes 1536 | tf_op args[7]
  1.4 5.2 %all-to-all-start = ((f32[3,2,32]{0,1,2:T(2,128)}), f32[3,2,32]{0,1,2:T(2,128)S(1)}, u32[]{:S(2)}, u32[]{:S(2)}) async-start(f32[3,2,32]{0,1,2:T(2,128)} %copy.16), calls=%async_computation | async-start | bytes 65536 | tf_op jit(solution)/shard_map/all_to_all | solution.py:307
  6.6 0.0 copy-start.3
  6.6 0.7 %copy-done.3 = f32[27,64]{1,0:T(8,128)S(1)} copy-done((f32[27,64]{1,0:T(8,128)S(1)}, f32[27,64]{1,0:T(8,128)}, u32[]{:S(2)}) %copy-start.3) | copy-done | bytes 6936
  7.3 0.0 copy-start.5
  7.3 0.7 %copy-done.5 = s32[8]{0:T(128)S(1)} copy-done((s32[8]{0:T(128)S(1)}, s32[8]{0:T(128)}, u32[]{:S(2)}) %copy-start.5) | copy-done | bytes 56
  7.9 5.2 %shard_map.82 = (bf16[6,64,24,128]{3,2,1,0:T(8,128)(2,1)S(1)}, bf16[64,96,256]{2,1,0:T(8,128)(2,1)S(1)}, bf16[6,24,128]{2,1,0:T(8,128)(2,1)S(1)}, bf16[6,24,128]{2,1,0:T(8,128)(2,1)S(1)}) custom-call(s32[8]{0:T(128)S(1)} %copy-done.5, bf16[6,64,24,128]{3,2,1,0:T(8,128)(2,1)} %feature.1, f32[27,64]{1,0:T(8,128)S(1)} %copy-done.3), custom_call_target="tpu_custom_call" | custom-call | tf_op jit(solution)/shard_map/pallas_call | solution.py:308
  13.2 0.0 copy-start.2
  13.2 1.6 %copy-done.2 = bf16[64,96,256]{2,1,0:T(8,128)(2,1)} copy-done((bf16[64,96,256]{2,1,0:T(8,128)(2,1)}, bf16[64,96,256]{2,1,0:T(8,128)(2,1)S(1)}, u32[]{:S(2)}) %copy-start.2) | copy-done | bytes 3145752
  14.8 2.0 %collective-permute-start = (bf16[6,24,128]{2,1,0:T(8,128)(2,1)S(1)}, bf16[6,24,128]{2,1,0:T(8,128)(2,1)S(1)}, u32[]{:S(2)}, u32[]{:S(2)}) collective-permute-start(bf16[6,24,128]{2,1,0:T(8,128)(2,1)S(1)} %get-tuple-element.17), channel_id=1, source_target_pairs={{0,1},{1,0},{2,3},{3,2},{4,5},{5,4},{6,7},{7,6},{8,9},{9,8},{10,11... | collective-permute-start | bytes 110600 | tf_op jit(solution)/shard_map/ppermute | solution.py:305
  16.9 1.5 %collective-permute-start.1 = (bf16[6,24,128]{2,1,0:T(8,128)(2,1)S(1)}, bf16[6,24,128]{2,1,0:T(8,128)(2,1)S(1)}, u32[]{:S(2)}, u32[]{:S(2)}) collective-permute-start(bf16[6,24,128]{2,1,0:T(8,128)(2,1)S(1)} %get-tuple-element.18), channel_id=1, source_target_pairs={{1,2},{2,1},{3,0},{0,3},{5,6},{6,5},{7,4},{4,7},{9,10},{10,9},{11,... | collective-permute-start | bytes 110600 | tf_op jit(solution)/shard_map/ppermute | solution.py:305
  18.3 0.0 copy-done.7
  18.3 0.0 copy-start.10
  18.3 0.0 copy-start.4
  18.3 0.0 copy-start.6
  18.3 0.0 copy-start.9
  18.4 6.6 %shard_map.83.depth.depth_in = f32[2,2048,128]{2,1,0:T(8,128)S(1)} custom-call(f32[64]{0:T(128)S(1)} %copy-done.7, bf16[6,64,24,128]{3,2,1,0:T(8,128)(2,1)S(1)} %get-tuple-element.16.planes, bf16[64,96,256]{2,1,0:T(8,128)(2,1)} %copy-done.2), custom_call_target="tpu_custom_call" | custom-call | flops 1000000000 | bytes 1000000 | tf_op jit(solution)/shard_map/pallas_call | solution.py:327
  24.9 0.0 copy-start
  25.0 1.4 %copy-done = bf16[6,64,24,128]{3,2,1,0:T(8,128)(2,1)} copy-done((bf16[6,64,24,128]{3,2,1,0:T(8,128)(2,1)}, bf16[6,64,24,128]{3,2,1,0:T(8,128)(2,1)S(1)}, u32[]{:S(2)}) %copy-start) | copy-done | bytes 2359320
  26.4 0.0 copy-done.10
  26.4 0.1 copy.18.lift
  26.5 0.0 all-to-all-done
  26.5 0.1 copy.17
  26.6 0.0 collective-permute-done.first
  26.6 0.0 collective-permute-done.1.second
  26.6 0.0 copy-done.4
  26.6 0.0 copy-done.6
  26.6 1.1 %shard_map.84 = (f32[2,2,24,128]{3,2,1,0:T(8,128)S(1)}, bf16[256,128]{1,0:T(8,128)(2,1)S(1)}, bf16[256,128]{1,0:T(8,128)(2,1)S(1)}) custom-call(s32[8]{0:T(128)S(1)} %copy-done.6, f32[27,64]{1,0:T(8,128)S(1)} %copy-done.4, bf16[6,24,128]{2,1,0:T(8,128)(2,1)S(1)} %collective-permute-done.first, bf16[6,24,128]{2,1,0:T(8,128)(2,1)S(1)} %collective-permute-done.1.second, ...), custom_call_target="tpu_custom_call" | custom-call | tf_op jit(solution)/shard_map/pallas_call | solution.py:335
  27.7 0.0 copy-start.1
  27.7 0.0 copy-start.8
  27.7 0.1 collective-permute-start.2
  27.8 3.7 %collective-permute-start.3 = (bf16[256,128]{1,0:T(8,128)(2,1)S(1)}, bf16[256,128]{1,0:T(8,128)(2,1)S(1)}, u32[]{:S(2)}, u32[]{:S(2)}) collective-permute-start(bf16[256,128]{1,0:T(8,128)(2,1)S(1)} %get-tuple-element.24), channel_id=1, source_target_pairs={{4,8},{8,4},{12,16},{16,12},{20,24},{24,20},{28,0},{0,28},{5,9},{9... | collective-permute-start | bytes 196616 | tf_op jit(solution)/shard_map/ppermute | solution.py:305
  31.5 0.0 copy-done.9
  31.5 1.6 %shard_map.85 = (f32[2,2048,128]{2,1,0:T(8,128)S(1)}, bf16[512,512]{1,0:T(8,128)(2,1)S(1)}, f32[3,24,128]{2,1,0:T(8,128)S(1)}) custom-call(s32[8]{0:T(128)S(1)} %copy-done.6, bf16[64,64]{1,0:T(8,128)(2,1)S(1)} %copy-done.9, f32[3,8,8]{2,1,0:T(8,128)S(1)} %bitcast.4, f32[2,2,24,128]{3,2,1,0:T(8,128)S(1)} %get-tuple-element.20.edge, ...), custom_call_target="tpu_custom_call", output_to_operand_aliasing={{0}: (4, {})} | custom-call | flops 1000000000 | bytes 1000000 | tf_op jit(solution)/shard_map/pallas_call | solution.py:350
  33.1 0.0 collective-permute-done.2.near
  33.1 0.5 %collective-permute-done.3.far = bf16[256,128]{1,0:T(8,128)(2,1)S(1)} collective-permute-done((bf16[256,128]{1,0:T(8,128)(2,1)S(1)}, bf16[256,128]{1,0:T(8,128)(2,1)S(1)}, u32[]{:S(2)}, u32[]{:S(2)}) %collective-permute-start.3) | collective-permute-done | bytes 65568 | tf_op jit(solution)/shard_map/ppermute | solution.py:305
  33.5 0.0 copy-done.1
  33.5 0.0 copy-done.8
  33.5 3.3 %shard_map.86 = (bf16[2,64,24,128]{3,2,1,0:T(8,128)(2,1)}, f32[2,2048,128]{2,1,0:T(8,128)S(1)}) custom-call(s32[8]{0:T(128)S(1)} %copy-done.6, f32[64]{0:T(128)S(1)} %copy-done.8, f32[64,3]{1,0:T(8,128)S(1)} %copy.18.lift, bf16[6,64,24,128]{3,2,1,0:T(8,128)(2,1)S(1)} %copy-done.1, ...), custom_call_target="tpu_custom_call", output_to_operand_aliasing={{1}: (8, {})} | custom-call | tf_op jit(solution)/shard_map/pallas_call | solution.py:359
Async XLA Ops:
  0.0 18.3 %copy-start.7 = (f32[64]{0:T(128)S(1)}, f32[64]{0:T(128)}, u32[]{:S(2)}) copy-start(f32[64]{0:T(128)} %bias.1) | copy-start | bytes 772
  1.4 25.1 %all-to-all-start = ((f32[3,2,32]{0,1,2:T(2,128)}), f32[3,2,32]{0,1,2:T(2,128)S(1)}, u32[]{:S(2)}, u32[]{:S(2)}) async-start(f32[3,2,32]{0,1,2:T(2,128)} %copy.16), calls=%async_computation | async-start | bytes 65536 | tf_op jit(solution)/shard_map/all_to_all | solution.py:307
  6.6 0.7 %copy-start.3 = (f32[27,64]{1,0:T(8,128)S(1)}, f32[27,64]{1,0:T(8,128)}, u32[]{:S(2)}) copy-start(f32[27,64]{1,0:T(8,128)} %taps.3) | copy-start | bytes 20740
  7.3 0.7 %copy-start.5 = (s32[8]{0:T(128)S(1)}, s32[8]{0:T(128)}, u32[]{:S(2)}) copy-start(s32[8]{0:T(128)} %widths.7) | copy-start | bytes 100
  13.2 1.7 %copy-start.2 = (bf16[64,96,256]{2,1,0:T(8,128)(2,1)}, bf16[64,96,256]{2,1,0:T(8,128)(2,1)S(1)}, u32[]{:S(2)}) copy-start(bf16[64,96,256]{2,1,0:T(8,128)(2,1)S(1)} %get-tuple-element.19.band) | copy-start | bytes 9437188
  14.8 11.8 %collective-permute-start = (bf16[6,24,128]{2,1,0:T(8,128)(2,1)S(1)}, bf16[6,24,128]{2,1,0:T(8,128)(2,1)S(1)}, u32[]{:S(2)}, u32[]{:S(2)}) collective-permute-start(bf16[6,24,128]{2,1,0:T(8,128)(2,1)S(1)} %get-tuple-element.17), channel_id=1, source_target_pairs={{0,1},{1,0},{2,3},{3,2},{4,5},{5,4},{6,7},{7,6},{8,9},{9,8},{10,11... | collective-permute-start | bytes 110600 | tf_op jit(solution)/shard_map/ppermute | solution.py:305
  16.9 9.7 %collective-permute-start.1 = (bf16[6,24,128]{2,1,0:T(8,128)(2,1)S(1)}, bf16[6,24,128]{2,1,0:T(8,128)(2,1)S(1)}, u32[]{:S(2)}, u32[]{:S(2)}) collective-permute-start(bf16[6,24,128]{2,1,0:T(8,128)(2,1)S(1)} %get-tuple-element.18), channel_id=1, source_target_pairs={{1,2},{2,1},{3,0},{0,3},{5,6},{6,5},{7,4},{4,7},{9,10},{10,9},{11,... | collective-permute-start | bytes 110600 | tf_op jit(solution)/shard_map/ppermute | solution.py:305
  18.3 8.0 %copy-start.10 = (f32[64,3]{0,1:T(4,128)S(1)}, f32[64,3]{0,1:T(4,128)}, u32[]{:S(2)}) copy-start(f32[64,3]{0,1:T(4,128)} %param.14) | copy-start | bytes 2308
  18.3 8.3 %copy-start.4 = (f32[27,64]{1,0:T(8,128)S(1)}, f32[27,64]{1,0:T(8,128)}, u32[]{:S(2)}) copy-start(f32[27,64]{1,0:T(8,128)} %taps.3) | copy-start | bytes 20740
  18.3 8.3 %copy-start.6 = (s32[8]{0:T(128)S(1)}, s32[8]{0:T(128)}, u32[]{:S(2)}) copy-start(s32[8]{0:T(128)} %widths.7) | copy-start | bytes 100
  18.3 13.2 %copy-start.9 = (bf16[64,64]{1,0:T(8,128)(2,1)S(1)}, bf16[64,64]{1,0:T(8,128)(2,1)}, u32[]{:S(2)}) copy-start(bf16[64,64]{1,0:T(8,128)(2,1)} %mix.1) | copy-start | bytes 24580
  24.9 1.4 %copy-start = (bf16[6,64,24,128]{3,2,1,0:T(8,128)(2,1)}, bf16[6,64,24,128]{3,2,1,0:T(8,128)(2,1)S(1)}, u32[]{:S(2)}) copy-start(bf16[6,64,24,128]{3,2,1,0:T(8,128)(2,1)S(1)} %get-tuple-element.16.planes) | copy-start | bytes 7077892
  27.7 5.9 %copy-start.1 = (bf16[6,64,24,128]{3,2,1,0:T(8,128)(2,1)S(1)}, bf16[6,64,24,128]{3,2,1,0:T(8,128)(2,1)}, u32[]{:S(2)}) copy-start(bf16[6,64,24,128]{3,2,1,0:T(8,128)(2,1)} %copy-done) | copy-start | bytes 7077892
  27.7 5.8 %copy-start.8 = (f32[64]{0:T(128)S(1)}, f32[64]{0:T(128)}, u32[]{:S(2)}) copy-start(f32[64]{0:T(128)} %pw_bias.1) | copy-start | bytes 772
  27.7 5.3 %collective-permute-start.2 = (bf16[256,128]{1,0:T(8,128)(2,1)S(1)}, bf16[256,128]{1,0:T(8,128)(2,1)S(1)}, u32[]{:S(2)}, u32[]{:S(2)}) collective-permute-start(bf16[256,128]{1,0:T(8,128)(2,1)S(1)} %get-tuple-element.23), channel_id=1, source_target_pairs={{0,4},{4,0},{8,12},{12,8},{16,20},{20,16},{24,28},{28,24},{1,5},{5... | collective-permute-start | bytes 196616 | tf_op jit(solution)/shard_map/ppermute | solution.py:305
  27.8 5.8 %collective-permute-start.3 = (bf16[256,128]{1,0:T(8,128)(2,1)S(1)}, bf16[256,128]{1,0:T(8,128)(2,1)S(1)}, u32[]{:S(2)}, u32[]{:S(2)}) collective-permute-start(bf16[256,128]{1,0:T(8,128)(2,1)S(1)} %get-tuple-element.24), channel_id=1, source_target_pairs={{4,8},{8,4},{12,16},{16,12},{20,24},{24,20},{28,0},{0,28},{5,9},{9... | collective-permute-start | bytes 196616 | tf_op jit(solution)/shard_map/ppermute | solution.py:305

commit v3 on v2

--- a/solution.py
+++ b/solution.py
@@ -1,3 +1,5 @@
+import functools
+
 import jax
 import jax.numpy as jnp
 from jax import lax
@@ -12,7 +14,7 @@
 OUTER = 32
 F32 = jnp.float32
 BF16 = jnp.bfloat16
-VMEM_BYTES = 48 * 1024 * 1024
+VMEM_BYTES = 14 * 1024 * 1024
 
 
 def lane_iota(shape):
@@ -31,8 +33,11 @@
     return lax.rem(lax.axis_index(axis), 2) == 0
 
 
-def pack_kernel(widths, feature, taps, planes, band, first, second, tap_rows, masks, sems):
-    width = widths[lax.axis_index("gx")]
+def pack_kernel(
+    widths_in, feature, taps_in, coarse_in,
+    planes, band, first, second,
+    tap_rows, widths, taps, coarse, tail, sems, small_sems,
+):
     count, channels, slots, tile = feature.shape
     depth = 3 * slots
     lanes = band.shape[2]
@@ -40,8 +45,17 @@
     def copy_of(z):
         return pltpu.make_async_copy(feature.at[z], planes.at[z], sems.at[z])
 
+    small = [
+        pltpu.make_async_copy(source, target, small_sems.at[i])
+        for i, (source, target) in enumerate(((taps_in, taps), (widths_in, widths), (coarse_in, coarse)))
+    ]
+    for copy in small:
+        copy.start()
     for z in range(count):
         copy_of(z).start()
+    for copy in small:
+        copy.wait()
+    width = widths[lax.axis_index("gx")]
 
     shape = (taps.shape[0], lanes)
     lane = lane_iota(shape)
@@ -64,19 +78,32 @@
     target = jnp.where(row < slots, row, jnp.where(row < slots + 2, row - slots - 2, row - slots - 2 + width))
     target = jnp.where(row < slots + 4, target, 4 * OUTER)
     known = (lane < 2 * depth) & (source < width)
-    for dx in (-1, 0, 1):
-        masks[dx + 1] = ((source == target + 2 * dx) & known).astype(F32)
+    masks = [((source == target + 2 * dx) & known).astype(BF16) for dx in (-1, 0, 1)]
 
     def build(c, carry):
         for dy in (-1, 0, 1):
             total = None
             for dx in (-1, 0, 1):
-                term = masks[dx + 1] * tap_rows[3 * (dx + 1) + dy + 1, pl.ds(c, 1), :]
+                weights = tap_rows[3 * (dx + 1) + dy + 1, pl.ds(c, 1), :]
+                weights = jnp.broadcast_to(weights, (OUTER // 2, lanes)).astype(BF16)
+                term = masks[dx + 1] * jnp.concatenate([weights, weights], axis=0)
                 total = term if total is None else total + term
-            band[c, OUTER * (dy + 1) : OUTER * (dy + 2), :] = total.astype(BF16)
+            band[c, OUTER * (dy + 1) : OUTER * (dy + 2), :] = total
         return carry
 
-    lax.fori_loop(0, channels, build, 0, unroll=2)
+    lax.fori_loop(0, channels, build, 0, unroll=4)
+
+    parts, own_rows, ncy = coarse.shape
+    tail[...] = jnp.zeros_like(tail)
+    for k in range(parts):
+        rest = coarse[k]
+        for p in range(3):
+            term = rest.astype(BF16).astype(F32)
+            rest = rest - term
+            at = (p * parts + k) * own_rows
+            tail[at : at + own_rows, 0:ncy] = term
+    for message in (first, second):
+        message[count * slots :, :] = tail[...].astype(BF16)
 
     lane = lane_iota((slots, tile))
     even = is_even("gy")
@@ -91,12 +118,17 @@
             return jnp.where(((lane + step // 2) & step) != 0, other, one)
         return jnp.where((lane & 2) != 0, other, one), jnp.where((lane & 2) != 0, one, other)
 
-    for z in range(count):
-        copy_of(z).wait()
-        left, right = merged(z, channels.bit_length() - 1, 0)
-        right = pltpu.roll(right, 2, 1)
-        first[z] = jnp.where(even, right, left).astype(BF16)
-        second[z] = jnp.where(even, left, right).astype(BF16)
+    for z in range(0, count, 2):
+        columns = []
+        for k in range(2):
+            copy_of(z + k).wait()
+            left, right = merged(z + k, channels.bit_length() - 1, 0)
+            columns.append((left, pltpu.roll(right, 2, 1)))
+        left = jnp.concatenate([columns[0][0], columns[1][0]], axis=0)
+        right = jnp.concatenate([columns[0][1], columns[1][1]], axis=0)
+        at = slice(z * slots, (z + 2) * slots)
+        first[at, :] = jnp.where(even, right, left).astype(BF16)
+        second[at, :] = jnp.where(even, left, right).astype(BF16)
 
 
 def shifted_sum(centre, before, after):
@@ -114,7 +146,7 @@
     def convolve(c, carry):
         cells = jnp.concatenate(
             [
-                jnp.concatenate([planes[z + ZOUT * m, c] for m in range(3)] * 2, axis=0)
+                jnp.concatenate([planes[z + ZOUT * m, c].astype(F32) for m in range(3)] * 2, axis=0).astype(BF16)
                 for z in range(ZOUT)
             ],
             axis=1,
@@ -132,7 +164,8 @@
 
 def rim_kernel(widths, taps, first, second, depth, edge, near, far, strips, held, beyond, tail):
     width = widths[lax.axis_index("gx")]
-    count, slots, tile = first.shape
+    count, slots = 3 * ZOUT, edge.shape[2]
+    tile = first.shape[1]
     channels = taps.shape[1]
     pad = 8
     wide = 2 * tile
@@ -143,9 +176,7 @@
     from_right = (row < tile) == is_even("gy")
     target = ((own >> 1) << 2) + (own & 1) + jnp.where(from_right, 0, 2)
     spread = (lane_iota(shape) == target).astype(BF16)
-    both = jnp.concatenate(
-        [first[...].reshape(count * slots, tile), second[...].reshape(count * slots, tile)], axis=1
-    )
+    both = jnp.concatenate([first[: count * slots, :], second[: count * slots, :]], axis=1)
     both = jnp.dot(both, spread, preferred_element_type=F32)
     valid = row_iota((slots, wide)) < width
     for z in range(count):
@@ -192,8 +223,16 @@
         far[at, :] = jnp.where(even, to_lower, to_upper).astype(BF16)
 
 
-def settle_kernel(widths, mix, coarse, edge, depth_in, depth, spread, lifted):
+def settle_kernel(gathered, widths, lift, mix, planes, *refs):
+    if gathered:
+        coarse, edge, depth_in, depth, spread, base = refs
+        parts, ncx, ncy = coarse.shape
+    else:
+        first, second, own_block, opposite, edge, depth_in, depth, spread, base, cells = refs
+        parts, own_rows, ncy = own_block.shape
+        ncx = 4 * own_rows
     slab = lax.axis_index("gx")
+    here = lax.axis_index("gy")
     slabs = widths.shape[0]
     channels = mix.shape[0]
     _, _, slots, tile = edge.shape
@@ -201,10 +240,10 @@
     per_tile = tile // 4
     for z in range(ZOUT):
         for c in range(channels):
-            cells = pltpu.roll(edge[z, c // per_tile], (tile - 2 - 4 * (c % per_tile)) % tile, 1)
-            cells = jnp.where((lane < 2) | (lane >= tile - 2), cells, 0.0)
+            cells_of = pltpu.roll(edge[z, c // per_tile], (tile - 2 - 4 * (c % per_tile)) % tile, 1)
+            cells_of = jnp.where((lane < 2) | (lane >= tile - 2), cells_of, 0.0)
             at = slice(c * OUTER, c * OUTER + slots)
-            depth[z, at, :] = depth_in[z, at, :] + cells
+            depth[z, at, :] = depth_in[z, at, :] + cells_of
 
     size = channels * ROWS
     tall = (size, channels)
@@ -221,25 +260,51 @@
     start = jnp.int32(0)
     for d in range(slabs):
         start = start + jnp.where(d < slab, widths[d], 0)
-    parts, ncx, own = coarse.shape
-    shape = (own, tile)
+    shape = (ncy, tile)
     cell = row_iota(shape) * CF
-    place = lane_iota(shape)
+    place = lane_iota(shape) + here * tile
     along_y = ((place >= cell) & (place < cell + CF)).astype(F32)
     shape = (slots, ncx)
-    cell = lane_iota(shape) * CF
+    cell = lane_iota(shape)
+    if not gathered:
+        even = is_even("gy")
+        after, before = lax.rem(here + 1, 4), lax.rem(here + 3, 4)
+        owners = (here, jnp.where(even, after, before), jnp.where(even, before, after), lax.rem(here + 2, 4))
+        index = cell
+        cell = jnp.zeros(shape, jnp.int32)
+        for i, owner in enumerate(owners):
+            inside = (index >= i * own_rows) & (index < (i + 1) * own_rows)
+            cell = jnp.where(inside, index + (owner - i) * own_rows, cell)
+        cells[...] = jnp.zeros_like(cells)
+        for k in range(parts):
+            cells[k, 0:own_rows, 0:ncy] = own_block[k]
+            cells[k, 3 * own_rows : ncx, 0:ncy] = opposite[k]
+        strip = slots * planes.shape[0]
+        for i, message in ((1, first), (2, second)):
+            terms = message[strip:, 0:ncy].astype(F32)
+            count = parts * own_rows
+            sums = terms[0:count] + terms[count : 2 * count] + terms[2 * count : 3 * count]
+            for k in range(parts):
+                cells[k, i * own_rows : (i + 1) * own_rows, :] = sums[k * own_rows : (k + 1) * own_rows]
+    cell = cell * CF
     place = row_iota(shape) + start
     place = jnp.where(place >= total, place - total, place)
     along_x = ((place >= cell) & (place < cell + CF)).astype(F32)
+    lifted = []
     for k in range(parts):
-        across = jnp.dot(coarse[k], along_y, precision=lax.Precision.HIGHEST, preferred_element_type=F32)
-        lifted[k] = jnp.dot(along_x, across, precision=lax.Precision.HIGHEST, preferred_element_type=F32)
-
-
-def finish_kernel(widths, pw_bias, lift, planes, spread, lifted, near, far, depth_in, out, depth, mixed_in, block, sems):
+        block = coarse[k] if gathered else cells[k]
+        across = jnp.dot(block, along_y, precision=lax.Precision.HIGHEST, preferred_element_type=F32)
+        lifted.append(jnp.dot(along_x, across, precision=lax.Precision.HIGHEST, preferred_element_type=F32))
+    for o in range(channels):
+        lift_o = lift[o, 0] * lifted[0] + lift[o, 1] * lifted[1] + lift[o, 2] * lifted[2]
+        for z in range(ZOUT):
+            base[z, o] = planes[2 + z, o].astype(F32) + lift_o
+
+
+def finish_kernel(widths, pw_bias, base, spread, near, far, depth_in, out, depth, mixed_in, mixed, block, sems):
     slab = lax.axis_index("gx")
     width = widths[slab]
-    count, channels, slots, tile = planes.shape
+    _, channels, slots, tile = base.shape
     even = is_even("gx")
     rows = ZOUT * channels
     for arrived, at_top in ((near, jnp.logical_not(even)), (far, even)):
@@ -249,31 +314,30 @@
                 at = pl.ds(begin + r, channels, stride=OUTER)
                 begin_row = r * rows + z * channels
                 depth[z, at, :] = depth_in[z, at, :] + arrived[begin_row : begin_row + channels, :].astype(F32)
-    for c in range(0, channels, 2):
-        for z in range(ZOUT):
-            for b in range(slots // ROWS):
+    for b in range(slots // ROWS):
+        for c in range(0, channels, 2):
+            for z in range(ZOUT):
                 both = [depth[z, (c + k) * OUTER + ROWS * b : (c + k) * OUTER + ROWS * (b + 1), :] for k in range(2)]
                 both = jnp.concatenate(both, axis=0).astype(BF16)
                 mixed_in[b, c * ROWS : (c + 2) * ROWS, z * tile : (z + 1) * tile] = both
+        mixed[b] = jnp.dot(spread[...], mixed_in[b], preferred_element_type=F32)
 
     valid = row_iota((slots, tile)) < width
     chunk = 16
     copies = []
     for part in range(channels // chunk):
-        picked = slice(part * chunk * ROWS, (part + 1) * chunk * ROWS)
-        mixed = [
-            jnp.dot(spread[picked, :], mixed_in[b], preferred_element_type=F32) for b in range(slots // ROWS)
-        ]
         for k in range(chunk):
             o = part * chunk + k
-            lift_o = lift[o, 0] * lifted[0] + lift[o, 1] * lifted[1] + lift[o, 2] * lifted[2]
             for z in range(ZOUT):
                 value = jnp.concatenate(
-                    [m[k * ROWS : (k + 1) * ROWS, z * tile : (z + 1) * tile] for m in mixed], axis=0
+                    [
+                        mixed[b, o * ROWS : (o + 1) * ROWS, z * tile : (z + 1) * tile]
+                        for b in range(slots // ROWS)
+                    ],
+                    axis=0,
                 )
                 value = value + pw_bias[o]
-                value = jnp.maximum(value, 0.2 * value) + lift_o
-                value = value + planes[2 + z, o].astype(F32)
+                value = jnp.maximum(value, 0.2 * value) + base[z, o]
                 block[z, o] = jnp.where(valid, value, 0.0).astype(BF16)
         for z in range(ZOUT):
             part_of = pl.ds(part * chunk, chunk)
@@ -286,13 +350,17 @@
 
 def shards(feature, widths, dw_weight, dw_bias, pw_weight, pw_bias, lift_weight, coarse):
     planes, channels, slots, tile = feature.shape
+    ny = lax.axis_size("gy")
+    parts, own_rows, ncy = coarse.shape
+    gathered = ny != 4
     smem = pl.BlockSpec(memory_space=pltpu.SMEM)
     vmem = pl.BlockSpec(memory_space=pltpu.VMEM)
     hbm = pl.BlockSpec(memory_space=pltpu.HBM)
     params = pltpu.CompilerParams(vmem_limit_bytes=VMEM_BYTES)
     shape = jax.ShapeDtypeStruct
-    strip = shape((planes, slots, tile), BF16)
+    strip = shape((planes * slots + 32, tile), BF16)
     depth_shape = pltpu.VMEM((ZOUT, channels * OUTER, tile), F32)
+    base_shape = pltpu.VMEM((ZOUT, channels, slots, tile), F32)
     message = shape((2 * ZOUT * channels, tile), BF16)
     size = channels * ROWS
 
@@ -304,7 +372,10 @@
             pairs += [(a, b), (b, a)]
         return lax.ppermute(array, axis, pairs)
 
-    local = lax.all_to_all(coarse, "gy", split_axis=2, concat_axis=1, tiled=True)
+    if gathered:
+        every = lax.all_gather(coarse, "gy", axis=1, tiled=True)
+    else:
+        opposite = lax.ppermute(coarse, "gy", [(i, (i + 2) % 4) for i in range(4)])
     held, band, first, second = pl.pallas_call(
         pack_kernel,
         out_shape=(
@@ -313,15 +384,19 @@
             strip,
             strip,
         ),
-        in_specs=[smem, hbm, vmem],
+        in_specs=[hbm] * 4,
         out_specs=(vmem,) * 4,
         scratch_shapes=[
             pltpu.VMEM((9, channels, 2 * tile), F32),
-            pltpu.VMEM((3, OUTER, 2 * tile), F32),
+            pltpu.SMEM(widths.shape, jnp.int32),
+            pltpu.VMEM(dw_weight.shape, F32),
+            pltpu.VMEM(coarse.shape, F32),
+            pltpu.VMEM((32, tile), F32),
             pltpu.SemaphoreType.DMA((planes,)),
+            pltpu.SemaphoreType.DMA((3,)),
         ],
         compiler_params=params,
-    )(widths, feature, dw_weight)
+    )(widths, feature, dw_weight, coarse)
     first = swapped(first, "gy", 0)
     second = swapped(second, "gy", 1)
     depth = pl.pallas_call(
@@ -347,28 +422,31 @@
     )(widths, dw_weight, first, second, depth)
     near = swapped(near, "gx", 0)
     far = swapped(far, "gx", 1)
-    depth, spread, lifted = pl.pallas_call(
-        settle_kernel,
-        out_shape=(depth_shape, pltpu.VMEM((size, size), BF16), pltpu.VMEM((3, slots, tile), F32)),
-        in_specs=[smem] + [vmem] * 4,
+    rows = (every,) if gathered else (first, second, coarse, opposite)
+    depth, spread, base = pl.pallas_call(
+        functools.partial(settle_kernel, gathered),
+        out_shape=(depth_shape, pltpu.VMEM((size, size), BF16), base_shape),
+        in_specs=[smem, smem] + [vmem] * (4 + len(rows)),
         out_specs=(vmem,) * 3,
-        input_output_aliases={4: 0},
+        scratch_shapes=[] if gathered else [pltpu.VMEM((parts, 4 * own_rows, ncy), F32)],
+        input_output_aliases={5 + len(rows): 0},
         compiler_params=params,
         cost_estimate=pl.CostEstimate(flops=10**9, bytes_accessed=10**6, transcendentals=0),
-    )(widths, pw_weight, local, edge, depth)
+    )(widths, lift_weight, pw_weight, held, *rows, edge, depth)
     out, _ = pl.pallas_call(
         finish_kernel,
         out_shape=(shape((ZOUT, channels, slots, tile), BF16), depth_shape),
-        in_specs=[smem, smem, smem] + [vmem] * 6,
+        in_specs=[smem, smem] + [vmem] * 5,
         out_specs=(hbm, vmem),
         scratch_shapes=[
             pltpu.VMEM((slots // ROWS, size, ZOUT * tile), BF16),
+            pltpu.VMEM((slots // ROWS, size, ZOUT * tile), F32),
             pltpu.VMEM((ZOUT, channels, slots, tile), BF16),
             pltpu.SemaphoreType.DMA((channels // 16, ZOUT)),
         ],
-        input_output_aliases={8: 1},
+        input_output_aliases={6: 1},
         compiler_params=params,
-    )(widths, pw_bias, lift_weight, held, spread, lifted, near, far, depth)
+    )(widths, pw_bias, base, spread, near, far, depth)
     return out
 
 

time: 37.2 us -> 32.8 us (0.88)
  starting transfers between devices: 12.4 us -> 8.78 us
  Pallas kernels: 17.7 us -> 16.7 us
  local copies, waits for them, and re-layouts: 6.09 us -> 6.92 us
  waiting for transfers between devices: 0.49 us -> 0.01 us
    all_to_all x1 -> x0, starting transfers between devices: 5.16 us -> none  [shards(): lax.all_to_all(coarse, 'gy', split_axis=2, concat_axis=1, tiled=True)]
    ppermute x0 -> x1, starting transfers between devices: none -> 2.97 us  [shards(): opposite = lax.ppermute(coarse, 'gy', [(i, (i + 2) % 4) for i in range(4)])]
    ppermute x4, starting transfers between devices: 7.26 us -> 5.81 us  [swapped(): return lax.ppermute(array, axis, pairs)]
    pallas_call x1, Pallas kernels: 6.59 us -> 5.2 us  [shards(): pl.pallas_call(conv_kernel, out_shape=depth_shape, in_specs=[smem, vmem,...]
    unnamed x24 -> x27, local copies, waits for them, and re-layouts: 5.96 us -> 6.92 us
    pallas_call x1, Pallas kernels: 1.55 us -> 2.42 us  [shards(): pl.pallas_call(functools.partial(settle_kernel, gathered), out_shape=(dep...]
    pallas_call x1, Pallas kernels: 3.29 us -> 2.64 us  [shards(): pl.pallas_call(finish_kernel, out_shape=(shape((ZOUT, channels, slots, ti...]
    ppermute x4, waiting for transfers between devices: 0.49 us -> 0.01 us  [swapped(): return lax.ppermute(array, axis, pairs)]
  transfers between devices with their start and end apart: 5 -> 5, of which waited for: 1 -> 0; matrix products, arithmetic and copies ran while one was open for 1% -> 0% of each run, Pallas kernels for 36% -> 43%
where the time goes in v3:
time: 32.8 us; the launch traced here: 32.6 us
  Pallas kernels  16.7 us (51%)
  starting transfers between devices  8.78 us (27%)
  local copies, waits for them, and re-layouts  6.92 us (21%)
    unnamed x27, local copies, waits for them, and re-layouts  6.92 us
    ppermute x4, starting transfers between devices, swapped(): return lax.ppermute(array, axis, pairs)  5.81 us
    pallas_call x1, Pallas kernels, shards(): pl.pallas_call(pack_kernel, out_shape=(pltpu.VMEM(feature.shape, BF16), p...  5.42 us
    pallas_call x1, Pallas kernels, shards(): pl.pallas_call(conv_kernel, out_shape=depth_shape, in_specs=[smem, vmem,...  5.2 us
    ppermute x1, starting transfers between devices, shards(): opposite = lax.ppermute(coarse, 'gy', [(i, (i + 2) % 4) for i in range(4)])  2.97 us
    pallas_call x1, Pallas kernels, shards(): pl.pallas_call(finish_kernel, out_shape=(shape((ZOUT, channels, slots, ti...  2.64 us
    pallas_call x1, Pallas kernels, shards(): pl.pallas_call(functools.partial(settle_kernel, gathered), out_shape=(dep...  2.42 us
    pallas_call x1, Pallas kernels, shards(): pl.pallas_call(rim_kernel, out_shape=(pltpu.VMEM((ZOUT, 2, slots, tile),...  1.06 us
  transfers between devices with their start and end apart: 5, of which 0 were waited for; matrix products, arithmetic and copies ran while one was open for 0% of the time, Pallas kernels for 43%

profile of v3, /device:TPU:0, one launch (start us, length us, event | category | flops | bytes accessed | tf_op | source)
XLA Modules:
  0.0 32.6 jit_solution(10172149888940529812)
XLA Ops:
  0.0 3.0 %collective-permute-start.2 = (f32[3,2,32]{2,1,0:T(2,128)}, f32[3,2,32]{2,1,0:T(2,128)S(1)}, u32[]{:S(2)}, u32[]{:S(2)}) collective-permute-start(f32[3,2,32]{2,1,0:T(2,128)} %refs_2_.1), channel_id=1, source_target_pairs={{0,2},{1,3},{2,0},{3,1},{4,6},{5,7},{6,4},{7,5},{8,10},{9,11},{10,... | collective-permute-start | bytes 2312 | tf_op jit(solution)/shard_map/ppermute | solution.py:378
  3.0 0.0 copy-start.2
  3.0 1.7 %copy-done.2 = bf16[6,64,24,128]{3,2,1,0:T(8,128)(2,1)S(1)} copy-done((bf16[6,64,24,128]{3,2,1,0:T(8,128)(2,1)S(1)}, bf16[6,64,24,128]{3,2,1,0:T(8,128)(2,1)}, u32[]{:S(2)}) %copy-start.2) | copy-done | bytes 2359320
  4.6 0.0 copy-start.3
  4.6 0.7 %copy-done.3 = f32[27,64]{1,0:T(8,128)S(1)} copy-done((f32[27,64]{1,0:T(8,128)S(1)}, f32[27,64]{1,0:T(8,128)}, u32[]{:S(2)}) %copy-start.3) | copy-done | bytes 6936
  5.4 0.0 copy-start.6
  5.4 0.7 %copy-done.6 = f32[3,2,32]{2,1,0:T(2,128)S(1)} copy-done((f32[3,2,32]{2,1,0:T(2,128)S(1)}, f32[3,2,32]{2,1,0:T(2,128)}, u32[]{:S(2)}) %copy-start.6) | copy-done | bytes 792
  6.0 0.0 copy-start.8
  6.0 0.7 %copy-done.8 = s32[8]{0:T(128)S(1)} copy-done((s32[8]{0:T(128)S(1)}, s32[8]{0:T(128)}, u32[]{:S(2)}) %copy-start.8) | copy-done | bytes 56
  6.7 0.0 copy-start.10
  6.7 5.4 %shard_map.82 = (bf16[6,64,24,128]{3,2,1,0:T(8,128)(2,1)S(1)}, bf16[64,96,256]{2,1,0:T(8,128)(2,1)S(1)}, bf16[176,128]{1,0:T(8,128)(2,1)S(1)}, bf16[176,128]{1,0:T(8,128)(2,1)S(1)}) custom-call(s32[8]{0:T(128)S(1)} %copy-done.8, bf16[6,64,24,128]{3,2,1,0:T(8,128)(2,1)S(1)} %copy-done.2, f32[27,64]{1,0:T(8,128)S(1)} %copy-done.3, f32[3,2,32]{2,1,0:T(2,128)S(1)} %copy-done.6), custom_call_target="tpu_custom_call" | custom-call | tf_op jit(solution)/shard_map/pallas_call | solution.py:379
  12.1 1.6 %collective-permute-start = (bf16[176,128]{1,0:T(8,128)(2,1)S(1)}, bf16[176,128]{1,0:T(8,128)(2,1)S(1)}, u32[]{:S(2)}, u32[]{:S(2)}) collective-permute-start(bf16[176,128]{1,0:T(8,128)(2,1)S(1)} %get-tuple-element.17), channel_id=1, source_target_pairs={{0,1},{1,0},{2,3},{3,2},{4,5},{5,4},{6,7},{7,6},{8,9},{9,8},{10,11... | collective-permute-start | bytes 135176 | tf_op jit(solution)/shard_map/ppermute | solution.py:373
  13.7 0.0 collective-permute-start.1
  13.7 0.0 copy-done.10
  13.7 0.0 copy-start.12
  13.7 0.0 copy-start.4
  13.7 0.0 copy-start.9
  13.7 5.2 %shard_map.83.depth.refs_5_ = f32[2,2048,128]{2,1,0:T(8,128)S(1)} custom-call(f32[64]{0:T(128)S(1)} %copy-done.10, bf16[6,64,24,128]{3,2,1,0:T(8,128)(2,1)S(1)} %get-tuple-element.16.planes, bf16[64,96,256]{2,1,0:T(8,128)(2,1)S(1)} %get-tuple-element.19.band), custom_call_target="tpu_custom_call" | custom-call | flops 1000000000 | bytes 1000000 | tf_op jit(solution)/shard_map/pallas_call | solution.py:402
  18.9 0.0 copy-start
  18.9 1.4 %copy-done = bf16[6,64,24,128]{3,2,1,0:T(8,128)(2,1)} copy-done((bf16[6,64,24,128]{3,2,1,0:T(8,128)(2,1)}, bf16[6,64,24,128]{3,2,1,0:T(8,128)(2,1)S(1)}, u32[]{:S(2)}) %copy-start) | copy-done | bytes 2359320
  20.4 0.0 copy-done.12
  20.4 0.0 copy-start.5
  20.4 0.0 copy-start.7
  20.4 0.1 copy.11.lift
  20.5 0.0 collective-permute-done.first.refs_0_
  20.5 0.0 collective-permute-done.1.second.refs_1_
  20.5 0.0 copy-done.4
  20.5 0.0 copy-done.9
  20.5 1.1 %shard_map.84 = (f32[2,2,24,128]{3,2,1,0:T(8,128)S(1)}, bf16[256,128]{1,0:T(8,128)(2,1)S(1)}, bf16[256,128]{1,0:T(8,128)(2,1)S(1)}) custom-call(s32[8]{0:T(128)S(1)} %copy-done.9, f32[27,64]{1,0:T(8,128)S(1)} %copy-done.4, bf16[176,128]{1,0:T(8,128)(2,1)S(1)} %collective-permute-done.first.refs_0_, ...), custom_call_target="tpu_custom_call" | custom-call | tf_op jit(solution)/shard_map/pallas_call | solution.py:410
  21.5 0.1 collective-permute-start.3
  21.6 4.2 %collective-permute-start.4 = (bf16[256,128]{1,0:T(8,128)(2,1)S(1)}, bf16[256,128]{1,0:T(8,128)(2,1)S(1)}, u32[]{:S(2)}, u32[]{:S(2)}) collective-permute-start(bf16[256,128]{1,0:T(8,128)(2,1)S(1)} %get-tuple-element.24), channel_id=1, source_target_pairs={{4,8},{8,4},{12,16},{16,12},{20,24},{24,20},{28,0},{0,28},{5,9},{9... | collective-permute-start | bytes 196616 | tf_op jit(solution)/shard_map/ppermute | solution.py:373
  25.8 0.0 collective-permute-done.2.refs_3_
  25.8 0.0 copy-done.5
  25.8 0.0 copy-done.7
  25.8 0.0 copy-start.1
  25.8 1.7 %copy-done.1 = bf16[6,64,24,128]{3,2,1,0:T(8,128)(2,1)S(1)} copy-done((bf16[6,64,24,128]{3,2,1,0:T(8,128)(2,1)S(1)}, bf16[6,64,24,128]{3,2,1,0:T(8,128)(2,1)}, u32[]{:S(2)}) %copy-start.1) | copy-done | bytes 2359320
  27.5 0.0 copy-start.11
  27.5 2.4 %shard_map.85 = (f32[2,2048,128]{2,1,0:T(8,128)S(1)}, bf16[512,512]{1,0:T(8,128)(2,1)S(1)}, f32[2,64,24,128]{3,2,1,0:T(8,128)S(1)}) custom-call(s32[8]{0:T(128)S(1)} %copy-done.9, f32[64,3]{1,0:T(8,128)S(1)} %copy.11.lift, bf16[64,64]{1,0:T(8,128)(2,1)S(1)} %copy-done.5, bf16[6,64,24,128]{3,2,1,0:T(8,128)(2,1)S(1)} %copy-done.1, ...), custom_call_target="tpu_custom_call", output_to_operand_aliasing={{0}: (9, {})} | custom-call | flops 1000000000 | bytes 1000000 | tf_op jit(solution)/shard_map/pallas_call | solution.py:426
  29.9 0.0 collective-permute-done.3.near
  29.9 0.0 collective-permute-done.4.far
  29.9 0.0 copy-done.11
  29.9 2.6 %shard_map.86 = (bf16[2,64,24,128]{3,2,1,0:T(8,128)(2,1)}, f32[2,2048,128]{2,1,0:T(8,128)S(1)}) custom-call(s32[8]{0:T(128)S(1)} %copy-done.9, f32[64]{0:T(128)S(1)} %copy-done.11, f32[2,64,24,128]{3,2,1,0:T(8,128)S(1)} %get-tuple-element.21.base, bf16[512,512]{1,0:T(8,128)(2,1)S(1)} %get-tuple-element.22.spread, ...), custom_call_target="tpu_custom_call", output_to_operand_aliasing={{1}: (6, {})} | custom-call | tf_op jit(solution)/shard_map/pallas_call | solution.py:436
Async XLA Ops:
  0.0 25.8 %collective-permute-start.2 = (f32[3,2,32]{2,1,0:T(2,128)}, f32[3,2,32]{2,1,0:T(2,128)S(1)}, u32[]{:S(2)}, u32[]{:S(2)}) collective-permute-start(f32[3,2,32]{2,1,0:T(2,128)} %refs_2_.1), channel_id=1, source_target_pairs={{0,2},{1,3},{2,0},{3,1},{4,6},{5,7},{6,4},{7,5},{8,10},{9,11},{10,... | collective-permute-start | bytes 2312 | tf_op jit(solution)/shard_map/ppermute | solution.py:378
  3.0 1.7 %copy-start.2 = (bf16[6,64,24,128]{3,2,1,0:T(8,128)(2,1)S(1)}, bf16[6,64,24,128]{3,2,1,0:T(8,128)(2,1)}, u32[]{:S(2)}) copy-start(bf16[6,64,24,128]{3,2,1,0:T(8,128)(2,1)} %feature.1) | copy-start | bytes 7077892
  4.6 0.7 %copy-start.3 = (f32[27,64]{1,0:T(8,128)S(1)}, f32[27,64]{1,0:T(8,128)}, u32[]{:S(2)}) copy-start(f32[27,64]{1,0:T(8,128)} %taps.1) | copy-start | bytes 20740
  5.4 0.7 %copy-start.6 = (f32[3,2,32]{2,1,0:T(2,128)S(1)}, f32[3,2,32]{2,1,0:T(2,128)}, u32[]{:S(2)}) copy-start(f32[3,2,32]{2,1,0:T(2,128)} %refs_2_.1) | copy-start | bytes 2308
  6.0 0.7 %copy-start.8 = (s32[8]{0:T(128)S(1)}, s32[8]{0:T(128)}, u32[]{:S(2)}) copy-start(s32[8]{0:T(128)} %widths.5) | copy-start | bytes 100
  6.7 7.0 %copy-start.10 = (f32[64]{0:T(128)S(1)}, f32[64]{0:T(128)}, u32[]{:S(2)}) copy-start(f32[64]{0:T(128)} %bias.1) | copy-start | bytes 772
  12.1 8.3 %collective-permute-start = (bf16[176,128]{1,0:T(8,128)(2,1)S(1)}, bf16[176,128]{1,0:T(8,128)(2,1)S(1)}, u32[]{:S(2)}, u32[]{:S(2)}) collective-permute-start(bf16[176,128]{1,0:T(8,128)(2,1)S(1)} %get-tuple-element.17), channel_id=1, source_target_pairs={{0,1},{1,0},{2,3},{3,2},{4,5},{5,4},{6,7},{7,6},{8,9},{9,8},{10,11... | collective-permute-start | bytes 135176 | tf_op jit(solution)/shard_map/ppermute | solution.py:373
  13.7 6.8 %collective-permute-start.1 = (bf16[176,128]{1,0:T(8,128)(2,1)S(1)}, bf16[176,128]{1,0:T(8,128)(2,1)S(1)}, u32[]{:S(2)}, u32[]{:S(2)}) collective-permute-start(bf16[176,128]{1,0:T(8,128)(2,1)S(1)} %get-tuple-element.18), channel_id=1, source_target_pairs={{1,2},{2,1},{3,0},{0,3},{5,6},{6,5},{7,4},{4,7},{9,10},{10,9},{11,... | collective-permute-start | bytes 135176 | tf_op jit(solution)/shard_map/ppermute | solution.py:373
  13.7 6.7 %copy-start.12 = (f32[64,3]{0,1:T(4,128)S(1)}, f32[64,3]{0,1:T(4,128)}, u32[]{:S(2)}) copy-start(f32[64,3]{0,1:T(4,128)} %param.14) | copy-start | bytes 2308
  13.7 6.8 %copy-start.4 = (f32[27,64]{1,0:T(8,128)S(1)}, f32[27,64]{1,0:T(8,128)}, u32[]{:S(2)}) copy-start(f32[27,64]{1,0:T(8,128)} %taps.1) | copy-start | bytes 20740
  13.7 6.8 %copy-start.9 = (s32[8]{0:T(128)S(1)}, s32[8]{0:T(128)}, u32[]{:S(2)}) copy-start(s32[8]{0:T(128)} %widths.5) | copy-start | bytes 100
  18.9 1.4 %copy-start = (bf16[6,64,24,128]{3,2,1,0:T(8,128)(2,1)}, bf16[6,64,24,128]{3,2,1,0:T(8,128)(2,1)S(1)}, u32[]{:S(2)}) copy-start(bf16[6,64,24,128]{3,2,1,0:T(8,128)(2,1)S(1)} %get-tuple-element.16.planes) | copy-start | bytes 7077892
  20.4 5.4 %copy-start.5 = (bf16[64,64]{1,0:T(8,128)(2,1)S(1)}, bf16[64,64]{1,0:T(8,128)(2,1)}, u32[]{:S(2)}) copy-start(bf16[64,64]{1,0:T(8,128)(2,1)} %mix.1) | copy-start | bytes 24580
  20.4 5.4 %copy-start.7 = (f32[3,2,32]{2,1,0:T(2,128)S(1)}, f32[3,2,32]{2,1,0:T(2,128)}, u32[]{:S(2)}) copy-start(f32[3,2,32]{2,1,0:T(2,128)} %refs_2_.1) | copy-start | bytes 2308
  21.5 8.4 %collective-permute-start.3 = (bf16[256,128]{1,0:T(8,128)(2,1)S(1)}, bf16[256,128]{1,0:T(8,128)(2,1)S(1)}, u32[]{:S(2)}, u32[]{:S(2)}) collective-permute-start(bf16[256,128]{1,0:T(8,128)(2,1)S(1)} %get-tuple-element.23), channel_id=1, source_target_pairs={{0,4},{4,0},{8,12},{12,8},{16,20},{20,16},{24,28},{28,24},{1,5},{5... | collective-permute-start | bytes 196616 | tf_op jit(solution)/shard_map/ppermute | solution.py:373
  21.6 8.3 %collective-permute-start.4 = (bf16[256,128]{1,0:T(8,128)(2,1)S(1)}, bf16[256,128]{1,0:T(8,128)(2,1)S(1)}, u32[]{:S(2)}, u32[]{:S(2)}) collective-permute-start(bf16[256,128]{1,0:T(8,128)(2,1)S(1)} %get-tuple-element.24), channel_id=1, source_target_pairs={{4,8},{8,4},{12,16},{16,12},{20,24},{24,20},{28,0},{0,28},{5,9},{9... | collective-permute-start | bytes 196616 | tf_op jit(solution)/shard_map/ppermute | solution.py:373
  25.8 1.7 %copy-start.1 = (bf16[6,64,24,128]{3,2,1,0:T(8,128)(2,1)S(1)}, bf16[6,64,24,128]{3,2,1,0:T(8,128)(2,1)}, u32[]{:S(2)}) copy-start(bf16[6,64,24,128]{3,2,1,0:T(8,128)(2,1)} %copy-done) | copy-start | bytes 7077892
  27.5 2.5 %copy-start.11 = (f32[64]{0:T(128)S(1)}, f32[64]{0:T(128)}, u32[]{:S(2)}) copy-start(f32[64]{0:T(128)} %pw_bias.1) | copy-start | bytes 772

commit v4 on v0

v4 whole, which is shorter than its diff:
```python
import functools

import jax
import jax.numpy as jnp
from jax import lax
from jax.experimental import pallas as pl
from jax.experimental.pallas import tpu as pltpu
from jax.sharding import PartitionSpec as P

XW = 16
ZOUT = 2
CF = 16
ROWS = 8
FIRST_LANE = 10
DW_BIAS, PW_BIAS, LIFT = 27, 28, 29
F32 = jnp.float32
BF16 = jnp.bfloat16
VMEM_BYTES = 14 * 1024 * 1024


def lane_iota(shape):
    return lax.broadcasted_iota(jnp.int32, shape, len(shape) - 1)


def row_iota(shape):
    return lax.broadcasted_iota(jnp.int32, shape, len(shape) - 2)


def tap_of(m, dx, dy):
    return 9 * m + 3 * (dx + 1) + (dy + 1)


def is_even(axis):
    return lax.rem(lax.axis_index(axis), 2) == 0


def pack_kernel(
    feature, widths_in, taps_in, dw_bias_in, pw_bias_in, lift_in, coarse_in,
    cells, weights, first, second,
    planes, widths, taps, dw_bias, pw_bias, lift, coarse, stacked, tail, sems, small_sems,
):
    count, channels, slots, tile = feature.shape

    def copy_of(z):
        return pltpu.make_async_copy(feature.at[z], planes.at[z], sems.at[z])

    small = [
        pltpu.make_async_copy(source, target, small_sems.at[i])
        for i, (source, target) in enumerate(
            (
                (widths_in, widths),
                (taps_in, taps),
                (dw_bias_in, dw_bias),
                (pw_bias_in, pw_bias),
                (lift_in, lift),
                (coarse_in, coarse),
            )
        )
    ]
    for copy in small:
        copy.start()
    for z in range(count):
        copy_of(z).start()
    for copy in small:
        copy.wait()
    width = widths[lax.axis_index("gx")]

    stacked[0:DW_BIAS, :] = taps[...]
    stacked[DW_BIAS : DW_BIAS + 1, :] = dw_bias[...]
    stacked[PW_BIAS : PW_BIAS + 1, :] = pw_bias[...]
    stacked[LIFT : LIFT + 3, :] = lift[...]
    turned = jnp.transpose(stacked[...])
    for t in range(stacked.shape[0]):
        weights[t] = jnp.broadcast_to(turned[:, t : t + 1], (channels, tile))

    parts, own_rows, ncy = coarse.shape
    tail[...] = jnp.zeros_like(tail)
    for k in range(parts):
        rest = coarse[k]
        for p in range(3):
            term = rest.astype(BF16).astype(F32)
            rest = rest - term
            at = (p * parts + k) * own_rows
            tail[at : at + own_rows, 0:ncy] = term
    strip = count // 2 * channels
    for message in (first, second):
        message[strip:, :] = tail[...].astype(BF16)

    valid = row_iota((slots, tile)) < width
    block = 16
    lane = lane_iota((block, tile))
    on_right = (lane & 2) != 0
    even = is_even("gy")

    for z in range(0, count, 2):
        for k in range(2):
            copy_of(z + k).wait()
            for c in range(channels):
                cells[z + k, c * slots : (c + 1) * slots, :] = jnp.where(valid, planes[z + k, c].astype(F32), 0.0)
        for c in range(0, channels, block):
            one = edge_columns(cells, z, c, block, slots, lane)
            two = pltpu.roll(edge_columns(cells, z + 1, c, block, slots, lane), 2, 1)
            left = jnp.where(on_right, two, one)
            right = jnp.where(on_right, one, two)
            at = slice(z // 2 * channels + c, z // 2 * channels + c + block)
            first[at, :] = jnp.where(even, right, left).astype(BF16)
            second[at, :] = jnp.where(even, left, right).astype(BF16)


def edge_columns(cells, z, c, block, slots, lane):
    def merged(x, stride):
        if x >= slots:
            return None
        if 4 * stride == lane.shape[1]:
            return cells[z, pl.ds(c * slots + x, block, stride=slots), :]
        one = merged(x, 2 * stride)
        other = merged(x + stride, 2 * stride)
        if other is None:
            return one
        other = pltpu.roll(other, 4 * stride, 1)
        return jnp.where(((lane + 2 * stride) & (4 * stride)) != 0, other, one)

    return merged(0, 1)


def conv_kernel(cells, weights, depth):
    channels, tile = weights.shape[1:]
    slots = cells.shape[1] // channels
    lane = lane_iota((ROWS, tile))

    def convolve(b, carry):
        at = pl.ds(pl.multiple_of(b * ROWS, ROWS), ROWS)
        tap = [weights[t, at, :] for t in range(27)]
        for z in range(ZOUT):
            for parity in range(2):
                sums = {}
                for x in range(parity, slots + 2, 2):
                    if x < slots:
                        rows = [cells[z + ZOUT * m, pl.ds(b * (ROWS * slots) + x, ROWS, stride=slots), :] for m in range(3)]
                        for m in range(3):
                            for dx in (1, 0, -1):
                                for dy in (-1, 0, 1):
                                    term = tap[tap_of(m, dx, dy)] * rows[m]
                                    key = (x - 2 * dx, dy)
                                    sums[key] = sums[key] + term if key in sums else term
                    done = [x - 2] if x < slots else [x - 2, x]
                    for out in done:
                        before, centre, after = (sums.pop((out, dy)) for dy in (-1, 0, 1))
                        before = jnp.where(lane < 2, 0.0, pltpu.roll(before, 2, 1))
                        after = jnp.where(lane >= tile - 2, 0.0, pltpu.roll(after, tile - 2, 1))
                        depth[z, out + 2, at, :] = centre + before + after
        return carry

    lax.fori_loop(0, channels // ROWS, convolve, 0)


def edge_term(edge, z, shift):
    cells = pltpu.roll(edge[z], shift, 1)
    lane = lane_iota(cells.shape)
    return jnp.where((lane < 2) | (lane >= cells.shape[1] - 2), cells, 0.0)


def edge_shift(x, tile):
    shift = tile - 2 - FIRST_LANE - 4 * x
    if isinstance(x, int):
        return shift % tile
    return lax.rem(shift + tile, tile)


def rim_kernel(widths, weights, first, second, depth, edge, near, far):
    width = widths[lax.axis_index("gx")]
    channels, tile = weights.shape[1:]
    even = is_even("gy")
    lane = lane_iota((channels, tile))
    inside = (lane >= FIRST_LANE) & (lane < FIRST_LANE + 4 * width)
    on_right = ((lane - FIRST_LANE) & 2) == 0
    halo = []
    for pair in range(3):
        at = slice(pair * channels, (pair + 1) * channels)
        one, two = first[at, :].astype(F32), second[at, :].astype(F32)
        right = jnp.where(even, one, two)
        left = jnp.where(even, two, one)
        for k in range(2):
            right_k = pltpu.roll(right, FIRST_LANE - 2 * k, 1)
            left_k = pltpu.roll(left, FIRST_LANE + 4 - 2 * k, 1)
            halo.append(jnp.where(inside, jnp.where(on_right, right_k, left_k), 0.0))
    for z in range(ZOUT):
        total = None
        for m in range(3):
            for dx in (-1, 0, 1):
                weight = jnp.where(on_right, weights[tap_of(m, dx, 1)], weights[tap_of(m, dx, -1)])
                rows = halo[z + ZOUT * m]
                if dx:
                    rows = pltpu.roll(rows, (-8 * dx) % tile, 1)
                total = weight * rows if total is None else total + weight * rows
        edge[z] = total
    even = is_even("gx")
    for z in range(ZOUT):
        for r in range(2):
            to_lower = depth[z, r] + edge_term(edge, z, edge_shift(r - 2, tile))
            to_upper = depth[z, width + 2 + r] + edge_term(edge, z, edge_shift(width + r, tile))
            at = slice((2 * z + r) * channels, (2 * z + r + 1) * channels)
            near[at, :] = jnp.where(even, to_upper, to_lower).astype(BF16)
            far[at, :] = jnp.where(even, to_lower, to_upper).astype(BF16)


def slab_start(widths):
    slab = lax.axis_index("gx")
    start = jnp.int32(0)
    for d in range(widths.shape[0]):
        start = start + jnp.where(d < slab, widths[d], 0)
    return start


def depth_row(weights, depth, edge, z, x, tile):
    return depth[z, x + 2] + weights[DW_BIAS] + edge_term(edge, z, edge_shift(x, tile))


def finished_row(weights, cells, lifted, phase, width, mixed, z, x):
    channels = weights.shape[1]
    slots = cells.shape[1] // channels
    mixed = mixed + weights[PW_BIAS]
    active = jnp.maximum(mixed, 0.2 * mixed)
    field = cells[2 + z, pl.ds(x, channels, stride=slots), :]
    value = active + (field + lifted[lax.div(phase + x, CF)])
    return jnp.where(x < width, value, 0.0)


def mix_kernel(gathered, widths, mix, cells, weights, depth, edge, *refs):
    if gathered:
        coarse, value, lifted, mixer, across = refs
        parts, ncx, ncy = coarse.shape
    else:
        first, second, own_block, opposite, value, lifted, mixer, across, blocks = refs
        parts, own_rows, ncy = own_block.shape
        ncx = 4 * own_rows
    width = widths[lax.axis_index("gx")]
    here = lax.axis_index("gy")
    start = slab_start(widths)
    phase = lax.rem(start, CF)
    channels, tile = weights.shape[1:]
    slots = cells.shape[1] // channels

    if not gathered:
        even = is_even("gy")
        after, before = lax.rem(here + 1, 4), lax.rem(here + 3, 4)
        count = parts * own_rows
        strip = 3 * channels
        for message, owner in (
            (first, jnp.where(even, after, before)),
            (second, jnp.where(even, before, after)),
        ):
            terms = message[strip:, 0:ncy].astype(F32)
            sums = terms[0:count] + terms[count : 2 * count] + terms[2 * count : 3 * count]
            for k in range(parts):
                blocks[k, pl.ds(owner * own_rows, own_rows), :] = sums[k * own_rows : (k + 1) * own_rows]
        for block, owner in ((own_block, here), (opposite, lax.rem(here + 2, 4))):
            for k in range(parts):
                blocks[k, pl.ds(owner * own_rows, own_rows), :] = block[k]
    shape = (ncy, tile)
    cell = row_iota(shape) * CF
    place = lane_iota(shape) + here * tile
    along_y = ((place >= cell) & (place < cell + CF)).astype(F32)
    for k in range(parts):
        block = coarse[k] if gathered else blocks[k]
        across[k] = jnp.dot(block, along_y, precision=lax.Precision.HIGHEST, preferred_element_type=F32)
    for i in range(3):
        cell = lax.rem(lax.div(start, CF) + i, ncx)
        total = None
        for k in range(parts):
            term = weights[LIFT + k] * across[k, pl.ds(cell, 1), :]
            total = term if total is None else total + term
        lifted[i] = total

    group = 4
    wide = jnp.concatenate([mix[...]] * group, axis=1)
    wide = jnp.concatenate([wide] * group, axis=0)
    size = group * channels
    row, column = row_iota((size, size)), lane_iota((size, size))
    same = sum(
        ((row >= i * channels) & (row < (i + 1) * channels) & (column >= i * channels) & (column < (i + 1) * channels)).astype(F32)
        for i in range(group)
    )
    mixer[...] = jnp.where(same > 0, wide.astype(F32), 0.0).astype(BF16)

    for x in range(0, slots, group):
        depths = [
            jnp.concatenate([depth_row(weights, depth, edge, z, x + i, tile) for i in range(group)], axis=0).astype(BF16)
            for z in range(ZOUT)
        ]
        mixed = jnp.dot(mixer[...], jnp.concatenate(depths, axis=1), preferred_element_type=F32)
        for i in range(group):
            for z in range(ZOUT):
                part = mixed[i * channels : (i + 1) * channels, z * tile : (z + 1) * tile]
                value[z, pl.ds(x + i, channels, stride=slots), :] = finished_row(
                    weights, cells, lifted, phase, width, part, z, x + i
                )


def finish_kernel(widths, cells, weights, depth, edge, lifted, mixer, near, far, value_in, out, value, block, sems):
    width = widths[lax.axis_index("gx")]
    phase = lax.rem(slab_start(widths), CF)
    channels, tile = weights.shape[1:]
    slots = cells.shape[1] // channels
    even = is_even("gx")
    at_top = jnp.where(even, far[...].astype(F32), near[...].astype(F32))
    at_end = jnp.where(even, near[...].astype(F32), far[...].astype(F32))
    rows = (0, 1, width - 2, width - 1)
    depths = []
    for z in range(ZOUT):
        parts = []
        for i, x in enumerate(rows):
            arrived = at_top if i < 2 else at_end
            begin = (2 * z + i % 2) * channels
            parts.append(depth_row(weights, depth, edge, z, x, tile) + arrived[begin : begin + channels, :])
        depths.append(jnp.concatenate(parts, axis=0).astype(BF16))
    mixed = jnp.dot(mixer[...], jnp.concatenate(depths, axis=1), preferred_element_type=F32)
    for i, x in enumerate(rows):
        for z in range(ZOUT):
            part = mixed[i * channels : (i + 1) * channels, z * tile : (z + 1) * tile]
            value[z, pl.ds(x, channels, stride=slots), :] = finished_row(
                weights, cells, lifted, phase, width, part, z, x
            )
    chunk = 16
    copies = []
    for z in range(ZOUT):
        for part in range(channels // chunk):
            for o in range(part * chunk, (part + 1) * chunk):
                block[z, o] = value[z, o * slots : (o + 1) * slots, :].astype(BF16)
            part_of = pl.ds(part * chunk, chunk)
            copy = pltpu.make_async_copy(block.at[z, part_of], out.at[z, part_of], sems.at[part, z])
            copy.start()
            copies.append(copy)
    for copy in copies:
        copy.wait()


def shards(feature, widths, dw_weight, dw_bias, pw_weight, pw_bias, lift_weight, coarse):
    planes, channels, slots, tile = feature.shape
    ny = lax.axis_size("gy")
    parts, own_rows, ncy = coarse.shape
    gathered = ny != 4
    ncx = ny * own_rows
    smem = pl.BlockSpec(memory_space=pltpu.SMEM)
    vmem = pl.BlockSpec(memory_space=pltpu.VMEM)
    hbm = pl.BlockSpec(memory_space=pltpu.HBM)
    params = pltpu.CompilerParams(vmem_limit_bytes=VMEM_BYTES)
    shape = jax.ShapeDtypeStruct
    strip = shape((planes // 2 * channels + 32, tile), BF16)
    cells_shape = pltpu.VMEM((planes, channels * slots, tile), F32)
    value_shape = pltpu.VMEM((ZOUT, channels * slots, tile), F32)
    message = shape((2 * ZOUT * channels, tile), BF16)

    def swapped(array, axis, first):
        count = lax.axis_size(axis)
        pairs = []
        for i in range(first, count + first, 2):
            a, b = i % count, (i + 1) % count
            pairs += [(a, b), (b, a)]
        return lax.ppermute(array, axis, pairs)

    def pinned(array):
        return pltpu.with_memory_space_constraint(array, pltpu.HBM)

    if gathered:
        every = lax.all_gather(coarse, "gy", axis=1, tiled=True)
    else:
        opposite = lax.ppermute(coarse, "gy", [(i, (i + 2) % 4) for i in range(4)])
    small = (
        widths,
        dw_weight,
        dw_bias.reshape(1, channels),
        pw_bias.reshape(1, channels),
        lift_weight.T,
        coarse,
    )
    cells, weights, first, second = pl.pallas_call(
        pack_kernel,
        out_shape=(cells_shape, pltpu.VMEM((32, channels, tile), F32), strip, strip),
        in_specs=[hbm] * 7,
        out_specs=(vmem,) * 4,
        scratch_shapes=[
            pltpu.VMEM(feature.shape, BF16),
            pltpu.SMEM(widths.shape, jnp.int32),
            pltpu.VMEM(dw_weight.shape, F32),
            pltpu.VMEM((1, channels), F32),
            pltpu.VMEM((1, channels), F32),
            pltpu.VMEM((parts, channels), F32),
            pltpu.VMEM(coarse.shape, F32),
            pltpu.VMEM((32, channels), F32),
            pltpu.VMEM((32, tile), F32),
            pltpu.SemaphoreType.DMA((planes,)),
            pltpu.SemaphoreType.DMA((len(small),)),
        ],
        compiler_params=params,
    )(pinned(feature), *(pinned(array) for array in small))
    first = swapped(first, "gy", 0)
    second = swapped(second, "gy", 1)
    depth = pl.pallas_call(
        conv_kernel,
        out_shape=pltpu.VMEM((ZOUT, slots + 4, channels, tile), F32),
        in_specs=[vmem, vmem],
        out_specs=vmem,
        compiler_params=params,
        cost_estimate=pl.CostEstimate(flops=10**9, bytes_accessed=10**6, transcendentals=0),
    )(cells, weights)
    edge, near, far = pl.pallas_call(
        rim_kernel,
        out_shape=(pltpu.VMEM((ZOUT, channels, tile), F32), message, message),
        in_specs=[smem] + [vmem] * 4,
        out_specs=(vmem,) * 3,
        compiler_params=params,
    )(widths, weights, first, second, depth)
    near = swapped(near, "gx", 0)
    far = swapped(far, "gx", 1)
    blocks = (every,) if gathered else (first, second, coarse, opposite)
    value, lifted, mixer = pl.pallas_call(
        functools.partial(mix_kernel, gathered),
        out_shape=(
            value_shape,
            pltpu.VMEM((3, channels, tile), F32),
            pltpu.VMEM((4 * channels, 4 * channels), BF16),
        ),
        in_specs=[smem] + [vmem] * (5 + len(blocks)),
        out_specs=(vmem,) * 3,
        scratch_shapes=[pltpu.VMEM((parts, ncx, tile), F32)]
        + ([] if gathered else [pltpu.VMEM((parts, ncx, ncy), F32)]),
        compiler_params=params,
        cost_estimate=pl.CostEstimate(flops=10**9, bytes_accessed=10**6, transcendentals=0),
    )(widths, pw_weight, cells, weights, depth, edge, *blocks)
    out, _ = pl.pallas_call(
        finish_kernel,
        out_shape=(shape((ZOUT, channels, slots, tile), BF16), value_shape),
        in_specs=[smem] + [vmem] * 9,
        out_specs=(hbm, vmem),
        scratch_shapes=[
            pltpu.VMEM((ZOUT, channels, slots, tile), BF16),
            pltpu.SemaphoreType.DMA((channels // 16, ZOUT)),
        ],
        input_output_aliases={9: 1},
        compiler_params=params,
    )(widths, cells, weights, depth, edge, lifted, mixer, near, far, value)
    return out


def solution(mesh):
    placed = (P(None, None, "gx", "gy"), P(), P(), P(), P(), P(), P(), P(None, "gy", None))
    return jax.shard_map(
        shards, mesh=mesh, in_specs=placed, out_specs=P(None, None, "gx", "gy"), check_vma=False
    )
```

time: 59.6 us -> 23 us (0.39)
  the two profiles are of different devices: /device:TPU:18 before, /device:TPU:0 now
where the time goes in v4:
time: 23 us; the launch traced here: 22.8 us
  Pallas kernels  12.2 us (53%)
  starting transfers between devices  8.32 us (36%)
  waiting for transfers between devices  2.19 us (10%)
    ppermute x4, starting transfers between devices, swapped(): return lax.ppermute(array, axis, pairs)  5.35 us
    pallas_call x1, Pallas kernels, shards(): pl.pallas_call(pack_kernel, out_shape=(cells_shape, pltpu.VMEM((32, chann...  4.68 us
    pallas_call x1, Pallas kernels, shards(): pl.pallas_call(conv_kernel, out_shape=pltpu.VMEM((ZOUT, slots + 4, channe...  3.21 us
    ppermute x1, starting transfers between devices, shards(): opposite = lax.ppermute(coarse, 'gy', [(i, (i + 2) % 4) for i in range(4)])  2.97 us
    ppermute x4, waiting for transfers between devices, swapped(): return lax.ppermute(array, axis, pairs)  2.18 us
    pallas_call x1, Pallas kernels, shards(): pl.pallas_call(finish_kernel, out_shape=(shape((ZOUT, channels, slots, ti...  1.84 us
    pallas_call x1, Pallas kernels, shards(): pl.pallas_call(functools.partial(mix_kernel, gathered), out_shape=(value_...  1.65 us
    pallas_call x1, Pallas kernels, shards(): pl.pallas_call(rim_kernel, out_shape=(pltpu.VMEM((ZOUT, channels, tile),...  0.87 us
  transfers between devices with their start and end apart: 5, of which 2 were waited for; matrix products, arithmetic and copies ran while one was open for 0% of the time, Pallas kernels for 46%

profile of v4, /device:TPU:0, one launch (start us, length us, event | category | flops | bytes accessed | tf_op | source)
XLA Modules:
  0.0 22.8 jit_solution(9830672663268898486)
XLA Ops:
  0.0 3.0 %collective-permute-start.2 = (f32[3,2,32]{2,1,0:T(2,128)}, f32[3,2,32]{2,1,0:T(2,128)S(1)}, u32[]{:S(2)}, u32[]{:S(2)}) collective-permute-start(f32[3,2,32]{2,1,0:T(2,128)} %refs_2_.1), channel_id=1, source_target_pairs={{0,2},{1,3},{2,0},{3,1},{4,6},{5,7},{6,4},{7,5},{8,10},{9,11},{10,... | collective-permute-start | bytes 2312 | tf_op jit(solution)/shard_map/ppermute | solution.py:368
  3.0 4.7 %shard_map.82 = (f32[6,1536,128]{2,1,0:T(8,128)S(1)}, f32[32,64,128]{2,1,0:T(8,128)S(1)}, bf16[224,128]{1,0:T(8,128)(2,1)S(1)}, bf16[224,128]{1,0:T(8,128)(2,1)S(1)}) custom-call(bf16[6,64,24,128]{3,2,1,0:T(8,128)(2,1)} %feature.1, s32[8]{0:T(128)} %widths.5, f32[27,64]{1,0:T(8,128)} %taps_in.1, f32[1,64]{1,0:T(1,128)} %bitcast.4, f32[1,64]{1,0:T(1,128)} %bitcast.5, ...), custom_call_target="tpu_custom_call" | custom-call | tf_op jit(solution)/shard_map/pallas_call | solution.py:377
  7.7 1.6 %collective-permute-start = (bf16[224,128]{1,0:T(8,128)(2,1)S(1)}, bf16[224,128]{1,0:T(8,128)(2,1)S(1)}, u32[]{:S(2)}, u32[]{:S(2)}) collective-permute-start(bf16[224,128]{1,0:T(8,128)(2,1)S(1)} %get-tuple-element.18), channel_id=1, source_target_pairs={{0,1},{1,0},{2,3},{3,2},{4,5},{5,4},{6,7},{7,6},{8,9},{9,8},{10,11... | collective-permute-start | bytes 172040 | tf_op jit(solution)/shard_map/ppermute | solution.py:360
  9.2 0.0 collective-permute-start.1
  9.2 0.0 copy-start.2
  9.2 3.2 %shard_map.83.depth = f32[2,28,64,128]{3,2,1,0:T(8,128)S(1)} custom-call(f32[6,1536,128]{2,1,0:T(8,128)S(1)} %get-tuple-element.16.cells, f32[32,64,128]{2,1,0:T(8,128)S(1)} %get-tuple-element.17.weights), custom_call_target="tpu_custom_call" | custom-call | flops 1000000000 | bytes 1000000 | tf_op jit(solution)/shard_map/pallas_call | solution.py:399
  12.4 0.0 copy-start
  12.5 0.0 copy-start.1
  12.5 0.0 collective-permute-done.first.refs_0_
  12.5 1.8 %collective-permute-done.1.second.refs_1_ = bf16[224,128]{1,0:T(8,128)(2,1)S(1)} collective-permute-done((bf16[224,128]{1,0:T(8,128)(2,1)S(1)}, bf16[224,128]{1,0:T(8,128)(2,1)S(1)}, u32[]{:S(2)}, u32[]{:S(2)}) %collective-permute-start.1) | collective-permute-done | bytes 57376 | tf_op jit(solution)/shard_map/ppermute | solution.py:360
  14.3 0.0 copy-done.2
  14.3 0.9 %shard_map.84 = (f32[2,64,128]{2,1,0:T(8,128)S(1)}, bf16[256,128]{1,0:T(8,128)(2,1)S(1)}, bf16[256,128]{1,0:T(8,128)(2,1)S(1)}) custom-call(s32[8]{0:T(128)S(1)} %copy-done.2, f32[32,64,128]{2,1,0:T(8,128)S(1)} %get-tuple-element.17.weights, bf16[224,128]{1,0:T(8,128)(2,1)S(1)} %collective-permute-done.first.refs_0_, ...), custom_call_target="tpu_custom_call" | custom-call | tf_op jit(solution)/shard_map/pallas_call | solution.py:407
  15.2 0.1 collective-permute-start.3
  15.2 3.7 %collective-permute-start.4 = (bf16[256,128]{1,0:T(8,128)(2,1)S(1)}, bf16[256,128]{1,0:T(8,128)(2,1)S(1)}, u32[]{:S(2)}, u32[]{:S(2)}) collective-permute-start(bf16[256,128]{1,0:T(8,128)(2,1)S(1)} %get-tuple-element.24), channel_id=1, source_target_pairs={{4,8},{8,4},{12,16},{16,12},{20,24},{24,20},{28,0},{0,28},{5,9},{9... | collective-permute-start | bytes 196616 | tf_op jit(solution)/shard_map/ppermute | solution.py:360
  19.0 0.0 collective-permute-done.2.refs_3_
  19.0 0.0 copy-done
  19.0 0.0 copy-done.1
  19.0 1.7 %shard_map.85 = (f32[2,1536,128]{2,1,0:T(8,128)S(1)}, f32[3,64,128]{2,1,0:T(8,128)S(1)}, bf16[256,256]{1,0:T(8,128)(2,1)S(1)}) custom-call(s32[8]{0:T(128)S(1)} %copy-done.2, bf16[64,64]{1,0:T(8,128)(2,1)S(1)} %copy-done, f32[6,1536,128]{2,1,0:T(8,128)S(1)} %get-tuple-element.16.cells, f32[32,64,128]{2,1,0:T(8,128)S(1)} %get-tuple-element.17.weights, ...), custom_call_target="tpu_custom_call" | custom-call | flops 1000000000 | bytes 1000000 | tf_op jit(solution)/shard_map/pallas_call | solution.py:417
  20.6 0.0 collective-permute-done.3.near
  20.6 0.4 %collective-permute-done.4.far = bf16[256,128]{1,0:T(8,128)(2,1)S(1)} collective-permute-done((bf16[256,128]{1,0:T(8,128)(2,1)S(1)}, bf16[256,128]{1,0:T(8,128)(2,1)S(1)}, u32[]{:S(2)}, u32[]{:S(2)}) %collective-permute-start.4) | collective-permute-done | bytes 65568 | tf_op jit(solution)/shard_map/ppermute | solution.py:360
  21.0 1.8 %shard_map.86 = (bf16[2,64,24,128]{3,2,1,0:T(8,128)(2,1)}, f32[2,1536,128]{2,1,0:T(8,128)S(1)}) custom-call(s32[8]{0:T(128)S(1)} %copy-done.2, f32[6,1536,128]{2,1,0:T(8,128)S(1)} %get-tuple-element.16.cells, f32[32,64,128]{2,1,0:T(8,128)S(1)} %get-tuple-element.17.weights, f32[2,28,64,128]{3,2,1,0:T(8,128)S(1)} %shard_map.83.depth, ...), custom_call_target="tpu_custom_call", output_to_operand_aliasing={{1}: (9, {})} | custom-call | tf_op jit(solution)/shard_map/pallas_call | solution.py:431
Async XLA Ops:
  0.0 19.0 %collective-permute-start.2 = (f32[3,2,32]{2,1,0:T(2,128)}, f32[3,2,32]{2,1,0:T(2,128)S(1)}, u32[]{:S(2)}, u32[]{:S(2)}) collective-permute-start(f32[3,2,32]{2,1,0:T(2,128)} %refs_2_.1), channel_id=1, source_target_pairs={{0,2},{1,3},{2,0},{3,1},{4,6},{5,7},{6,4},{7,5},{8,10},{9,11},{10,... | collective-permute-start | bytes 2312 | tf_op jit(solution)/shard_map/ppermute | solution.py:368
  7.7 4.8 %collective-permute-start = (bf16[224,128]{1,0:T(8,128)(2,1)S(1)}, bf16[224,128]{1,0:T(8,128)(2,1)S(1)}, u32[]{:S(2)}, u32[]{:S(2)}) collective-permute-start(bf16[224,128]{1,0:T(8,128)(2,1)S(1)} %get-tuple-element.18), channel_id=1, source_target_pairs={{0,1},{1,0},{2,3},{3,2},{4,5},{5,4},{6,7},{7,6},{8,9},{9,8},{10,11... | collective-permute-start | bytes 172040 | tf_op jit(solution)/shard_map/ppermute | solution.py:360
  9.2 5.1 %collective-permute-start.1 = (bf16[224,128]{1,0:T(8,128)(2,1)S(1)}, bf16[224,128]{1,0:T(8,128)(2,1)S(1)}, u32[]{:S(2)}, u32[]{:S(2)}) collective-permute-start(bf16[224,128]{1,0:T(8,128)(2,1)S(1)} %get-tuple-element.19), channel_id=1, source_target_pairs={{1,2},{2,1},{3,0},{0,3},{5,6},{6,5},{7,4},{4,7},{9,10},{10,9},{11,... | collective-permute-start | bytes 172040 | tf_op jit(solution)/shard_map/ppermute | solution.py:360
  9.2 5.1 %copy-start.2 = (s32[8]{0:T(128)S(1)}, s32[8]{0:T(128)}, u32[]{:S(2)}) copy-start(s32[8]{0:T(128)} %widths.5) | copy-start | bytes 100
  12.4 6.5 %copy-start = (bf16[64,64]{1,0:T(8,128)(2,1)S(1)}, bf16[64,64]{1,0:T(8,128)(2,1)}, u32[]{:S(2)}) copy-start(bf16[64,64]{1,0:T(8,128)(2,1)} %mix.1) | copy-start | bytes 24580
  12.5 6.5 %copy-start.1 = (f32[3,2,32]{2,1,0:T(2,128)S(1)}, f32[3,2,32]{2,1,0:T(2,128)}, u32[]{:S(2)}) copy-start(f32[3,2,32]{2,1,0:T(2,128)} %refs_2_.1) | copy-start | bytes 2308
  15.2 5.5 %collective-permute-start.3 = (bf16[256,128]{1,0:T(8,128)(2,1)S(1)}, bf16[256,128]{1,0:T(8,128)(2,1)S(1)}, u32[]{:S(2)}, u32[]{:S(2)}) collective-permute-start(bf16[256,128]{1,0:T(8,128)(2,1)S(1)} %get-tuple-element.23), channel_id=1, source_target_pairs={{0,4},{4,0},{8,12},{12,8},{16,20},{20,16},{24,28},{28,24},{1,5},{5... | collective-permute-start | bytes 196616 | tf_op jit(solution)/shard_map/ppermute | solution.py:360
  15.2 5.8 %collective-permute-start.4 = (bf16[256,128]{1,0:T(8,128)(2,1)S(1)}, bf16[256,128]{1,0:T(8,128)(2,1)S(1)}, u32[]{:S(2)}, u32[]{:S(2)}) collective-permute-start(bf16[256,128]{1,0:T(8,128)(2,1)S(1)} %get-tuple-element.24), channel_id=1, source_target_pairs={{4,8},{8,4},{12,16},{16,12},{20,24},{24,20},{28,0},{0,28},{5,9},{9... | collective-permute-start | bytes 196616 | tf_op jit(solution)/shard_map/ppermute | solution.py:360

commit v5 on v4

v5 whole, which is shorter than its diff:
```python
import functools

import jax
import jax.numpy as jnp
from jax import lax
from jax.experimental import pallas as pl
from jax.experimental.pallas import tpu as pltpu
from jax.sharding import PartitionSpec as P

XW = 16
ZOUT = 2
CF = 16
ROWS = 8
SPLIT = 4
CHUNK = 16
DW_BIAS, PW_BIAS, LIFT = 27, 28, 29
F32 = jnp.float32
BF16 = jnp.bfloat16
VMEM_BYTES = 14 * 1024 * 1024


def lane_iota(shape):
    return lax.broadcasted_iota(jnp.int32, shape, len(shape) - 1)


def row_iota(shape):
    return lax.broadcasted_iota(jnp.int32, shape, len(shape) - 2)


def tap_of(m, dx, dy):
    return 9 * m + 3 * (dx + 1) + (dy + 1)


def is_even(axis):
    return lax.rem(lax.axis_index(axis), 2) == 0


def pack_kernel(
    feature, widths_in, taps_in, dw_bias_in, pw_bias_in, lift_in, coarse_in,
    planes, weights, first, second,
    widths, taps, dw_bias, pw_bias, lift, coarse, stacked, tail, picked, sems, small_sems,
):
    count, channels, slots, tile = feature.shape
    chunks = range(0, channels, CHUNK)

    def copy_of(c):
        at = pl.ds(c, CHUNK)
        return pltpu.make_async_copy(feature.at[:, at], planes.at[:, at], sems.at[c // CHUNK])

    small = [
        pltpu.make_async_copy(source, target, small_sems.at[i])
        for i, (source, target) in enumerate(
            (
                (widths_in, widths),
                (taps_in, taps),
                (dw_bias_in, dw_bias),
                (pw_bias_in, pw_bias),
                (lift_in, lift),
                (coarse_in, coarse),
            )
        )
    ]
    for copy in small:
        copy.start()
    for c in chunks:
        copy_of(c).start()

    shape = (tile, tile)
    lane, row = lane_iota(shape), row_iota(shape)
    column = jnp.where((lane & 3) < 2, tile - 2 + (lane & 3), (lane & 3) - 2)
    plane = (lane & 31) >> 2
    picks = jnp.concatenate(
        [((row == column) & (plane == z)).astype(F32) for z in range(count)], axis=0
    ).astype(BF16)

    for copy in small:
        copy.wait()
    width = widths[lax.axis_index("gx")]
    stacked[0:DW_BIAS, :] = taps[...]
    stacked[DW_BIAS : DW_BIAS + 1, :] = dw_bias[...]
    stacked[PW_BIAS : PW_BIAS + 1, :] = pw_bias[...]
    stacked[LIFT : LIFT + 3, :] = lift[...]
    turned = jnp.transpose(stacked[...])
    for t in range(stacked.shape[0]):
        weights[t] = jnp.broadcast_to(turned[:, t : t + 1], (channels, tile))

    parts, own_rows, ncy = coarse.shape
    tail[...] = jnp.zeros_like(tail)
    if 3 * ncy <= tile:
        for k in range(parts):
            rest = coarse[k]
            for p in range(3):
                term = rest.astype(BF16).astype(F32)
                rest = rest - term
                tail[k * own_rows : (k + 1) * own_rows, p * ncy : (p + 1) * ncy] = term
    for message in (first, second):
        message[channels:, :] = tail[...].astype(BF16)

    shape = (channels, tile)
    lane = lane_iota(shape)
    member = (lane & 31) >> 3
    on_left = (lane & 2) != 0
    scale = []
    for dx in (-1, 0, 1):
        total = None
        for m in range(3):
            weight = jnp.where(on_left, weights[tap_of(m, dx, 1)], weights[tap_of(m, dx, -1)])
            total = weight if total is None else jnp.where(member == m, weight, total)
        scale.append(total)

    for c in chunks:
        copy_of(c).wait()
        rows = [
            jnp.concatenate([planes[z, c + k].astype(F32) for k in range(CHUNK)], axis=0).astype(BF16)
            for z in range(count)
        ]
        picked[c * slots : (c + CHUNK) * slots, :] = jnp.dot(
            jnp.concatenate(rows, axis=1), picks, preferred_element_type=F32
        )

    groups = slots // 4
    held, moved = {}, {}
    for q in range(groups):
        rows = [picked[pl.ds(4 * q + i, channels, stride=slots), :] for i in range(4)]
        rows = jnp.where(
            lane < 64, jnp.where(lane < 32, rows[0], rows[1]), jnp.where(lane < 96, rows[2], rows[3])
        )
        held[q] = jnp.where(4 * q + (lane >> 5) < width, rows, 0.0)
    for q in range(-1, groups):
        low = held.get(q + 1, jnp.zeros(shape, F32))
        high = held.get(q, jnp.zeros(shape, F32))
        moved[q] = pltpu.roll(jnp.where(lane < 64, low, high), 64, 1)
    sums = []
    for q in range(-1, groups + 1):
        total = None
        for weight, rows in ((scale[0], moved.get(q - 1)), (scale[1], held.get(q)), (scale[2], moved.get(q))):
            if rows is not None:
                total = weight * rows if total is None else total + weight * rows
        sums.append(total + pltpu.roll(total, tile - 8, 1) + pltpu.roll(total, tile - 16, 1))
    packed = []
    for half in range(2):
        total = sums[4 * half]
        for k in range(1, 4):
            total = jnp.where(((lane >> 3) & 3) == k, pltpu.roll(sums[4 * half + k], 8 * k, 1), total)
        packed.append(total)
    left = jnp.where(on_left, packed[0], pltpu.roll(packed[1], tile - 2, 1))
    right = jnp.where(on_left, pltpu.roll(packed[1], 2, 1), packed[0])
    even = is_even("gy")
    first[0:channels, :] = jnp.where(even, right, left).astype(BF16)
    second[0:channels, :] = jnp.where(even, left, right).astype(BF16)


def shifted_sum(before, centre, after):
    lane = lane_iota(centre.shape)
    tile = centre.shape[-1]
    before = jnp.where(lane < 2, 0.0, pltpu.roll(before, 2, 1))
    after = jnp.where(lane >= tile - 2, 0.0, pltpu.roll(after, tile - 2, 1))
    return centre + before + after


def convolve_block(cells, weights, depth, b, first_block):
    channels = weights.shape[1]
    slots = cells.shape[1] // channels
    at = pl.ds(pl.multiple_of(b * ROWS, ROWS), ROWS)
    to = pl.ds(pl.multiple_of((b - first_block) * ROWS, ROWS), ROWS)
    tap = [weights[t, at, :] for t in range(27)]
    for z in range(ZOUT):
        for parity in range(2):
            sums = {}
            for x in range(parity, slots, 2):
                rows = [cells[z + ZOUT * m, pl.ds(b * (ROWS * slots) + x, ROWS, stride=slots), :] for m in range(3)]
                for m in range(3):
                    for dx in (1, 0, -1):
                        out = x - 2 * dx
                        if 0 <= out < slots:
                            for dy in (-1, 0, 1):
                                term = tap[tap_of(m, dx, dy)] * rows[m]
                                key = (out, dy)
                                sums[key] = sums[key] + term if key in sums else term
                for out in [x - 2] if x + 2 < slots else [x - 2, x]:
                    if out >= 0:
                        depth[z, out, to, :] = shifted_sum(*(sums.pop((out, dy)) for dy in (-1, 0, 1)))


def conv_kernel(widths, planes, weights, cells, depth, rims):
    width = widths[lax.axis_index("gx")]
    count, channels, slots, tile = planes.shape
    valid = row_iota((slots, tile)) < width

    def outer_rows(b, carry):
        for z in range(count):
            for k in range(ROWS):
                at = pl.ds(pl.multiple_of((b * ROWS + k) * slots, ROWS), slots)
                cells[z, at, :] = jnp.where(valid, planes[z, b * ROWS + k].astype(F32), 0.0)
        at = pl.ds(pl.multiple_of(b * ROWS, ROWS), ROWS)
        for i, (x, dx) in enumerate(((0, 1), (1, 1), (width - 2, -1), (width - 1, -1))):
            for z in range(ZOUT):
                rows = [cells[z + ZOUT * m, pl.ds(b * (ROWS * slots) + x, ROWS, stride=slots), :] for m in range(3)]
                parts = [
                    sum(weights[tap_of(m, dx, dy), at, :] * rows[m] for m in range(3)) for dy in (-1, 0, 1)
                ]
                rims[z, i, at, :] = shifted_sum(*parts)
        return carry

    lax.fori_loop(0, channels // ROWS, outer_rows, 0)

    def convolve(b, carry):
        convolve_block(cells, weights, depth, b, 0)
        return carry

    lax.fori_loop(0, SPLIT, convolve, 0)


def edge_term(edge, z, x):
    tile = edge.shape[2]
    group = x // 4 + 1 if isinstance(x, int) else lax.div(x, 4) + 1
    at = x % 4 if isinstance(x, int) else lax.rem(x, 4)
    begin = 32 * at + 8 * (group & 3) + 4 * z
    cells = pltpu.roll(edge[group >> 2], tile - 2 - begin, 1)
    lane = lane_iota(cells.shape)
    return jnp.where((lane < 2) | (lane >= tile - 2), cells, 0.0)


def rim_kernel(widths, first, second, rims, edge, near, far):
    width = widths[lax.axis_index("gx")]
    _, _, channels, tile = rims.shape
    even = is_even("gy")
    one, two = first[0:channels, :].astype(F32), second[0:channels, :].astype(F32)
    right = jnp.where(even, one, two)
    left = jnp.where(even, two, one)
    on_left = (lane_iota((channels, tile)) & 2) != 0
    edge[0] = jnp.where(on_left, pltpu.roll(left, 2, 1), pltpu.roll(right, tile - 2, 1))
    edge[1] = jnp.where(on_left, left, right)
    even = is_even("gx")
    for z in range(ZOUT):
        for r in range(2):
            to_lower = rims[z, r] + edge_term(edge, z, r - 2)
            to_upper = rims[z, 2 + r] + edge_term(edge, z, width + r)
            at = slice((2 * z + r) * channels, (2 * z + r + 1) * channels)
            near[at, :] = jnp.where(even, to_upper, to_lower).astype(BF16)
            far[at, :] = jnp.where(even, to_lower, to_upper).astype(BF16)


def slab_start(widths):
    slab = lax.axis_index("gx")
    start = jnp.int32(0)
    for d in range(widths.shape[0]):
        start = start + jnp.where(d < slab, widths[d], 0)
    return start


def depth_row(weights, depths, edge, z, x):
    own = jnp.concatenate([depth[z, x] for depth in depths], axis=0)
    return own + weights[DW_BIAS] + edge_term(edge, z, x)


def finished_row(weights, cells, lifted, phase, width, mixed, z, x):
    channels = weights.shape[1]
    slots = cells.shape[1] // channels
    mixed = mixed + weights[PW_BIAS]
    active = jnp.maximum(mixed, 0.2 * mixed)
    field = cells[2 + z, pl.ds(x, channels, stride=slots), :]
    value = active + (field + lifted[lax.div(phase + x, CF)])
    return jnp.where(x < width, value, 0.0)


def mix_kernel(gathered, widths, mix, cells, weights, depth, edge, *refs):
    if gathered:
        coarse, value, rest, lifted, mixer, across = refs
        parts, ncx, ncy = coarse.shape
    else:
        first, second, own_block, opposite, value, rest, lifted, mixer, across, blocks = refs
        parts, own_rows, ncy = own_block.shape
        ncx = 4 * own_rows
    width = widths[lax.axis_index("gx")]
    here = lax.axis_index("gy")
    start = slab_start(widths)
    phase = lax.rem(start, CF)
    channels, tile = weights.shape[1:]
    slots = cells.shape[1] // channels

    def convolve(b, carry):
        convolve_block(cells, weights, rest, b, SPLIT)
        return carry

    lax.fori_loop(SPLIT, channels // ROWS, convolve, 0)

    if not gathered:
        even = is_even("gy")
        after, before = lax.rem(here + 1, 4), lax.rem(here + 3, 4)
        count = parts * own_rows
        for message, owner in (
            (first, jnp.where(even, after, before)),
            (second, jnp.where(even, before, after)),
        ):
            terms = message[channels:, :].astype(F32)[0:count, :]
            sums = terms[:, 0:ncy] + terms[:, ncy : 2 * ncy] + terms[:, 2 * ncy : 3 * ncy]
            for k in range(parts):
                blocks[k, pl.ds(owner * own_rows, own_rows), :] = sums[k * own_rows : (k + 1) * own_rows]
        for block, owner in ((own_block, here), (opposite, lax.rem(here + 2, 4))):
            for k in range(parts):
                blocks[k, pl.ds(owner * own_rows, own_rows), :] = block[k]
    shape = (ncy, tile)
    cell = row_iota(shape) * CF
    place = lane_iota(shape) + here * tile
    along_y = ((place >= cell) & (place < cell + CF)).astype(F32)
    for k in range(parts):
        block = coarse[k] if gathered else blocks[k]
        across[k] = jnp.dot(block, along_y, precision=lax.Precision.HIGHEST, preferred_element_type=F32)
    for i in range(3):
        cell = lax.rem(lax.div(start, CF) + i, ncx)
        total = None
        for k in range(parts):
            term = weights[LIFT + k] * across[k, pl.ds(cell, 1), :]
            total = term if total is None else total + term
        lifted[i] = total

    group = 4
    wide = jnp.concatenate([mix[...]] * group, axis=1)
    wide = jnp.concatenate([wide] * group, axis=0)
    size = group * channels
    row, column = row_iota((size, size)), lane_iota((size, size))
    same = sum(
        ((row >= i * channels) & (row < (i + 1) * channels) & (column >= i * channels) & (column < (i + 1) * channels)).astype(F32)
        for i in range(group)
    )
    mixer[...] = jnp.where(same > 0, wide.astype(F32), 0.0).astype(BF16)

    for x in range(0, slots, group):
        depths = [
            jnp.concatenate([depth_row(weights, (depth, rest), edge, z, x + i) for i in range(group)], axis=0).astype(BF16)
            for z in range(ZOUT)
        ]
        mixed = jnp.dot(mixer[...], jnp.concatenate(depths, axis=1), preferred_element_type=F32)
        for i in range(group):
            for z in range(ZOUT):
                part = mixed[i * channels : (i + 1) * channels, z * tile : (z + 1) * tile]
                value[z, pl.ds(x + i, channels, stride=slots), :] = finished_row(
                    weights, cells, lifted, phase, width, part, z, x + i
                )


def finish_kernel(widths, cells, weights, depth, rest, edge, lifted, mixer, near, far, value_in, out, value, block, sems):
    width = widths[lax.axis_index("gx")]
    phase = lax.rem(slab_start(widths), CF)
    channels, tile = weights.shape[1:]
    slots = cells.shape[1] // channels
    even = is_even("gx")
    at_top = jnp.where(even, far[...].astype(F32), near[...].astype(F32))
    at_end = jnp.where(even, near[...].astype(F32), far[...].astype(F32))
    rows = (0, 1, width - 2, width - 1)
    depths = []
    for z in range(ZOUT):
        parts = []
        for i, x in enumerate(rows):
            arrived = at_top if i < 2 else at_end
            begin = (2 * z + i % 2) * channels
            parts.append(depth_row(weights, (depth, rest), edge, z, x) + arrived[begin : begin + channels, :])
        depths.append(jnp.concatenate(parts, axis=0).astype(BF16))
    mixed = jnp.dot(mixer[...], jnp.concatenate(depths, axis=1), preferred_element_type=F32)
    for i, x in enumerate(rows):
        for z in range(ZOUT):
            part = mixed[i * channels : (i + 1) * channels, z * tile : (z + 1) * tile]
            value[z, pl.ds(x, channels, stride=slots), :] = finished_row(
                weights, cells, lifted, phase, width, part, z, x
            )
    chunk = 16
    copies = []
    for z in range(ZOUT):
        for part in range(channels // chunk):
            for o in range(part * chunk, (part + 1) * chunk):
                block[z, o] = value[z, o * slots : (o + 1) * slots, :].astype(BF16)
            part_of = pl.ds(part * chunk, chunk)
            copy = pltpu.make_async_copy(block.at[z, part_of], out.at[z, part_of], sems.at[part, z])
            copy.start()
            copies.append(copy)
    for copy in copies:
        copy.wait()


def shards(feature, widths, dw_weight, dw_bias, pw_weight, pw_bias, lift_weight, coarse):
    planes, channels, slots, tile = feature.shape
    ny = lax.axis_size("gy")
    parts, own_rows, ncy = coarse.shape
    gathered = ny != 4
    ncx = ny * own_rows
    smem = pl.BlockSpec(memory_space=pltpu.SMEM)
    vmem = pl.BlockSpec(memory_space=pltpu.VMEM)
    hbm = pl.BlockSpec(memory_space=pltpu.HBM)
    params = pltpu.CompilerParams(vmem_limit_bytes=VMEM_BYTES)
    shape = jax.ShapeDtypeStruct
    strip = shape((channels + 16, tile), BF16)
    cells_shape = pltpu.VMEM((planes, channels * slots, tile), F32)
    value_shape = pltpu.VMEM((ZOUT, channels * slots, tile), F32)
    message = shape((2 * ZOUT * channels, tile), BF16)

    def swapped(array, axis, first):
        count = lax.axis_size(axis)
        pairs = []
        for i in range(first, count + first, 2):
            a, b = i % count, (i + 1) % count
            pairs += [(a, b), (b, a)]
        return lax.ppermute(array, axis, pairs)

    def pinned(array):
        return pltpu.with_memory_space_constraint(array, pltpu.HBM)

    if gathered:
        every = lax.all_gather(coarse, "gy", axis=1, tiled=True)
    else:
        opposite = lax.ppermute(coarse, "gy", [(i, (i + 2) % 4) for i in range(4)])
    small = (
        widths,
        dw_weight,
        dw_bias.reshape(1, channels),
        pw_bias.reshape(1, channels),
        lift_weight.T,
        coarse,
    )
    held, weights, first, second = pl.pallas_call(
        pack_kernel,
        out_shape=(pltpu.VMEM(feature.shape, BF16), pltpu.VMEM((32, channels, tile), F32), strip, strip),
        in_specs=[hbm] * 7,
        out_specs=(vmem,) * 4,
        scratch_shapes=[
            pltpu.SMEM(widths.shape, jnp.int32),
            pltpu.VMEM(dw_weight.shape, F32),
            pltpu.VMEM((1, channels), F32),
            pltpu.VMEM((1, channels), F32),
            pltpu.VMEM((parts, channels), F32),
            pltpu.VMEM(coarse.shape, F32),
            pltpu.VMEM((32, channels), F32),
            pltpu.VMEM((16, tile), F32),
            pltpu.VMEM((channels * slots, tile), F32),
            pltpu.SemaphoreType.DMA((channels // CHUNK,)),
            pltpu.SemaphoreType.DMA((len(small),)),
        ],
        compiler_params=params,
    )(pinned(feature), *(pinned(array) for array in small))
    first = swapped(first, "gy", 0)
    second = swapped(second, "gy", 1)
    early = SPLIT * ROWS
    cells, depth, rims = pl.pallas_call(
        conv_kernel,
        out_shape=(
            cells_shape,
            pltpu.VMEM((ZOUT, slots, early, tile), F32),
            pltpu.VMEM((ZOUT, 4, channels, tile), F32),
        ),
        in_specs=[smem, vmem, vmem],
        out_specs=(vmem,) * 3,
        compiler_params=params,
        cost_estimate=pl.CostEstimate(flops=10**9, bytes_accessed=10**6, transcendentals=0),
    )(widths, held, weights)
    edge, near, far = pl.pallas_call(
        rim_kernel,
        out_shape=(pltpu.VMEM((2, channels, tile), F32), message, message),
        in_specs=[smem] + [vmem] * 3,
        out_specs=(vmem,) * 3,
        compiler_params=params,
    )(widths, first, second, rims)
    near = swapped(near, "gx", 0)
    far = swapped(far, "gx", 1)
    blocks = (every,) if gathered else (first, second, coarse, opposite)
    value, rest, lifted, mixer = pl.pallas_call(
        functools.partial(mix_kernel, gathered),
        out_shape=(
            value_shape,
            pltpu.VMEM((ZOUT, slots, channels - early, tile), F32),
            pltpu.VMEM((3, channels, tile), F32),
            pltpu.VMEM((4 * channels, 4 * channels), BF16),
        ),
        in_specs=[smem] + [vmem] * (5 + len(blocks)),
        out_specs=(vmem,) * 4,
        scratch_shapes=[pltpu.VMEM((parts, ncx, tile), F32)]
        + ([] if gathered else [pltpu.VMEM((parts, ncx, ncy), F32)]),
        compiler_params=params,
        cost_estimate=pl.CostEstimate(flops=10**9, bytes_accessed=10**6, transcendentals=0),
    )(widths, pw_weight, cells, weights, depth, edge, *blocks)
    out, _ = pl.pallas_call(
        finish_kernel,
        out_shape=(shape((ZOUT, channels, slots, tile), BF16), value_shape),
        in_specs=[smem] + [vmem] * 10,
        out_specs=(hbm, vmem),
        scratch_shapes=[
            pltpu.VMEM((ZOUT, channels, slots, tile), BF16),
            pltpu.SemaphoreType.DMA((channels // 16, ZOUT)),
        ],
        input_output_aliases={10: 1},
        compiler_params=params,
    )(widths, cells, weights, depth, rest, edge, lifted, mixer, near, far, value)
    return out


def solution(mesh):
    placed = (P(None, None, "gx", "gy"), P(), P(), P(), P(), P(), P(), P(None, "gy", None))
    return jax.shard_map(
        shards, mesh=mesh, in_specs=placed, out_specs=P(None, None, "gx", "gy"), check_vma=False
    )
```

time: 23 us -> 23 us (level)
  Pallas kernels: 12.2 us -> 13 us
  waiting for transfers between devices: 2.19 us -> 1.41 us
    pallas_call x1, Pallas kernels: 1.65 us -> 3.2 us  [shards(): pl.pallas_call(functools.partial(mix_kernel, gathered), out_shape=(value_...]
    ppermute x4, waiting for transfers between devices: 2.18 us -> 1.4 us  [swapped(): return lax.ppermute(array, axis, pairs)]
    pallas_call x3, Pallas kernels: 8.76 us -> 7.99 us  [the longest x1 4 us: shards(): pl.pallas_call(pack_kernel, out_shape=(pltpu.VMEM(feature.shape, BF16), p...]
  transfers between devices with their start and end apart: 5 -> 5, of which waited for: 2 -> 1; matrix products, arithmetic and copies ran while one was open for 0% -> 0% of each run, Pallas kernels for 46% -> 49%
where the time goes in v5:
time: 23 us; the launch traced here: 22.9 us
  Pallas kernels  13 us (57%)
  starting transfers between devices  8.32 us (36%)
  waiting for transfers between devices  1.41 us (6%)
    ppermute x4, starting transfers between devices, swapped(): return lax.ppermute(array, axis, pairs)  5.35 us
    pallas_call x1, Pallas kernels, shards(): pl.pallas_call(pack_kernel, out_shape=(pltpu.VMEM(feature.shape, BF16), p...  4 us
    pallas_call x1, Pallas kernels, shards(): pl.pallas_call(conv_kernel, out_shape=(cells_shape, pltpu.VMEM((ZOUT, slo...  3.24 us
    pallas_call x1, Pallas kernels, shards(): pl.pallas_call(functools.partial(mix_kernel, gathered), out_shape=(value_...  3.2 us
    ppermute x1, starting transfers between devices, shards(): opposite = lax.ppermute(coarse, 'gy', [(i, (i + 2) % 4) for i in range(4)])  2.97 us
    pallas_call x1, Pallas kernels, shards(): pl.pallas_call(finish_kernel, out_shape=(shape((ZOUT, channels, slots, ti...  1.84 us
    ppermute x4, waiting for transfers between devices, swapped(): return lax.ppermute(array, axis, pairs)  1.4 us
    pallas_call x1, Pallas kernels, shards(): pl.pallas_call(rim_kernel, out_shape=(pltpu.VMEM((2, channels, tile), F32...  0.75 us
  transfers between devices with their start and end apart: 5, of which 1 were waited for; matrix products, arithmetic and copies ran while one was open for 0% of the time, Pallas kernels for 49%

profile of v5, /device:TPU:0, one launch (start us, length us, event | category | flops | bytes accessed | tf_op | source)
XLA Modules:
  0.0 22.9 jit_solution(2408831427827919308)
XLA Ops:
  0.0 0.0 copy-start.2
  0.0 3.0 %collective-permute-start.2 = (f32[3,2,32]{2,1,0:T(2,128)}, f32[3,2,32]{2,1,0:T(2,128)S(1)}, u32[]{:S(2)}, u32[]{:S(2)}) collective-permute-start(f32[3,2,32]{2,1,0:T(2,128)} %refs_2_.1), channel_id=1, source_target_pairs={{0,2},{1,3},{2,0},{3,1},{4,6},{5,7},{6,4},{7,5},{8,10},{9,11},{10,... | collective-permute-start | bytes 2312 | tf_op jit(solution)/shard_map/ppermute | solution.py:411
  3.0 4.0 %shard_map.82 = (bf16[6,64,24,128]{3,2,1,0:T(8,128)(2,1)S(1)}, f32[32,64,128]{2,1,0:T(8,128)S(1)}, bf16[80,128]{1,0:T(8,128)(2,1)S(1)}, bf16[80,128]{1,0:T(8,128)(2,1)S(1)}) custom-call(bf16[6,64,24,128]{3,2,1,0:T(8,128)(2,1)} %feature.1, s32[8]{0:T(128)} %widths.7, f32[27,64]{1,0:T(8,128)} %taps_in.1, f32[1,64]{1,0:T(1,128)} %bitcast.4, f32[1,64]{1,0:T(1,128)} %bitcast.5, ...), custom_call_target="tpu_custom_call" | custom-call | tf_op jit(solution)/shard_map/pallas_call | solution.py:420
  7.0 0.0 copy-start
  7.0 0.0 copy-start.1
  7.0 1.6 %collective-permute-start = (bf16[80,128]{1,0:T(8,128)(2,1)S(1)}, bf16[80,128]{1,0:T(8,128)(2,1)S(1)}, u32[]{:S(2)}, u32[]{:S(2)}) collective-permute-start(bf16[80,128]{1,0:T(8,128)(2,1)S(1)} %get-tuple-element.24), channel_id=1, source_target_pairs={{0,1},{1,0},{2,3},{3,2},{4,5},{5,4},{6,7},{7,6},{8,9},{9,8},{10,11... | collective-permute-start | bytes 61448 | tf_op jit(solution)/shard_map/ppermute | solution.py:403
  8.6 0.0 collective-permute-start.1
  8.6 0.0 copy-done.2
  8.6 3.2 %shard_map.83 = (f32[6,1536,128]{2,1,0:T(8,128)S(1)}, f32[2,24,32,128]{3,2,1,0:T(8,128)S(1)}, f32[2,4,64,128]{3,2,1,0:T(8,128)S(1)}) custom-call(s32[8]{0:T(128)S(1)} %copy-done.2, bf16[6,64,24,128]{3,2,1,0:T(8,128)(2,1)S(1)} %get-tuple-element.20.planes, f32[32,64,128]{2,1,0:T(8,128)S(1)} %get-tuple-element.21.weights), custom_call_target="tpu_custom_call" | custom-call | flops 1000000000 | bytes 1000000 | tf_op jit(solution)/shard_map/pallas_call | solution.py:443
  11.8 0.0 collective-permute-done.first.refs_0_
  11.8 1.4 %collective-permute-done.1.second.refs_1_ = bf16[80,128]{1,0:T(8,128)(2,1)S(1)} collective-permute-done((bf16[80,128]{1,0:T(8,128)(2,1)S(1)}, bf16[80,128]{1,0:T(8,128)(2,1)S(1)}, u32[]{:S(2)}, u32[]{:S(2)}) %collective-permute-start.1) | collective-permute-done | bytes 20512 | tf_op jit(solution)/shard_map/ppermute | solution.py:403
  13.2 0.7 %shard_map.84 = (f32[2,64,128]{2,1,0:T(8,128)S(1)}, bf16[256,128]{1,0:T(8,128)(2,1)S(1)}, bf16[256,128]{1,0:T(8,128)(2,1)S(1)}) custom-call(s32[8]{0:T(128)S(1)} %copy-done.2, bf16[80,128]{1,0:T(8,128)(2,1)S(1)} %collective-permute-done.first.refs_0_, bf16[80,128]{1,0:T(8,128)(2,1)S(1)} %collective-permute-done.1.second.refs_1_, ...), custom_call_target="tpu_custom_call" | custom-call | tf_op jit(solution)/shard_map/pallas_call | solution.py:455
  14.0 0.1 collective-permute-start.3
  14.1 3.7 %collective-permute-start.4 = (bf16[256,128]{1,0:T(8,128)(2,1)S(1)}, bf16[256,128]{1,0:T(8,128)(2,1)S(1)}, u32[]{:S(2)}, u32[]{:S(2)}) collective-permute-start(bf16[256,128]{1,0:T(8,128)(2,1)S(1)} %get-tuple-element.32), channel_id=1, source_target_pairs={{4,8},{8,4},{12,16},{16,12},{20,24},{24,20},{28,0},{0,28},{5,9},{9... | collective-permute-start | bytes 196616 | tf_op jit(solution)/shard_map/ppermute | solution.py:403
  17.8 0.0 collective-permute-done.2.refs_3_
  17.8 0.0 copy-done
  17.8 0.0 copy-done.1
  17.8 3.2 %shard_map.85 = (f32[2,1536,128]{2,1,0:T(8,128)S(1)}, f32[2,24,32,128]{3,2,1,0:T(8,128)S(1)}, f32[3,64,128]{2,1,0:T(8,128)S(1)}, bf16[256,256]{1,0:T(8,128)(2,1)S(1)}) custom-call(s32[8]{0:T(128)S(1)} %copy-done.2, bf16[64,64]{1,0:T(8,128)(2,1)S(1)} %copy-done, f32[6,1536,128]{2,1,0:T(8,128)S(1)} %get-tuple-element.22.cells, ...), custom_call_target="tpu_custom_call" | custom-call | flops 1000000000 | bytes 1000000 | tf_op jit(solution)/shard_map/pallas_call | solution.py:465
  21.0 0.0 collective-permute-done.3.near
  21.0 0.0 collective-permute-done.4.far
  21.0 1.8 %shard_map.86 = (bf16[2,64,24,128]{3,2,1,0:T(8,128)(2,1)}, f32[2,1536,128]{2,1,0:T(8,128)S(1)}) custom-call(s32[8]{0:T(128)S(1)} %copy-done.2, f32[6,1536,128]{2,1,0:T(8,128)S(1)} %get-tuple-element.22.cells, f32[32,64,128]{2,1,0:T(8,128)S(1)} %get-tuple-element.21.weights, ...), custom_call_target="tpu_custom_call", output_to_operand_aliasing={{1}: (10, {})} | custom-call | tf_op jit(solution)/shard_map/pallas_call | solution.py:480
Async XLA Ops:
  0.0 8.6 %copy-start.2 = (s32[8]{0:T(128)S(1)}, s32[8]{0:T(128)}, u32[]{:S(2)}) copy-start(s32[8]{0:T(128)} %widths.7) | copy-start | bytes 100
  0.0 17.8 %collective-permute-start.2 = (f32[3,2,32]{2,1,0:T(2,128)}, f32[3,2,32]{2,1,0:T(2,128)S(1)}, u32[]{:S(2)}, u32[]{:S(2)}) collective-permute-start(f32[3,2,32]{2,1,0:T(2,128)} %refs_2_.1), channel_id=1, source_target_pairs={{0,2},{1,3},{2,0},{3,1},{4,6},{5,7},{6,4},{7,5},{8,10},{9,11},{10,... | collective-permute-start | bytes 2312 | tf_op jit(solution)/shard_map/ppermute | solution.py:411
  7.0 10.8 %copy-start = (bf16[64,64]{1,0:T(8,128)(2,1)S(1)}, bf16[64,64]{1,0:T(8,128)(2,1)}, u32[]{:S(2)}) copy-start(bf16[64,64]{1,0:T(8,128)(2,1)} %mix.1) | copy-start | bytes 24580
  7.0 10.8 %copy-start.1 = (f32[3,2,32]{2,1,0:T(2,128)S(1)}, f32[3,2,32]{2,1,0:T(2,128)}, u32[]{:S(2)}) copy-start(f32[3,2,32]{2,1,0:T(2,128)} %refs_2_.1) | copy-start | bytes 2308
  7.0 4.8 %collective-permute-start = (bf16[80,128]{1,0:T(8,128)(2,1)S(1)}, bf16[80,128]{1,0:T(8,128)(2,1)S(1)}, u32[]{:S(2)}, u32[]{:S(2)}) collective-permute-start(bf16[80,128]{1,0:T(8,128)(2,1)S(1)} %get-tuple-element.24), channel_id=1, source_target_pairs={{0,1},{1,0},{2,3},{3,2},{4,5},{5,4},{6,7},{7,6},{8,9},{9,8},{10,11... | collective-permute-start | bytes 61448 | tf_op jit(solution)/shard_map/ppermute | solution.py:403
  8.6 4.7 %collective-permute-start.1 = (bf16[80,128]{1,0:T(8,128)(2,1)S(1)}, bf16[80,128]{1,0:T(8,128)(2,1)S(1)}, u32[]{:S(2)}, u32[]{:S(2)}) collective-permute-start(bf16[80,128]{1,0:T(8,128)(2,1)S(1)} %get-tuple-element.25), channel_id=1, source_target_pairs={{1,2},{2,1},{3,0},{0,3},{5,6},{6,5},{7,4},{4,7},{9,10},{10,9},{11,... | collective-permute-start | bytes 61448 | tf_op jit(solution)/shard_map/ppermute | solution.py:403
  14.0 7.0 %collective-permute-start.3 = (bf16[256,128]{1,0:T(8,128)(2,1)S(1)}, bf16[256,128]{1,0:T(8,128)(2,1)S(1)}, u32[]{:S(2)}, u32[]{:S(2)}) collective-permute-start(bf16[256,128]{1,0:T(8,128)(2,1)S(1)} %get-tuple-element.31), channel_id=1, source_target_pairs={{0,4},{4,0},{8,12},{12,8},{16,20},{20,16},{24,28},{28,24},{1,5},{5... | collective-permute-start | bytes 196616 | tf_op jit(solution)/shard_map/ppermute | solution.py:403
  14.1 6.9 %collective-permute-start.4 = (bf16[256,128]{1,0:T(8,128)(2,1)S(1)}, bf16[256,128]{1,0:T(8,128)(2,1)S(1)}, u32[]{:S(2)}, u32[]{:S(2)}) collective-permute-start(bf16[256,128]{1,0:T(8,128)(2,1)S(1)} %get-tuple-element.32), channel_id=1, source_target_pairs={{4,8},{8,4},{12,16},{16,12},{20,24},{24,20},{28,0},{0,28},{5,9},{9... | collective-permute-start | bytes 196616 | tf_op jit(solution)/shard_map/ppermute | solution.py:403

commit v6 on v5

--- a/solution.py
+++ b/solution.py
@@ -11,7 +11,7 @@
 ZOUT = 2
 CF = 16
 ROWS = 8
-SPLIT = 4
+SPLIT = 5
 CHUNK = 16
 DW_BIAS, PW_BIAS, LIFT = 27, 28, 29
 F32 = jnp.float32
@@ -37,8 +37,8 @@
 
 def pack_kernel(
     feature, widths_in, taps_in, dw_bias_in, pw_bias_in, lift_in, coarse_in,
-    planes, weights, first, second,
-    widths, taps, dw_bias, pw_bias, lift, coarse, stacked, tail, picked, sems, small_sems,
+    cells, weights, first, second, own_block,
+    planes, widths, taps, dw_bias, pw_bias, lift, coarse, stacked, tail, picked, sems, small_sems,
 ):
     count, channels, slots, tile = feature.shape
     chunks = range(0, channels, CHUNK)
@@ -65,14 +65,6 @@
     for c in chunks:
         copy_of(c).start()
 
-    shape = (tile, tile)
-    lane, row = lane_iota(shape), row_iota(shape)
-    column = jnp.where((lane & 3) < 2, tile - 2 + (lane & 3), (lane & 3) - 2)
-    plane = (lane & 31) >> 2
-    picks = jnp.concatenate(
-        [((row == column) & (plane == z)).astype(F32) for z in range(count)], axis=0
-    ).astype(BF16)
-
     for copy in small:
         copy.wait()
     width = widths[lax.axis_index("gx")]
@@ -84,6 +76,7 @@
     for t in range(stacked.shape[0]):
         weights[t] = jnp.broadcast_to(turned[:, t : t + 1], (channels, tile))
 
+    own_block[...] = coarse[...]
     parts, own_rows, ncy = coarse.shape
     tail[...] = jnp.zeros_like(tail)
     if 3 * ncy <= tile:
@@ -108,24 +101,31 @@
             total = weight if total is None else jnp.where(member == m, weight, total)
         scale.append(total)
 
+    valid = row_iota((slots, tile)) < width
+    across = lane_iota((slots, tile))
     for c in chunks:
         copy_of(c).wait()
-        rows = [
-            jnp.concatenate([planes[z, c + k].astype(F32) for k in range(CHUNK)], axis=0).astype(BF16)
-            for z in range(count)
-        ]
-        picked[c * slots : (c + CHUNK) * slots, :] = jnp.dot(
-            jnp.concatenate(rows, axis=1), picks, preferred_element_type=F32
-        )
+        for k in range(CHUNK):
+            at = slice((c + k) * slots, (c + k + 1) * slots)
+            total = None
+            for z in range(count):
+                rows = jnp.where(valid, planes[z, c + k].astype(F32), 0.0)
+                cells[z, at, :] = rows
+                if z:
+                    inside = (across >= 4 * z - 2) & (across < 4 * z + 2)
+                    total = jnp.where(inside, pltpu.roll(rows, 4 * z, 1), total)
+                else:
+                    total = rows
+            picked[at, :] = total
 
     groups = slots // 4
     held, moved = {}, {}
     for q in range(groups):
-        rows = [picked[pl.ds(4 * q + i, channels, stride=slots), :] for i in range(4)]
+        rows = [pltpu.roll(picked[pl.ds(4 * q + i, channels, stride=slots), :], 32 * i + 2, 1) for i in range(4)]
         rows = jnp.where(
             lane < 64, jnp.where(lane < 32, rows[0], rows[1]), jnp.where(lane < 96, rows[2], rows[3])
         )
-        held[q] = jnp.where(4 * q + (lane >> 5) < width, rows, 0.0)
+        held[q] = rows
     for q in range(-1, groups):
         low = held.get(q + 1, jnp.zeros(shape, F32))
         high = held.get(q, jnp.zeros(shape, F32))
@@ -182,16 +182,12 @@
                         depth[z, out, to, :] = shifted_sum(*(sums.pop((out, dy)) for dy in (-1, 0, 1)))
 
 
-def conv_kernel(widths, planes, weights, cells, depth, rims):
+def conv_kernel(widths, cells, weights, depth, rims):
     width = widths[lax.axis_index("gx")]
-    count, channels, slots, tile = planes.shape
-    valid = row_iota((slots, tile)) < width
+    channels = weights.shape[1]
+    slots = cells.shape[1] // channels
 
     def outer_rows(b, carry):
-        for z in range(count):
-            for k in range(ROWS):
-                at = pl.ds(pl.multiple_of((b * ROWS + k) * slots, ROWS), slots)
-                cells[z, at, :] = jnp.where(valid, planes[z, b * ROWS + k].astype(F32), 0.0)
         at = pl.ds(pl.multiple_of(b * ROWS, ROWS), ROWS)
         for i, (x, dx) in enumerate(((0, 1), (1, 1), (width - 2, -1), (width - 1, -1))):
             for z in range(ZOUT):
@@ -221,7 +217,7 @@
     return jnp.where((lane < 2) | (lane >= tile - 2), cells, 0.0)
 
 
-def rim_kernel(widths, first, second, rims, edge, near, far):
+def rim_kernel(widths, second, first, rims, edge, far, near):
     width = widths[lax.axis_index("gx")]
     _, _, channels, tile = rims.shape
     even = is_even("gy")
@@ -269,7 +265,7 @@
         coarse, value, rest, lifted, mixer, across = refs
         parts, ncx, ncy = coarse.shape
     else:
-        first, second, own_block, opposite, value, rest, lifted, mixer, across, blocks = refs
+        second, first, own_block, opposite, value, rest, lifted, mixer, across, blocks = refs
         parts, own_rows, ncy = own_block.shape
         ncx = 4 * own_rows
     width = widths[lax.axis_index("gx")]
@@ -340,7 +336,7 @@
                 )
 
 
-def finish_kernel(widths, cells, weights, depth, rest, edge, lifted, mixer, near, far, value_in, out, value, block, sems):
+def finish_kernel(widths, cells, weights, depth, rest, edge, lifted, mixer, far, near, value_in, out, value, block, sems):
     width = widths[lax.axis_index("gx")]
     phase = lax.rem(slab_start(widths), CF)
     channels, tile = weights.shape[1:]
@@ -407,8 +403,6 @@
 
     if gathered:
         every = lax.all_gather(coarse, "gy", axis=1, tiled=True)
-    else:
-        opposite = lax.ppermute(coarse, "gy", [(i, (i + 2) % 4) for i in range(4)])
     small = (
         widths,
         dw_weight,
@@ -417,12 +411,19 @@
         lift_weight.T,
         coarse,
     )
-    held, weights, first, second = pl.pallas_call(
+    cells, weights, first, second, own_block = pl.pallas_call(
         pack_kernel,
-        out_shape=(pltpu.VMEM(feature.shape, BF16), pltpu.VMEM((32, channels, tile), F32), strip, strip),
+        out_shape=(
+            cells_shape,
+            pltpu.VMEM((32, channels, tile), F32),
+            strip,
+            strip,
+            pltpu.VMEM(coarse.shape, F32),
+        ),
         in_specs=[hbm] * 7,
-        out_specs=(vmem,) * 4,
+        out_specs=(vmem,) * 5,
         scratch_shapes=[
+            pltpu.VMEM(feature.shape, BF16),
             pltpu.SMEM(widths.shape, jnp.int32),
             pltpu.VMEM(dw_weight.shape, F32),
             pltpu.VMEM((1, channels), F32),
@@ -437,31 +438,32 @@
         ],
         compiler_params=params,
     )(pinned(feature), *(pinned(array) for array in small))
+    second = swapped(second, "gy", 1)
     first = swapped(first, "gy", 0)
-    second = swapped(second, "gy", 1)
+    if not gathered:
+        opposite = lax.ppermute(own_block, "gy", [(i, (i + 2) % 4) for i in range(4)])
     early = SPLIT * ROWS
-    cells, depth, rims = pl.pallas_call(
+    depth, rims = pl.pallas_call(
         conv_kernel,
         out_shape=(
-            cells_shape,
             pltpu.VMEM((ZOUT, slots, early, tile), F32),
             pltpu.VMEM((ZOUT, 4, channels, tile), F32),
         ),
         in_specs=[smem, vmem, vmem],
-        out_specs=(vmem,) * 3,
+        out_specs=(vmem,) * 2,
         compiler_params=params,
         cost_estimate=pl.CostEstimate(flops=10**9, bytes_accessed=10**6, transcendentals=0),
-    )(widths, held, weights)
-    edge, near, far = pl.pallas_call(
+    )(widths, cells, weights)
+    edge, far, near = pl.pallas_call(
         rim_kernel,
         out_shape=(pltpu.VMEM((2, channels, tile), F32), message, message),
         in_specs=[smem] + [vmem] * 3,
         out_specs=(vmem,) * 3,
         compiler_params=params,
-    )(widths, first, second, rims)
+    )(widths, second, first, rims)
+    far = swapped(far, "gx", 1)
     near = swapped(near, "gx", 0)
-    far = swapped(far, "gx", 1)
-    blocks = (every,) if gathered else (first, second, coarse, opposite)
+    blocks = (every,) if gathered else (second, first, own_block, opposite)
     value, rest, lifted, mixer = pl.pallas_call(
         functools.partial(mix_kernel, gathered),
         out_shape=(
@@ -488,7 +490,7 @@
         ],
         input_output_aliases={10: 1},
         compiler_params=params,
-    )(widths, cells, weights, depth, rest, edge, lifted, mixer, near, far, value)
+    )(widths, cells, weights, depth, rest, edge, lifted, mixer, far, near, value)
     return out
 
 

time: 23 us -> 20.3 us (0.88)
  starting transfers between devices: 8.32 us -> 6.87 us
  Pallas kernels: 13 us -> 11.9 us
    ppermute x4, starting transfers between devices: 5.35 us -> 3.84 us  [swapped(): return lax.ppermute(array, axis, pairs)]
    pallas_call x2, Pallas kernels: 7.24 us -> 6.57 us  [the longest x1 3.33 us: shards(): pl.pallas_call(pack_kernel, out_shape=(cells_shape, pltpu.VMEM((32, chann...]
    pallas_call x1, Pallas kernels: 3.2 us -> 2.78 us  [shards(): pl.pallas_call(functools.partial(mix_kernel, gathered), out_shape=(value_...]
  transfers between devices with their start and end apart: 5 -> 5, of which waited for: 1 -> 2; matrix products, arithmetic and copies ran while one was open for 0% -> 0% of each run, Pallas kernels for 49% -> 34%
where the time goes in v6:
time: 20.3 us; the launch traced here: 20.1 us
  Pallas kernels  11.9 us (59%)
  starting transfers between devices  6.87 us (34%)
  waiting for transfers between devices  1.28 us (6%)
    ppermute x4, starting transfers between devices, swapped(): return lax.ppermute(array, axis, pairs)  3.84 us
    pallas_call x1, Pallas kernels, shards(): pl.pallas_call(pack_kernel, out_shape=(cells_shape, pltpu.VMEM((32, chann...  3.33 us
    pallas_call x1, Pallas kernels, shards(): pl.pallas_call(conv_kernel, out_shape=(pltpu.VMEM((ZOUT, slots, early, ti...  3.24 us
    ppermute x1, starting transfers between devices, shards(): lax.ppermute(own_block, 'gy', [(i, (i + 2) % 4) for i in range(4)])  3.03 us
    pallas_call x1, Pallas kernels, shards(): pl.pallas_call(functools.partial(mix_kernel, gathered), out_shape=(value_...  2.78 us
    pallas_call x1, Pallas kernels, shards(): pl.pallas_call(finish_kernel, out_shape=(shape((ZOUT, channels, slots, ti...  1.84 us
    ppermute x4, waiting for transfers between devices, swapped(): return lax.ppermute(array, axis, pairs)  1.28 us
    pallas_call x1, Pallas kernels, shards(): pl.pallas_call(rim_kernel, out_shape=(pltpu.VMEM((2, channels, tile), F32...  0.75 us
  transfers between devices with their start and end apart: 5, of which 2 were waited for; matrix products, arithmetic and copies ran while one was open for 0% of the time, Pallas kernels for 34%

profile of v6, /device:TPU:0, one launch (start us, length us, event | category | flops | bytes accessed | tf_op | source)
XLA Modules:
  0.0 20.1 jit_solution(10065122400039317554)
XLA Ops:
  0.0 0.0 copy-start.1
  0.0 3.3 %shard_map.82 = (f32[6,1536,128]{2,1,0:T(8,128)S(1)}, f32[32,64,128]{2,1,0:T(8,128)S(1)}, bf16[80,128]{1,0:T(8,128)(2,1)S(1)}, bf16[80,128]{1,0:T(8,128)(2,1)S(1)}, f32[3,2,32]{2,1,0:T(2,128)S(1)}) custom-call(bf16[6,64,24,128]{3,2,1,0:T(8,128)(2,1)} %feature.1, s32[8]{0:T(128)} %widths.7, f32[27,64]{1,0:T(8,128)} %taps_in.1, f32[1,64]{1,0:T(1,128)} %bitcast.4, ...), custom_call_target="tpu_custom_call" | custom-call | tf_op jit(solution)/shard_map/pallas_call | solution.py:414
  3.3 3.0 %collective-permute-start.2 = (f32[3,2,32]{2,1,0:T(2,128)S(1)}, f32[3,2,32]{2,1,0:T(2,128)S(1)}, u32[]{:S(2)}, u32[]{:S(2)}) collective-permute-start(f32[3,2,32]{2,1,0:T(2,128)S(1)} %get-tuple-element.27.refs_2_), channel_id=1, source_target_pairs={{0,2},{1,3},{2,0},{3,1},{4,6},{5,7},{6,4},{7,5},{8,10},{9,11},{10,... | collective-permute-start | bytes 2312 | tf_op jit(solution)/shard_map/ppermute | solution.py:444
  6.4 1.4 %collective-permute-start = (bf16[80,128]{1,0:T(8,128)(2,1)S(1)}, bf16[80,128]{1,0:T(8,128)(2,1)S(1)}, u32[]{:S(2)}, u32[]{:S(2)}) collective-permute-start(bf16[80,128]{1,0:T(8,128)(2,1)S(1)} %get-tuple-element.23), channel_id=1, source_target_pairs={{1,2},{2,1},{3,0},{0,3},{5,6},{6,5},{7,4},{4,7},{9,10},{10,9},{11,... | collective-permute-start | bytes 61448 | tf_op jit(solution)/shard_map/ppermute | solution.py:399
  7.8 0.1 collective-permute-start.1
  7.9 0.0 copy-done.1
  7.9 0.0 copy-start
  7.9 3.2 %shard_map.83 = (f32[2,24,40,128]{3,2,1,0:T(8,128)S(1)}, f32[2,4,64,128]{3,2,1,0:T(8,128)S(1)}) custom-call(s32[8]{0:T(128)S(1)} %copy-done.1, f32[6,1536,128]{2,1,0:T(8,128)S(1)} %get-tuple-element.20.cells, f32[32,64,128]{2,1,0:T(8,128)S(1)} %get-tuple-element.21.weights), custom_call_target="tpu_custom_call" | custom-call | flops 1000000000 | bytes 1000000 | tf_op jit(solution)/shard_map/pallas_call | solution.py:446
  11.2 0.0 collective-permute-done.second.refs_0_
  11.2 0.4 %collective-permute-done.1.first.refs_1_ = bf16[80,128]{1,0:T(8,128)(2,1)S(1)} collective-permute-done((bf16[80,128]{1,0:T(8,128)(2,1)S(1)}, bf16[80,128]{1,0:T(8,128)(2,1)S(1)}, u32[]{:S(2)}, u32[]{:S(2)}) %collective-permute-start.1) | collective-permute-done | bytes 20512 | tf_op jit(solution)/shard_map/ppermute | solution.py:399
  11.6 0.7 %shard_map.84 = (f32[2,64,128]{2,1,0:T(8,128)S(1)}, bf16[256,128]{1,0:T(8,128)(2,1)S(1)}, bf16[256,128]{1,0:T(8,128)(2,1)S(1)}) custom-call(s32[8]{0:T(128)S(1)} %copy-done.1, bf16[80,128]{1,0:T(8,128)(2,1)S(1)} %collective-permute-done.second.refs_0_, bf16[80,128]{1,0:T(8,128)(2,1)S(1)} %collective-permute-done.1.first.refs_1_, ...), custom_call_target="tpu_custom_call" | custom-call | tf_op jit(solution)/shard_map/pallas_call | solution.py:457
  12.3 2.3 %collective-permute-start.3 = (bf16[256,128]{1,0:T(8,128)(2,1)S(1)}, bf16[256,128]{1,0:T(8,128)(2,1)S(1)}, u32[]{:S(2)}, u32[]{:S(2)}) collective-permute-start(bf16[256,128]{1,0:T(8,128)(2,1)S(1)} %get-tuple-element.31), channel_id=1, source_target_pairs={{4,8},{8,4},{12,16},{16,12},{20,24},{24,20},{28,0},{0,28},{5,9},{9... | collective-permute-start | bytes 196616 | tf_op jit(solution)/shard_map/ppermute | solution.py:399
  14.6 0.0 collective-permute-start.4
  14.6 0.0 collective-permute-done.2.refs_3_
  14.6 0.0 copy-done
  14.7 2.8 %shard_map.85 = (f32[2,1536,128]{2,1,0:T(8,128)S(1)}, f32[2,24,24,128]{3,2,1,0:T(8,128)S(1)}, f32[3,64,128]{2,1,0:T(8,128)S(1)}, bf16[256,256]{1,0:T(8,128)(2,1)S(1)}) custom-call(s32[8]{0:T(128)S(1)} %copy-done.1, bf16[64,64]{1,0:T(8,128)(2,1)S(1)} %copy-done, f32[6,1536,128]{2,1,0:T(8,128)S(1)} %get-tuple-element.20.cells, ...), custom_call_target="tpu_custom_call" | custom-call | flops 1000000000 | bytes 1000000 | tf_op jit(solution)/shard_map/pallas_call | solution.py:467
  17.4 0.9 %collective-permute-done.3.far = bf16[256,128]{1,0:T(8,128)(2,1)S(1)} collective-permute-done((bf16[256,128]{1,0:T(8,128)(2,1)S(1)}, bf16[256,128]{1,0:T(8,128)(2,1)S(1)}, u32[]{:S(2)}, u32[]{:S(2)}) %collective-permute-start.3) | collective-permute-done | bytes 65568 | tf_op jit(solution)/shard_map/ppermute | solution.py:399
  18.3 0.0 collective-permute-done.4.near
  18.3 1.8 %shard_map.86 = (bf16[2,64,24,128]{3,2,1,0:T(8,128)(2,1)}, f32[2,1536,128]{2,1,0:T(8,128)S(1)}) custom-call(s32[8]{0:T(128)S(1)} %copy-done.1, f32[6,1536,128]{2,1,0:T(8,128)S(1)} %get-tuple-element.20.cells, f32[32,64,128]{2,1,0:T(8,128)S(1)} %get-tuple-element.21.weights, ...), custom_call_target="tpu_custom_call", output_to_operand_aliasing={{1}: (10, {})} | custom-call | tf_op jit(solution)/shard_map/pallas_call | solution.py:482
Async XLA Ops:
  0.0 7.9 %copy-start.1 = (s32[8]{0:T(128)S(1)}, s32[8]{0:T(128)}, u32[]{:S(2)}) copy-start(s32[8]{0:T(128)} %widths.7) | copy-start | bytes 100
  3.3 11.3 %collective-permute-start.2 = (f32[3,2,32]{2,1,0:T(2,128)S(1)}, f32[3,2,32]{2,1,0:T(2,128)S(1)}, u32[]{:S(2)}, u32[]{:S(2)}) collective-permute-start(f32[3,2,32]{2,1,0:T(2,128)S(1)} %get-tuple-element.27.refs_2_), channel_id=1, source_target_pairs={{0,2},{1,3},{2,0},{3,1},{4,6},{5,7},{6,4},{7,5},{8,10},{9,11},{10,... | collective-permute-start | bytes 2312 | tf_op jit(solution)/shard_map/ppermute | solution.py:444
  6.4 4.8 %collective-permute-start = (bf16[80,128]{1,0:T(8,128)(2,1)S(1)}, bf16[80,128]{1,0:T(8,128)(2,1)S(1)}, u32[]{:S(2)}, u32[]{:S(2)}) collective-permute-start(bf16[80,128]{1,0:T(8,128)(2,1)S(1)} %get-tuple-element.23), channel_id=1, source_target_pairs={{1,2},{2,1},{3,0},{0,3},{5,6},{6,5},{7,4},{4,7},{9,10},{10,9},{11,... | collective-permute-start | bytes 61448 | tf_op jit(solution)/shard_map/ppermute | solution.py:399
  7.8 3.8 %collective-permute-start.1 = (bf16[80,128]{1,0:T(8,128)(2,1)S(1)}, bf16[80,128]{1,0:T(8,128)(2,1)S(1)}, u32[]{:S(2)}, u32[]{:S(2)}) collective-permute-start(bf16[80,128]{1,0:T(8,128)(2,1)S(1)} %get-tuple-element.24), channel_id=1, source_target_pairs={{0,1},{1,0},{2,3},{3,2},{4,5},{5,4},{6,7},{7,6},{8,9},{9,8},{10,11... | collective-permute-start | bytes 61448 | tf_op jit(solution)/shard_map/ppermute | solution.py:399
  7.9 6.7 %copy-start = (bf16[64,64]{1,0:T(8,128)(2,1)S(1)}, bf16[64,64]{1,0:T(8,128)(2,1)}, u32[]{:S(2)}) copy-start(bf16[64,64]{1,0:T(8,128)(2,1)} %mix.1) | copy-start | bytes 24580
  12.3 6.0 %collective-permute-start.3 = (bf16[256,128]{1,0:T(8,128)(2,1)S(1)}, bf16[256,128]{1,0:T(8,128)(2,1)S(1)}, u32[]{:S(2)}, u32[]{:S(2)}) collective-permute-start(bf16[256,128]{1,0:T(8,128)(2,1)S(1)} %get-tuple-element.31), channel_id=1, source_target_pairs={{4,8},{8,4},{12,16},{16,12},{20,24},{24,20},{28,0},{0,28},{5,9},{9... | collective-permute-start | bytes 196616 | tf_op jit(solution)/shard_map/ppermute | solution.py:399
  14.6 3.7 %collective-permute-start.4 = (bf16[256,128]{1,0:T(8,128)(2,1)S(1)}, bf16[256,128]{1,0:T(8,128)(2,1)S(1)}, u32[]{:S(2)}, u32[]{:S(2)}) collective-permute-start(bf16[256,128]{1,0:T(8,128)(2,1)S(1)} %get-tuple-element.32), channel_id=1, source_target_pairs={{0,4},{4,0},{8,12},{12,8},{16,20},{20,16},{24,28},{28,24},{1,5},{5... | collective-permute-start | bytes 196616 | tf_op jit(solution)/shard_map/ppermute | solution.py:399

commit v7 on v6

--- a/solution.py
+++ b/solution.py
@@ -101,7 +101,6 @@
             total = weight if total is None else jnp.where(member == m, weight, total)
         scale.append(total)
 
-    valid = row_iota((slots, tile)) < width
     across = lane_iota((slots, tile))
     for c in chunks:
         copy_of(c).wait()
@@ -109,7 +108,7 @@
             at = slice((c + k) * slots, (c + k + 1) * slots)
             total = None
             for z in range(count):
-                rows = jnp.where(valid, planes[z, c + k].astype(F32), 0.0)
+                rows = planes[z, c + k].astype(F32)
                 cells[z, at, :] = rows
                 if z:
                     inside = (across >= 4 * z - 2) & (across < 4 * z + 2)
@@ -117,6 +116,12 @@
                 else:
                     total = rows
             picked[at, :] = total
+    for r in range(2):
+
+        @pl.when(width + r < slots)
+        def _():
+            for z in range(count):
+                cells[z, pl.ds(width + r, channels, stride=slots), :] = jnp.zeros((channels, tile), F32)
 
     groups = slots // 4
     held, moved = {}, {}
@@ -125,7 +130,7 @@
         rows = jnp.where(
             lane < 64, jnp.where(lane < 32, rows[0], rows[1]), jnp.where(lane < 96, rows[2], rows[3])
         )
-        held[q] = rows
+        held[q] = jnp.where(4 * q + (lane >> 5) < width, rows, 0.0)
     for q in range(-1, groups):
         low = held.get(q + 1, jnp.zeros(shape, F32))
         high = held.get(q, jnp.zeros(shape, F32))
@@ -182,23 +187,24 @@
                         depth[z, out, to, :] = shifted_sum(*(sums.pop((out, dy)) for dy in (-1, 0, 1)))
 
 
-def conv_kernel(widths, cells, weights, depth, rims):
+def conv_kernel(widths, cells, weights, coarse, depth, rims, own_block):
     width = widths[lax.axis_index("gx")]
     channels = weights.shape[1]
     slots = cells.shape[1] // channels
-
-    def outer_rows(b, carry):
-        at = pl.ds(pl.multiple_of(b * ROWS, ROWS), ROWS)
-        for i, (x, dx) in enumerate(((0, 1), (1, 1), (width - 2, -1), (width - 1, -1))):
-            for z in range(ZOUT):
-                rows = [cells[z + ZOUT * m, pl.ds(b * (ROWS * slots) + x, ROWS, stride=slots), :] for m in range(3)]
-                parts = [
-                    sum(weights[tap_of(m, dx, dy), at, :] * rows[m] for m in range(3)) for dy in (-1, 0, 1)
-                ]
-                rims[z, i, at, :] = shifted_sum(*parts)
-        return carry
-
-    lax.fori_loop(0, channels // ROWS, outer_rows, 0)
+    own_block[...] = coarse[...]
+
+    for b in range(channels // ROWS):
+        at = slice(b * ROWS, (b + 1) * ROWS)
+        for side, dx in enumerate((1, -1)):
+            tap = [[weights[tap_of(m, dx, dy), at, :] for m in range(3)] for dy in (-1, 0, 1)]
+            for r in range(2):
+                x = r if side == 0 else width - 2 + r
+                for z in range(ZOUT):
+                    rows = [
+                        cells[z + ZOUT * m, pl.ds(b * (ROWS * slots) + x, ROWS, stride=slots), :] for m in range(3)
+                    ]
+                    parts = [sum(weight * row for weight, row in zip(weights_of, rows)) for weights_of in tap]
+                    rims[z, 2 * side + r, at, :] = shifted_sum(*parts)
 
     def convolve(b, carry):
         convolve_block(cells, weights, depth, b, 0)
@@ -345,24 +351,19 @@
     at_top = jnp.where(even, far[...].astype(F32), near[...].astype(F32))
     at_end = jnp.where(even, near[...].astype(F32), far[...].astype(F32))
     rows = (0, 1, width - 2, width - 1)
-    depths = []
+    chunk = 16
+    copies = []
     for z in range(ZOUT):
         parts = []
         for i, x in enumerate(rows):
             arrived = at_top if i < 2 else at_end
             begin = (2 * z + i % 2) * channels
             parts.append(depth_row(weights, (depth, rest), edge, z, x) + arrived[begin : begin + channels, :])
-        depths.append(jnp.concatenate(parts, axis=0).astype(BF16))
-    mixed = jnp.dot(mixer[...], jnp.concatenate(depths, axis=1), preferred_element_type=F32)
-    for i, x in enumerate(rows):
-        for z in range(ZOUT):
-            part = mixed[i * channels : (i + 1) * channels, z * tile : (z + 1) * tile]
+        mixed = jnp.dot(mixer[...], jnp.concatenate(parts, axis=0).astype(BF16), preferred_element_type=F32)
+        for i, x in enumerate(rows):
             value[z, pl.ds(x, channels, stride=slots), :] = finished_row(
-                weights, cells, lifted, phase, width, part, z, x
+                weights, cells, lifted, phase, width, mixed[i * channels : (i + 1) * channels, :], z, x
             )
-    chunk = 16
-    copies = []
-    for z in range(ZOUT):
         for part in range(channels // chunk):
             for o in range(part * chunk, (part + 1) * chunk):
                 block[z, o] = value[z, o * slots : (o + 1) * slots, :].astype(BF16)
@@ -411,7 +412,7 @@
         lift_weight.T,
         coarse,
     )
-    cells, weights, first, second, own_block = pl.pallas_call(
+    cells, weights, first, second, block = pl.pallas_call(
         pack_kernel,
         out_shape=(
             cells_shape,
@@ -440,20 +441,21 @@
     )(pinned(feature), *(pinned(array) for array in small))
     second = swapped(second, "gy", 1)
     first = swapped(first, "gy", 0)
-    if not gathered:
-        opposite = lax.ppermute(own_block, "gy", [(i, (i + 2) % 4) for i in range(4)])
     early = SPLIT * ROWS
-    depth, rims = pl.pallas_call(
+    depth, rims, own_block = pl.pallas_call(
         conv_kernel,
         out_shape=(
             pltpu.VMEM((ZOUT, slots, early, tile), F32),
             pltpu.VMEM((ZOUT, 4, channels, tile), F32),
+            pltpu.VMEM(coarse.shape, F32),
         ),
-        in_specs=[smem, vmem, vmem],
-        out_specs=(vmem,) * 2,
+        in_specs=[smem, vmem, vmem, vmem],
+        out_specs=(vmem,) * 3,
         compiler_params=params,
         cost_estimate=pl.CostEstimate(flops=10**9, bytes_accessed=10**6, transcendentals=0),
-    )(widths, cells, weights)
+    )(widths, cells, weights, block)
+    if not gathered:
+        opposite = lax.ppermute(own_block, "gy", [(i, (i + 2) % 4) for i in range(4)])
     edge, far, near = pl.pallas_call(
         rim_kernel,
         out_shape=(pltpu.VMEM((2, channels, tile), F32), message, message),

time: 20.3 us -> 19.8 us (0.975)
  Pallas kernels: 11.9 us -> 11.5 us
    ppermute x4, starting transfers between devices: 3.84 us -> 6.8 us  [swapped(): return lax.ppermute(array, axis, pairs)]
    ppermute x1, starting transfers between devices: 3.03 us -> 0.17 us  [shards(): lax.ppermute(own_block, 'gy', [(i, (i + 2) % 4) for i in range(4)])]
    pallas_call x1, Pallas kernels: 3.24 us -> 2.7 us  [shards(): pl.pallas_call(conv_kernel, out_shape=(pltpu.VMEM((ZOUT, slots, early, ti...]
  transfers between devices with their start and end apart: 5 -> 5, of which waited for: 2 -> 3; matrix products, arithmetic and copies ran while one was open for 0% -> 0% of each run, Pallas kernels for 34% -> 31%
where the time goes in v7:
time: 19.8 us
  Pallas kernels  11.5 us (58%)
  starting transfers between devices  6.97 us (35%)
  waiting for transfers between devices  1.21 us (6%)
    ppermute x4, starting transfers between devices, swapped(): return lax.ppermute(array, axis, pairs)  6.8 us
    pallas_call x1, Pallas kernels, shards(): pl.pallas_call(pack_kernel, out_shape=(cells_shape, pltpu.VMEM((32, chann...  3.46 us
    pallas_call x1, Pallas kernels, shards(): pl.pallas_call(functools.partial(mix_kernel, gathered), out_shape=(value_...  2.78 us
    pallas_call x1, Pallas kernels, shards(): pl.pallas_call(conv_kernel, out_shape=(pltpu.VMEM((ZOUT, slots, early, ti...  2.7 us
    pallas_call x1, Pallas kernels, shards(): pl.pallas_call(finish_kernel, out_shape=(shape((ZOUT, channels, slots, ti...  1.85 us
    ppermute x4, waiting for transfers between devices, swapped(): return lax.ppermute(array, axis, pairs)  1.15 us
    pallas_call x1, Pallas kernels, shards(): pl.pallas_call(rim_kernel, out_shape=(pltpu.VMEM((2, channels, tile), F32...  0.75 us
  transfers between devices with their start and end apart: 5, of which 3 were waited for; matrix products, arithmetic and copies ran while one was open for 0% of the time, Pallas kernels for 31%

profile of v7, /device:TPU:0, one launch (start us, length us, event | category | flops | bytes accessed | tf_op | source)
XLA Modules:
  0.0 19.8 jit_solution(12170054568186385013)
XLA Ops:
  0.0 0.0 copy-start.1
  0.0 3.5 %shard_map.82 = (f32[6,1536,128]{2,1,0:T(8,128)S(1)}, f32[32,64,128]{2,1,0:T(8,128)S(1)}, bf16[80,128]{1,0:T(8,128)(2,1)S(1)}, bf16[80,128]{1,0:T(8,128)(2,1)S(1)}, f32[3,2,32]{2,1,0:T(2,128)S(1)}) custom-call(bf16[6,64,24,128]{3,2,1,0:T(8,128)(2,1)} %feature.1, s32[8]{0:T(128)} %widths.7, f32[27,64]{1,0:T(8,128)} %taps_in.1, f32[1,64]{1,0:T(1,128)} %bitcast.4, ...), custom_call_target="tpu_custom_call" | custom-call | tf_op jit(solution)/shard_map/pallas_call | solution.py:415
  3.5 4.0 %collective-permute-start = (bf16[80,128]{1,0:T(8,128)(2,1)S(1)}, bf16[80,128]{1,0:T(8,128)(2,1)S(1)}, u32[]{:S(2)}, u32[]{:S(2)}) collective-permute-start(bf16[80,128]{1,0:T(8,128)(2,1)S(1)} %get-tuple-element.25), channel_id=1, source_target_pairs={{1,2},{2,1},{3,0},{0,3},{5,6},{6,5},{7,4},{4,7},{9,10},{10,9},{11,... | collective-permute-start | bytes 61448 | tf_op jit(solution)/shard_map/ppermute | solution.py:400
  7.4 0.5 %collective-permute-start.1 = (bf16[80,128]{1,0:T(8,128)(2,1)S(1)}, bf16[80,128]{1,0:T(8,128)(2,1)S(1)}, u32[]{:S(2)}, u32[]{:S(2)}) collective-permute-start(bf16[80,128]{1,0:T(8,128)(2,1)S(1)} %get-tuple-element.26), channel_id=1, source_target_pairs={{0,1},{1,0},{2,3},{3,2},{4,5},{5,4},{6,7},{7,6},{8,9},{9,8},{10,11... | collective-permute-start | bytes 61448 | tf_op jit(solution)/shard_map/ppermute | solution.py:400
  8.0 0.0 copy-done.1
  8.0 0.0 copy-start
  8.0 2.7 %shard_map.83 = (f32[2,24,40,128]{3,2,1,0:T(8,128)S(1)}, f32[2,4,64,128]{3,2,1,0:T(8,128)S(1)}, f32[3,2,32]{2,1,0:T(2,128)S(1)}) custom-call(s32[8]{0:T(128)S(1)} %copy-done.1, f32[6,1536,128]{2,1,0:T(8,128)S(1)} %get-tuple-element.21.cells, f32[32,64,128]{2,1,0:T(8,128)S(1)} %get-tuple-element.22.weights, f32[3,2,32]{2,1,0:T(2,128)S(1)} %get-tuple-element.23.coarse), custom_call_target="tpu_custom_call" | custom-call | flops 1000000000 | bytes 1000000 | tf_op jit(solution)/shard_map/pallas_call | solution.py:445
  10.7 0.2 collective-permute-start.2
  10.9 0.0 collective-permute-done.second.refs_0_
  10.9 0.4 %collective-permute-done.1.first.refs_1_ = bf16[80,128]{1,0:T(8,128)(2,1)S(1)} collective-permute-done((bf16[80,128]{1,0:T(8,128)(2,1)S(1)}, bf16[80,128]{1,0:T(8,128)(2,1)S(1)}, u32[]{:S(2)}, u32[]{:S(2)}) %collective-permute-start.1) | collective-permute-done | bytes 20512 | tf_op jit(solution)/shard_map/ppermute | solution.py:400
  11.2 0.7 %shard_map.84 = (f32[2,64,128]{2,1,0:T(8,128)S(1)}, bf16[256,128]{1,0:T(8,128)(2,1)S(1)}, bf16[256,128]{1,0:T(8,128)(2,1)S(1)}) custom-call(s32[8]{0:T(128)S(1)} %copy-done.1, bf16[80,128]{1,0:T(8,128)(2,1)S(1)} %collective-permute-done.second.refs_0_, bf16[80,128]{1,0:T(8,128)(2,1)S(1)} %collective-permute-done.1.first.refs_1_, ...), custom_call_target="tpu_custom_call" | custom-call | tf_op jit(solution)/shard_map/pallas_call | solution.py:459
  12.0 2.3 %collective-permute-start.3 = (bf16[256,128]{1,0:T(8,128)(2,1)S(1)}, bf16[256,128]{1,0:T(8,128)(2,1)S(1)}, u32[]{:S(2)}, u32[]{:S(2)}) collective-permute-start(bf16[256,128]{1,0:T(8,128)(2,1)S(1)} %get-tuple-element.33), channel_id=1, source_target_pairs={{4,8},{8,4},{12,16},{16,12},{20,24},{24,20},{28,0},{0,28},{5,9},{9... | collective-permute-start | bytes 196616 | tf_op jit(solution)/shard_map/ppermute | solution.py:400
  14.3 0.0 collective-permute-start.4
  14.3 0.1 collective-permute-done.2.refs_3_
  14.3 0.0 copy-done
  14.3 2.8 %shard_map.85 = (f32[2,1536,128]{2,1,0:T(8,128)S(1)}, f32[2,24,24,128]{3,2,1,0:T(8,128)S(1)}, f32[3,64,128]{2,1,0:T(8,128)S(1)}, bf16[256,256]{1,0:T(8,128)(2,1)S(1)}) custom-call(s32[8]{0:T(128)S(1)} %copy-done.1, bf16[64,64]{1,0:T(8,128)(2,1)S(1)} %copy-done, f32[6,1536,128]{2,1,0:T(8,128)S(1)} %get-tuple-element.21.cells, ...), custom_call_target="tpu_custom_call" | custom-call | flops 1000000000 | bytes 1000000 | tf_op jit(solution)/shard_map/pallas_call | solution.py:469
  17.1 0.8 %collective-permute-done.3.far = bf16[256,128]{1,0:T(8,128)(2,1)S(1)} collective-permute-done((bf16[256,128]{1,0:T(8,128)(2,1)S(1)}, bf16[256,128]{1,0:T(8,128)(2,1)S(1)}, u32[]{:S(2)}, u32[]{:S(2)}) %collective-permute-start.3) | collective-permute-done | bytes 65568 | tf_op jit(solution)/shard_map/ppermute | solution.py:400
  17.9 0.0 collective-permute-done.4.near
  17.9 1.8 %shard_map.86 = (bf16[2,64,24,128]{3,2,1,0:T(8,128)(2,1)}, f32[2,1536,128]{2,1,0:T(8,128)S(1)}) custom-call(s32[8]{0:T(128)S(1)} %copy-done.1, f32[6,1536,128]{2,1,0:T(8,128)S(1)} %get-tuple-element.21.cells, f32[32,64,128]{2,1,0:T(8,128)S(1)} %get-tuple-element.22.weights, ...), custom_call_target="tpu_custom_call", output_to_operand_aliasing={{1}: (10, {})} | custom-call | tf_op jit(solution)/shard_map/pallas_call | solution.py:484
Async XLA Ops:
  0.0 8.0 %copy-start.1 = (s32[8]{0:T(128)S(1)}, s32[8]{0:T(128)}, u32[]{:S(2)}) copy-start(s32[8]{0:T(128)} %widths.7) | copy-start | bytes 100
  3.5 7.4 %collective-permute-start = (bf16[80,128]{1,0:T(8,128)(2,1)S(1)}, bf16[80,128]{1,0:T(8,128)(2,1)S(1)}, u32[]{:S(2)}, u32[]{:S(2)}) collective-permute-start(bf16[80,128]{1,0:T(8,128)(2,1)S(1)} %get-tuple-element.25), channel_id=1, source_target_pairs={{1,2},{2,1},{3,0},{0,3},{5,6},{6,5},{7,4},{4,7},{9,10},{10,9},{11,... | collective-permute-start | bytes 61448 | tf_op jit(solution)/shard_map/ppermute | solution.py:400
  7.4 3.8 %collective-permute-start.1 = (bf16[80,128]{1,0:T(8,128)(2,1)S(1)}, bf16[80,128]{1,0:T(8,128)(2,1)S(1)}, u32[]{:S(2)}, u32[]{:S(2)}) collective-permute-start(bf16[80,128]{1,0:T(8,128)(2,1)S(1)} %get-tuple-element.26), channel_id=1, source_target_pairs={{0,1},{1,0},{2,3},{3,2},{4,5},{5,4},{6,7},{7,6},{8,9},{9,8},{10,11... | collective-permute-start | bytes 61448 | tf_op jit(solution)/shard_map/ppermute | solution.py:400
  8.0 6.4 %copy-start = (bf16[64,64]{1,0:T(8,128)(2,1)S(1)}, bf16[64,64]{1,0:T(8,128)(2,1)}, u32[]{:S(2)}) copy-start(bf16[64,64]{1,0:T(8,128)(2,1)} %mix.1) | copy-start | bytes 24580
  10.7 3.7 %collective-permute-start.2 = (f32[3,2,32]{2,1,0:T(2,128)S(1)}, f32[3,2,32]{2,1,0:T(2,128)S(1)}, u32[]{:S(2)}, u32[]{:S(2)}) collective-permute-start(f32[3,2,32]{2,1,0:T(2,128)S(1)} %get-tuple-element.29.refs_2_), channel_id=1, source_target_pairs={{0,2},{1,3},{2,0},{3,1},{4,6},{5,7},{6,4},{7,5},{8,10},{9,11},{10,... | collective-permute-start | bytes 2312 | tf_op jit(solution)/shard_map/ppermute | solution.py:458
  12.0 5.9 %collective-permute-start.3 = (bf16[256,128]{1,0:T(8,128)(2,1)S(1)}, bf16[256,128]{1,0:T(8,128)(2,1)S(1)}, u32[]{:S(2)}, u32[]{:S(2)}) collective-permute-start(bf16[256,128]{1,0:T(8,128)(2,1)S(1)} %get-tuple-element.33), channel_id=1, source_target_pairs={{4,8},{8,4},{12,16},{16,12},{20,24},{24,20},{28,0},{0,28},{5,9},{9... | collective-permute-start | bytes 196616 | tf_op jit(solution)/shard_map/ppermute | solution.py:400
  14.3 3.6 %collective-permute-start.4 = (bf16[256,128]{1,0:T(8,128)(2,1)S(1)}, bf16[256,128]{1,0:T(8,128)(2,1)S(1)}, u32[]{:S(2)}, u32[]{:S(2)}) collective-permute-start(bf16[256,128]{1,0:T(8,128)(2,1)S(1)} %get-tuple-element.34), channel_id=1, source_target_pairs={{0,4},{4,0},{8,12},{12,8},{16,20},{20,16},{24,28},{28,24},{1,5},{5... | collective-permute-start | bytes 196616 | tf_op jit(solution)/shard_map/ppermute | solution.py:400

commit v8 on v7

--- a/solution.py
+++ b/solution.py
@@ -37,8 +37,8 @@
 
 def pack_kernel(
     feature, widths_in, taps_in, dw_bias_in, pw_bias_in, lift_in, coarse_in,
-    cells, weights, first, second, own_block,
-    planes, widths, taps, dw_bias, pw_bias, lift, coarse, stacked, tail, picked, sems, small_sems,
+    cells, weights, first, second, own_block, widths,
+    planes, widths_here, taps, dw_bias, pw_bias, lift, coarse, stacked, tail, picked, sems, small_sems,
 ):
     count, channels, slots, tile = feature.shape
     chunks = range(0, channels, CHUNK)
@@ -51,7 +51,7 @@
         pltpu.make_async_copy(source, target, small_sems.at[i])
         for i, (source, target) in enumerate(
             (
-                (widths_in, widths),
+                (widths_in, widths_here),
                 (taps_in, taps),
                 (dw_bias_in, dw_bias),
                 (pw_bias_in, pw_bias),
@@ -67,7 +67,9 @@
 
     for copy in small:
         copy.wait()
-    width = widths[lax.axis_index("gx")]
+    for d in range(widths.shape[0]):
+        widths[d] = widths_here[d]
+    width = widths_here[lax.axis_index("gx")]
     stacked[0:DW_BIAS, :] = taps[...]
     stacked[DW_BIAS : DW_BIAS + 1, :] = dw_bias[...]
     stacked[PW_BIAS : PW_BIAS + 1, :] = pw_bias[...]
@@ -91,31 +93,36 @@
 
     shape = (channels, tile)
     lane = lane_iota(shape)
-    member = (lane & 31) >> 3
     on_left = (lane & 2) != 0
+    row, along = row_iota((taps.shape[0], tile)), lane_iota((taps.shape[0], tile))
+    of_plane = 9 * ((along & 31) >> 3) + jnp.where((along & 2) != 0, 2, 0)
+    terms, rest = [], taps[...]
+    for _ in range(3):
+        terms.append(rest.astype(BF16))
+        rest = rest - terms[-1].astype(F32)
     scale = []
     for dx in (-1, 0, 1):
-        total = None
-        for m in range(3):
-            weight = jnp.where(on_left, weights[tap_of(m, dx, 1)], weights[tap_of(m, dx, -1)])
-            total = weight if total is None else jnp.where(member == m, weight, total)
-        scale.append(total)
-
-    across = lane_iota((slots, tile))
+        chosen = (row == of_plane + 3 * (dx + 1)).astype(BF16)
+        scale.append(
+            sum(
+                lax.dot_general(term, chosen, (((0,), (0,)), ((), ())), preferred_element_type=F32) for term in terms
+            )
+        )
+
+    across = lane_iota((CHUNK * slots, tile))
     for c in chunks:
         copy_of(c).wait()
-        for k in range(CHUNK):
-            at = slice((c + k) * slots, (c + k + 1) * slots)
-            total = None
-            for z in range(count):
-                rows = planes[z, c + k].astype(F32)
-                cells[z, at, :] = rows
-                if z:
-                    inside = (across >= 4 * z - 2) & (across < 4 * z + 2)
-                    total = jnp.where(inside, pltpu.roll(rows, 4 * z, 1), total)
-                else:
-                    total = rows
-            picked[at, :] = total
+        at = slice(c * slots, (c + CHUNK) * slots)
+        total = None
+        for z in range(count):
+            rows = planes[z, c : c + CHUNK].reshape(CHUNK * slots, tile)
+            cells[z, at, :] = rows.astype(F32)
+            if z:
+                inside = (across >= 4 * z - 2) & (across < 4 * z + 2)
+                total = jnp.where(inside, pltpu.roll(rows, 4 * z, 1), total)
+            else:
+                total = rows
+        picked[at, :] = total.astype(F32)
     for r in range(2):
 
         @pl.when(width + r < slots)
@@ -412,7 +419,7 @@
         lift_weight.T,
         coarse,
     )
-    cells, weights, first, second, block = pl.pallas_call(
+    cells, weights, first, second, block, slab_widths = pl.pallas_call(
         pack_kernel,
         out_shape=(
             cells_shape,
@@ -420,9 +427,10 @@
             strip,
             strip,
             pltpu.VMEM(coarse.shape, F32),
+            pltpu.SMEM(widths.shape, jnp.int32),
         ),
         in_specs=[hbm] * 7,
-        out_specs=(vmem,) * 5,
+        out_specs=(vmem,) * 5 + (smem,),
         scratch_shapes=[
             pltpu.VMEM(feature.shape, BF16),
             pltpu.SMEM(widths.shape, jnp.int32),
@@ -453,7 +461,7 @@
         out_specs=(vmem,) * 3,
         compiler_params=params,
         cost_estimate=pl.CostEstimate(flops=10**9, bytes_accessed=10**6, transcendentals=0),
-    )(widths, cells, weights, block)
+    )(slab_widths, cells, weights, block)
     if not gathered:
         opposite = lax.ppermute(own_block, "gy", [(i, (i + 2) % 4) for i in range(4)])
     edge, far, near = pl.pallas_call(
@@ -462,7 +470,7 @@
         in_specs=[smem] + [vmem] * 3,
         out_specs=(vmem,) * 3,
         compiler_params=params,
-    )(widths, second, first, rims)
+    )(slab_widths, second, first, rims)
     far = swapped(far, "gx", 1)
     near = swapped(near, "gx", 0)
     blocks = (every,) if gathered else (second, first, own_block, opposite)
@@ -480,7 +488,7 @@
         + ([] if gathered else [pltpu.VMEM((parts, ncx, ncy), F32)]),
         compiler_params=params,
         cost_estimate=pl.CostEstimate(flops=10**9, bytes_accessed=10**6, transcendentals=0),
-    )(widths, pw_weight, cells, weights, depth, edge, *blocks)
+    )(slab_widths, pw_weight, cells, weights, depth, edge, *blocks)
     out, _ = pl.pallas_call(
         finish_kernel,
         out_shape=(shape((ZOUT, channels, slots, tile), BF16), value_shape),
@@ -492,7 +500,7 @@
         ],
         input_output_aliases={10: 1},
         compiler_params=params,
-    )(widths, cells, weights, depth, rest, edge, lifted, mixer, far, near, value)
+    )(slab_widths, cells, weights, depth, rest, edge, lifted, mixer, far, near, value)
     return out
 
 

time: 19.8 us -> 18.8 us (0.949)
  Pallas kernels: 11.5 us -> 9.26 us
  waiting for transfers between devices: 1.21 us -> 2.69 us
  starting transfers between devices: 6.97 us -> 6.65 us
    ppermute x4, waiting for transfers between devices: 1.15 us -> 2.31 us  [swapped(): return lax.ppermute(array, axis, pairs)]
    pallas_call x1, Pallas kernels: 2.78 us -> 2.21 us  [shards(): pl.pallas_call(functools.partial(mix_kernel, gathered), out_shape=(value_...]
    pallas_call x1, Pallas kernels: 2.7 us -> 2.15 us  [shards(): pl.pallas_call(conv_kernel, out_shape=(pltpu.VMEM((ZOUT, slots, early, ti...]
    pallas_call x1, Pallas kernels: 1.85 us -> 1.3 us  [shards(): pl.pallas_call(finish_kernel, out_shape=(shape((ZOUT, channels, slots, ti...]
    pallas_call x1, Pallas kernels: 0.75 us -> 0.2 us  [shards(): pl.pallas_call(rim_kernel, out_shape=(pltpu.VMEM((2, channels, tile), F32...]
    ppermute x4, starting transfers between devices: 6.8 us -> 6.48 us  [swapped(): return lax.ppermute(array, axis, pairs)]
    ppermute x1, waiting for transfers between devices: 0.07 us -> 0.38 us  [shards(): lax.ppermute(own_block, 'gy', [(i, (i + 2) % 4) for i in range(4)])]
  transfers between devices with their start and end apart: 5 -> 5, of which waited for: 3 -> 3; matrix products, arithmetic and copies ran while one was open for 0% -> 0% of each run, Pallas kernels for 31% -> 25%
where the time goes in v8:
time: 18.8 us; the launch traced here: 18.6 us
  Pallas kernels  9.26 us (49%)
  starting transfers between devices  6.65 us (35%)
  waiting for transfers between devices  2.69 us (14%)
    ppermute x4, starting transfers between devices, swapped(): return lax.ppermute(array, axis, pairs)  6.48 us
    pallas_call x1, Pallas kernels, shards(): pl.pallas_call(pack_kernel, out_shape=(cells_shape, pltpu.VMEM((32, chann...  3.39 us
    ppermute x4, waiting for transfers between devices, swapped(): return lax.ppermute(array, axis, pairs)  2.31 us
    pallas_call x1, Pallas kernels, shards(): pl.pallas_call(functools.partial(mix_kernel, gathered), out_shape=(value_...  2.21 us
    pallas_call x1, Pallas kernels, shards(): pl.pallas_call(conv_kernel, out_shape=(pltpu.VMEM((ZOUT, slots, early, ti...  2.15 us
    pallas_call x1, Pallas kernels, shards(): pl.pallas_call(finish_kernel, out_shape=(shape((ZOUT, channels, slots, ti...  1.3 us
    ppermute x1, waiting for transfers between devices, shards(): lax.ppermute(own_block, 'gy', [(i, (i + 2) % 4) for i in range(4)])  0.38 us
  transfers between devices with their start and end apart: 5, of which 3 were waited for; matrix products, arithmetic and copies ran while one was open for 0% of the time, Pallas kernels for 25%

profile of v8, /device:TPU:0, one launch (start us, length us, event | category | flops | bytes accessed | tf_op | source)
XLA Modules:
  0.0 18.6 jit_solution(16616902174525412592)
XLA Ops:
  0.0 3.4 %shard_map.82 = (f32[6,1536,128]{2,1,0:T(8,128)S(1)}, f32[32,64,128]{2,1,0:T(8,128)S(1)}, bf16[80,128]{1,0:T(8,128)(2,1)S(1)}, bf16[80,128]{1,0:T(8,128)(2,1)S(1...) custom-call(bf16[6,64,24,128]{3,2,1,0:T(8,128)(2,1)} %feature.1, s32[8]{0:T(128)} %widths_in.1, f32[27,64]{1,0:T(8,128)} %taps_in.1, ...), custom_call_target="tpu_custom_call" | custom-call | tf_op jit(solution)/shard_map/pallas_call | solution.py:422
  3.4 4.0 %collective-permute-start = (bf16[80,128]{1,0:T(8,128)(2,1)S(1)}, bf16[80,128]{1,0:T(8,128)(2,1)S(1)}, u32[]{:S(2)}, u32[]{:S(2)}) collective-permute-start(bf16[80,128]{1,0:T(8,128)(2,1)S(1)} %get-tuple-element.27), channel_id=1, source_target_pairs={{1,2},{2,1},{3,0},{0,3},{5,6},{6,5},{7,4},{4,7},{9,10},{10,9},{11,... | collective-permute-start | bytes 61448 | tf_op jit(solution)/shard_map/ppermute | solution.py:407
  7.4 0.5 %collective-permute-start.1 = (bf16[80,128]{1,0:T(8,128)(2,1)S(1)}, bf16[80,128]{1,0:T(8,128)(2,1)S(1)}, u32[]{:S(2)}, u32[]{:S(2)}) collective-permute-start(bf16[80,128]{1,0:T(8,128)(2,1)S(1)} %get-tuple-element.28), channel_id=1, source_target_pairs={{0,1},{1,0},{2,3},{3,2},{4,5},{5,4},{6,7},{7,6},{8,9},{9,8},{10,11... | collective-permute-start | bytes 61448 | tf_op jit(solution)/shard_map/ppermute | solution.py:407
  7.9 0.0 copy-start
  7.9 2.1 %shard_map.83 = (f32[2,24,40,128]{3,2,1,0:T(8,128)S(1)}, f32[2,4,64,128]{3,2,1,0:T(8,128)S(1)}, f32[3,2,32]{2,1,0:T(2,128)S(1)}) custom-call(s32[8]{0:T(128)S(4)} %get-tuple-element.22.widths, f32[6,1536,128]{2,1,0:T(8,128)S(1)} %get-tuple-element.23.cells, f32[32,64,128]{2,1,0:T(8,128)S(1)} %get-tuple-element.24.weights, ...), custom_call_target="tpu_custom_call" | custom-call | flops 1000000000 | bytes 1000000 | tf_op jit(solution)/shard_map/pallas_call | solution.py:453
  10.1 0.2 collective-permute-start.2
  10.2 0.0 collective-permute-done.second.refs_0_
  10.2 0.9 %collective-permute-done.1.first.refs_1_ = bf16[80,128]{1,0:T(8,128)(2,1)S(1)} collective-permute-done((bf16[80,128]{1,0:T(8,128)(2,1)S(1)}, bf16[80,128]{1,0:T(8,128)(2,1)S(1)}, u32[]{:S(2)}, u32[]{:S(2)}) %collective-permute-start.1) | collective-permute-done | bytes 20512 | tf_op jit(solution)/shard_map/ppermute | solution.py:407
  11.1 0.2 %shard_map.84 = (f32[2,64,128]{2,1,0:T(8,128)S(1)}, bf16[256,128]{1,0:T(8,128)(2,1)S(1)}, bf16[256,128]{1,0:T(8,128)(2,1)S(1)}) custom-call(s32[8]{0:T(128)S(4)} %get-tuple-element.22.widths, bf16[80,128]{1,0:T(8,128)(2,1)S(1)} %collective-permute-done.second.refs_0_, bf16[80,128]{1,0:T(8,128)(2,1)S(1)} %collective-permute-done.1.first.refs_1_, ...), custom_call_target="tpu_custom_call" | custom-call | tf_op jit(solution)/shard_map/pallas_call | solution.py:467
  11.4 2.0 %collective-permute-start.3 = (bf16[256,128]{1,0:T(8,128)(2,1)S(1)}, bf16[256,128]{1,0:T(8,128)(2,1)S(1)}, u32[]{:S(2)}, u32[]{:S(2)}) collective-permute-start(bf16[256,128]{1,0:T(8,128)(2,1)S(1)} %get-tuple-element.35), channel_id=1, source_target_pairs={{4,8},{8,4},{12,16},{16,12},{20,24},{24,20},{28,0},{0,28},{5,9},{9... | collective-permute-start | bytes 196616 | tf_op jit(solution)/shard_map/ppermute | solution.py:407
  13.3 0.0 collective-permute-start.4
  13.3 0.4 %collective-permute-done.2.refs_3_ = f32[3,2,32]{2,1,0:T(2,128)S(1)} collective-permute-done((f32[3,2,32]{2,1,0:T(2,128)S(1)}, f32[3,2,32]{2,1,0:T(2,128)S(1)}, u32[]{:S(2)}, u32[]{:S(2)}) %collective-permute-start.2) | collective-permute-done | bytes 800 | tf_op jit(solution)/shard_map/ppermute | solution.py:466
  13.7 0.0 copy-done
  13.7 2.2 %shard_map.85 = (f32[2,1536,128]{2,1,0:T(8,128)S(1)}, f32[2,24,24,128]{3,2,1,0:T(8,128)S(1)}, f32[3,64,128]{2,1,0:T(8,128)S(1)}, bf16[256,256]{1,0:T(8,128)(2,1)S(1)}) custom-call(s32[8]{0:T(128)S(4)} %get-tuple-element.22.widths, bf16[64,64]{1,0:T(8,128)(2,1)S(1)} %copy-done, f32[6,1536,128]{2,1,0:T(8,128)S(1)} %get-tuple-element.23.cells, ...), custom_call_target="tpu_custom_call" | custom-call | flops 1000000000 | bytes 1000000 | tf_op jit(solution)/shard_map/pallas_call | solution.py:477
  15.9 1.4 %collective-permute-done.3.far = bf16[256,128]{1,0:T(8,128)(2,1)S(1)} collective-permute-done((bf16[256,128]{1,0:T(8,128)(2,1)S(1)}, bf16[256,128]{1,0:T(8,128)(2,1)S(1)}, u32[]{:S(2)}, u32[]{:S(2)}) %collective-permute-start.3) | collective-permute-done | bytes 65568 | tf_op jit(solution)/shard_map/ppermute | solution.py:407
  17.3 0.0 collective-permute-done.4.near
  17.3 1.3 %shard_map.86 = (bf16[2,64,24,128]{3,2,1,0:T(8,128)(2,1)}, f32[2,1536,128]{2,1,0:T(8,128)S(1)}) custom-call(s32[8]{0:T(128)S(4)} %get-tuple-element.22.widths, f32[6,1536,128]{2,1,0:T(8,128)S(1)} %get-tuple-element.23.cells, f32[32,64,128]{2,1,0:T(8,128)S(1)} %get-tuple-element.24.weights, ...), custom_call_target="tpu_custom_call", output_to_operand_aliasing={{1}: (10, {})} | custom-call | tf_op jit(solution)/shard_map/pallas_call | solution.py:492
Async XLA Ops:
  3.4 6.8 %collective-permute-start = (bf16[80,128]{1,0:T(8,128)(2,1)S(1)}, bf16[80,128]{1,0:T(8,128)(2,1)S(1)}, u32[]{:S(2)}, u32[]{:S(2)}) collective-permute-start(bf16[80,128]{1,0:T(8,128)(2,1)S(1)} %get-tuple-element.27), channel_id=1, source_target_pairs={{1,2},{2,1},{3,0},{0,3},{5,6},{6,5},{7,4},{4,7},{9,10},{10,9},{11,... | collective-permute-start | bytes 61448 | tf_op jit(solution)/shard_map/ppermute | solution.py:407
  7.4 3.8 %collective-permute-start.1 = (bf16[80,128]{1,0:T(8,128)(2,1)S(1)}, bf16[80,128]{1,0:T(8,128)(2,1)S(1)}, u32[]{:S(2)}, u32[]{:S(2)}) collective-permute-start(bf16[80,128]{1,0:T(8,128)(2,1)S(1)} %get-tuple-element.28), channel_id=1, source_target_pairs={{0,1},{1,0},{2,3},{3,2},{4,5},{5,4},{6,7},{7,6},{8,9},{9,8},{10,11... | collective-permute-start | bytes 61448 | tf_op jit(solution)/shard_map/ppermute | solution.py:407
  7.9 5.8 %copy-start = (bf16[64,64]{1,0:T(8,128)(2,1)S(1)}, bf16[64,64]{1,0:T(8,128)(2,1)}, u32[]{:S(2)}) copy-start(bf16[64,64]{1,0:T(8,128)(2,1)} %mix.1) | copy-start | bytes 24580
  10.1 3.7 %collective-permute-start.2 = (f32[3,2,32]{2,1,0:T(2,128)S(1)}, f32[3,2,32]{2,1,0:T(2,128)S(1)}, u32[]{:S(2)}, u32[]{:S(2)}) collective-permute-start(f32[3,2,32]{2,1,0:T(2,128)S(1)} %get-tuple-element.31.refs_2_), channel_id=1, source_target_pairs={{0,2},{1,3},{2,0},{3,1},{4,6},{5,7},{6,4},{7,5},{8,10},{9,11},{10,... | collective-permute-start | bytes 2312 | tf_op jit(solution)/shard_map/ppermute | solution.py:466
  11.4 6.0 %collective-permute-start.3 = (bf16[256,128]{1,0:T(8,128)(2,1)S(1)}, bf16[256,128]{1,0:T(8,128)(2,1)S(1)}, u32[]{:S(2)}, u32[]{:S(2)}) collective-permute-start(bf16[256,128]{1,0:T(8,128)(2,1)S(1)} %get-tuple-element.35), channel_id=1, source_target_pairs={{4,8},{8,4},{12,16},{16,12},{20,24},{24,20},{28,0},{0,28},{5,9},{9... | collective-permute-start | bytes 196616 | tf_op jit(solution)/shard_map/ppermute | solution.py:407
  13.3 4.0 %collective-permute-start.4 = (bf16[256,128]{1,0:T(8,128)(2,1)S(1)}, bf16[256,128]{1,0:T(8,128)(2,1)S(1)}, u32[]{:S(2)}, u32[]{:S(2)}) collective-permute-start(bf16[256,128]{1,0:T(8,128)(2,1)S(1)} %get-tuple-element.36), channel_id=1, source_target_pairs={{0,4},{4,0},{8,12},{12,8},{16,20},{20,16},{24,28},{28,24},{1,5},{5... | collective-permute-start | bytes 196616 | tf_op jit(solution)/shard_map/ppermute | solution.py:407

commit v9 on v8

--- a/solution.py
+++ b/solution.py
@@ -37,15 +37,15 @@
 
 def pack_kernel(
     feature, widths_in, taps_in, dw_bias_in, pw_bias_in, lift_in, coarse_in,
-    cells, weights, first, second, own_block, widths,
-    planes, widths_here, taps, dw_bias, pw_bias, lift, coarse, stacked, tail, picked, sems, small_sems,
+    cells, first, second, stacked, own_block, widths,
+    planes, widths_here, taps, dw_bias, pw_bias, lift, coarse, tail, picked, sems, small_sems,
 ):
     count, channels, slots, tile = feature.shape
     chunks = range(0, channels, CHUNK)
 
-    def copy_of(c):
+    def copy_of(z, c):
         at = pl.ds(c, CHUNK)
-        return pltpu.make_async_copy(feature.at[:, at], planes.at[:, at], sems.at[c // CHUNK])
+        return pltpu.make_async_copy(feature.at[z, at], planes.at[z, at], sems.at[z, c // CHUNK])
 
     small = [
         pltpu.make_async_copy(source, target, small_sems.at[i])
@@ -63,8 +63,8 @@
     for copy in small:
         copy.start()
     for c in chunks:
-        copy_of(c).start()
-
+        for z in range(count):
+            copy_of(z, c).start()
     for copy in small:
         copy.wait()
     for d in range(widths.shape[0]):
@@ -74,9 +74,6 @@
     stacked[DW_BIAS : DW_BIAS + 1, :] = dw_bias[...]
     stacked[PW_BIAS : PW_BIAS + 1, :] = pw_bias[...]
     stacked[LIFT : LIFT + 3, :] = lift[...]
-    turned = jnp.transpose(stacked[...])
-    for t in range(stacked.shape[0]):
-        weights[t] = jnp.broadcast_to(turned[:, t : t + 1], (channels, tile))
 
     own_block[...] = coarse[...]
     parts, own_rows, ncy = coarse.shape
@@ -91,9 +88,6 @@
     for message in (first, second):
         message[channels:, :] = tail[...].astype(BF16)
 
-    shape = (channels, tile)
-    lane = lane_iota(shape)
-    on_left = (lane & 2) != 0
     row, along = row_iota((taps.shape[0], tile)), lane_iota((taps.shape[0], tile))
     of_plane = 9 * ((along & 31) >> 3) + jnp.where((along & 2) != 0, 2, 0)
     terms, rest = [], taps[...]
@@ -110,11 +104,16 @@
         )
 
     across = lane_iota((CHUNK * slots, tile))
+    shape = (CHUNK, tile)
+    lane = lane_iota(shape)
+    on_left = (lane & 2) != 0
+    even = is_even("gy")
+    groups = slots // 4
     for c in chunks:
-        copy_of(c).wait()
         at = slice(c * slots, (c + CHUNK) * slots)
         total = None
         for z in range(count):
+            copy_of(z, c).wait()
             rows = planes[z, c : c + CHUNK].reshape(CHUNK * slots, tile)
             cells[z, at, :] = rows.astype(F32)
             if z:
@@ -123,43 +122,39 @@
             else:
                 total = rows
         picked[at, :] = total.astype(F32)
-    for r in range(2):
-
-        @pl.when(width + r < slots)
-        def _():
-            for z in range(count):
-                cells[z, pl.ds(width + r, channels, stride=slots), :] = jnp.zeros((channels, tile), F32)
-
-    groups = slots // 4
-    held, moved = {}, {}
-    for q in range(groups):
-        rows = [pltpu.roll(picked[pl.ds(4 * q + i, channels, stride=slots), :], 32 * i + 2, 1) for i in range(4)]
-        rows = jnp.where(
-            lane < 64, jnp.where(lane < 32, rows[0], rows[1]), jnp.where(lane < 96, rows[2], rows[3])
-        )
-        held[q] = jnp.where(4 * q + (lane >> 5) < width, rows, 0.0)
-    for q in range(-1, groups):
-        low = held.get(q + 1, jnp.zeros(shape, F32))
-        high = held.get(q, jnp.zeros(shape, F32))
-        moved[q] = pltpu.roll(jnp.where(lane < 64, low, high), 64, 1)
-    sums = []
-    for q in range(-1, groups + 1):
-        total = None
-        for weight, rows in ((scale[0], moved.get(q - 1)), (scale[1], held.get(q)), (scale[2], moved.get(q))):
-            if rows is not None:
-                total = weight * rows if total is None else total + weight * rows
-        sums.append(total + pltpu.roll(total, tile - 8, 1) + pltpu.roll(total, tile - 16, 1))
-    packed = []
-    for half in range(2):
-        total = sums[4 * half]
-        for k in range(1, 4):
-            total = jnp.where(((lane >> 3) & 3) == k, pltpu.roll(sums[4 * half + k], 8 * k, 1), total)
-        packed.append(total)
-    left = jnp.where(on_left, packed[0], pltpu.roll(packed[1], tile - 2, 1))
-    right = jnp.where(on_left, pltpu.roll(packed[1], 2, 1), packed[0])
-    even = is_even("gy")
-    first[0:channels, :] = jnp.where(even, right, left).astype(BF16)
-    second[0:channels, :] = jnp.where(even, left, right).astype(BF16)
+
+        held, moved = {}, {}
+        for q in range(groups):
+            rows = [
+                pltpu.roll(picked[pl.ds(c * slots + 4 * q + i, CHUNK, stride=slots), :], 32 * i + 2, 1)
+                for i in range(4)
+            ]
+            rows = jnp.where(
+                lane < 64, jnp.where(lane < 32, rows[0], rows[1]), jnp.where(lane < 96, rows[2], rows[3])
+            )
+            held[q] = jnp.where(4 * q + (lane >> 5) < width, rows, 0.0)
+        for q in range(-1, groups):
+            low = held.get(q + 1, jnp.zeros(shape, F32))
+            high = held.get(q, jnp.zeros(shape, F32))
+            moved[q] = pltpu.roll(jnp.where(lane < 64, low, high), 64, 1)
+        sums = []
+        for q in range(-1, groups + 1):
+            total = None
+            for weight, rows in ((scale[0], moved.get(q - 1)), (scale[1], held.get(q)), (scale[2], moved.get(q))):
+                if rows is not None:
+                    term = weight[c : c + CHUNK, :] * rows
+                    total = term if total is None else total + term
+            sums.append(total + pltpu.roll(total, tile - 8, 1) + pltpu.roll(total, tile - 16, 1))
+        packed = []
+        for half in range(2):
+            total = sums[4 * half]
+            for k in range(1, 4):
+                total = jnp.where(((lane >> 3) & 3) == k, pltpu.roll(sums[4 * half + k], 8 * k, 1), total)
+            packed.append(total)
+        left = jnp.where(on_left, packed[0], pltpu.roll(packed[1], tile - 2, 1))
+        right = jnp.where(on_left, pltpu.roll(packed[1], 2, 1), packed[0])
+        first[c : c + CHUNK, :] = jnp.where(even, right, left).astype(BF16)
+        second[c : c + CHUNK, :] = jnp.where(even, left, right).astype(BF16)
 
 
 def shifted_sum(before, centre, after):
@@ -194,11 +189,20 @@
                         depth[z, out, to, :] = shifted_sum(*(sums.pop((out, dy)) for dy in (-1, 0, 1)))
 
 
-def conv_kernel(widths, cells, weights, coarse, depth, rims, own_block):
+def conv_kernel(widths, stacked, coarse, cells_in, cells, weights, depth, rims, own_block):
     width = widths[lax.axis_index("gx")]
-    channels = weights.shape[1]
+    channels, tile = weights.shape[1:]
     slots = cells.shape[1] // channels
     own_block[...] = coarse[...]
+    turned = jnp.transpose(stacked[...])
+    for t in range(stacked.shape[0]):
+        weights[t] = jnp.broadcast_to(turned[:, t : t + 1], (channels, tile))
+    for r in range(2):
+
+        @pl.when(width + r < slots)
+        def _():
+            for z in range(cells.shape[0]):
+                cells[z, pl.ds(width + r, channels, stride=slots), :] = jnp.zeros((channels, tile), F32)
 
     for b in range(channels // ROWS):
         at = slice(b * ROWS, (b + 1) * ROWS)
@@ -263,22 +267,23 @@
     return own + weights[DW_BIAS] + edge_term(edge, z, x)
 
 
-def finished_row(weights, cells, lifted, phase, width, mixed, z, x):
-    channels = weights.shape[1]
+def base_row(cells, lifted, phase, z, x):
+    channels = lifted.shape[1]
     slots = cells.shape[1] // channels
+    return cells[2 + z, pl.ds(x, channels, stride=slots), :] + lifted[lax.div(phase + x, CF)]
+
+
+def active(weights, mixed):
     mixed = mixed + weights[PW_BIAS]
-    active = jnp.maximum(mixed, 0.2 * mixed)
-    field = cells[2 + z, pl.ds(x, channels, stride=slots), :]
-    value = active + (field + lifted[lax.div(phase + x, CF)])
-    return jnp.where(x < width, value, 0.0)
+    return jnp.maximum(mixed, 0.2 * mixed)
 
 
 def mix_kernel(gathered, widths, mix, cells, weights, depth, edge, *refs):
     if gathered:
-        coarse, value, rest, lifted, mixer, across = refs
+        coarse, value, ends, bases, mixer, rest, lifted, across = refs
         parts, ncx, ncy = coarse.shape
     else:
-        second, first, own_block, opposite, value, rest, lifted, mixer, across, blocks = refs
+        second, first, own_block, opposite, value, ends, bases, mixer, rest, lifted, across, blocks = refs
         parts, own_rows, ncy = own_block.shape
         ncx = 4 * own_rows
     width = widths[lax.axis_index("gx")]
@@ -344,37 +349,33 @@
         for i in range(group):
             for z in range(ZOUT):
                 part = mixed[i * channels : (i + 1) * channels, z * tile : (z + 1) * tile]
-                value[z, pl.ds(x + i, channels, stride=slots), :] = finished_row(
-                    weights, cells, lifted, phase, width, part, z, x + i
-                )
-
-
-def finish_kernel(widths, cells, weights, depth, rest, edge, lifted, mixer, far, near, value_in, out, value, block, sems):
+                part = active(weights, part) + base_row(cells, lifted, phase, z, x + i)
+                value[z, pl.ds(x + i, channels, stride=slots), :] = jnp.where(x + i < width, part, 0.0)
+    for z in range(ZOUT):
+        for i, x in enumerate((0, 1, width - 2, width - 1)):
+            ends[z, i * channels : (i + 1) * channels, :] = depth_row(weights, (depth, rest), edge, z, x)
+            bases[z, i * channels : (i + 1) * channels, :] = base_row(cells, lifted, phase, z, x)
+
+
+def finish_kernel(widths, weights, ends, bases, mixer, far, near, value_in, out, value, block, sems):
     width = widths[lax.axis_index("gx")]
-    phase = lax.rem(slab_start(widths), CF)
-    channels, tile = weights.shape[1:]
-    slots = cells.shape[1] // channels
+    channels = weights.shape[1]
+    slots = block.shape[2]
     even = is_even("gx")
-    at_top = jnp.where(even, far[...].astype(F32), near[...].astype(F32))
-    at_end = jnp.where(even, near[...].astype(F32), far[...].astype(F32))
-    rows = (0, 1, width - 2, width - 1)
-    chunk = 16
+    half = 2 * channels
     copies = []
     for z in range(ZOUT):
-        parts = []
-        for i, x in enumerate(rows):
-            arrived = at_top if i < 2 else at_end
-            begin = (2 * z + i % 2) * channels
-            parts.append(depth_row(weights, (depth, rest), edge, z, x) + arrived[begin : begin + channels, :])
-        mixed = jnp.dot(mixer[...], jnp.concatenate(parts, axis=0).astype(BF16), preferred_element_type=F32)
-        for i, x in enumerate(rows):
-            value[z, pl.ds(x, channels, stride=slots), :] = finished_row(
-                weights, cells, lifted, phase, width, mixed[i * channels : (i + 1) * channels, :], z, x
-            )
-        for part in range(channels // chunk):
-            for o in range(part * chunk, (part + 1) * chunk):
+        at = slice(z * half, (z + 1) * half)
+        one, two = far[at, :].astype(F32), near[at, :].astype(F32)
+        arrived = jnp.concatenate([jnp.where(even, one, two), jnp.where(even, two, one)], axis=0)
+        mixed = jnp.dot(mixer[...], (ends[z] + arrived).astype(BF16), preferred_element_type=F32)
+        for i, x in enumerate((0, 1, width - 2, width - 1)):
+            at = slice(i * channels, (i + 1) * channels)
+            value[z, pl.ds(x, channels, stride=slots), :] = active(weights, mixed[at, :]) + bases[z, at, :]
+        for part in range(channels // CHUNK):
+            for o in range(part * CHUNK, (part + 1) * CHUNK):
                 block[z, o] = value[z, o * slots : (o + 1) * slots, :].astype(BF16)
-            part_of = pl.ds(part * chunk, chunk)
+            part_of = pl.ds(part * CHUNK, CHUNK)
             copy = pltpu.make_async_copy(block.at[z, part_of], out.at[z, part_of], sems.at[part, z])
             copy.start()
             copies.append(copy)
@@ -419,13 +420,13 @@
         lift_weight.T,
         coarse,
     )
-    cells, weights, first, second, block, slab_widths = pl.pallas_call(
+    cells, first, second, stacked, block, slab_widths = pl.pallas_call(
         pack_kernel,
         out_shape=(
             cells_shape,
-            pltpu.VMEM((32, channels, tile), F32),
             strip,
             strip,
+            pltpu.VMEM((32, channels), F32),
             pltpu.VMEM(coarse.shape, F32),
             pltpu.SMEM(widths.shape, jnp.int32),
         ),
@@ -439,10 +440,9 @@
             pltpu.VMEM((1, channels), F32),
             pltpu.VMEM((parts, channels), F32),
             pltpu.VMEM(coarse.shape, F32),
-            pltpu.VMEM((32, channels), F32),
             pltpu.VMEM((16, tile), F32),
             pltpu.VMEM((channels * slots, tile), F32),
-            pltpu.SemaphoreType.DMA((channels // CHUNK,)),
+            pltpu.SemaphoreType.DMA((planes, channels // CHUNK)),
             pltpu.SemaphoreType.DMA((len(small),)),
         ],
         compiler_params=params,
@@ -450,18 +450,21 @@
     second = swapped(second, "gy", 1)
     first = swapped(first, "gy", 0)
     early = SPLIT * ROWS
-    depth, rims, own_block = pl.pallas_call(
+    cells, weights, depth, rims, own_block = pl.pallas_call(
         conv_kernel,
         out_shape=(
+            cells_shape,
+            pltpu.VMEM((32, channels, tile), F32),
             pltpu.VMEM((ZOUT, slots, early, tile), F32),
             pltpu.VMEM((ZOUT, 4, channels, tile), F32),
             pltpu.VMEM(coarse.shape, F32),
         ),
-        in_specs=[smem, vmem, vmem, vmem],
-        out_specs=(vmem,) * 3,
+        in_specs=[smem] + [vmem] * 3,
+        out_specs=(vmem,) * 5,
+        input_output_aliases={3: 0},
         compiler_params=params,
         cost_estimate=pl.CostEstimate(flops=10**9, bytes_accessed=10**6, transcendentals=0),
-    )(slab_widths, cells, weights, block)
+    )(slab_widths, stacked, block, cells)
     if not gathered:
         opposite = lax.ppermute(own_block, "gy", [(i, (i + 2) % 4) for i in range(4)])
     edge, far, near = pl.pallas_call(
@@ -474,17 +477,17 @@
     far = swapped(far, "gx", 1)
     near = swapped(near, "gx", 0)
     blocks = (every,) if gathered else (second, first, own_block, opposite)
-    value, rest, lifted, mixer = pl.pallas_call(
+    ends_shape = pltpu.VMEM((ZOUT, 4 * channels, tile), F32)
+    value, ends, bases, mixer = pl.pallas_call(
         functools.partial(mix_kernel, gathered),
-        out_shape=(
-            value_shape,
+        out_shape=(value_shape, ends_shape, ends_shape, pltpu.VMEM((4 * channels, 4 * channels), BF16)),
+        in_specs=[smem] + [vmem] * (5 + len(blocks)),
+        out_specs=(vmem,) * 4,
+        scratch_shapes=[
             pltpu.VMEM((ZOUT, slots, channels - early, tile), F32),
             pltpu.VMEM((3, channels, tile), F32),
-            pltpu.VMEM((4 * channels, 4 * channels), BF16),
-        ),
-        in_specs=[smem] + [vmem] * (5 + len(blocks)),
-        out_specs=(vmem,) * 4,
-        scratch_shapes=[pltpu.VMEM((parts, ncx, tile), F32)]
+            pltpu.VMEM((parts, ncx, tile), F32),
+        ]
         + ([] if gathered else [pltpu.VMEM((parts, ncx, ncy), F32)]),
         compiler_params=params,
         cost_estimate=pl.CostEstimate(flops=10**9, bytes_accessed=10**6, transcendentals=0),
@@ -492,15 +495,15 @@
     out, _ = pl.pallas_call(
         finish_kernel,
         out_shape=(shape((ZOUT, channels, slots, tile), BF16), value_shape),
-        in_specs=[smem] + [vmem] * 10,
+        in_specs=[smem] + [vmem] * 7,
         out_specs=(hbm, vmem),
         scratch_shapes=[
             pltpu.VMEM((ZOUT, channels, slots, tile), BF16),
-            pltpu.SemaphoreType.DMA((channels // 16, ZOUT)),
+            pltpu.SemaphoreType.DMA((channels // CHUNK, ZOUT)),
         ],
-        input_output_aliases={10: 1},
+        input_output_aliases={7: 1},
         compiler_params=params,
-    )(slab_widths, cells, weights, depth, rest, edge, lifted, mixer, far, near, value)
+    )(slab_widths, weights, ends, bases, mixer, far, near, value)
     return out
 
 

time: 18.8 us -> 20.8 us (1.11)
  Pallas kernels: 9.26 us -> 11.9 us
  waiting for transfers between devices: 2.69 us -> 1.66 us
  starting transfers between devices: 6.65 us -> 6.98 us
    pallas_call x2, Pallas kernels: 5.54 us -> 8.19 us  [the longest x1 5.49 us: shards(): pl.pallas_call(pack_kernel, out_shape=(cells_shape, strip, strip, pltpu.V...]
    ppermute x4, waiting for transfers between devices: 2.31 us -> 1.06 us  [swapped(): return lax.ppermute(array, axis, pairs)]
    ppermute x4, starting transfers between devices: 6.48 us -> 6.81 us  [swapped(): return lax.ppermute(array, axis, pairs)]
    ppermute x1, waiting for transfers between devices: 0.38 us -> 0.6 us  [shards(): lax.ppermute(own_block, 'gy', [(i, (i + 2) % 4) for i in range(4)])]
where the time goes in v9:
time: 20.8 us; the launch traced here: 20.6 us
  Pallas kernels  11.9 us (57%)
  starting transfers between devices  6.98 us (34%)
  waiting for transfers between devices  1.66 us (8%)
    ppermute x4, starting transfers between devices, swapped(): return lax.ppermute(array, axis, pairs)  6.81 us
    pallas_call x1, Pallas kernels, shards(): pl.pallas_call(pack_kernel, out_shape=(cells_shape, strip, strip, pltpu.V...  5.49 us
    pallas_call x1, Pallas kernels, shards(): pl.pallas_call(conv_kernel, out_shape=(cells_shape, pltpu.VMEM((32, chann...  2.7 us
    pallas_call x1, Pallas kernels, shards(): pl.pallas_call(functools.partial(mix_kernel, gathered), out_shape=(value_...  2.31 us
    pallas_call x1, Pallas kernels, shards(): pl.pallas_call(finish_kernel, out_shape=(shape((ZOUT, channels, slots, ti...  1.2 us
    ppermute x4, waiting for transfers between devices, swapped(): return lax.ppermute(array, axis, pairs)  1.06 us
    ppermute x1, waiting for transfers between devices, shards(): lax.ppermute(own_block, 'gy', [(i, (i + 2) % 4) for i in range(4)])  0.6 us
  transfers between devices with their start and end apart: 5, of which 3 were waited for; matrix products, arithmetic and copies ran while one was open for 0% of the time, Pallas kernels for 25%

profile of v9, /device:TPU:0, one launch (start us, length us, event | category | flops | bytes accessed | tf_op | source)
XLA Modules:
  0.0 20.6 jit_solution(350902992350192715)
XLA Ops:
  0.0 5.5 %shard_map.82 = (f32[6,1536,128]{2,1,0:T(8,128)S(1)}, bf16[80,128]{1,0:T(8,128)(2,1)S(1)}, bf16[80,128]{1,0:T(8,128)(2,1)S(1)}, f32[32,64]{1,0:T(8,128)S(1)}, f32[3,2,32]{2,1,0:T(2,128)S(1)}, /*index=5*/s32[8]{0:T(128)S(4)}) custom-call(bf16[6,64,24,128]{3,2,1,0:T(8,128)(2,1)} %feature.1, s32[8]{0:T(128)} %widths_in.1, f32[27,64]{1,0:T(8,128)} %taps_in.1, ...), custom_call_target="tpu_custom_call" | custom-call | tf_op jit(solution)/shard_map/pallas_call | solution.py:423
  5.5 4.0 %collective-permute-start = (bf16[80,128]{1,0:T(8,128)(2,1)S(1)}, bf16[80,128]{1,0:T(8,128)(2,1)S(1)}, u32[]{:S(2)}, u32[]{:S(2)}) collective-permute-start(bf16[80,128]{1,0:T(8,128)(2,1)S(1)} %get-tuple-element.31), channel_id=1, source_target_pairs={{1,2},{2,1},{3,0},{0,3},{5,6},{6,5},{7,4},{4,7},{9,10},{10,9},{11,... | collective-permute-start | bytes 61448 | tf_op jit(solution)/shard_map/ppermute | solution.py:408
  9.5 0.5 %collective-permute-start.1 = (bf16[80,128]{1,0:T(8,128)(2,1)S(1)}, bf16[80,128]{1,0:T(8,128)(2,1)S(1)}, u32[]{:S(2)}, u32[]{:S(2)}) collective-permute-start(bf16[80,128]{1,0:T(8,128)(2,1)S(1)} %get-tuple-element.32), channel_id=1, source_target_pairs={{0,1},{1,0},{2,3},{3,2},{4,5},{5,4},{6,7},{7,6},{8,9},{9,8},{10,11... | collective-permute-start | bytes 61448 | tf_op jit(solution)/shard_map/ppermute | solution.py:408
  10.0 0.0 copy-start
  10.0 2.7 %shard_map.83 = (f32[6,1536,128]{2,1,0:T(8,128)S(1)}, f32[32,64,128]{2,1,0:T(8,128)S(1)}, f32[2,24,40,128]{3,2,1,0:T(8,128)S(1)}, f32[2,4,64,128]{3,2,1,0:T(8,128)S(1)}, f32[3,2,32]{2,1,0:T(2,128)S(1)}) custom-call(s32[8]{0:T(128)S(4)} %get-tuple-element.24.widths, f32[32,64]{1,0:T(8,128)S(1)} %get-tuple-element.25.stacked, ...), custom_call_target="tpu_custom_call", output_to_operand_aliasing={{0}: (3, {})} | custom-call | flops 1000000000 | bytes 1000000 | tf_op jit(solution)/shard_map/pallas_call | solution.py:453
  12.7 0.2 collective-permute-start.2
  12.9 0.0 collective-permute-done.second.refs_0_
  12.9 0.4 %collective-permute-done.1.first.refs_1_ = bf16[80,128]{1,0:T(8,128)(2,1)S(1)} collective-permute-done((bf16[80,128]{1,0:T(8,128)(2,1)S(1)}, bf16[80,128]{1,0:T(8,128)(2,1)S(1)}, u32[]{:S(2)}, u32[]{:S(2)}) %collective-permute-start.1) | collective-permute-done | bytes 20512 | tf_op jit(solution)/shard_map/ppermute | solution.py:408
  13.2 0.2 shard_map.84
  13.5 2.3 %collective-permute-start.3 = (bf16[256,128]{1,0:T(8,128)(2,1)S(1)}, bf16[256,128]{1,0:T(8,128)(2,1)S(1)}, u32[]{:S(2)}, u32[]{:S(2)}) collective-permute-start(bf16[256,128]{1,0:T(8,128)(2,1)S(1)} %get-tuple-element.39), channel_id=1, source_target_pairs={{4,8},{8,4},{12,16},{16,12},{20,24},{24,20},{28,0},{0,28},{5,9},{9... | collective-permute-start | bytes 196616 | tf_op jit(solution)/shard_map/ppermute | solution.py:408
  15.8 0.0 collective-permute-start.4
  15.8 0.6 %collective-permute-done.2.refs_3_ = f32[3,2,32]{2,1,0:T(2,128)S(1)} collective-permute-done((f32[3,2,32]{2,1,0:T(2,128)S(1)}, f32[3,2,32]{2,1,0:T(2,128)S(1)}, u32[]{:S(2)}, u32[]{:S(2)}) %collective-permute-start.2) | collective-permute-done | bytes 800 | tf_op jit(solution)/shard_map/ppermute | solution.py:469
  16.4 0.0 copy-done
  16.4 2.3 %shard_map.85 = (f32[2,1536,128]{2,1,0:T(8,128)S(1)}, f32[2,256,128]{2,1,0:T(8,128)S(1)}, f32[2,256,128]{2,1,0:T(8,128)S(1)}, bf16[256,256]{1,0:T(8,128)(2,1)S(1)}) custom-call(s32[8]{0:T(128)S(4)} %get-tuple-element.24.widths, bf16[64,64]{1,0:T(8,128)(2,1)S(1)} %copy-done, f32[6,1536,128]{2,1,0:T(8,128)S(1)} %get-tuple-element.29.cells, ...), custom_call_target="tpu_custom_call" | custom-call | flops 1000000000 | bytes 1000000 | tf_op jit(solution)/shard_map/pallas_call | solution.py:481
  18.7 0.7 %collective-permute-done.3.far = bf16[256,128]{1,0:T(8,128)(2,1)S(1)} collective-permute-done((bf16[256,128]{1,0:T(8,128)(2,1)S(1)}, bf16[256,128]{1,0:T(8,128)(2,1)S(1)}, u32[]{:S(2)}, u32[]{:S(2)}) %collective-permute-start.3) | collective-permute-done | bytes 65568 | tf_op jit(solution)/shard_map/ppermute | solution.py:408
  19.4 0.0 collective-permute-done.4.near
  19.4 1.2 %shard_map.86 = (bf16[2,64,24,128]{3,2,1,0:T(8,128)(2,1)}, f32[2,1536,128]{2,1,0:T(8,128)S(1)}) custom-call(s32[8]{0:T(128)S(4)} %get-tuple-element.24.widths, f32[32,64,128]{2,1,0:T(8,128)S(1)} %get-tuple-element.28.weights, f32[2,256,128]{2,1,0:T(8,128)S(1)} %get-tuple-element.36.ends, ...), custom_call_target="tpu_custom_call", output_to_operand_aliasing={{1}: (7, {})} | custom-call | tf_op jit(solution)/shard_map/pallas_call | solution.py:495
Async XLA Ops:
  5.5 7.4 %collective-permute-start = (bf16[80,128]{1,0:T(8,128)(2,1)S(1)}, bf16[80,128]{1,0:T(8,128)(2,1)S(1)}, u32[]{:S(2)}, u32[]{:S(2)}) collective-permute-start(bf16[80,128]{1,0:T(8,128)(2,1)S(1)} %get-tuple-element.31), channel_id=1, source_target_pairs={{1,2},{2,1},{3,0},{0,3},{5,6},{6,5},{7,4},{4,7},{9,10},{10,9},{11,... | collective-permute-start | bytes 61448 | tf_op jit(solution)/shard_map/ppermute | solution.py:408
  9.5 3.8 %collective-permute-start.1 = (bf16[80,128]{1,0:T(8,128)(2,1)S(1)}, bf16[80,128]{1,0:T(8,128)(2,1)S(1)}, u32[]{:S(2)}, u32[]{:S(2)}) collective-permute-start(bf16[80,128]{1,0:T(8,128)(2,1)S(1)} %get-tuple-element.32), channel_id=1, source_target_pairs={{0,1},{1,0},{2,3},{3,2},{4,5},{5,4},{6,7},{7,6},{8,9},{9,8},{10,11... | collective-permute-start | bytes 61448 | tf_op jit(solution)/shard_map/ppermute | solution.py:408
  10.0 6.4 %copy-start = (bf16[64,64]{1,0:T(8,128)(2,1)S(1)}, bf16[64,64]{1,0:T(8,128)(2,1)}, u32[]{:S(2)}) copy-start(bf16[64,64]{1,0:T(8,128)(2,1)} %mix.1) | copy-start | bytes 24580
  12.7 3.7 %collective-permute-start.2 = (f32[3,2,32]{2,1,0:T(2,128)S(1)}, f32[3,2,32]{2,1,0:T(2,128)S(1)}, u32[]{:S(2)}, u32[]{:S(2)}) collective-permute-start(f32[3,2,32]{2,1,0:T(2,128)S(1)} %get-tuple-element.35.refs_2_), channel_id=1, source_target_pairs={{0,2},{1,3},{2,0},{3,1},{4,6},{5,7},{6,4},{7,5},{8,10},{9,11},{10,... | collective-permute-start | bytes 2312 | tf_op jit(solution)/shard_map/ppermute | solution.py:469
  13.5 5.9 %collective-permute-start.3 = (bf16[256,128]{1,0:T(8,128)(2,1)S(1)}, bf16[256,128]{1,0:T(8,128)(2,1)S(1)}, u32[]{:S(2)}, u32[]{:S(2)}) collective-permute-start(bf16[256,128]{1,0:T(8,128)(2,1)S(1)} %get-tuple-element.39), channel_id=1, source_target_pairs={{4,8},{8,4},{12,16},{16,12},{20,24},{24,20},{28,0},{0,28},{5,9},{9... | collective-permute-start | bytes 196616 | tf_op jit(solution)/shard_map/ppermute | solution.py:408
  15.8 3.6 %collective-permute-start.4 = (bf16[256,128]{1,0:T(8,128)(2,1)S(1)}, bf16[256,128]{1,0:T(8,128)(2,1)S(1)}, u32[]{:S(2)}, u32[]{:S(2)}) collective-permute-start(bf16[256,128]{1,0:T(8,128)(2,1)S(1)} %get-tuple-element.40), channel_id=1, source_target_pairs={{0,4},{4,0},{8,12},{12,8},{16,20},{20,16},{24,28},{28,24},{1,5},{5... | collective-permute-start | bytes 196616 | tf_op jit(solution)/shard_map/ppermute | solution.py:408

commit v10 on v9

--- a/solution.py
+++ b/solution.py
@@ -37,15 +37,15 @@
 
 def pack_kernel(
     feature, widths_in, taps_in, dw_bias_in, pw_bias_in, lift_in, coarse_in,
-    cells, first, second, stacked, own_block, widths,
-    planes, widths_here, taps, dw_bias, pw_bias, lift, coarse, tail, picked, sems, small_sems,
+    cells, weights, first, second, own_block, widths,
+    planes, widths_here, taps, dw_bias, pw_bias, lift, coarse, stacked, tail, picked, sems, small_sems,
 ):
     count, channels, slots, tile = feature.shape
     chunks = range(0, channels, CHUNK)
 
-    def copy_of(z, c):
+    def copy_of(c):
         at = pl.ds(c, CHUNK)
-        return pltpu.make_async_copy(feature.at[z, at], planes.at[z, at], sems.at[z, c // CHUNK])
+        return pltpu.make_async_copy(feature.at[:, at], planes.at[:, at], sems.at[c // CHUNK])
 
     small = [
         pltpu.make_async_copy(source, target, small_sems.at[i])
@@ -63,8 +63,7 @@
     for copy in small:
         copy.start()
     for c in chunks:
-        for z in range(count):
-            copy_of(z, c).start()
+        copy_of(c).start()
     for copy in small:
         copy.wait()
     for d in range(widths.shape[0]):
@@ -89,72 +88,82 @@
         message[channels:, :] = tail[...].astype(BF16)
 
     row, along = row_iota((taps.shape[0], tile)), lane_iota((taps.shape[0], tile))
-    of_plane = 9 * ((along & 31) >> 3) + jnp.where((along & 2) != 0, 2, 0)
+    by_side = jnp.where((along & 2) != 0, 2, 0)
     terms, rest = [], taps[...]
     for _ in range(3):
         terms.append(rest.astype(BF16))
         rest = rest - terms[-1].astype(F32)
-    scale = []
-    for dx in (-1, 0, 1):
-        chosen = (row == of_plane + 3 * (dx + 1)).astype(BF16)
-        scale.append(
-            sum(
-                lax.dot_general(term, chosen, (((0,), (0,)), ((), ())), preferred_element_type=F32) for term in terms
-            )
-        )
-
-    across = lane_iota((CHUNK * slots, tile))
+    chosen = jnp.concatenate(
+        [(row == tap_of(m, dx, -1) + by_side).astype(BF16) for m in range(3) for dx in (-1, 0, 1)], axis=1
+    )
+    scale = sum(lax.dot_general(term, chosen, (((0,), (0,)), ((), ())), preferred_element_type=F32) for term in terms)
+    turned = jnp.transpose(stacked[...])
+    for t in range(stacked.shape[0]):
+        weights[t] = jnp.broadcast_to(turned[:, t : t + 1], (channels, tile))
+
+    lane, row = lane_iota((slots, tile)), row_iota((slots, tile))
+    mine = (lane >> 3) == (row & 15)
+    in_even, in_odd = mine & ((lane & 4) == 0), mine & ((lane & 4) != 0)
+    shape = (2 * CHUNK, CHUNK * slots)
+    row, column = row_iota(shape), lane_iota(shape)
+    begin = (row & (CHUNK - 1)) * slots
+    low = jnp.where(row < CHUNK, begin, begin + 16)
+    high = jnp.where(row < CHUNK, begin + 16, begin + slots)
+    gather = ((column >= low) & (column < high)).astype(BF16)
     shape = (CHUNK, tile)
+    for c in chunks:
+        copy_of(c).wait()
+        spread = []
+        for m in range(3):
+            rows = []
+            for k in range(c, c + CHUNK):
+                both = []
+                for z in range(ZOUT):
+                    plane = planes[ZOUT * m + z, k].astype(F32)
+                    cells[ZOUT * m + z, k * slots : (k + 1) * slots, :] = plane
+                    both.append(
+                        jnp.concatenate(
+                            [
+                                pltpu.roll(plane[x : x + ROWS], (2 + 4 * z + 8 * x) % tile, 1, stride=8, stride_axis=0)
+                                for x in range(0, slots, ROWS)
+                            ],
+                            axis=0,
+                        )
+                    )
+                rows.append(jnp.where(in_even, both[0], jnp.where(in_odd, both[1], 0.0)))
+            spread.append(jnp.concatenate(rows, axis=0).astype(BF16))
+        sums = jnp.dot(gather, jnp.concatenate(spread, axis=1), preferred_element_type=F32)
+        for half in range(2):
+            inside = 16 * half + (lane_iota(shape) >> 3) < width
+            for m in range(3):
+                part = sums[half * CHUNK : (half + 1) * CHUNK, m * tile : (m + 1) * tile]
+                picked[m, half, c : c + CHUNK, :] = jnp.where(inside, part, 0.0)
+
+    shape = (channels, tile)
     lane = lane_iota(shape)
     on_left = (lane & 2) != 0
+    packed = [None, None]
+    for m in range(3):
+        low, high = picked[m, 0], picked[m, 1]
+        moved = {
+            -1: tuple(
+                pltpu.roll(jnp.where(lane < tile - 16, one, two), 16, 1) for one, two in ((low, high), (high, low))
+            ),
+            0: (low, high),
+            1: tuple(
+                pltpu.roll(jnp.where(lane >= 16, one, two), tile - 16, 1) for one, two in ((low, high), (high, low))
+            ),
+        }
+        for dx in (-1, 0, 1):
+            begin = (3 * m + dx + 1) * tile
+            for half in range(2):
+                term = scale[:, begin : begin + tile] * moved[dx][half]
+                packed[half] = term if packed[half] is None else packed[half] + term
+    left = jnp.where(on_left, packed[0], pltpu.roll(packed[1], tile - 2, 1))
+    right = jnp.where(on_left, pltpu.roll(packed[1], 2, 1), packed[0])
     even = is_even("gy")
-    groups = slots // 4
-    for c in chunks:
-        at = slice(c * slots, (c + CHUNK) * slots)
-        total = None
-        for z in range(count):
-            copy_of(z, c).wait()
-            rows = planes[z, c : c + CHUNK].reshape(CHUNK * slots, tile)
-            cells[z, at, :] = rows.astype(F32)
-            if z:
-                inside = (across >= 4 * z - 2) & (across < 4 * z + 2)
-                total = jnp.where(inside, pltpu.roll(rows, 4 * z, 1), total)
-            else:
-                total = rows
-        picked[at, :] = total.astype(F32)
-
-        held, moved = {}, {}
-        for q in range(groups):
-            rows = [
-                pltpu.roll(picked[pl.ds(c * slots + 4 * q + i, CHUNK, stride=slots), :], 32 * i + 2, 1)
-                for i in range(4)
-            ]
-            rows = jnp.where(
-                lane < 64, jnp.where(lane < 32, rows[0], rows[1]), jnp.where(lane < 96, rows[2], rows[3])
-            )
-            held[q] = jnp.where(4 * q + (lane >> 5) < width, rows, 0.0)
-        for q in range(-1, groups):
-            low = held.get(q + 1, jnp.zeros(shape, F32))
-            high = held.get(q, jnp.zeros(shape, F32))
-            moved[q] = pltpu.roll(jnp.where(lane < 64, low, high), 64, 1)
-        sums = []
-        for q in range(-1, groups + 1):
-            total = None
-            for weight, rows in ((scale[0], moved.get(q - 1)), (scale[1], held.get(q)), (scale[2], moved.get(q))):
-                if rows is not None:
-                    term = weight[c : c + CHUNK, :] * rows
-                    total = term if total is None else total + term
-            sums.append(total + pltpu.roll(total, tile - 8, 1) + pltpu.roll(total, tile - 16, 1))
-        packed = []
-        for half in range(2):
-            total = sums[4 * half]
-            for k in range(1, 4):
-                total = jnp.where(((lane >> 3) & 3) == k, pltpu.roll(sums[4 * half + k], 8 * k, 1), total)
-            packed.append(total)
-        left = jnp.where(on_left, packed[0], pltpu.roll(packed[1], tile - 2, 1))
-        right = jnp.where(on_left, pltpu.roll(packed[1], 2, 1), packed[0])
-        first[c : c + CHUNK, :] = jnp.where(even, right, left).astype(BF16)
-        second[c : c + CHUNK, :] = jnp.where(even, left, right).astype(BF16)
+    first[0:channels, :] = jnp.where(even, right, left).astype(BF16)
+    second[0:channels, :] = jnp.where(even, left, right).astype(BF16)
 
 
 def shifted_sum(before, centre, after):
@@ -189,14 +198,11 @@
                         depth[z, out, to, :] = shifted_sum(*(sums.pop((out, dy)) for dy in (-1, 0, 1)))
 
 
-def conv_kernel(widths, stacked, coarse, cells_in, cells, weights, depth, rims, own_block):
+def conv_kernel(widths, weights, coarse, cells_in, cells, depth, rims, own_block):
     width = widths[lax.axis_index("gx")]
     channels, tile = weights.shape[1:]
     slots = cells.shape[1] // channels
     own_block[...] = coarse[...]
-    turned = jnp.transpose(stacked[...])
-    for t in range(stacked.shape[0]):
-        weights[t] = jnp.broadcast_to(turned[:, t : t + 1], (channels, tile))
     for r in range(2):
 
         @pl.when(width + r < slots)
@@ -226,10 +232,8 @@
 
 def edge_term(edge, z, x):
     tile = edge.shape[2]
-    group = x // 4 + 1 if isinstance(x, int) else lax.div(x, 4) + 1
-    at = x % 4 if isinstance(x, int) else lax.rem(x, 4)
-    begin = 32 * at + 8 * (group & 3) + 4 * z
-    cells = pltpu.roll(edge[group >> 2], tile - 2 - begin, 1)
+    begin = 8 * (x & 15) + 4 * z
+    cells = pltpu.roll(edge[(x >> 4) & 1], (tile - 2 - begin) & (tile - 1), 1)
     lane = lane_iota(cells.shape)
     return jnp.where((lane < 2) | (lane >= tile - 2), cells, 0.0)
 
@@ -420,13 +424,13 @@
         lift_weight.T,
         coarse,
     )
-    cells, first, second, stacked, block, slab_widths = pl.pallas_call(
+    cells, weights, first, second, block, slab_widths = pl.pallas_call(
         pack_kernel,
         out_shape=(
             cells_shape,
+            pltpu.VMEM((32, channels, tile), F32),
             strip,
             strip,
-            pltpu.VMEM((32, channels), F32),
             pltpu.VMEM(coarse.shape, F32),
             pltpu.SMEM(widths.shape, jnp.int32),
         ),
@@ -440,9 +444,10 @@
             pltpu.VMEM((1, channels), F32),
             pltpu.VMEM((parts, channels), F32),
             pltpu.VMEM(coarse.shape, F32),
+            pltpu.VMEM((32, channels), F32),
             pltpu.VMEM((16, tile), F32),
-            pltpu.VMEM((channels * slots, tile), F32),
-            pltpu.SemaphoreType.DMA((planes, channels // CHUNK)),
+            pltpu.VMEM((3, 2, channels, tile), F32),
+            pltpu.SemaphoreType.DMA((channels // CHUNK,)),
             pltpu.SemaphoreType.DMA((len(small),)),
         ],
         compiler_params=params,
@@ -450,21 +455,20 @@
     second = swapped(second, "gy", 1)
     first = swapped(first, "gy", 0)
     early = SPLIT * ROWS
-    cells, weights, depth, rims, own_block = pl.pallas_call(
+    cells, depth, rims, own_block = pl.pallas_call(
         conv_kernel,
         out_shape=(
             cells_shape,
-            pltpu.VMEM((32, channels, tile), F32),
             pltpu.VMEM((ZOUT, slots, early, tile), F32),
             pltpu.VMEM((ZOUT, 4, channels, tile), F32),
             pltpu.VMEM(coarse.shape, F32),
         ),
         in_specs=[smem] + [vmem] * 3,
-        out_specs=(vmem,) * 5,
+        out_specs=(vmem,) * 4,
         input_output_aliases={3: 0},
         compiler_params=params,
         cost_estimate=pl.CostEstimate(flops=10**9, bytes_accessed=10**6, transcendentals=0),
-    )(slab_widths, stacked, block, cells)
+    )(slab_widths, weights, block, cells)
     if not gathered:
         opposite = lax.ppermute(own_block, "gy", [(i, (i + 2) % 4) for i in range(4)])
     edge, far, near = pl.pallas_call(

time: 20.8 us -> 18.8 us (0.904)
  Pallas kernels: 11.9 us -> 9.41 us
  waiting for transfers between devices: 1.66 us -> 2.52 us
  starting transfers between devices: 6.98 us -> 6.67 us
    pallas_call x2, Pallas kernels: 8.19 us -> 5.74 us  [the longest x1 3.5 us: shards(): pl.pallas_call(pack_kernel, out_shape=(cells_shape, pltpu.VMEM((32, chann...]
    ppermute x4, waiting for transfers between devices: 1.06 us -> 2.05 us  [swapped(): return lax.ppermute(array, axis, pairs)]
    ppermute x4, starting transfers between devices: 6.81 us -> 6.5 us  [swapped(): return lax.ppermute(array, axis, pairs)]
where the time goes in v10:
time: 18.8 us; the launch traced here: 18.6 us
  Pallas kernels  9.41 us (50%)
  starting transfers between devices  6.67 us (35%)
  waiting for transfers between devices  2.52 us (13%)
    ppermute x4, starting transfers between devices, swapped(): return lax.ppermute(array, axis, pairs)  6.5 us
    pallas_call x1, Pallas kernels, shards(): pl.pallas_call(pack_kernel, out_shape=(cells_shape, pltpu.VMEM((32, chann...  3.5 us
    pallas_call x1, Pallas kernels, shards(): pl.pallas_call(functools.partial(mix_kernel, gathered), out_shape=(value_...  2.28 us
    pallas_call x1, Pallas kernels, shards(): pl.pallas_call(conv_kernel, out_shape=(cells_shape, pltpu.VMEM((ZOUT, slo...  2.24 us
    ppermute x4, waiting for transfers between devices, swapped(): return lax.ppermute(array, axis, pairs)  2.05 us
    pallas_call x1, Pallas kernels, shards(): pl.pallas_call(finish_kernel, out_shape=(shape((ZOUT, channels, slots, ti...  1.21 us
    ppermute x1, waiting for transfers between devices, shards(): lax.ppermute(own_block, 'gy', [(i, (i + 2) % 4) for i in range(4)])  0.47 us
  transfers between devices with their start and end apart: 5, of which 3 were waited for; matrix products, arithmetic and copies ran while one was open for 0% of the time, Pallas kernels for 25%

profile of v10, /device:TPU:0, one launch (start us, length us, event | category | flops | bytes accessed | tf_op | source)
XLA Modules:
  0.0 18.6 jit_solution(17946673702635625705)
XLA Ops:
  0.0 3.5 %shard_map.82 = (f32[6,1536,128]{2,1,0:T(8,128)S(1)}, f32[32,64,128]{2,1,0:T(8,128)S(1)}, bf16[80,128]{1,0:T(8,128)(2,1)S(1)}, bf16[80,128]{1,0:T(8,128)(2,1)S(1...) custom-call(bf16[6,64,24,128]{3,2,1,0:T(8,128)(2,1)} %feature.1, s32[8]{0:T(128)} %widths_in.1, f32[27,64]{1,0:T(8,128)} %taps_in.1, ...), custom_call_target="tpu_custom_call" | custom-call | tf_op jit(solution)/shard_map/pallas_call | solution.py:427
  3.5 4.0 %collective-permute-start = (bf16[80,128]{1,0:T(8,128)(2,1)S(1)}, bf16[80,128]{1,0:T(8,128)(2,1)S(1)}, u32[]{:S(2)}, u32[]{:S(2)}) collective-permute-start(bf16[80,128]{1,0:T(8,128)(2,1)S(1)} %get-tuple-element.29), channel_id=1, source_target_pairs={{1,2},{2,1},{3,0},{0,3},{5,6},{6,5},{7,4},{4,7},{9,10},{10,9},{11,... | collective-permute-start | bytes 61448 | tf_op jit(solution)/shard_map/ppermute | solution.py:412
  7.5 0.5 %collective-permute-start.1 = (bf16[80,128]{1,0:T(8,128)(2,1)S(1)}, bf16[80,128]{1,0:T(8,128)(2,1)S(1)}, u32[]{:S(2)}, u32[]{:S(2)}) collective-permute-start(bf16[80,128]{1,0:T(8,128)(2,1)S(1)} %get-tuple-element.30), channel_id=1, source_target_pairs={{0,1},{1,0},{2,3},{3,2},{4,5},{5,4},{6,7},{7,6},{8,9},{9,8},{10,11... | collective-permute-start | bytes 61448 | tf_op jit(solution)/shard_map/ppermute | solution.py:412
  8.0 0.0 copy-start
  8.0 2.2 %shard_map.83 = (f32[6,1536,128]{2,1,0:T(8,128)S(1)}, f32[2,24,40,128]{3,2,1,0:T(8,128)S(1)}, f32[2,4,64,128]{3,2,1,0:T(8,128)S(1)}, f32[3,2,32]{2,1,0:T(2,128)S(1)}) custom-call(s32[8]{0:T(128)S(4)} %get-tuple-element.23.widths, f32[32,64,128]{2,1,0:T(8,128)S(1)} %get-tuple-element.24.weights, ...), custom_call_target="tpu_custom_call", output_to_operand_aliasing={{0}: (3, {})} | custom-call | flops 1000000000 | bytes 1000000 | tf_op jit(solution)/shard_map/pallas_call | solution.py:458
  10.3 0.2 collective-permute-start.2
  10.4 0.0 collective-permute-done.second.refs_0_
  10.4 0.8 %collective-permute-done.1.first.refs_1_ = bf16[80,128]{1,0:T(8,128)(2,1)S(1)} collective-permute-done((bf16[80,128]{1,0:T(8,128)(2,1)S(1)}, bf16[80,128]{1,0:T(8,128)(2,1)S(1)}, u32[]{:S(2)}, u32[]{:S(2)}) %collective-permute-start.1) | collective-permute-done | bytes 20512 | tf_op jit(solution)/shard_map/ppermute | solution.py:412
  11.2 0.2 %shard_map.84 = (f32[2,64,128]{2,1,0:T(8,128)S(1)}, bf16[256,128]{1,0:T(8,128)(2,1)S(1)}, bf16[256,128]{1,0:T(8,128)(2,1)S(1)}) custom-call(s32[8]{0:T(128)S(4)} %get-tuple-element.23.widths, bf16[80,128]{1,0:T(8,128)(2,1)S(1)} %collective-permute-done.second.refs_0_, bf16[80,128]{1,0:T(8,128)(2,1)S(1)} %collective-permute-done.1.first.refs_1_, ...), custom_call_target="tpu_custom_call" | custom-call | tf_op jit(solution)/shard_map/pallas_call | solution.py:474
  11.4 2.0 %collective-permute-start.3 = (bf16[256,128]{1,0:T(8,128)(2,1)S(1)}, bf16[256,128]{1,0:T(8,128)(2,1)S(1)}, u32[]{:S(2)}, u32[]{:S(2)}) collective-permute-start(bf16[256,128]{1,0:T(8,128)(2,1)S(1)} %get-tuple-element.37), channel_id=1, source_target_pairs={{4,8},{8,4},{12,16},{16,12},{20,24},{24,20},{28,0},{0,28},{5,9},{9... | collective-permute-start | bytes 196616 | tf_op jit(solution)/shard_map/ppermute | solution.py:412
  13.4 0.0 collective-permute-start.4
  13.4 0.5 %collective-permute-done.2.refs_3_ = f32[3,2,32]{2,1,0:T(2,128)S(1)} collective-permute-done((f32[3,2,32]{2,1,0:T(2,128)S(1)}, f32[3,2,32]{2,1,0:T(2,128)S(1)}, u32[]{:S(2)}, u32[]{:S(2)}) %collective-permute-start.2) | collective-permute-done | bytes 800 | tf_op jit(solution)/shard_map/ppermute | solution.py:473
  13.9 0.0 copy-done
  13.9 2.3 %shard_map.85 = (f32[2,1536,128]{2,1,0:T(8,128)S(1)}, f32[2,256,128]{2,1,0:T(8,128)S(1)}, f32[2,256,128]{2,1,0:T(8,128)S(1)}, bf16[256,256]{1,0:T(8,128)(2,1)S(1)}) custom-call(s32[8]{0:T(128)S(4)} %get-tuple-element.23.widths, bf16[64,64]{1,0:T(8,128)(2,1)S(1)} %copy-done, f32[6,1536,128]{2,1,0:T(8,128)S(1)} %get-tuple-element.27.cells, ...), custom_call_target="tpu_custom_call" | custom-call | flops 1000000000 | bytes 1000000 | tf_op jit(solution)/shard_map/pallas_call | solution.py:485
  16.2 1.2 %collective-permute-done.3.far = bf16[256,128]{1,0:T(8,128)(2,1)S(1)} collective-permute-done((bf16[256,128]{1,0:T(8,128)(2,1)S(1)}, bf16[256,128]{1,0:T(8,128)(2,1)S(1)}, u32[]{:S(2)}, u32[]{:S(2)}) %collective-permute-start.3) | collective-permute-done | bytes 65568 | tf_op jit(solution)/shard_map/ppermute | solution.py:412
  17.4 0.0 collective-permute-done.4.near
  17.4 1.2 %shard_map.86 = (bf16[2,64,24,128]{3,2,1,0:T(8,128)(2,1)}, f32[2,1536,128]{2,1,0:T(8,128)S(1)}) custom-call(s32[8]{0:T(128)S(4)} %get-tuple-element.23.widths, f32[32,64,128]{2,1,0:T(8,128)S(1)} %get-tuple-element.24.weights, f32[2,256,128]{2,1,0:T(8,128)S(1)} %get-tuple-element.34.ends, ...), custom_call_target="tpu_custom_call", output_to_operand_aliasing={{1}: (7, {})} | custom-call | tf_op jit(solution)/shard_map/pallas_call | solution.py:499
Async XLA Ops:
  3.5 6.9 %collective-permute-start = (bf16[80,128]{1,0:T(8,128)(2,1)S(1)}, bf16[80,128]{1,0:T(8,128)(2,1)S(1)}, u32[]{:S(2)}, u32[]{:S(2)}) collective-permute-start(bf16[80,128]{1,0:T(8,128)(2,1)S(1)} %get-tuple-element.29), channel_id=1, source_target_pairs={{1,2},{2,1},{3,0},{0,3},{5,6},{6,5},{7,4},{4,7},{9,10},{10,9},{11,... | collective-permute-start | bytes 61448 | tf_op jit(solution)/shard_map/ppermute | solution.py:412
  7.5 3.8 %collective-permute-start.1 = (bf16[80,128]{1,0:T(8,128)(2,1)S(1)}, bf16[80,128]{1,0:T(8,128)(2,1)S(1)}, u32[]{:S(2)}, u32[]{:S(2)}) collective-permute-start(bf16[80,128]{1,0:T(8,128)(2,1)S(1)} %get-tuple-element.30), channel_id=1, source_target_pairs={{0,1},{1,0},{2,3},{3,2},{4,5},{5,4},{6,7},{7,6},{8,9},{9,8},{10,11... | collective-permute-start | bytes 61448 | tf_op jit(solution)/shard_map/ppermute | solution.py:412
  8.0 5.9 %copy-start = (bf16[64,64]{1,0:T(8,128)(2,1)S(1)}, bf16[64,64]{1,0:T(8,128)(2,1)}, u32[]{:S(2)}) copy-start(bf16[64,64]{1,0:T(8,128)(2,1)} %mix.1) | copy-start | bytes 24580
  10.3 3.7 %collective-permute-start.2 = (f32[3,2,32]{2,1,0:T(2,128)S(1)}, f32[3,2,32]{2,1,0:T(2,128)S(1)}, u32[]{:S(2)}, u32[]{:S(2)}) collective-permute-start(f32[3,2,32]{2,1,0:T(2,128)S(1)} %get-tuple-element.33.refs_2_), channel_id=1, source_target_pairs={{0,2},{1,3},{2,0},{3,1},{4,6},{5,7},{6,4},{7,5},{8,10},{9,11},{10,... | collective-permute-start | bytes 2312 | tf_op jit(solution)/shard_map/ppermute | solution.py:473
  11.4 6.0 %collective-permute-start.3 = (bf16[256,128]{1,0:T(8,128)(2,1)S(1)}, bf16[256,128]{1,0:T(8,128)(2,1)S(1)}, u32[]{:S(2)}, u32[]{:S(2)}) collective-permute-start(bf16[256,128]{1,0:T(8,128)(2,1)S(1)} %get-tuple-element.37), channel_id=1, source_target_pairs={{4,8},{8,4},{12,16},{16,12},{20,24},{24,20},{28,0},{0,28},{5,9},{9... | collective-permute-start | bytes 196616 | tf_op jit(solution)/shard_map/ppermute | solution.py:412
  13.4 4.0 %collective-permute-start.4 = (bf16[256,128]{1,0:T(8,128)(2,1)S(1)}, bf16[256,128]{1,0:T(8,128)(2,1)S(1)}, u32[]{:S(2)}, u32[]{:S(2)}) collective-permute-start(bf16[256,128]{1,0:T(8,128)(2,1)S(1)} %get-tuple-element.38), channel_id=1, source_target_pairs={{0,4},{4,0},{8,12},{12,8},{16,20},{20,16},{24,28},{28,24},{1,5},{5... | collective-permute-start | bytes 196616 | tf_op jit(solution)/shard_map/ppermute | solution.py:412

commit v11 on v10

--- a/solution.py
+++ b/solution.py
@@ -43,9 +43,9 @@
     count, channels, slots, tile = feature.shape
     chunks = range(0, channels, CHUNK)
 
-    def copy_of(c):
-        at = pl.ds(c, CHUNK)
-        return pltpu.make_async_copy(feature.at[:, at], planes.at[:, at], sems.at[c // CHUNK])
+    def copy_of(m):
+        at = pl.ds(ZOUT * m, ZOUT)
+        return pltpu.make_async_copy(feature.at[at], planes.at[at], sems.at[m])
 
     small = [
         pltpu.make_async_copy(source, target, small_sems.at[i])
@@ -62,8 +62,8 @@
     ]
     for copy in small:
         copy.start()
-    for c in chunks:
-        copy_of(c).start()
+    for m in range(3):
+        copy_of(m).start()
     for copy in small:
         copy.wait()
     for d in range(widths.shape[0]):
@@ -111,10 +111,9 @@
     high = jnp.where(row < CHUNK, begin + 16, begin + slots)
     gather = ((column >= low) & (column < high)).astype(BF16)
     shape = (CHUNK, tile)
-    for c in chunks:
-        copy_of(c).wait()
-        spread = []
-        for m in range(3):
+    for m in range(3):
+        copy_of(m).wait()
+        for c in chunks:
             rows = []
             for k in range(c, c + CHUNK):
                 both = []
@@ -131,12 +130,10 @@
                         )
                     )
                 rows.append(jnp.where(in_even, both[0], jnp.where(in_odd, both[1], 0.0)))
-            spread.append(jnp.concatenate(rows, axis=0).astype(BF16))
-        sums = jnp.dot(gather, jnp.concatenate(spread, axis=1), preferred_element_type=F32)
-        for half in range(2):
-            inside = 16 * half + (lane_iota(shape) >> 3) < width
-            for m in range(3):
-                part = sums[half * CHUNK : (half + 1) * CHUNK, m * tile : (m + 1) * tile]
+            sums = jnp.dot(gather, jnp.concatenate(rows, axis=0).astype(BF16), preferred_element_type=F32)
+            for half in range(2):
+                inside = 16 * half + (lane_iota(shape) >> 3) < width
+                part = sums[half * CHUNK : (half + 1) * CHUNK, :]
                 picked[m, half, c : c + CHUNK, :] = jnp.where(inside, part, 0.0)
 
     shape = (channels, tile)
@@ -447,7 +444,7 @@
             pltpu.VMEM((32, channels), F32),
             pltpu.VMEM((16, tile), F32),
             pltpu.VMEM((3, 2, channels, tile), F32),
-            pltpu.SemaphoreType.DMA((channels // CHUNK,)),
+            pltpu.SemaphoreType.DMA((3,)),
             pltpu.SemaphoreType.DMA((len(small),)),
         ],
         compiler_params=params,

time: 18.8 us -> 18.5 us (0.984)
  Pallas kernels: 9.41 us -> 9.02 us
    pallas_call x1, Pallas kernels: 3.5 us -> 3.2 us  [shards(): pl.pallas_call(pack_kernel, out_shape=(cells_shape, pltpu.VMEM((32, chann...]
    ppermute x4, waiting for transfers between devices: 2.05 us -> 2.26 us  [swapped(): return lax.ppermute(array, axis, pairs)]
where the time goes in v11:
time: 18.5 us; the launch traced here: 18.4 us
  Pallas kernels  9.02 us (49%)
  starting transfers between devices  6.65 us (36%)
  waiting for transfers between devices  2.64 us (14%)
    ppermute x4, starting transfers between devices, swapped(): return lax.ppermute(array, axis, pairs)  6.48 us
    pallas_call x1, Pallas kernels, shards(): pl.pallas_call(pack_kernel, out_shape=(cells_shape, pltpu.VMEM((32, chann...  3.2 us
    pallas_call x1, Pallas kernels, shards(): pl.pallas_call(functools.partial(mix_kernel, gathered), out_shape=(value_...  2.28 us
    ppermute x4, waiting for transfers between devices, swapped(): return lax.ppermute(array, axis, pairs)  2.26 us
    pallas_call x1, Pallas kernels, shards(): pl.pallas_call(conv_kernel, out_shape=(cells_shape, pltpu.VMEM((ZOUT, slo...  2.14 us
    pallas_call x1, Pallas kernels, shards(): pl.pallas_call(finish_kernel, out_shape=(shape((ZOUT, channels, slots, ti...  1.21 us
    ppermute x1, waiting for transfers between devices, shards(): lax.ppermute(own_block, 'gy', [(i, (i + 2) % 4) for i in range(4)])  0.38 us
  transfers between devices with their start and end apart: 5, of which 3 were waited for; matrix products, arithmetic and copies ran while one was open for 0% of the time, Pallas kernels for 25%

profile of v11, /device:TPU:0, one launch (start us, length us, event | category | flops | bytes accessed | tf_op | source)
XLA Modules:
  0.0 18.4 jit_solution(14187411917750464974)
XLA Ops:
  0.0 3.2 %shard_map.82 = (f32[6,1536,128]{2,1,0:T(8,128)S(1)}, f32[32,64,128]{2,1,0:T(8,128)S(1)}, bf16[80,128]{1,0:T(8,128)(2,1)S(1)}, bf16[80,128]{1,0:T(8,128)(2,1)S(1...) custom-call(bf16[6,64,24,128]{3,2,1,0:T(8,128)(2,1)} %feature.1, s32[8]{0:T(128)} %widths_in.1, f32[27,64]{1,0:T(8,128)} %taps_in.1, ...), custom_call_target="tpu_custom_call" | custom-call | tf_op jit(solution)/shard_map/pallas_call | solution.py:424
  3.2 4.0 %collective-permute-start = (bf16[80,128]{1,0:T(8,128)(2,1)S(1)}, bf16[80,128]{1,0:T(8,128)(2,1)S(1)}, u32[]{:S(2)}, u32[]{:S(2)}) collective-permute-start(bf16[80,128]{1,0:T(8,128)(2,1)S(1)} %get-tuple-element.29), channel_id=1, source_target_pairs={{1,2},{2,1},{3,0},{0,3},{5,6},{6,5},{7,4},{4,7},{9,10},{10,9},{11,... | collective-permute-start | bytes 61448 | tf_op jit(solution)/shard_map/ppermute | solution.py:409
  7.2 0.5 %collective-permute-start.1 = (bf16[80,128]{1,0:T(8,128)(2,1)S(1)}, bf16[80,128]{1,0:T(8,128)(2,1)S(1)}, u32[]{:S(2)}, u32[]{:S(2)}) collective-permute-start(bf16[80,128]{1,0:T(8,128)(2,1)S(1)} %get-tuple-element.30), channel_id=1, source_target_pairs={{0,1},{1,0},{2,3},{3,2},{4,5},{5,4},{6,7},{7,6},{8,9},{9,8},{10,11... | collective-permute-start | bytes 61448 | tf_op jit(solution)/shard_map/ppermute | solution.py:409
  7.7 0.0 copy-start
  7.7 2.1 %shard_map.83 = (f32[6,1536,128]{2,1,0:T(8,128)S(1)}, f32[2,24,40,128]{3,2,1,0:T(8,128)S(1)}, f32[2,4,64,128]{3,2,1,0:T(8,128)S(1)}, f32[3,2,32]{2,1,0:T(2,128)S(1)}) custom-call(s32[8]{0:T(128)S(4)} %get-tuple-element.23.widths, f32[32,64,128]{2,1,0:T(8,128)S(1)} %get-tuple-element.24.weights, ...), custom_call_target="tpu_custom_call", output_to_operand_aliasing={{0}: (3, {})} | custom-call | flops 1000000000 | bytes 1000000 | tf_op jit(solution)/shard_map/pallas_call | solution.py:455
  9.9 0.2 collective-permute-start.2
  10.0 0.0 collective-permute-done.second.refs_0_
  10.0 0.9 %collective-permute-done.1.first.refs_1_ = bf16[80,128]{1,0:T(8,128)(2,1)S(1)} collective-permute-done((bf16[80,128]{1,0:T(8,128)(2,1)S(1)}, bf16[80,128]{1,0:T(8,128)(2,1)S(1)}, u32[]{:S(2)}, u32[]{:S(2)}) %collective-permute-start.1) | collective-permute-done | bytes 20512 | tf_op jit(solution)/shard_map/ppermute | solution.py:409
  11.0 0.2 %shard_map.84 = (f32[2,64,128]{2,1,0:T(8,128)S(1)}, bf16[256,128]{1,0:T(8,128)(2,1)S(1)}, bf16[256,128]{1,0:T(8,128)(2,1)S(1)}) custom-call(s32[8]{0:T(128)S(4)} %get-tuple-element.23.widths, bf16[80,128]{1,0:T(8,128)(2,1)S(1)} %collective-permute-done.second.refs_0_, bf16[80,128]{1,0:T(8,128)(2,1)S(1)} %collective-permute-done.1.first.refs_1_, ...), custom_call_target="tpu_custom_call" | custom-call | tf_op jit(solution)/shard_map/pallas_call | solution.py:471
  11.2 2.0 %collective-permute-start.3 = (bf16[256,128]{1,0:T(8,128)(2,1)S(1)}, bf16[256,128]{1,0:T(8,128)(2,1)S(1)}, u32[]{:S(2)}, u32[]{:S(2)}) collective-permute-start(bf16[256,128]{1,0:T(8,128)(2,1)S(1)} %get-tuple-element.37), channel_id=1, source_target_pairs={{4,8},{8,4},{12,16},{16,12},{20,24},{24,20},{28,0},{0,28},{5,9},{9... | collective-permute-start | bytes 196616 | tf_op jit(solution)/shard_map/ppermute | solution.py:409
  13.1 0.0 collective-permute-start.4
  13.1 0.4 %collective-permute-done.2.refs_3_ = f32[3,2,32]{2,1,0:T(2,128)S(1)} collective-permute-done((f32[3,2,32]{2,1,0:T(2,128)S(1)}, f32[3,2,32]{2,1,0:T(2,128)S(1)}, u32[]{:S(2)}, u32[]{:S(2)}) %collective-permute-start.2) | collective-permute-done | bytes 800 | tf_op jit(solution)/shard_map/ppermute | solution.py:470
  13.5 0.0 copy-done
  13.5 2.3 %shard_map.85 = (f32[2,1536,128]{2,1,0:T(8,128)S(1)}, f32[2,256,128]{2,1,0:T(8,128)S(1)}, f32[2,256,128]{2,1,0:T(8,128)S(1)}, bf16[256,256]{1,0:T(8,128)(2,1)S(1)}) custom-call(s32[8]{0:T(128)S(4)} %get-tuple-element.23.widths, bf16[64,64]{1,0:T(8,128)(2,1)S(1)} %copy-done, f32[6,1536,128]{2,1,0:T(8,128)S(1)} %get-tuple-element.27.cells, ...), custom_call_target="tpu_custom_call" | custom-call | flops 1000000000 | bytes 1000000 | tf_op jit(solution)/shard_map/pallas_call | solution.py:482
  15.8 1.3 %collective-permute-done.3.far = bf16[256,128]{1,0:T(8,128)(2,1)S(1)} collective-permute-done((bf16[256,128]{1,0:T(8,128)(2,1)S(1)}, bf16[256,128]{1,0:T(8,128)(2,1)S(1)}, u32[]{:S(2)}, u32[]{:S(2)}) %collective-permute-start.3) | collective-permute-done | bytes 65568 | tf_op jit(solution)/shard_map/ppermute | solution.py:409
  17.1 0.0 collective-permute-done.4.near
  17.1 1.2 %shard_map.86 = (bf16[2,64,24,128]{3,2,1,0:T(8,128)(2,1)}, f32[2,1536,128]{2,1,0:T(8,128)S(1)}) custom-call(s32[8]{0:T(128)S(4)} %get-tuple-element.23.widths, f32[32,64,128]{2,1,0:T(8,128)S(1)} %get-tuple-element.24.weights, f32[2,256,128]{2,1,0:T(8,128)S(1)} %get-tuple-element.34.ends, ...), custom_call_target="tpu_custom_call", output_to_operand_aliasing={{1}: (7, {})} | custom-call | tf_op jit(solution)/shard_map/pallas_call | solution.py:496
Async XLA Ops:
  3.2 6.8 %collective-permute-start = (bf16[80,128]{1,0:T(8,128)(2,1)S(1)}, bf16[80,128]{1,0:T(8,128)(2,1)S(1)}, u32[]{:S(2)}, u32[]{:S(2)}) collective-permute-start(bf16[80,128]{1,0:T(8,128)(2,1)S(1)} %get-tuple-element.29), channel_id=1, source_target_pairs={{1,2},{2,1},{3,0},{0,3},{5,6},{6,5},{7,4},{4,7},{9,10},{10,9},{11,... | collective-permute-start | bytes 61448 | tf_op jit(solution)/shard_map/ppermute | solution.py:409
  7.2 3.8 %collective-permute-start.1 = (bf16[80,128]{1,0:T(8,128)(2,1)S(1)}, bf16[80,128]{1,0:T(8,128)(2,1)S(1)}, u32[]{:S(2)}, u32[]{:S(2)}) collective-permute-start(bf16[80,128]{1,0:T(8,128)(2,1)S(1)} %get-tuple-element.30), channel_id=1, source_target_pairs={{0,1},{1,0},{2,3},{3,2},{4,5},{5,4},{6,7},{7,6},{8,9},{9,8},{10,11... | collective-permute-start | bytes 61448 | tf_op jit(solution)/shard_map/ppermute | solution.py:409
  7.7 5.8 %copy-start = (bf16[64,64]{1,0:T(8,128)(2,1)S(1)}, bf16[64,64]{1,0:T(8,128)(2,1)}, u32[]{:S(2)}) copy-start(bf16[64,64]{1,0:T(8,128)(2,1)} %mix.1) | copy-start | bytes 24580
  9.9 3.7 %collective-permute-start.2 = (f32[3,2,32]{2,1,0:T(2,128)S(1)}, f32[3,2,32]{2,1,0:T(2,128)S(1)}, u32[]{:S(2)}, u32[]{:S(2)}) collective-permute-start(f32[3,2,32]{2,1,0:T(2,128)S(1)} %get-tuple-element.33.refs_2_), channel_id=1, source_target_pairs={{0,2},{1,3},{2,0},{3,1},{4,6},{5,7},{6,4},{7,5},{8,10},{9,11},{10,... | collective-permute-start | bytes 2312 | tf_op jit(solution)/shard_map/ppermute | solution.py:470
  11.2 6.0 %collective-permute-start.3 = (bf16[256,128]{1,0:T(8,128)(2,1)S(1)}, bf16[256,128]{1,0:T(8,128)(2,1)S(1)}, u32[]{:S(2)}, u32[]{:S(2)}) collective-permute-start(bf16[256,128]{1,0:T(8,128)(2,1)S(1)} %get-tuple-element.37), channel_id=1, source_target_pairs={{4,8},{8,4},{12,16},{16,12},{20,24},{24,20},{28,0},{0,28},{5,9},{9... | collective-permute-start | bytes 196616 | tf_op jit(solution)/shard_map/ppermute | solution.py:409
  13.1 4.0 %collective-permute-start.4 = (bf16[256,128]{1,0:T(8,128)(2,1)S(1)}, bf16[256,128]{1,0:T(8,128)(2,1)S(1)}, u32[]{:S(2)}, u32[]{:S(2)}) collective-permute-start(bf16[256,128]{1,0:T(8,128)(2,1)S(1)} %get-tuple-element.38), channel_id=1, source_target_pairs={{0,4},{4,0},{8,12},{12,8},{16,20},{20,16},{24,28},{28,24},{1,5},{5... | collective-permute-start | bytes 196616 | tf_op jit(solution)/shard_map/ppermute | solution.py:409

commit v12 on v11

--- a/solution.py
+++ b/solution.py
@@ -37,11 +37,10 @@
 
 def pack_kernel(
     feature, widths_in, taps_in, dw_bias_in, pw_bias_in, lift_in, coarse_in,
-    cells, weights, first, second, own_block, widths,
-    planes, widths_here, taps, dw_bias, pw_bias, lift, coarse, stacked, tail, picked, sems, small_sems,
+    cells, first, second, stacked, own_block, widths,
+    planes, widths_here, taps, dw_bias, pw_bias, lift, coarse, tail, picked, sems, small_sems,
 ):
     count, channels, slots, tile = feature.shape
-    chunks = range(0, channels, CHUNK)
 
     def copy_of(m):
         at = pl.ds(ZOUT * m, ZOUT)
@@ -64,84 +63,88 @@
         copy.start()
     for m in range(3):
         copy_of(m).start()
-    for copy in small:
-        copy.wait()
-    for d in range(widths.shape[0]):
-        widths[d] = widths_here[d]
-    width = widths_here[lax.axis_index("gx")]
-    stacked[0:DW_BIAS, :] = taps[...]
-    stacked[DW_BIAS : DW_BIAS + 1, :] = dw_bias[...]
-    stacked[PW_BIAS : PW_BIAS + 1, :] = pw_bias[...]
-    stacked[LIFT : LIFT + 3, :] = lift[...]
-
-    own_block[...] = coarse[...]
-    parts, own_rows, ncy = coarse.shape
-    tail[...] = jnp.zeros_like(tail)
-    if 3 * ncy <= tile:
-        for k in range(parts):
-            rest = coarse[k]
-            for p in range(3):
-                term = rest.astype(BF16).astype(F32)
-                rest = rest - term
-                tail[k * own_rows : (k + 1) * own_rows, p * ncy : (p + 1) * ncy] = term
-    for message in (first, second):
-        message[channels:, :] = tail[...].astype(BF16)
-
-    row, along = row_iota((taps.shape[0], tile)), lane_iota((taps.shape[0], tile))
-    by_side = jnp.where((along & 2) != 0, 2, 0)
-    terms, rest = [], taps[...]
-    for _ in range(3):
-        terms.append(rest.astype(BF16))
-        rest = rest - terms[-1].astype(F32)
-    chosen = jnp.concatenate(
-        [(row == tap_of(m, dx, -1) + by_side).astype(BF16) for m in range(3) for dx in (-1, 0, 1)], axis=1
-    )
-    scale = sum(lax.dot_general(term, chosen, (((0,), (0,)), ((), ())), preferred_element_type=F32) for term in terms)
-    turned = jnp.transpose(stacked[...])
-    for t in range(stacked.shape[0]):
-        weights[t] = jnp.broadcast_to(turned[:, t : t + 1], (channels, tile))
+    def weights_by_lane():
+        for copy in small:
+            copy.wait()
+        for d in range(widths.shape[0]):
+            widths[d] = widths_here[d]
+        stacked[0:DW_BIAS, :] = taps[...]
+        stacked[DW_BIAS : DW_BIAS + 1, :] = dw_bias[...]
+        stacked[PW_BIAS : PW_BIAS + 1, :] = pw_bias[...]
+        stacked[LIFT : LIFT + 3, :] = lift[...]
+
+        own_block[...] = coarse[...]
+        parts, own_rows, ncy = coarse.shape
+        tail[...] = jnp.zeros_like(tail)
+        if 3 * ncy <= tile:
+            for k in range(parts):
+                rest = coarse[k]
+                for p in range(3):
+                    term = rest.astype(BF16).astype(F32)
+                    rest = rest - term
+                    tail[k * own_rows : (k + 1) * own_rows, p * ncy : (p + 1) * ncy] = term
+        for message in (first, second):
+            message[channels:, :] = tail[...].astype(BF16)
+
+        row, along = row_iota((taps.shape[0], tile)), lane_iota((taps.shape[0], tile))
+        by_side = jnp.where((along & 2) != 0, 2, 0)
+        chosen = jnp.concatenate(
+            [(row == tap_of(m, dx, -1) + by_side).astype(BF16) for m in range(3) for dx in (-1, 0, 1)], axis=1
+        )
+        total, rest = None, taps[...]
+        for _ in range(3):
+            term = rest.astype(BF16)
+            rest = rest - term.astype(F32)
+            part = lax.dot_general(term, chosen, (((0,), (0,)), ((), ())), preferred_element_type=F32)
+            total = part if total is None else total + part
+        return total
 
     lane, row = lane_iota((slots, tile)), row_iota((slots, tile))
     mine = (lane >> 3) == (row & 15)
     in_even, in_odd = mine & ((lane & 4) == 0), mine & ((lane & 4) != 0)
-    shape = (2 * CHUNK, CHUNK * slots)
-    row, column = row_iota(shape), lane_iota(shape)
-    begin = (row & (CHUNK - 1)) * slots
-    low = jnp.where(row < CHUNK, begin, begin + 16)
-    high = jnp.where(row < CHUNK, begin + 16, begin + slots)
-    gather = ((column >= low) & (column < high)).astype(BF16)
-    shape = (CHUNK, tile)
+    sublane = row_iota((ROWS, tile))
+
+    def placed(m, k):
+        both = []
+        for z in range(ZOUT):
+            plane = planes[ZOUT * m + z, k].astype(F32)
+            cells[ZOUT * m + z, k * slots : (k + 1) * slots, :] = plane
+            both.append(
+                jnp.concatenate(
+                    [
+                        pltpu.roll(plane[x : x + ROWS], (2 + 4 * z + 8 * x) % tile, 1, stride=8, stride_axis=0)
+                        for x in range(0, slots, ROWS)
+                    ],
+                    axis=0,
+                )
+            )
+        rows = jnp.where(in_even, both[0], jnp.where(in_odd, both[1], 0.0))
+        return rows[0:ROWS] + rows[ROWS : 2 * ROWS], rows[2 * ROWS :]
+
+    def summed(m, k, step):
+        if step == 0:
+            return placed(m, k)
+        one, two = summed(m, k, step // 2), summed(m, k + step, step // 2)
+        turn = (sublane & step) != 0
+        return tuple(
+            jnp.where(turn, b, a) + pltpu.roll(jnp.where(turn, a, b), step, 0) for a, b in zip(one, two)
+        )
+
     for m in range(3):
         copy_of(m).wait()
-        for c in chunks:
-            rows = []
-            for k in range(c, c + CHUNK):
-                both = []
-                for z in range(ZOUT):
-                    plane = planes[ZOUT * m + z, k].astype(F32)
-                    cells[ZOUT * m + z, k * slots : (k + 1) * slots, :] = plane
-                    both.append(
-                        jnp.concatenate(
-                            [
-                                pltpu.roll(plane[x : x + ROWS], (2 + 4 * z + 8 * x) % tile, 1, stride=8, stride_axis=0)
-                                for x in range(0, slots, ROWS)
-                            ],
-                            axis=0,
-                        )
-                    )
-                rows.append(jnp.where(in_even, both[0], jnp.where(in_odd, both[1], 0.0)))
-            sums = jnp.dot(gather, jnp.concatenate(rows, axis=0).astype(BF16), preferred_element_type=F32)
-            for half in range(2):
-                inside = 16 * half + (lane_iota(shape) >> 3) < width
-                part = sums[half * CHUNK : (half + 1) * CHUNK, :]
-                picked[m, half, c : c + CHUNK, :] = jnp.where(inside, part, 0.0)
+        for c in range(0, channels, ROWS):
+            for half, part in enumerate(summed(m, c, ROWS // 2)):
+                picked[m, half, c : c + ROWS, :] = part
+        if m == 0:
+            scale = weights_by_lane()
+    width = widths_here[lax.axis_index("gx")]
 
     shape = (channels, tile)
     lane = lane_iota(shape)
     on_left = (lane & 2) != 0
     packed = [None, None]
     for m in range(3):
-        low, high = picked[m, 0], picked[m, 1]
+        low, high = (jnp.where(16 * half + (lane >> 3) < width, picked[m, half], 0.0) for half in range(2))
         moved = {
             -1: tuple(
                 pltpu.roll(jnp.where(lane < tile - 16, one, two), 16, 1) for one, two in ((low, high), (high, low))
@@ -195,11 +198,14 @@
                         depth[z, out, to, :] = shifted_sum(*(sums.pop((out, dy)) for dy in (-1, 0, 1)))
 
 
-def conv_kernel(widths, weights, coarse, cells_in, cells, depth, rims, own_block):
+def conv_kernel(widths, stacked, coarse, cells_in, cells, weights, depth, rims, own_block):
     width = widths[lax.axis_index("gx")]
     channels, tile = weights.shape[1:]
     slots = cells.shape[1] // channels
     own_block[...] = coarse[...]
+    turned = jnp.transpose(stacked[...])
+    for t in range(stacked.shape[0]):
+        weights[t] = jnp.broadcast_to(turned[:, t : t + 1], (channels, tile))
     for r in range(2):
 
         @pl.when(width + r < slots)
@@ -421,13 +427,13 @@
         lift_weight.T,
         coarse,
     )
-    cells, weights, first, second, block, slab_widths = pl.pallas_call(
+    cells, first, second, stacked, block, slab_widths = pl.pallas_call(
         pack_kernel,
         out_shape=(
             cells_shape,
-            pltpu.VMEM((32, channels, tile), F32),
             strip,
             strip,
+            pltpu.VMEM((32, channels), F32),
             pltpu.VMEM(coarse.shape, F32),
             pltpu.SMEM(widths.shape, jnp.int32),
         ),
@@ -441,7 +447,6 @@
             pltpu.VMEM((1, channels), F32),
             pltpu.VMEM((parts, channels), F32),
             pltpu.VMEM(coarse.shape, F32),
-            pltpu.VMEM((32, channels), F32),
             pltpu.VMEM((16, tile), F32),
             pltpu.VMEM((3, 2, channels, tile), F32),
             pltpu.SemaphoreType.DMA((3,)),
@@ -452,20 +457,21 @@
     second = swapped(second, "gy", 1)
     first = swapped(first, "gy", 0)
     early = SPLIT * ROWS
-    cells, depth, rims, own_block = pl.pallas_call(
+    cells, weights, depth, rims, own_block = pl.pallas_call(
         conv_kernel,
         out_shape=(
             cells_shape,
+            pltpu.VMEM((32, channels, tile), F32),
             pltpu.VMEM((ZOUT, slots, early, tile), F32),
             pltpu.VMEM((ZOUT, 4, channels, tile), F32),
             pltpu.VMEM(coarse.shape, F32),
         ),
         in_specs=[smem] + [vmem] * 3,
-        out_specs=(vmem,) * 4,
+        out_specs=(vmem,) * 5,
         input_output_aliases={3: 0},
         compiler_params=params,
         cost_estimate=pl.CostEstimate(flops=10**9, bytes_accessed=10**6, transcendentals=0),
-    )(slab_widths, weights, block, cells)
+    )(slab_widths, stacked, block, cells)
     if not gathered:
         opposite = lax.ppermute(own_block, "gy", [(i, (i + 2) % 4) for i in range(4)])
     edge, far, near = pl.pallas_call(

time: 18.5 us -> 17.9 us (0.968)
  waiting for transfers between devices: 2.64 us -> 1.72 us
  starting transfers between devices: 6.65 us -> 6.98 us
    ppermute x4, waiting for transfers between devices: 2.26 us -> 1.1 us  [swapped(): return lax.ppermute(array, axis, pairs)]
    ppermute x4, starting transfers between devices: 6.48 us -> 6.81 us  [swapped(): return lax.ppermute(array, axis, pairs)]
    ppermute x1, waiting for transfers between devices: 0.38 us -> 0.61 us  [shards(): lax.ppermute(own_block, 'gy', [(i, (i + 2) % 4) for i in range(4)])]
  transfers between devices with their start and end apart: 5 -> 5, of which waited for: 3 -> 3; matrix products, arithmetic and copies ran while one was open for 0% -> 0% of each run, Pallas kernels for 25% -> 29%
where the time goes in v12:
time: 17.9 us; the launch traced here: 17.8 us
  Pallas kernels  9.06 us (51%)
  starting transfers between devices  6.98 us (39%)
  waiting for transfers between devices  1.72 us (10%)
    ppermute x4, starting transfers between devices, swapped(): return lax.ppermute(array, axis, pairs)  6.81 us
    pallas_call x1, Pallas kernels, shards(): pl.pallas_call(conv_kernel, out_shape=(cells_shape, pltpu.VMEM((32, chann...  2.7 us
    pallas_call x1, Pallas kernels, shards(): pl.pallas_call(pack_kernel, out_shape=(cells_shape, strip, strip, pltpu.V...  2.65 us
    pallas_call x1, Pallas kernels, shards(): pl.pallas_call(functools.partial(mix_kernel, gathered), out_shape=(value_...  2.3 us
    pallas_call x1, Pallas kernels, shards(): pl.pallas_call(finish_kernel, out_shape=(shape((ZOUT, channels, slots, ti...  1.21 us
    ppermute x4, waiting for transfers between devices, swapped(): return lax.ppermute(array, axis, pairs)  1.1 us
    ppermute x1, waiting for transfers between devices, shards(): lax.ppermute(own_block, 'gy', [(i, (i + 2) % 4) for i in range(4)])  0.61 us
  transfers between devices with their start and end apart: 5, of which 3 were waited for; matrix products, arithmetic and copies ran while one was open for 0% of the time, Pallas kernels for 29%

profile of v12, /device:TPU:0, one launch (start us, length us, event | category | flops | bytes accessed | tf_op | source)
XLA Modules:
  0.0 17.8 jit_solution(9404699958171549143)
XLA Ops:
  0.0 2.7 %shard_map.82 = (f32[6,1536,128]{2,1,0:T(8,128)S(1)}, bf16[80,128]{1,0:T(8,128)(2,1)S(1)}, bf16[80,128]{1,0:T(8,128)(2,1)S(1)}, f32[32,64]{1,0:T(8,128)S(1)}, f32[3,2,32]{2,1,0:T(2,128)S(1)}, /*index=5*/s32[8]{0:T(128)S(4)}) custom-call(bf16[6,64,24,128]{3,2,1,0:T(8,128)(2,1)} %feature.1, s32[8]{0:T(128)} %widths_in.1, f32[27,64]{1,0:T(8,128)} %taps_in.1, ...), custom_call_target="tpu_custom_call" | custom-call | tf_op jit(solution)/shard_map/pallas_call | solution.py:430
  2.7 4.0 %collective-permute-start = (bf16[80,128]{1,0:T(8,128)(2,1)S(1)}, bf16[80,128]{1,0:T(8,128)(2,1)S(1)}, u32[]{:S(2)}, u32[]{:S(2)}) collective-permute-start(bf16[80,128]{1,0:T(8,128)(2,1)S(1)} %get-tuple-element.31), channel_id=1, source_target_pairs={{1,2},{2,1},{3,0},{0,3},{5,6},{6,5},{7,4},{4,7},{9,10},{10,9},{11,... | collective-permute-start | bytes 61448 | tf_op jit(solution)/shard_map/ppermute | solution.py:415
  6.6 0.5 %collective-permute-start.1 = (bf16[80,128]{1,0:T(8,128)(2,1)S(1)}, bf16[80,128]{1,0:T(8,128)(2,1)S(1)}, u32[]{:S(2)}, u32[]{:S(2)}) collective-permute-start(bf16[80,128]{1,0:T(8,128)(2,1)S(1)} %get-tuple-element.32), channel_id=1, source_target_pairs={{0,1},{1,0},{2,3},{3,2},{4,5},{5,4},{6,7},{7,6},{8,9},{9,8},{10,11... | collective-permute-start | bytes 61448 | tf_op jit(solution)/shard_map/ppermute | solution.py:415
  7.2 0.0 copy-start
  7.2 2.7 %shard_map.83 = (f32[6,1536,128]{2,1,0:T(8,128)S(1)}, f32[32,64,128]{2,1,0:T(8,128)S(1)}, f32[2,24,40,128]{3,2,1,0:T(8,128)S(1)}, f32[2,4,64,128]{3,2,1,0:T(8,128)S(1)}, f32[3,2,32]{2,1,0:T(2,128)S(1)}) custom-call(s32[8]{0:T(128)S(4)} %get-tuple-element.24.widths, f32[32,64]{1,0:T(8,128)S(1)} %get-tuple-element.25.stacked, ...), custom_call_target="tpu_custom_call", output_to_operand_aliasing={{0}: (3, {})} | custom-call | flops 1000000000 | bytes 1000000 | tf_op jit(solution)/shard_map/pallas_call | solution.py:460
  9.9 0.2 collective-permute-start.2
  10.0 0.0 collective-permute-done.second.refs_0_
  10.0 0.4 %collective-permute-done.1.first.refs_1_ = bf16[80,128]{1,0:T(8,128)(2,1)S(1)} collective-permute-done((bf16[80,128]{1,0:T(8,128)(2,1)S(1)}, bf16[80,128]{1,0:T(8,128)(2,1)S(1)}, u32[]{:S(2)}, u32[]{:S(2)}) %collective-permute-start.1) | collective-permute-done | bytes 20512 | tf_op jit(solution)/shard_map/ppermute | solution.py:415
  10.4 0.2 %shard_map.84 = (f32[2,64,128]{2,1,0:T(8,128)S(1)}, bf16[256,128]{1,0:T(8,128)(2,1)S(1)}, bf16[256,128]{1,0:T(8,128)(2,1)S(1)}) custom-call(s32[8]{0:T(128)S(4)} %get-tuple-element.24.widths, bf16[80,128]{1,0:T(8,128)(2,1)S(1)} %collective-permute-done.second.refs_0_, bf16[80,128]{1,0:T(8,128)(2,1)S(1)} %collective-permute-done.1.first.refs_1_, ...), custom_call_target="tpu_custom_call" | custom-call | tf_op jit(solution)/shard_map/pallas_call | solution.py:477
  10.6 2.3 %collective-permute-start.3 = (bf16[256,128]{1,0:T(8,128)(2,1)S(1)}, bf16[256,128]{1,0:T(8,128)(2,1)S(1)}, u32[]{:S(2)}, u32[]{:S(2)}) collective-permute-start(bf16[256,128]{1,0:T(8,128)(2,1)S(1)} %get-tuple-element.39), channel_id=1, source_target_pairs={{4,8},{8,4},{12,16},{16,12},{20,24},{24,20},{28,0},{0,28},{5,9},{9... | collective-permute-start | bytes 196616 | tf_op jit(solution)/shard_map/ppermute | solution.py:415
  12.9 0.0 collective-permute-start.4
  12.9 0.6 %collective-permute-done.2.refs_3_ = f32[3,2,32]{2,1,0:T(2,128)S(1)} collective-permute-done((f32[3,2,32]{2,1,0:T(2,128)S(1)}, f32[3,2,32]{2,1,0:T(2,128)S(1)}, u32[]{:S(2)}, u32[]{:S(2)}) %collective-permute-start.2) | collective-permute-done | bytes 800 | tf_op jit(solution)/shard_map/ppermute | solution.py:476
  13.5 0.0 copy-done
  13.5 2.3 %shard_map.85 = (f32[2,1536,128]{2,1,0:T(8,128)S(1)}, f32[2,256,128]{2,1,0:T(8,128)S(1)}, f32[2,256,128]{2,1,0:T(8,128)S(1)}, bf16[256,256]{1,0:T(8,128)(2,1)S(1)}) custom-call(s32[8]{0:T(128)S(4)} %get-tuple-element.24.widths, bf16[64,64]{1,0:T(8,128)(2,1)S(1)} %copy-done, f32[6,1536,128]{2,1,0:T(8,128)S(1)} %get-tuple-element.29.cells, ...), custom_call_target="tpu_custom_call" | custom-call | flops 1000000000 | bytes 1000000 | tf_op jit(solution)/shard_map/pallas_call | solution.py:488
  15.8 0.7 %collective-permute-done.3.far = bf16[256,128]{1,0:T(8,128)(2,1)S(1)} collective-permute-done((bf16[256,128]{1,0:T(8,128)(2,1)S(1)}, bf16[256,128]{1,0:T(8,128)(2,1)S(1)}, u32[]{:S(2)}, u32[]{:S(2)}) %collective-permute-start.3) | collective-permute-done | bytes 65568 | tf_op jit(solution)/shard_map/ppermute | solution.py:415
  16.6 0.0 collective-permute-done.4.near
  16.6 1.2 %shard_map.86 = (bf16[2,64,24,128]{3,2,1,0:T(8,128)(2,1)}, f32[2,1536,128]{2,1,0:T(8,128)S(1)}) custom-call(s32[8]{0:T(128)S(4)} %get-tuple-element.24.widths, f32[32,64,128]{2,1,0:T(8,128)S(1)} %get-tuple-element.28.weights, f32[2,256,128]{2,1,0:T(8,128)S(1)} %get-tuple-element.36.ends, ...), custom_call_target="tpu_custom_call", output_to_operand_aliasing={{1}: (7, {})} | custom-call | tf_op jit(solution)/shard_map/pallas_call | solution.py:502
Async XLA Ops:
  2.7 7.4 %collective-permute-start = (bf16[80,128]{1,0:T(8,128)(2,1)S(1)}, bf16[80,128]{1,0:T(8,128)(2,1)S(1)}, u32[]{:S(2)}, u32[]{:S(2)}) collective-permute-start(bf16[80,128]{1,0:T(8,128)(2,1)S(1)} %get-tuple-element.31), channel_id=1, source_target_pairs={{1,2},{2,1},{3,0},{0,3},{5,6},{6,5},{7,4},{4,7},{9,10},{10,9},{11,... | collective-permute-start | bytes 61448 | tf_op jit(solution)/shard_map/ppermute | solution.py:415
  6.6 3.8 %collective-permute-start.1 = (bf16[80,128]{1,0:T(8,128)(2,1)S(1)}, bf16[80,128]{1,0:T(8,128)(2,1)S(1)}, u32[]{:S(2)}, u32[]{:S(2)}) collective-permute-start(bf16[80,128]{1,0:T(8,128)(2,1)S(1)} %get-tuple-element.32), channel_id=1, source_target_pairs={{0,1},{1,0},{2,3},{3,2},{4,5},{5,4},{6,7},{7,6},{8,9},{9,8},{10,11... | collective-permute-start | bytes 61448 | tf_op jit(solution)/shard_map/ppermute | solution.py:415
  7.2 6.4 %copy-start = (bf16[64,64]{1,0:T(8,128)(2,1)S(1)}, bf16[64,64]{1,0:T(8,128)(2,1)}, u32[]{:S(2)}) copy-start(bf16[64,64]{1,0:T(8,128)(2,1)} %mix.1) | copy-start | bytes 24580
  9.9 3.7 %collective-permute-start.2 = (f32[3,2,32]{2,1,0:T(2,128)S(1)}, f32[3,2,32]{2,1,0:T(2,128)S(1)}, u32[]{:S(2)}, u32[]{:S(2)}) collective-permute-start(f32[3,2,32]{2,1,0:T(2,128)S(1)} %get-tuple-element.35.refs_2_), channel_id=1, source_target_pairs={{0,2},{1,3},{2,0},{3,1},{4,6},{5,7},{6,4},{7,5},{8,10},{9,11},{10,... | collective-permute-start | bytes 2312 | tf_op jit(solution)/shard_map/ppermute | solution.py:476
  10.6 6.0 %collective-permute-start.3 = (bf16[256,128]{1,0:T(8,128)(2,1)S(1)}, bf16[256,128]{1,0:T(8,128)(2,1)S(1)}, u32[]{:S(2)}, u32[]{:S(2)}) collective-permute-start(bf16[256,128]{1,0:T(8,128)(2,1)S(1)} %get-tuple-element.39), channel_id=1, source_target_pairs={{4,8},{8,4},{12,16},{16,12},{20,24},{24,20},{28,0},{0,28},{5,9},{9... | collective-permute-start | bytes 196616 | tf_op jit(solution)/shard_map/ppermute | solution.py:415
  12.9 3.7 %collective-permute-start.4 = (bf16[256,128]{1,0:T(8,128)(2,1)S(1)}, bf16[256,128]{1,0:T(8,128)(2,1)S(1)}, u32[]{:S(2)}, u32[]{:S(2)}) collective-permute-start(bf16[256,128]{1,0:T(8,128)(2,1)S(1)} %get-tuple-element.40), channel_id=1, source_target_pairs={{0,4},{4,0},{8,12},{12,8},{16,20},{20,16},{24,28},{28,24},{1,5},{5... | collective-permute-start | bytes 196616 | tf_op jit(solution)/shard_map/ppermute | solution.py:415

commit v13 on v12

--- a/solution.py
+++ b/solution.py
@@ -11,7 +11,7 @@
 ZOUT = 2
 CF = 16
 ROWS = 8
-SPLIT = 5
+SPLIT = 4
 CHUNK = 16
 DW_BIAS, PW_BIAS, LIFT = 27, 28, 29
 F32 = jnp.float32
@@ -285,12 +285,20 @@
     return jnp.maximum(mixed, 0.2 * mixed)
 
 
-def mix_kernel(gathered, widths, mix, cells, weights, depth, edge, *refs):
+def rest_kernel(edge, cells, weights, rest):
+    def convolve(b, carry):
+        convolve_block(cells, weights, rest, b, SPLIT)
+        return carry
+
+    lax.fori_loop(SPLIT, weights.shape[1] // ROWS, convolve, 0)
+
+
+def mix_kernel(gathered, widths, mix, cells, weights, depth, rest, edge, *refs):
     if gathered:
-        coarse, value, ends, bases, mixer, rest, lifted, across = refs
+        coarse, value, ends, bases, lifted, across = refs
         parts, ncx, ncy = coarse.shape
     else:
-        second, first, own_block, opposite, value, ends, bases, mixer, rest, lifted, across, blocks = refs
+        second, first, own_block, opposite, value, ends, bases, lifted, across, blocks = refs
         parts, own_rows, ncy = own_block.shape
         ncx = 4 * own_rows
     width = widths[lax.axis_index("gx")]
@@ -299,12 +307,6 @@
     phase = lax.rem(start, CF)
     channels, tile = weights.shape[1:]
     slots = cells.shape[1] // channels
-
-    def convolve(b, carry):
-        convolve_block(cells, weights, rest, b, SPLIT)
-        return carry
-
-    lax.fori_loop(SPLIT, channels // ROWS, convolve, 0)
 
     if not gathered:
         even = is_even("gy")
@@ -345,14 +347,14 @@
         ((row >= i * channels) & (row < (i + 1) * channels) & (column >= i * channels) & (column < (i + 1) * channels)).astype(F32)
         for i in range(group)
     )
-    mixer[...] = jnp.where(same > 0, wide.astype(F32), 0.0).astype(BF16)
+    mixer = jnp.where(same > 0, wide.astype(F32), 0.0).astype(BF16)
 
     for x in range(0, slots, group):
         depths = [
             jnp.concatenate([depth_row(weights, (depth, rest), edge, z, x + i) for i in range(group)], axis=0).astype(BF16)
             for z in range(ZOUT)
         ]
-        mixed = jnp.dot(mixer[...], jnp.concatenate(depths, axis=1), preferred_element_type=F32)
+        mixed = jnp.dot(mixer, jnp.concatenate(depths, axis=1), preferred_element_type=F32)
         for i in range(group):
             for z in range(ZOUT):
                 part = mixed[i * channels : (i + 1) * channels, z * tile : (z + 1) * tile]
@@ -360,25 +362,30 @@
                 value[z, pl.ds(x + i, channels, stride=slots), :] = jnp.where(x + i < width, part, 0.0)
     for z in range(ZOUT):
         for i, x in enumerate((0, 1, width - 2, width - 1)):
-            ends[z, i * channels : (i + 1) * channels, :] = depth_row(weights, (depth, rest), edge, z, x)
-            bases[z, i * channels : (i + 1) * channels, :] = base_row(cells, lifted, phase, z, x)
-
-
-def finish_kernel(widths, weights, ends, bases, mixer, far, near, value_in, out, value, block, sems):
+            ends[z, i] = depth_row(weights, (depth, rest), edge, z, x)
+            bases[z, i] = base_row(cells, lifted, phase, z, x)
+
+
+def finish_kernel(widths, mix, weights, ends, bases, far, near, value_in, out, value, block, sems):
     width = widths[lax.axis_index("gx")]
-    channels = weights.shape[1]
+    channels, tile = weights.shape[1:]
     slots = block.shape[2]
     even = is_even("gx")
-    half = 2 * channels
+    mixed = []
+    for z in range(ZOUT):
+        sums = []
+        for i in range(4):
+            at = slice((2 * z + i % 2) * channels, (2 * z + i % 2 + 1) * channels)
+            one, two = far[at, :].astype(F32), near[at, :].astype(F32)
+            arrived = jnp.where(even, one, two) if i < 2 else jnp.where(even, two, one)
+            sums.append((ends[z, i] + arrived).astype(BF16))
+        mixed.append(jnp.dot(mix[...], jnp.concatenate(sums, axis=1), preferred_element_type=F32))
     copies = []
     for z in range(ZOUT):
-        at = slice(z * half, (z + 1) * half)
-        one, two = far[at, :].astype(F32), near[at, :].astype(F32)
-        arrived = jnp.concatenate([jnp.where(even, one, two), jnp.where(even, two, one)], axis=0)
-        mixed = jnp.dot(mixer[...], (ends[z] + arrived).astype(BF16), preferred_element_type=F32)
         for i, x in enumerate((0, 1, width - 2, width - 1)):
-            at = slice(i * channels, (i + 1) * channels)
-            value[z, pl.ds(x, channels, stride=slots), :] = active(weights, mixed[at, :]) + bases[z, at, :]
+            value[z, pl.ds(x, channels, stride=slots), :] = (
+                active(weights, mixed[z][:, i * tile : (i + 1) * tile]) + bases[z, i]
+            )
         for part in range(channels // CHUNK):
             for o in range(part * CHUNK, (part + 1) * CHUNK):
                 block[z, o] = value[z, o * slots : (o + 1) * slots, :].astype(BF16)
@@ -484,21 +491,25 @@
     far = swapped(far, "gx", 1)
     near = swapped(near, "gx", 0)
     blocks = (every,) if gathered else (second, first, own_block, opposite)
-    ends_shape = pltpu.VMEM((ZOUT, 4 * channels, tile), F32)
-    value, ends, bases, mixer = pl.pallas_call(
+    rest = pl.pallas_call(
+        rest_kernel,
+        out_shape=pltpu.VMEM((ZOUT, slots, channels - early, tile), F32),
+        in_specs=[vmem] * 3,
+        out_specs=vmem,
+        compiler_params=params,
+        cost_estimate=pl.CostEstimate(flops=10**9, bytes_accessed=10**6, transcendentals=0),
+    )(edge, cells, weights)
+    ends_shape = pltpu.VMEM((ZOUT, 4, channels, tile), F32)
+    value, ends, bases = pl.pallas_call(
         functools.partial(mix_kernel, gathered),
-        out_shape=(value_shape, ends_shape, ends_shape, pltpu.VMEM((4 * channels, 4 * channels), BF16)),
-        in_specs=[smem] + [vmem] * (5 + len(blocks)),
-        out_specs=(vmem,) * 4,
-        scratch_shapes=[
-            pltpu.VMEM((ZOUT, slots, channels - early, tile), F32),
-            pltpu.VMEM((3, channels, tile), F32),
-            pltpu.VMEM((parts, ncx, tile), F32),
-        ]
+        out_shape=(value_shape, ends_shape, ends_shape),
+        in_specs=[smem] + [vmem] * (6 + len(blocks)),
+        out_specs=(vmem,) * 3,
+        scratch_shapes=[pltpu.VMEM((3, channels, tile), F32), pltpu.VMEM((parts, ncx, tile), F32)]
         + ([] if gathered else [pltpu.VMEM((parts, ncx, ncy), F32)]),
         compiler_params=params,
         cost_estimate=pl.CostEstimate(flops=10**9, bytes_accessed=10**6, transcendentals=0),
-    )(slab_widths, pw_weight, cells, weights, depth, edge, *blocks)
+    )(slab_widths, pw_weight, cells, weights, depth, rest, edge, *blocks)
     out, _ = pl.pallas_call(
         finish_kernel,
         out_shape=(shape((ZOUT, channels, slots, tile), BF16), value_shape),
@@ -510,7 +521,7 @@
         ],
         input_output_aliases={7: 1},
         compiler_params=params,
-    )(slab_widths, weights, ends, bases, mixer, far, near, value)
+    )(slab_widths, pw_weight, weights, ends, bases, far, near, value)
     return out
 
 

time: 17.9 us -> 17.9 us (level)
  starting transfers between devices: 6.98 us -> 6.65 us
  waiting for transfers between devices: 1.72 us -> 2.05 us
    pallas_call x0 -> x1, Pallas kernels: none -> 1.49 us  [shards(): pl.pallas_call(rest_kernel, out_shape=pltpu.VMEM((ZOUT, slots, channels -...]
    pallas_call x1, Pallas kernels: 2.3 us -> 1.15 us  [shards(): pl.pallas_call(functools.partial(mix_kernel, gathered), out_shape=(value_...]
    ppermute x4, waiting for transfers between devices: 1.1 us -> 2.05 us  [swapped(): return lax.ppermute(array, axis, pairs)]
    ppermute x1, waiting for transfers between devices: 0.61 us -> 0.01 us  [shards(): lax.ppermute(own_block, 'gy', [(i, (i + 2) % 4) for i in range(4)])]
    pallas_call x1, Pallas kernels: 2.7 us -> 2.34 us  [shards(): pl.pallas_call(conv_kernel, out_shape=(cells_shape, pltpu.VMEM((32, chann...]
    ppermute x4, starting transfers between devices: 6.81 us -> 6.48 us  [swapped(): return lax.ppermute(array, axis, pairs)]
  transfers between devices with their start and end apart: 5 -> 5, of which waited for: 3 -> 2; matrix products, arithmetic and copies ran while one was open for 0% -> 0% of each run, Pallas kernels for 29% -> 29%
where the time goes in v13:
time: 17.9 us; the launch traced here: 17.7 us
  Pallas kernels  8.97 us (50%)
  starting transfers between devices  6.65 us (37%)
  waiting for transfers between devices  2.05 us (11%)
    ppermute x4, starting transfers between devices, swapped(): return lax.ppermute(array, axis, pairs)  6.48 us
    pallas_call x1, Pallas kernels, shards(): pl.pallas_call(pack_kernel, out_shape=(cells_shape, strip, strip, pltpu.V...  2.65 us
    pallas_call x1, Pallas kernels, shards(): pl.pallas_call(conv_kernel, out_shape=(cells_shape, pltpu.VMEM((32, chann...  2.34 us
    ppermute x4, waiting for transfers between devices, swapped(): return lax.ppermute(array, axis, pairs)  2.05 us
    pallas_call x1, Pallas kernels, shards(): pl.pallas_call(rest_kernel, out_shape=pltpu.VMEM((ZOUT, slots, channels -...  1.49 us
    pallas_call x1, Pallas kernels, shards(): pl.pallas_call(functools.partial(mix_kernel, gathered), out_shape=(value_...  1.15 us
    pallas_call x1, Pallas kernels, shards(): pl.pallas_call(finish_kernel, out_shape=(shape((ZOUT, channels, slots, ti...  1.14 us
  transfers between devices with their start and end apart: 5, of which 2 were waited for; matrix products, arithmetic and copies ran while one was open for 0% of the time, Pallas kernels for 29%

profile of v13, /device:TPU:0, one launch (start us, length us, event | category | flops | bytes accessed | tf_op | source)
XLA Modules:
  0.0 17.7 jit_solution(17224103342613271521)
XLA Ops:
  0.0 2.7 %shard_map.82 = (f32[6,1536,128]{2,1,0:T(8,128)S(1)}, bf16[80,128]{1,0:T(8,128)(2,1)S(1)}, bf16[80,128]{1,0:T(8,128)(2,1)S(1)}, f32[32,64]{1,0:T(8,128)S(1)}, f32[3,2,32]{2,1,0:T(2,128)S(1)}, /*index=5*/s32[8]{0:T(128)S(4)}) custom-call(bf16[6,64,24,128]{3,2,1,0:T(8,128)(2,1)} %feature.1, s32[8]{0:T(128)} %widths_in.1, f32[27,64]{1,0:T(8,128)} %taps_in.1, ...), custom_call_target="tpu_custom_call" | custom-call | tf_op jit(solution)/shard_map/pallas_call | solution.py:437
  2.7 4.0 %collective-permute-start = (bf16[80,128]{1,0:T(8,128)(2,1)S(1)}, bf16[80,128]{1,0:T(8,128)(2,1)S(1)}, u32[]{:S(2)}, u32[]{:S(2)}) collective-permute-start(bf16[80,128]{1,0:T(8,128)(2,1)S(1)} %get-tuple-element.30), channel_id=1, source_target_pairs={{1,2},{2,1},{3,0},{0,3},{5,6},{6,5},{7,4},{4,7},{9,10},{10,9},{11,... | collective-permute-start | bytes 61448 | tf_op jit(solution)/shard_map/ppermute | solution.py:422
  6.6 0.5 %collective-permute-start.1 = (bf16[80,128]{1,0:T(8,128)(2,1)S(1)}, bf16[80,128]{1,0:T(8,128)(2,1)S(1)}, u32[]{:S(2)}, u32[]{:S(2)}) collective-permute-start(bf16[80,128]{1,0:T(8,128)(2,1)S(1)} %get-tuple-element.31), channel_id=1, source_target_pairs={{0,1},{1,0},{2,3},{3,2},{4,5},{5,4},{6,7},{7,6},{8,9},{9,8},{10,11... | collective-permute-start | bytes 61448 | tf_op jit(solution)/shard_map/ppermute | solution.py:422
  7.2 2.3 %shard_map.83 = (f32[6,1536,128]{2,1,0:T(8,128)S(1)}, f32[32,64,128]{2,1,0:T(8,128)S(1)}, f32[2,24,32,128]{3,2,1,0:T(8,128)S(1)}, f32[2,4,64,128]{3,2,1,0:T(8,128)S(1)}, f32[3,2,32]{2,1,0:T(2,128)S(1)}) custom-call(s32[8]{0:T(128)S(4)} %get-tuple-element.23.widths, f32[32,64]{1,0:T(8,128)S(1)} %get-tuple-element.24.stacked, ...), custom_call_target="tpu_custom_call", output_to_operand_aliasing={{0}: (3, {})} | custom-call | flops 1000000000 | bytes 1000000 | tf_op jit(solution)/shard_map/pallas_call | solution.py:467
  9.5 0.2 collective-permute-start.2
  9.7 0.0 collective-permute-done.second.refs_0_
  9.7 0.7 %collective-permute-done.1.first.refs_1_ = bf16[80,128]{1,0:T(8,128)(2,1)S(1)} collective-permute-done((bf16[80,128]{1,0:T(8,128)(2,1)S(1)}, bf16[80,128]{1,0:T(8,128)(2,1)S(1)}, u32[]{:S(2)}, u32[]{:S(2)}) %collective-permute-start.1) | collective-permute-done | bytes 20512 | tf_op jit(solution)/shard_map/ppermute | solution.py:422
  10.4 0.2 %shard_map.84 = (f32[2,64,128]{2,1,0:T(8,128)S(1)}, bf16[256,128]{1,0:T(8,128)(2,1)S(1)}, bf16[256,128]{1,0:T(8,128)(2,1)S(1)}) custom-call(s32[8]{0:T(128)S(4)} %get-tuple-element.23.widths, bf16[80,128]{1,0:T(8,128)(2,1)S(1)} %collective-permute-done.second.refs_0_, bf16[80,128]{1,0:T(8,128)(2,1)S(1)} %collective-permute-done.1.first.refs_1_, ...), custom_call_target="tpu_custom_call" | custom-call | tf_op jit(solution)/shard_map/pallas_call | solution.py:484
  10.6 2.0 %collective-permute-start.3 = (bf16[256,128]{1,0:T(8,128)(2,1)S(1)}, bf16[256,128]{1,0:T(8,128)(2,1)S(1)}, u32[]{:S(2)}, u32[]{:S(2)}) collective-permute-start(bf16[256,128]{1,0:T(8,128)(2,1)S(1)} %get-tuple-element.37), channel_id=1, source_target_pairs={{4,8},{8,4},{12,16},{16,12},{20,24},{24,20},{28,0},{0,28},{5,9},{9... | collective-permute-start | bytes 196616 | tf_op jit(solution)/shard_map/ppermute | solution.py:422
  12.6 0.0 collective-permute-start.4
  12.6 0.0 copy-start
  12.6 1.5 %shard_map.85.rest = f32[2,24,32,128]{3,2,1,0:T(8,128)S(1)} custom-call(f32[2,64,128]{2,1,0:T(8,128)S(1)} %get-tuple-element.33.edge, f32[6,1536,128]{2,1,0:T(8,128)S(1)} %get-tuple-element.28.cells, f32[32,64,128]{2,1,0:T(8,128)S(1)} %get-tuple-element.27.weights), custom_call_target="tpu_custom_call" | custom-call | flops 1000000000 | bytes 1000000 | tf_op jit(solution)/shard_map/pallas_call | solution.py:494
  14.1 0.0 collective-permute-done.2.refs_3_
  14.1 0.0 copy-done
  14.1 1.2 %shard_map.86 = (f32[2,1536,128]{2,1,0:T(8,128)S(1)}, f32[2,4,64,128]{3,2,1,0:T(8,128)S(1)}, f32[2,4,64,128]{3,2,1,0:T(8,128)S(1)}) custom-call(s32[8]{0:T(128)S(4)} %get-tuple-element.23.widths, bf16[64,64]{1,0:T(8,128)(2,1)S(1)} %copy-done, f32[6,1536,128]{2,1,0:T(8,128)S(1)} %get-tuple-element.28.cells, f32[32,64,128]{2,1,0:T(8,128)S(1)} %get-tuple-element.27.weights, ...), custom_call_target="tpu_custom_call" | custom-call | flops 1000000000 | bytes 1000000 | tf_op jit(solution)/shard_map/pallas_call | solution.py:503
  15.3 1.3 %collective-permute-done.3.far = bf16[256,128]{1,0:T(8,128)(2,1)S(1)} collective-permute-done((bf16[256,128]{1,0:T(8,128)(2,1)S(1)}, bf16[256,128]{1,0:T(8,128)(2,1)S(1)}, u32[]{:S(2)}, u32[]{:S(2)}) %collective-permute-start.3) | collective-permute-done | bytes 65568 | tf_op jit(solution)/shard_map/ppermute | solution.py:422
  16.6 0.0 collective-permute-done.4.near
  16.6 1.1 %shard_map.87 = (bf16[2,64,24,128]{3,2,1,0:T(8,128)(2,1)}, f32[2,1536,128]{2,1,0:T(8,128)S(1)}) custom-call(s32[8]{0:T(128)S(4)} %get-tuple-element.23.widths, bf16[64,64]{1,0:T(8,128)(2,1)S(1)} %copy-done, f32[32,64,128]{2,1,0:T(8,128)S(1)} %get-tuple-element.27.weights, ...), custom_call_target="tpu_custom_call", output_to_operand_aliasing={{1}: (7, {})} | custom-call | tf_op jit(solution)/shard_map/pallas_call | solution.py:513
Async XLA Ops:
  2.7 7.0 %collective-permute-start = (bf16[80,128]{1,0:T(8,128)(2,1)S(1)}, bf16[80,128]{1,0:T(8,128)(2,1)S(1)}, u32[]{:S(2)}, u32[]{:S(2)}) collective-permute-start(bf16[80,128]{1,0:T(8,128)(2,1)S(1)} %get-tuple-element.30), channel_id=1, source_target_pairs={{1,2},{2,1},{3,0},{0,3},{5,6},{6,5},{7,4},{4,7},{9,10},{10,9},{11,... | collective-permute-start | bytes 61448 | tf_op jit(solution)/shard_map/ppermute | solution.py:422
  6.6 3.8 %collective-permute-start.1 = (bf16[80,128]{1,0:T(8,128)(2,1)S(1)}, bf16[80,128]{1,0:T(8,128)(2,1)S(1)}, u32[]{:S(2)}, u32[]{:S(2)}) collective-permute-start(bf16[80,128]{1,0:T(8,128)(2,1)S(1)} %get-tuple-element.31), channel_id=1, source_target_pairs={{0,1},{1,0},{2,3},{3,2},{4,5},{5,4},{6,7},{7,6},{8,9},{9,8},{10,11... | collective-permute-start | bytes 61448 | tf_op jit(solution)/shard_map/ppermute | solution.py:422
  9.5 4.6 %collective-permute-start.2 = (f32[3,2,32]{2,1,0:T(2,128)S(1)}, f32[3,2,32]{2,1,0:T(2,128)S(1)}, u32[]{:S(2)}, u32[]{:S(2)}) collective-permute-start(f32[3,2,32]{2,1,0:T(2,128)S(1)} %get-tuple-element.34.refs_2_), channel_id=1, source_target_pairs={{0,2},{1,3},{2,0},{3,1},{4,6},{5,7},{6,4},{7,5},{8,10},{9,11},{10,... | collective-permute-start | bytes 2312 | tf_op jit(solution)/shard_map/ppermute | solution.py:483
  10.6 6.0 %collective-permute-start.3 = (bf16[256,128]{1,0:T(8,128)(2,1)S(1)}, bf16[256,128]{1,0:T(8,128)(2,1)S(1)}, u32[]{:S(2)}, u32[]{:S(2)}) collective-permute-start(bf16[256,128]{1,0:T(8,128)(2,1)S(1)} %get-tuple-element.37), channel_id=1, source_target_pairs={{4,8},{8,4},{12,16},{16,12},{20,24},{24,20},{28,0},{0,28},{5,9},{9... | collective-permute-start | bytes 196616 | tf_op jit(solution)/shard_map/ppermute | solution.py:422
  12.6 4.0 %collective-permute-start.4 = (bf16[256,128]{1,0:T(8,128)(2,1)S(1)}, bf16[256,128]{1,0:T(8,128)(2,1)S(1)}, u32[]{:S(2)}, u32[]{:S(2)}) collective-permute-start(bf16[256,128]{1,0:T(8,128)(2,1)S(1)} %get-tuple-element.38), channel_id=1, source_target_pairs={{0,4},{4,0},{8,12},{12,8},{16,20},{20,16},{24,28},{28,24},{1,5},{5... | collective-permute-start | bytes 196616 | tf_op jit(solution)/shard_map/ppermute | solution.py:422
  12.6 1.5 %copy-start = (bf16[64,64]{1,0:T(8,128)(2,1)S(1)}, bf16[64,64]{1,0:T(8,128)(2,1)}, u32[]{:S(2)}) copy-start(bf16[64,64]{1,0:T(8,128)(2,1)} %mix.3) | copy-start | bytes 24580

commit v14 on v13

--- a/solution.py
+++ b/solution.py
@@ -11,8 +11,8 @@
 ZOUT = 2
 CF = 16
 ROWS = 8
-SPLIT = 4
 CHUNK = 16
+TAIL = 32
 DW_BIAS, PW_BIAS, LIFT = 27, 28, 29
 F32 = jnp.float32
 BF16 = jnp.bfloat16
@@ -37,7 +37,7 @@
 
 def pack_kernel(
     feature, widths_in, taps_in, dw_bias_in, pw_bias_in, lift_in, coarse_in,
-    cells, first, second, stacked, own_block, widths,
+    cells, packets, stacked, widths,
     planes, widths_here, taps, dw_bias, pw_bias, lift, coarse, tail, picked, sems, small_sems,
 ):
     count, channels, slots, tile = feature.shape
@@ -73,18 +73,17 @@
         stacked[PW_BIAS : PW_BIAS + 1, :] = pw_bias[...]
         stacked[LIFT : LIFT + 3, :] = lift[...]
 
-        own_block[...] = coarse[...]
         parts, own_rows, ncy = coarse.shape
         tail[...] = jnp.zeros_like(tail)
-        if 3 * ncy <= tile:
-            for k in range(parts):
-                rest = coarse[k]
-                for p in range(3):
-                    term = rest.astype(BF16).astype(F32)
-                    rest = rest - term
-                    tail[k * own_rows : (k + 1) * own_rows, p * ncy : (p + 1) * ncy] = term
-        for message in (first, second):
-            message[channels:, :] = tail[...].astype(BF16)
+        for k in range(parts):
+            rest = coarse[k]
+            for p in range(3):
+                term = rest.astype(BF16).astype(F32)
+                rest = rest - term
+                at = (p * parts + k) * own_rows
+                tail[at : at + own_rows, 0:ncy] = term
+        for begin in range(0, packets.shape[0], channels + TAIL):
+            packets[begin + channels : begin + channels + TAIL, :] = tail[...].astype(BF16)
 
         row, along = row_iota((taps.shape[0], tile)), lane_iota((taps.shape[0], tile))
         by_side = jnp.where((along & 2) != 0, 2, 0)
@@ -161,9 +160,14 @@
                 packed[half] = term if packed[half] is None else packed[half] + term
     left = jnp.where(on_left, packed[0], pltpu.roll(packed[1], tile - 2, 1))
     right = jnp.where(on_left, pltpu.roll(packed[1], 2, 1), packed[0])
-    even = is_even("gy")
-    first[0:channels, :] = jnp.where(even, right, left).astype(BF16)
-    second[0:channels, :] = jnp.where(even, left, right).astype(BF16)
+    for message, by in ((left, -1), (right, 1)):
+        packets[packet_rows(by, channels), :] = message.astype(BF16)
+
+
+def packet_rows(by, channels):
+    count = lax.axis_size("gy")
+    beside = lax.rem(lax.axis_index("gy") + by + count, count)
+    return pl.ds(pl.multiple_of(beside * (channels + TAIL), 16), channels)
 
 
 def shifted_sum(before, centre, after):
@@ -174,35 +178,10 @@
     return centre + before + after
 
 
-def convolve_block(cells, weights, depth, b, first_block):
-    channels = weights.shape[1]
-    slots = cells.shape[1] // channels
-    at = pl.ds(pl.multiple_of(b * ROWS, ROWS), ROWS)
-    to = pl.ds(pl.multiple_of((b - first_block) * ROWS, ROWS), ROWS)
-    tap = [weights[t, at, :] for t in range(27)]
-    for z in range(ZOUT):
-        for parity in range(2):
-            sums = {}
-            for x in range(parity, slots, 2):
-                rows = [cells[z + ZOUT * m, pl.ds(b * (ROWS * slots) + x, ROWS, stride=slots), :] for m in range(3)]
-                for m in range(3):
-                    for dx in (1, 0, -1):
-                        out = x - 2 * dx
-                        if 0 <= out < slots:
-                            for dy in (-1, 0, 1):
-                                term = tap[tap_of(m, dx, dy)] * rows[m]
-                                key = (out, dy)
-                                sums[key] = sums[key] + term if key in sums else term
-                for out in [x - 2] if x + 2 < slots else [x - 2, x]:
-                    if out >= 0:
-                        depth[z, out, to, :] = shifted_sum(*(sums.pop((out, dy)) for dy in (-1, 0, 1)))
-
-
-def conv_kernel(widths, stacked, coarse, cells_in, cells, weights, depth, rims, own_block):
+def outer_kernel(widths, stacked, cells_in, cells, weights, rims):
     width = widths[lax.axis_index("gx")]
     channels, tile = weights.shape[1:]
     slots = cells.shape[1] // channels
-    own_block[...] = coarse[...]
     turned = jnp.transpose(stacked[...])
     for t in range(stacked.shape[0]):
         weights[t] = jnp.broadcast_to(turned[:, t : t + 1], (channels, tile))
@@ -226,11 +205,33 @@
                     parts = [sum(weight * row for weight, row in zip(weights_of, rows)) for weights_of in tap]
                     rims[z, 2 * side + r, at, :] = shifted_sum(*parts)
 
+
+def conv_kernel(edge, cells, weights, depth):
+    channels = weights.shape[1]
+    slots = cells.shape[1] // channels
+
     def convolve(b, carry):
-        convolve_block(cells, weights, depth, b, 0)
+        at = pl.ds(pl.multiple_of(b * ROWS, ROWS), ROWS)
+        tap = [weights[t, at, :] for t in range(27)]
+        for z in range(ZOUT):
+            for parity in range(2):
+                sums = {}
+                for x in range(parity, slots, 2):
+                    rows = [cells[z + ZOUT * m, pl.ds(b * (ROWS * slots) + x, ROWS, stride=slots), :] for m in range(3)]
+                    for m in range(3):
+                        for dx in (1, 0, -1):
+                            out = x - 2 * dx
+                            if 0 <= out < slots:
+                                for dy in (-1, 0, 1):
+                                    term = tap[tap_of(m, dx, dy)] * rows[m]
+                                    key = (out, dy)
+                                    sums[key] = sums[key] + term if key in sums else term
+                    for out in [x - 2] if x + 2 < slots else [x - 2, x]:
+                        if out >= 0:
+                            depth[z, out, at, :] = shifted_sum(*(sums.pop((out, dy)) for dy in (-1, 0, 1)))
         return carry
 
-    lax.fori_loop(0, SPLIT, convolve, 0)
+    lax.fori_loop(0, channels // ROWS, convolve, 0)
 
 
 def edge_term(edge, z, x):
@@ -241,13 +242,11 @@
     return jnp.where((lane < 2) | (lane >= tile - 2), cells, 0.0)
 
 
-def rim_kernel(widths, second, first, rims, edge, far, near):
+def rim_kernel(widths, packets, rims, edge, far, near):
     width = widths[lax.axis_index("gx")]
     _, _, channels, tile = rims.shape
-    even = is_even("gy")
-    one, two = first[0:channels, :].astype(F32), second[0:channels, :].astype(F32)
-    right = jnp.where(even, one, two)
-    left = jnp.where(even, two, one)
+    left = packets[packet_rows(-1, channels), :].astype(F32)
+    right = packets[packet_rows(1, channels), :].astype(F32)
     on_left = (lane_iota((channels, tile)) & 2) != 0
     edge[0] = jnp.where(on_left, pltpu.roll(left, 2, 1), pltpu.roll(right, tile - 2, 1))
     edge[1] = jnp.where(on_left, left, right)
@@ -269,9 +268,8 @@
     return start
 
 
-def depth_row(weights, depths, edge, z, x):
-    own = jnp.concatenate([depth[z, x] for depth in depths], axis=0)
-    return own + weights[DW_BIAS] + edge_term(edge, z, x)
+def depth_row(weights, depth, edge, z, x):
+    return depth[z, x] + weights[DW_BIAS] + edge_term(edge, z, x)
 
 
 def base_row(cells, lifted, phase, z, x):
@@ -285,51 +283,28 @@
     return jnp.maximum(mixed, 0.2 * mixed)
 
 
-def rest_kernel(edge, cells, weights, rest):
-    def convolve(b, carry):
-        convolve_block(cells, weights, rest, b, SPLIT)
-        return carry
-
-    lax.fori_loop(SPLIT, weights.shape[1] // ROWS, convolve, 0)
-
-
-def mix_kernel(gathered, widths, mix, cells, weights, depth, rest, edge, *refs):
-    if gathered:
-        coarse, value, ends, bases, lifted, across = refs
-        parts, ncx, ncy = coarse.shape
-    else:
-        second, first, own_block, opposite, value, ends, bases, lifted, across, blocks = refs
-        parts, own_rows, ncy = own_block.shape
-        ncx = 4 * own_rows
+def mix_kernel(grid, widths, mix, packets, cells, weights, depth, edge, value, ends, bases, lifted, across, blocks):
+    parts, own_rows, ncy = grid
+    ncx = blocks.shape[1]
     width = widths[lax.axis_index("gx")]
     here = lax.axis_index("gy")
     start = slab_start(widths)
     phase = lax.rem(start, CF)
     channels, tile = weights.shape[1:]
     slots = cells.shape[1] // channels
-
-    if not gathered:
-        even = is_even("gy")
-        after, before = lax.rem(here + 1, 4), lax.rem(here + 3, 4)
-        count = parts * own_rows
-        for message, owner in (
-            (first, jnp.where(even, after, before)),
-            (second, jnp.where(even, before, after)),
-        ):
-            terms = message[channels:, :].astype(F32)[0:count, :]
-            sums = terms[:, 0:ncy] + terms[:, ncy : 2 * ncy] + terms[:, 2 * ncy : 3 * ncy]
-            for k in range(parts):
-                blocks[k, pl.ds(owner * own_rows, own_rows), :] = sums[k * own_rows : (k + 1) * own_rows]
-        for block, owner in ((own_block, here), (opposite, lax.rem(here + 2, 4))):
-            for k in range(parts):
-                blocks[k, pl.ds(owner * own_rows, own_rows), :] = block[k]
+    count = parts * own_rows
+    for owner in range(ncx // own_rows):
+        begin = owner * (channels + TAIL) + channels
+        terms = packets[begin : begin + TAIL, :].astype(F32)
+        sums = terms[0:count] + terms[count : 2 * count] + terms[2 * count : 3 * count]
+        for k in range(parts):
+            blocks[k, owner * own_rows : (owner + 1) * own_rows, :] = sums[k * own_rows : (k + 1) * own_rows, 0:ncy]
     shape = (ncy, tile)
     cell = row_iota(shape) * CF
     place = lane_iota(shape) + here * tile
     along_y = ((place >= cell) & (place < cell + CF)).astype(F32)
     for k in range(parts):
-        block = coarse[k] if gathered else blocks[k]
-        across[k] = jnp.dot(block, along_y, precision=lax.Precision.HIGHEST, preferred_element_type=F32)
+        across[k] = jnp.dot(blocks[k], along_y, precision=lax.Precision.HIGHEST, preferred_element_type=F32)
     for i in range(3):
         cell = lax.rem(lax.div(start, CF) + i, ncx)
         total = None
@@ -351,7 +326,7 @@
 
     for x in range(0, slots, group):
         depths = [
-            jnp.concatenate([depth_row(weights, (depth, rest), edge, z, x + i) for i in range(group)], axis=0).astype(BF16)
+            jnp.concatenate([depth_row(weights, depth, edge, z, x + i) for i in range(group)], axis=0).astype(BF16)
             for z in range(ZOUT)
         ]
         mixed = jnp.dot(mixer, jnp.concatenate(depths, axis=1), preferred_element_type=F32)
@@ -362,7 +337,7 @@
                 value[z, pl.ds(x + i, channels, stride=slots), :] = jnp.where(x + i < width, part, 0.0)
     for z in range(ZOUT):
         for i, x in enumerate((0, 1, width - 2, width - 1)):
-            ends[z, i] = depth_row(weights, (depth, rest), edge, z, x)
+            ends[z, i] = depth_row(weights, depth, edge, z, x)
             bases[z, i] = base_row(cells, lifted, phase, z, x)
 
 
@@ -401,14 +376,12 @@
     planes, channels, slots, tile = feature.shape
     ny = lax.axis_size("gy")
     parts, own_rows, ncy = coarse.shape
-    gathered = ny != 4
     ncx = ny * own_rows
     smem = pl.BlockSpec(memory_space=pltpu.SMEM)
     vmem = pl.BlockSpec(memory_space=pltpu.VMEM)
     hbm = pl.BlockSpec(memory_space=pltpu.HBM)
     params = pltpu.CompilerParams(vmem_limit_bytes=VMEM_BYTES)
     shape = jax.ShapeDtypeStruct
-    strip = shape((channels + 16, tile), BF16)
     cells_shape = pltpu.VMEM((planes, channels * slots, tile), F32)
     value_shape = pltpu.VMEM((ZOUT, channels * slots, tile), F32)
     message = shape((2 * ZOUT * channels, tile), BF16)
@@ -424,8 +397,6 @@
     def pinned(array):
         return pltpu.with_memory_space_constraint(array, pltpu.HBM)
 
-    if gathered:
-        every = lax.all_gather(coarse, "gy", axis=1, tiled=True)
     small = (
         widths,
         dw_weight,
@@ -434,18 +405,16 @@
         lift_weight.T,
         coarse,
     )
-    cells, first, second, stacked, block, slab_widths = pl.pallas_call(
+    cells, packets, stacked, slab_widths = pl.pallas_call(
         pack_kernel,
         out_shape=(
             cells_shape,
-            strip,
-            strip,
+            shape((ny * (channels + TAIL), tile), BF16),
             pltpu.VMEM((32, channels), F32),
-            pltpu.VMEM(coarse.shape, F32),
             pltpu.SMEM(widths.shape, jnp.int32),
         ),
         in_specs=[hbm] * 7,
-        out_specs=(vmem,) * 5 + (smem,),
+        out_specs=(vmem,) * 3 + (smem,),
         scratch_shapes=[
             pltpu.VMEM(feature.shape, BF16),
             pltpu.SMEM(widths.shape, jnp.int32),
@@ -454,46 +423,39 @@
             pltpu.VMEM((1, channels), F32),
             pltpu.VMEM((parts, channels), F32),
             pltpu.VMEM(coarse.shape, F32),
-            pltpu.VMEM((16, tile), F32),
+            pltpu.VMEM((TAIL, tile), F32),
             pltpu.VMEM((3, 2, channels, tile), F32),
             pltpu.SemaphoreType.DMA((3,)),
             pltpu.SemaphoreType.DMA((len(small),)),
         ],
         compiler_params=params,
     )(pinned(feature), *(pinned(array) for array in small))
-    second = swapped(second, "gy", 1)
-    first = swapped(first, "gy", 0)
-    early = SPLIT * ROWS
-    cells, weights, depth, rims, own_block = pl.pallas_call(
-        conv_kernel,
+    packets = lax.all_to_all(packets, "gy", split_axis=0, concat_axis=0, tiled=True)
+    cells, weights, rims = pl.pallas_call(
+        outer_kernel,
         out_shape=(
             cells_shape,
             pltpu.VMEM((32, channels, tile), F32),
-            pltpu.VMEM((ZOUT, slots, early, tile), F32),
             pltpu.VMEM((ZOUT, 4, channels, tile), F32),
-            pltpu.VMEM(coarse.shape, F32),
         ),
-        in_specs=[smem] + [vmem] * 3,
-        out_specs=(vmem,) * 5,
-        input_output_aliases={3: 0},
+        in_specs=[smem] + [vmem] * 2,
+        out_specs=(vmem,) * 3,
+        input_output_aliases={2: 0},
         compiler_params=params,
         cost_estimate=pl.CostEstimate(flops=10**9, bytes_accessed=10**6, transcendentals=0),
-    )(slab_widths, stacked, block, cells)
-    if not gathered:
-        opposite = lax.ppermute(own_block, "gy", [(i, (i + 2) % 4) for i in range(4)])
+    )(slab_widths, stacked, cells)
     edge, far, near = pl.pallas_call(
         rim_kernel,
         out_shape=(pltpu.VMEM((2, channels, tile), F32), message, message),
-        in_specs=[smem] + [vmem] * 3,
+        in_specs=[smem] + [vmem] * 2,
         out_specs=(vmem,) * 3,
         compiler_params=params,
-    )(slab_widths, second, first, rims)
+    )(slab_widths, packets, rims)
     far = swapped(far, "gx", 1)
     near = swapped(near, "gx", 0)
-    blocks = (every,) if gathered else (second, first, own_block, opposite)
-    rest = pl.pallas_call(
-        rest_kernel,
-        out_shape=pltpu.VMEM((ZOUT, slots, channels - early, tile), F32),
+    depth = pl.pallas_call(
+        conv_kernel,
+        out_shape=pltpu.VMEM((ZOUT, slots, channels, tile), F32),
         in_specs=[vmem] * 3,
         out_specs=vmem,
         compiler_params=params,
@@ -501,15 +463,18 @@
     )(edge, cells, weights)
     ends_shape = pltpu.VMEM((ZOUT, 4, channels, tile), F32)
     value, ends, bases = pl.pallas_call(
-        functools.partial(mix_kernel, gathered),
+        functools.partial(mix_kernel, coarse.shape),
         out_shape=(value_shape, ends_shape, ends_shape),
-        in_specs=[smem] + [vmem] * (6 + len(blocks)),
+        in_specs=[smem] + [vmem] * 6,
         out_specs=(vmem,) * 3,
-        scratch_shapes=[pltpu.VMEM((3, channels, tile), F32), pltpu.VMEM((parts, ncx, tile), F32)]
-        + ([] if gathered else [pltpu.VMEM((parts, ncx, ncy), F32)]),
+        scratch_shapes=[
+            pltpu.VMEM((3, channels, tile), F32),
+            pltpu.VMEM((parts, ncx, tile), F32),
+            pltpu.VMEM((parts, ncx, ncy), F32),
+        ],
         compiler_params=params,
         cost_estimate=pl.CostEstimate(flops=10**9, bytes_accessed=10**6, transcendentals=0),
-    )(slab_widths, pw_weight, cells, weights, depth, rest, edge, *blocks)
+    )(slab_widths, pw_weight, packets, cells, weights, depth, edge)
     out, _ = pl.pallas_call(
         finish_kernel,
         out_shape=(shape((ZOUT, channels, slots, tile), BF16), value_shape),

time: 17.9 us -> 26.8 us (1.50)
  local copies, waits for them, and re-layouts: 0.01 us -> 8.92 us
  waiting for transfers between devices: 2.05 us -> 0.01 us
  starting transfers between devices: 6.65 us -> 7.9 us
  Pallas kernels: 8.97 us -> 9.53 us
    unnamed x2 -> x10, local copies, waits for them, and re-layouts: 0.01 us -> 8.92 us
    all_to_all x0 -> x1, starting transfers between devices: none -> 5.16 us  [shards(): lax.all_to_all(packets, 'gy', split_axis=0, concat_axis=0, tiled=True)]
    ppermute x4 -> x2, starting transfers between devices: 6.48 us -> 2.74 us  [swapped(): return lax.ppermute(array, axis, pairs)]
    ppermute x4 -> x2, waiting for transfers between devices: 2.05 us -> 0.01 us  [swapped(): return lax.ppermute(array, axis, pairs)]
    pallas_call x4, Pallas kernels: 7.64 us -> 8.2 us  [the longest x1 3.3 us: shards(): pl.pallas_call(pack_kernel, out_shape=(cells_shape, shape((ny * (channels...]
  transfers between devices with their start and end apart: 5 -> 3, of which waited for: 2 -> 0; matrix products, arithmetic and copies ran while one was open for 0% -> 0% of each run, Pallas kernels for 29% -> 19%
where the time goes in v14:
time: 26.8 us; the launch traced here: 26.4 us
  Pallas kernels  9.53 us (36%)
  local copies, waits for them, and re-layouts  8.92 us (33%)
  starting transfers between devices  7.9 us (29%)
    unnamed x10, local copies, waits for them, and re-layouts  8.92 us
    all_to_all x1, starting transfers between devices, shards(): lax.all_to_all(packets, 'gy', split_axis=0, concat_axis=0, tiled=True)  5.16 us
    pallas_call x1, Pallas kernels, shards(): pl.pallas_call(pack_kernel, out_shape=(cells_shape, shape((ny * (channels...  3.3 us
    pallas_call x1, Pallas kernels, shards(): pl.pallas_call(conv_kernel, out_shape=pltpu.VMEM((ZOUT, slots, channels,...  2.98 us
    ppermute x2, starting transfers between devices, swapped(): return lax.ppermute(array, axis, pairs)  2.74 us
    pallas_call x1, Pallas kernels, shards(): pl.pallas_call(finish_kernel, out_shape=(shape((ZOUT, channels, slots, ti...  1.15 us
    pallas_call x1, Pallas kernels, shards(): pl.pallas_call(functools.partial(mix_kernel, coarse.shape), out_shape=(va...  1.07 us
    pallas_call x1, Pallas kernels, shards(): pl.pallas_call(outer_kernel, out_shape=(cells_shape, pltpu.VMEM((32, chan...  0.85 us
  transfers between devices with their start and end apart: 3, of which 0 were waited for; matrix products, arithmetic and copies ran while one was open for 0% of the time, Pallas kernels for 19%

profile of v14, /device:TPU:0, one launch (start us, length us, event | category | flops | bytes accessed | tf_op | source)
XLA Modules:
  0.0 26.4 jit_solution(17715963343596665111)
XLA Ops:
  0.0 3.3 %shard_map.82 = (f32[6,1536,128]{2,1,0:T(8,128)S(1)}, bf16[384,128]{1,0:T(8,128)(2,1)}, f32[32,64]{1,0:T(8,128)S(1)}, s32[8]{0:T(128)S(4)}) custom-call(bf16[6,64,24,128]{3,2,1,0:T(8,128)(2,1)} %feature.1, s32[8]{0:T(128)} %widths_in.1, f32[27,64]{1,0:T(8,128)} %taps_in.1, f32[1,64]{1,0:T(1,128)} %bitcast.8, f32[1,64]{1,0:T(1,128)} %bitcast.9, ...), custom_call_target="tpu_custom_call" | custom-call | tf_op jit(solution)/shard_map/pallas_call | solution.py:408
  3.3 0.0 copy-start
  3.3 2.1 %copy-done = f32[6,1536,128]{2,1,0:T(8,128)} copy-done((f32[6,1536,128]{2,1,0:T(8,128)}, f32[6,1536,128]{2,1,0:T(8,128)S(1)}, u32[]{:S(2)}) %copy-start) | copy-done | bytes 4718616
  5.4 5.2 %all-to-all-start = ((bf16[4,96,128]{2,1,0:T(8,128)(2,1)}), bf16[4,96,128]{2,1,0:T(8,128)(2,1)S(1)}, u32[]{:S(2)}, u32[]{:S(2)}) async-start(bf16[4,96,128]{2,1,0:T(8,128)(2,1)} %bitcast.3), calls=%async_computation | async-start | bytes 196608 | tf_op jit(solution)/shard_map/all_to_all | solution.py:433
  10.6 0.0 copy-start.1
  10.6 2.3 %copy-done.1 = f32[6,1536,128]{2,1,0:T(8,128)S(1)} copy-done((f32[6,1536,128]{2,1,0:T(8,128)S(1)}, f32[6,1536,128]{2,1,0:T(8,128)}, u32[]{:S(2)}) %copy-start.1) | copy-done | bytes 4718616
  12.9 0.9 %shard_map.83 = (f32[6,1536,128]{2,1,0:T(8,128)S(1)}, f32[32,64,128]{2,1,0:T(8,128)S(1)}, f32[2,4,64,128]{3,2,1,0:T(8,128)S(1)}) custom-call(s32[8]{0:T(128)S(4)} %get-tuple-element.19.widths, f32[32,64]{1,0:T(8,128)S(1)} %get-tuple-element.20.stacked, f32[6,1536,128]{2,1,0:T(8,128)S(1)} %copy-done.1), custom_call_target="tpu_custom_call", output_to_operand_aliasing={{0}: (2, {})} | custom-call | flops 1000000000 | bytes 1000000 | tf_op jit(solution)/shard_map/pallas_call | solution.py:434
  13.8 0.0 copy-start.2
  13.8 2.1 %copy-done.2 = f32[6,1536,128]{2,1,0:T(8,128)} copy-done((f32[6,1536,128]{2,1,0:T(8,128)}, f32[6,1536,128]{2,1,0:T(8,128)S(1)}, u32[]{:S(2)}) %copy-start.2) | copy-done | bytes 4718616
  15.9 0.0 all-to-all-done
  15.9 0.2 shard_map.84
  16.1 2.7 %collective-permute-start = (bf16[256,128]{1,0:T(8,128)(2,1)S(1)}, bf16[256,128]{1,0:T(8,128)(2,1)S(1)}, u32[]{:S(2)}, u32[]{:S(2)}) collective-permute-start(bf16[256,128]{1,0:T(8,128)(2,1)S(1)} %get-tuple-element.29), channel_id=1, source_target_pairs={{4,8},{8,4},{12,16},{16,12},{20,24},{24,20},{28,0},{0,28},{5,9},{9... | collective-permute-start | bytes 196616 | tf_op jit(solution)/shard_map/ppermute | solution.py:395
  18.9 0.0 collective-permute-start.1
  18.9 0.0 copy-start.3
  18.9 2.3 %copy-done.3 = f32[6,1536,128]{2,1,0:T(8,128)S(1)} copy-done((f32[6,1536,128]{2,1,0:T(8,128)S(1)}, f32[6,1536,128]{2,1,0:T(8,128)}, u32[]{:S(2)}) %copy-start.3) | copy-done | bytes 4718616
  21.2 0.0 copy-start.4
  21.2 3.0 %shard_map.85.depth = f32[2,24,64,128]{3,2,1,0:T(8,128)S(1)} custom-call(f32[2,64,128]{2,1,0:T(8,128)S(1)} %get-tuple-element.26.edge, f32[6,1536,128]{2,1,0:T(8,128)S(1)} %copy-done.3, f32[32,64,128]{2,1,0:T(8,128)S(1)} %get-tuple-element.22.weights), custom_call_target="tpu_custom_call" | custom-call | flops 1000000000 | bytes 1000000 | tf_op jit(solution)/shard_map/pallas_call | solution.py:456
  24.2 0.0 copy-done.4
  24.2 1.1 %shard_map.86 = (f32[2,1536,128]{2,1,0:T(8,128)S(1)}, f32[2,4,64,128]{3,2,1,0:T(8,128)S(1)}, f32[2,4,64,128]{3,2,1,0:T(8,128)S(1)}) custom-call(s32[8]{0:T(128)S(4)} %get-tuple-element.19.widths, bf16[64,64]{1,0:T(8,128)(2,1)S(1)} %copy-done.4, bf16[384,128]{1,0:T(8,128)(2,1)S(1)} %bitcast.6, f32[6,1536,128]{2,1,0:T(8,128)S(1)} %copy-done.3, ...), custom_call_target="tpu_custom_call" | custom-call | flops 1000000000 | bytes 1000000 | tf_op jit(solution)/shard_map/pallas_call | solution.py:465
  25.3 0.0 collective-permute-done.far
  25.3 0.0 collective-permute-done.1.near
  25.3 1.2 %shard_map.87 = (bf16[2,64,24,128]{3,2,1,0:T(8,128)(2,1)}, f32[2,1536,128]{2,1,0:T(8,128)S(1)}) custom-call(s32[8]{0:T(128)S(4)} %get-tuple-element.19.widths, bf16[64,64]{1,0:T(8,128)(2,1)S(1)} %copy-done.4, f32[32,64,128]{2,1,0:T(8,128)S(1)} %get-tuple-element.22.weights, ...), custom_call_target="tpu_custom_call", output_to_operand_aliasing={{1}: (7, {})} | custom-call | tf_op jit(solution)/shard_map/pallas_call | solution.py:478
Async XLA Ops:
  3.3 2.1 %copy-start = (f32[6,1536,128]{2,1,0:T(8,128)}, f32[6,1536,128]{2,1,0:T(8,128)S(1)}, u32[]{:S(2)}) copy-start(f32[6,1536,128]{2,1,0:T(8,128)S(1)} %get-tuple-element.21.cells_in) | copy-start | bytes 14155780
  5.4 10.5 %all-to-all-start = ((bf16[4,96,128]{2,1,0:T(8,128)(2,1)}), bf16[4,96,128]{2,1,0:T(8,128)(2,1)S(1)}, u32[]{:S(2)}, u32[]{:S(2)}) async-start(bf16[4,96,128]{2,1,0:T(8,128)(2,1)} %bitcast.3), calls=%async_computation | async-start | bytes 196608 | tf_op jit(solution)/shard_map/all_to_all | solution.py:433
  10.6 2.3 %copy-start.1 = (f32[6,1536,128]{2,1,0:T(8,128)S(1)}, f32[6,1536,128]{2,1,0:T(8,128)}, u32[]{:S(2)}) copy-start(f32[6,1536,128]{2,1,0:T(8,128)} %copy-done) | copy-start | bytes 14155780
  13.8 2.1 %copy-start.2 = (f32[6,1536,128]{2,1,0:T(8,128)}, f32[6,1536,128]{2,1,0:T(8,128)S(1)}, u32[]{:S(2)}) copy-start(f32[6,1536,128]{2,1,0:T(8,128)S(1)} %get-tuple-element.24.cells) | copy-start | bytes 14155780
  16.1 9.2 %collective-permute-start = (bf16[256,128]{1,0:T(8,128)(2,1)S(1)}, bf16[256,128]{1,0:T(8,128)(2,1)S(1)}, u32[]{:S(2)}, u32[]{:S(2)}) collective-permute-start(bf16[256,128]{1,0:T(8,128)(2,1)S(1)} %get-tuple-element.29), channel_id=1, source_target_pairs={{4,8},{8,4},{12,16},{16,12},{20,24},{24,20},{28,0},{0,28},{5,9},{9... | collective-permute-start | bytes 196616 | tf_op jit(solution)/shard_map/ppermute | solution.py:395
  18.9 6.4 %collective-permute-start.1 = (bf16[256,128]{1,0:T(8,128)(2,1)S(1)}, bf16[256,128]{1,0:T(8,128)(2,1)S(1)}, u32[]{:S(2)}, u32[]{:S(2)}) collective-permute-start(bf16[256,128]{1,0:T(8,128)(2,1)S(1)} %get-tuple-element.30), channel_id=1, source_target_pairs={{0,4},{4,0},{8,12},{12,8},{16,20},{20,16},{24,28},{28,24},{1,5},{5... | collective-permute-start | bytes 196616 | tf_op jit(solution)/shard_map/ppermute | solution.py:395
  18.9 2.3 %copy-start.3 = (f32[6,1536,128]{2,1,0:T(8,128)S(1)}, f32[6,1536,128]{2,1,0:T(8,128)}, u32[]{:S(2)}) copy-start(f32[6,1536,128]{2,1,0:T(8,128)} %copy-done.2) | copy-start | bytes 14155780
  21.2 3.0 %copy-start.4 = (bf16[64,64]{1,0:T(8,128)(2,1)S(1)}, bf16[64,64]{1,0:T(8,128)(2,1)}, u32[]{:S(2)}) copy-start(bf16[64,64]{1,0:T(8,128)(2,1)} %mix.3) | copy-start | bytes 24580

commit v15 on v13

--- a/solution.py
+++ b/solution.py
@@ -161,9 +161,8 @@
                 packed[half] = term if packed[half] is None else packed[half] + term
     left = jnp.where(on_left, packed[0], pltpu.roll(packed[1], tile - 2, 1))
     right = jnp.where(on_left, pltpu.roll(packed[1], 2, 1), packed[0])
-    even = is_even("gy")
-    first[0:channels, :] = jnp.where(even, right, left).astype(BF16)
-    second[0:channels, :] = jnp.where(even, left, right).astype(BF16)
+    first[0:channels, :] = right.astype(BF16)
+    second[0:channels, :] = left.astype(BF16)
 
 
 def shifted_sum(before, centre, after):
@@ -241,13 +240,10 @@
     return jnp.where((lane < 2) | (lane >= tile - 2), cells, 0.0)
 
 
-def rim_kernel(widths, second, first, rims, edge, far, near):
+def rim_kernel(widths, first, second, rims, edge, far, near):
     width = widths[lax.axis_index("gx")]
     _, _, channels, tile = rims.shape
-    even = is_even("gy")
-    one, two = first[0:channels, :].astype(F32), second[0:channels, :].astype(F32)
-    right = jnp.where(even, one, two)
-    left = jnp.where(even, two, one)
+    left, right = first[0:channels, :].astype(F32), second[0:channels, :].astype(F32)
     on_left = (lane_iota((channels, tile)) & 2) != 0
     edge[0] = jnp.where(on_left, pltpu.roll(left, 2, 1), pltpu.roll(right, tile - 2, 1))
     edge[1] = jnp.where(on_left, left, right)
@@ -298,7 +294,7 @@
         coarse, value, ends, bases, lifted, across = refs
         parts, ncx, ncy = coarse.shape
     else:
-        second, first, own_block, opposite, value, ends, bases, lifted, across, blocks = refs
+        first, second, own_block, opposite, value, ends, bases, lifted, across, blocks = refs
         parts, own_rows, ncy = own_block.shape
         ncx = 4 * own_rows
     width = widths[lax.axis_index("gx")]
@@ -309,13 +305,8 @@
     slots = cells.shape[1] // channels
 
     if not gathered:
-        even = is_even("gy")
-        after, before = lax.rem(here + 1, 4), lax.rem(here + 3, 4)
         count = parts * own_rows
-        for message, owner in (
-            (first, jnp.where(even, after, before)),
-            (second, jnp.where(even, before, after)),
-        ):
+        for message, owner in ((first, lax.rem(here + 3, 4)), (second, lax.rem(here + 1, 4))):
             terms = message[channels:, :].astype(F32)[0:count, :]
             sums = terms[:, 0:ncy] + terms[:, ncy : 2 * ncy] + terms[:, 2 * ncy : 3 * ncy]
             for k in range(parts):
@@ -461,8 +452,8 @@
         ],
         compiler_params=params,
     )(pinned(feature), *(pinned(array) for array in small))
-    second = swapped(second, "gy", 1)
-    first = swapped(first, "gy", 0)
+    first = lax.ppermute(first, "gy", [(i, (i + 1) % ny) for i in range(ny)])
+    second = lax.ppermute(second, "gy", [((i + 1) % ny, i) for i in range(ny)])
     early = SPLIT * ROWS
     cells, weights, depth, rims, own_block = pl.pallas_call(
         conv_kernel,
@@ -487,10 +478,10 @@
         in_specs=[smem] + [vmem] * 3,
         out_specs=(vmem,) * 3,
         compiler_params=params,
-    )(slab_widths, second, first, rims)
+    )(slab_widths, first, second, rims)
     far = swapped(far, "gx", 1)
     near = swapped(near, "gx", 0)
-    blocks = (every,) if gathered else (second, first, own_block, opposite)
+    blocks = (every,) if gathered else (first, second, own_block, opposite)
     rest = pl.pallas_call(
         rest_kernel,
         out_shape=pltpu.VMEM((ZOUT, slots, channels - early, tile), F32),

time: 17.9 us -> 18.5 us (1.034)
  starting transfers between devices: 6.65 us -> 8.23 us
  waiting for transfers between devices: 2.05 us -> 1.1 us
    ppermute x4 -> x2, starting transfers between devices: 6.48 us -> 2.22 us  [swapped(): return lax.ppermute(array, axis, pairs)]
    ppermute x0 -> x2, starting transfers between devices: none -> 4.01 us  [the longest x1 2.99 us: shards(): first = lax.ppermute(first, 'gy', [(i, (i + 1) % ny) for i in range(ny)])]
    ppermute x1, starting transfers between devices: 0.17 us -> 2 us  [shards(): lax.ppermute(own_block, 'gy', [(i, (i + 2) % 4) for i in range(4)])]
    ppermute x4 -> x2, waiting for transfers between devices: 2.05 us -> 1.09 us  [swapped(): return lax.ppermute(array, axis, pairs)]
  transfers between devices with their start and end apart: 5 -> 5, of which waited for: 2 -> 1; matrix products, arithmetic and copies ran while one was open for 0% -> 0% of each run, Pallas kernels for 29% -> 28%
where the time goes in v15:
time: 18.5 us; the launch traced here: 18.3 us
  Pallas kernels  8.96 us (48%)
  starting transfers between devices  8.23 us (44%)
  waiting for transfers between devices  1.1 us (6%)
    ppermute x1, starting transfers between devices, shards(): first = lax.ppermute(first, 'gy', [(i, (i + 1) % ny) for i in range(ny)])  2.99 us
    pallas_call x1, Pallas kernels, shards(): pl.pallas_call(pack_kernel, out_shape=(cells_shape, strip, strip, pltpu.V...  2.65 us
    pallas_call x1, Pallas kernels, shards(): pl.pallas_call(conv_kernel, out_shape=(cells_shape, pltpu.VMEM((32, chann...  2.34 us
    ppermute x2, starting transfers between devices, swapped(): return lax.ppermute(array, axis, pairs)  2.22 us
    ppermute x1, starting transfers between devices, shards(): lax.ppermute(own_block, 'gy', [(i, (i + 2) % 4) for i in range(4)])  2 us
    pallas_call x1, Pallas kernels, shards(): pl.pallas_call(rest_kernel, out_shape=pltpu.VMEM((ZOUT, slots, channels -...  1.49 us
    pallas_call x1, Pallas kernels, shards(): pl.pallas_call(functools.partial(mix_kernel, gathered), out_shape=(value_...  1.15 us
    pallas_call x1, Pallas kernels, shards(): pl.pallas_call(finish_kernel, out_shape=(shape((ZOUT, channels, slots, ti...  1.14 us
  transfers between devices with their start and end apart: 5, of which 1 were waited for; matrix products, arithmetic and copies ran while one was open for 0% of the time, Pallas kernels for 28%

profile of v15, /device:TPU:0, one launch (start us, length us, event | category | flops | bytes accessed | tf_op | source)
XLA Modules:
  0.0 18.3 jit_solution(3609989475077442483)
XLA Ops:
  0.0 2.7 %shard_map.82 = (f32[6,1536,128]{2,1,0:T(8,128)S(1)}, bf16[80,128]{1,0:T(8,128)(2,1)S(1)}, bf16[80,128]{1,0:T(8,128)(2,1)S(1)}, f32[32,64]{1,0:T(8,128)S(1)}, f32[3,2,32]{2,1,0:T(2,128)S(1)}, /*index=5*/s32[8]{0:T(128)S(4)}) custom-call(bf16[6,64,24,128]{3,2,1,0:T(8,128)(2,1)} %feature.1, s32[8]{0:T(128)} %widths_in.1, f32[27,64]{1,0:T(8,128)} %taps_in.1, ...), custom_call_target="tpu_custom_call" | custom-call | tf_op jit(solution)/shard_map/pallas_call | solution.py:428
  2.7 3.0 %collective-permute-start = (bf16[80,128]{1,0:T(8,128)(2,1)S(1)}, bf16[80,128]{1,0:T(8,128)(2,1)S(1)}, u32[]{:S(2)}, u32[]{:S(2)}) collective-permute-start(bf16[80,128]{1,0:T(8,128)(2,1)S(1)} %get-tuple-element.30), channel_id=1, source_target_pairs={{0,1},{1,2},{2,3},{3,0},{4,5},{5,6},{6,7},{7,4},{8,9},{9,10},{10,1... | collective-permute-start | bytes 61448 | tf_op jit(solution)/shard_map/ppermute | solution.py:455
  5.7 1.0 %collective-permute-start.1 = (bf16[80,128]{1,0:T(8,128)(2,1)S(1)}, bf16[80,128]{1,0:T(8,128)(2,1)S(1)}, u32[]{:S(2)}, u32[]{:S(2)}) collective-permute-start(bf16[80,128]{1,0:T(8,128)(2,1)S(1)} %get-tuple-element.31), channel_id=1, source_target_pairs={{1,0},{2,1},{3,2},{0,3},{5,4},{6,5},{7,6},{4,7},{9,8},{10,9},{11,1... | collective-permute-start | bytes 61448 | tf_op jit(solution)/shard_map/ppermute | solution.py:456
  6.7 2.3 %shard_map.83 = (f32[6,1536,128]{2,1,0:T(8,128)S(1)}, f32[32,64,128]{2,1,0:T(8,128)S(1)}, f32[2,24,32,128]{3,2,1,0:T(8,128)S(1)}, f32[2,4,64,128]{3,2,1,0:T(8,128)S(1)}, f32[3,2,32]{2,1,0:T(2,128)S(1)}) custom-call(s32[8]{0:T(128)S(4)} %get-tuple-element.23.widths, f32[32,64]{1,0:T(8,128)S(1)} %get-tuple-element.24.stacked, ...), custom_call_target="tpu_custom_call", output_to_operand_aliasing={{0}: (3, {})} | custom-call | flops 1000000000 | bytes 1000000 | tf_op jit(solution)/shard_map/pallas_call | solution.py:458
  9.0 2.0 %collective-permute-start.2 = (f32[3,2,32]{2,1,0:T(2,128)S(1)}, f32[3,2,32]{2,1,0:T(2,128)S(1)}, u32[]{:S(2)}, u32[]{:S(2)}) collective-permute-start(f32[3,2,32]{2,1,0:T(2,128)S(1)} %get-tuple-element.34.refs_2_), channel_id=1, source_target_pairs={{0,2},{1,3},{2,0},{3,1},{4,6},{5,7},{6,4},{7,5},{8,10},{9,11},{10,... | collective-permute-start | bytes 2312 | tf_op jit(solution)/shard_map/ppermute | solution.py:474
  11.0 0.0 collective-permute-done.first.refs_0_
  11.0 0.0 collective-permute-done.1.second.refs_1_
  11.0 0.2 %shard_map.84 = (f32[2,64,128]{2,1,0:T(8,128)S(1)}, bf16[256,128]{1,0:T(8,128)(2,1)S(1)}, bf16[256,128]{1,0:T(8,128)(2,1)S(1)}) custom-call(s32[8]{0:T(128)S(4)} %get-tuple-element.23.widths, bf16[80,128]{1,0:T(8,128)(2,1)S(1)} %collective-permute-done.first.refs_0_, bf16[80,128]{1,0:T(8,128)(2,1)S(1)} %collective-permute-done.1.second.refs_1_, ...), custom_call_target="tpu_custom_call" | custom-call | tf_op jit(solution)/shard_map/pallas_call | solution.py:475
  11.2 2.2 %collective-permute-start.3 = (bf16[256,128]{1,0:T(8,128)(2,1)S(1)}, bf16[256,128]{1,0:T(8,128)(2,1)S(1)}, u32[]{:S(2)}, u32[]{:S(2)}) collective-permute-start(bf16[256,128]{1,0:T(8,128)(2,1)S(1)} %get-tuple-element.37), channel_id=1, source_target_pairs={{4,8},{8,4},{12,16},{16,12},{20,24},{24,20},{28,0},{0,28},{5,9},{9... | collective-permute-start | bytes 196616 | tf_op jit(solution)/shard_map/ppermute | solution.py:413
  13.4 0.0 collective-permute-start.4
  13.4 0.0 copy-start
  13.4 1.5 %shard_map.85.rest = f32[2,24,32,128]{3,2,1,0:T(8,128)S(1)} custom-call(f32[2,64,128]{2,1,0:T(8,128)S(1)} %get-tuple-element.33.edge, f32[6,1536,128]{2,1,0:T(8,128)S(1)} %get-tuple-element.28.cells, f32[32,64,128]{2,1,0:T(8,128)S(1)} %get-tuple-element.27.weights), custom_call_target="tpu_custom_call" | custom-call | flops 1000000000 | bytes 1000000 | tf_op jit(solution)/shard_map/pallas_call | solution.py:485
  14.9 0.0 collective-permute-done.2.refs_3_
  14.9 0.0 copy-done
  15.0 1.1 %shard_map.86 = (f32[2,1536,128]{2,1,0:T(8,128)S(1)}, f32[2,4,64,128]{3,2,1,0:T(8,128)S(1)}, f32[2,4,64,128]{3,2,1,0:T(8,128)S(1)}) custom-call(s32[8]{0:T(128)S(4)} %get-tuple-element.23.widths, bf16[64,64]{1,0:T(8,128)(2,1)S(1)} %copy-done, f32[6,1536,128]{2,1,0:T(8,128)S(1)} %get-tuple-element.28.cells, f32[32,64,128]{2,1,0:T(8,128)S(1)} %get-tuple-element.27.weights, ...), custom_call_target="tpu_custom_call" | custom-call | flops 1000000000 | bytes 1000000 | tf_op jit(solution)/shard_map/pallas_call | solution.py:494
  16.1 1.1 %collective-permute-done.3.far = bf16[256,128]{1,0:T(8,128)(2,1)S(1)} collective-permute-done((bf16[256,128]{1,0:T(8,128)(2,1)S(1)}, bf16[256,128]{1,0:T(8,128)(2,1)S(1)}, u32[]{:S(2)}, u32[]{:S(2)}) %collective-permute-start.3) | collective-permute-done | bytes 65568 | tf_op jit(solution)/shard_map/ppermute | solution.py:413
  17.2 0.0 collective-permute-done.4.near
  17.2 1.1 %shard_map.87 = (bf16[2,64,24,128]{3,2,1,0:T(8,128)(2,1)}, f32[2,1536,128]{2,1,0:T(8,128)S(1)}) custom-call(s32[8]{0:T(128)S(4)} %get-tuple-element.23.widths, bf16[64,64]{1,0:T(8,128)(2,1)S(1)} %copy-done, f32[32,64,128]{2,1,0:T(8,128)S(1)} %get-tuple-element.27.weights, ...), custom_call_target="tpu_custom_call", output_to_operand_aliasing={{1}: (7, {})} | custom-call | tf_op jit(solution)/shard_map/pallas_call | solution.py:504
Async XLA Ops:
  2.7 8.4 %collective-permute-start = (bf16[80,128]{1,0:T(8,128)(2,1)S(1)}, bf16[80,128]{1,0:T(8,128)(2,1)S(1)}, u32[]{:S(2)}, u32[]{:S(2)}) collective-permute-start(bf16[80,128]{1,0:T(8,128)(2,1)S(1)} %get-tuple-element.30), channel_id=1, source_target_pairs={{0,1},{1,2},{2,3},{3,0},{4,5},{5,6},{6,7},{7,4},{8,9},{9,10},{10,1... | collective-permute-start | bytes 61448 | tf_op jit(solution)/shard_map/ppermute | solution.py:455
  5.7 5.4 %collective-permute-start.1 = (bf16[80,128]{1,0:T(8,128)(2,1)S(1)}, bf16[80,128]{1,0:T(8,128)(2,1)S(1)}, u32[]{:S(2)}, u32[]{:S(2)}) collective-permute-start(bf16[80,128]{1,0:T(8,128)(2,1)S(1)} %get-tuple-element.31), channel_id=1, source_target_pairs={{1,0},{2,1},{3,2},{0,3},{5,4},{6,5},{7,6},{4,7},{9,8},{10,9},{11,1... | collective-permute-start | bytes 61448 | tf_op jit(solution)/shard_map/ppermute | solution.py:456
  9.0 5.9 %collective-permute-start.2 = (f32[3,2,32]{2,1,0:T(2,128)S(1)}, f32[3,2,32]{2,1,0:T(2,128)S(1)}, u32[]{:S(2)}, u32[]{:S(2)}) collective-permute-start(f32[3,2,32]{2,1,0:T(2,128)S(1)} %get-tuple-element.34.refs_2_), channel_id=1, source_target_pairs={{0,2},{1,3},{2,0},{3,1},{4,6},{5,7},{6,4},{7,5},{8,10},{9,11},{10,... | collective-permute-start | bytes 2312 | tf_op jit(solution)/shard_map/ppermute | solution.py:474
  11.2 6.0 %collective-permute-start.3 = (bf16[256,128]{1,0:T(8,128)(2,1)S(1)}, bf16[256,128]{1,0:T(8,128)(2,1)S(1)}, u32[]{:S(2)}, u32[]{:S(2)}) collective-permute-start(bf16[256,128]{1,0:T(8,128)(2,1)S(1)} %get-tuple-element.37), channel_id=1, source_target_pairs={{4,8},{8,4},{12,16},{16,12},{20,24},{24,20},{28,0},{0,28},{5,9},{9... | collective-permute-start | bytes 196616 | tf_op jit(solution)/shard_map/ppermute | solution.py:413
  13.4 3.8 %collective-permute-start.4 = (bf16[256,128]{1,0:T(8,128)(2,1)S(1)}, bf16[256,128]{1,0:T(8,128)(2,1)S(1)}, u32[]{:S(2)}, u32[]{:S(2)}) collective-permute-start(bf16[256,128]{1,0:T(8,128)(2,1)S(1)} %get-tuple-element.38), channel_id=1, source_target_pairs={{0,4},{4,0},{8,12},{12,8},{16,20},{20,16},{24,28},{28,24},{1,5},{5... | collective-permute-start | bytes 196616 | tf_op jit(solution)/shard_map/ppermute | solution.py:413
  13.4 1.5 %copy-start = (bf16[64,64]{1,0:T(8,128)(2,1)S(1)}, bf16[64,64]{1,0:T(8,128)(2,1)}, u32[]{:S(2)}) copy-start(bf16[64,64]{1,0:T(8,128)(2,1)} %mix.3) | copy-start | bytes 24580

commit v16 on v15

--- a/solution.py
+++ b/solution.py
@@ -11,7 +11,7 @@
 ZOUT = 2
 CF = 16
 ROWS = 8
-SPLIT = 4
+SPLIT = 2
 CHUNK = 16
 DW_BIAS, PW_BIAS, LIFT = 27, 28, 29
 F32 = jnp.float32
@@ -42,9 +42,11 @@
 ):
     count, channels, slots, tile = feature.shape
 
-    def copy_of(m):
-        at = pl.ds(ZOUT * m, ZOUT)
-        return pltpu.make_async_copy(feature.at[at], planes.at[at], sems.at[m])
+    half_of = channels // 2
+
+    def copy_of(m, part):
+        at = (pl.ds(ZOUT * m, ZOUT), pl.ds(part * half_of, half_of))
+        return pltpu.make_async_copy(feature.at[at], planes.at[at], sems.at[m, part])
 
     small = [
         pltpu.make_async_copy(source, target, small_sems.at[i])
@@ -62,7 +64,8 @@
     for copy in small:
         copy.start()
     for m in range(3):
-        copy_of(m).start()
+        for part in range(2):
+            copy_of(m, part).start()
     def weights_by_lane():
         for copy in small:
             copy.wait()
@@ -131,10 +134,11 @@
         )
 
     for m in range(3):
-        copy_of(m).wait()
-        for c in range(0, channels, ROWS):
-            for half, part in enumerate(summed(m, c, ROWS // 2)):
-                picked[m, half, c : c + ROWS, :] = part
+        for part in range(2):
+            copy_of(m, part).wait()
+            for c in range(part * half_of, (part + 1) * half_of, ROWS):
+                for half, total in enumerate(summed(m, c, ROWS // 2)):
+                    picked[m, half, c : c + ROWS, :] = total
         if m == 0:
             scale = weights_by_lane()
     width = widths_here[lax.axis_index("gx")]
@@ -197,7 +201,7 @@
                         depth[z, out, to, :] = shifted_sum(*(sums.pop((out, dy)) for dy in (-1, 0, 1)))
 
 
-def conv_kernel(widths, stacked, coarse, cells_in, cells, weights, depth, rims, own_block):
+def spread_kernel(widths, stacked, coarse, cells_in, cells, weights, own_block):
     width = widths[lax.axis_index("gx")]
     channels, tile = weights.shape[1:]
     slots = cells.shape[1] // channels
@@ -212,6 +216,11 @@
             for z in range(cells.shape[0]):
                 cells[z, pl.ds(width + r, channels, stride=slots), :] = jnp.zeros((channels, tile), F32)
 
+
+def conv_kernel(widths, cells, weights, depth, rims):
+    width = widths[lax.axis_index("gx")]
+    channels, tile = weights.shape[1:]
+    slots = cells.shape[1] // channels
     for b in range(channels // ROWS):
         at = slice(b * ROWS, (b + 1) * ROWS)
         for side, dx in enumerate((1, -1)):
@@ -447,7 +456,7 @@
             pltpu.VMEM(coarse.shape, F32),
             pltpu.VMEM((16, tile), F32),
             pltpu.VMEM((3, 2, channels, tile), F32),
-            pltpu.SemaphoreType.DMA((3,)),
+            pltpu.SemaphoreType.DMA((3, 2)),
             pltpu.SemaphoreType.DMA((len(small),)),
         ],
         compiler_params=params,
@@ -455,23 +464,28 @@
     first = lax.ppermute(first, "gy", [(i, (i + 1) % ny) for i in range(ny)])
     second = lax.ppermute(second, "gy", [((i + 1) % ny, i) for i in range(ny)])
     early = SPLIT * ROWS
-    cells, weights, depth, rims, own_block = pl.pallas_call(
-        conv_kernel,
-        out_shape=(
-            cells_shape,
-            pltpu.VMEM((32, channels, tile), F32),
-            pltpu.VMEM((ZOUT, slots, early, tile), F32),
-            pltpu.VMEM((ZOUT, 4, channels, tile), F32),
-            pltpu.VMEM(coarse.shape, F32),
-        ),
+    cells, weights, own_block = pl.pallas_call(
+        spread_kernel,
+        out_shape=(cells_shape, pltpu.VMEM((32, channels, tile), F32), pltpu.VMEM(coarse.shape, F32)),
         in_specs=[smem] + [vmem] * 3,
-        out_specs=(vmem,) * 5,
+        out_specs=(vmem,) * 3,
         input_output_aliases={3: 0},
         compiler_params=params,
-        cost_estimate=pl.CostEstimate(flops=10**9, bytes_accessed=10**6, transcendentals=0),
+        cost_estimate=pl.CostEstimate(flops=10**8, bytes_accessed=10**6, transcendentals=0),
     )(slab_widths, stacked, block, cells)
     if not gathered:
         opposite = lax.ppermute(own_block, "gy", [(i, (i + 2) % 4) for i in range(4)])
+    depth, rims = pl.pallas_call(
+        conv_kernel,
+        out_shape=(
+            pltpu.VMEM((ZOUT, slots, early, tile), F32),
+            pltpu.VMEM((ZOUT, 4, channels, tile), F32),
+        ),
+        in_specs=[smem] + [vmem] * 2,
+        out_specs=(vmem,) * 2,
+        compiler_params=params,
+        cost_estimate=pl.CostEstimate(flops=10**9, bytes_accessed=10**6, transcendentals=0),
+    )(slab_widths, cells, weights)
     edge, far, near = pl.pallas_call(
         rim_kernel,
         out_shape=(pltpu.VMEM((2, channels, tile), F32), message, message),

time: 18.5 us -> 17.8 us (0.962)
  waiting for transfers between devices: 1.1 us -> 0.17 us
    ppermute x2, waiting for transfers between devices: 1.09 us -> 0.16 us  [swapped(): return lax.ppermute(array, axis, pairs)]
    pallas_call x1 -> x2, Pallas kernels: 2.34 us -> 1.5 us  [the longest x1 1.02 us: shards(): pl.pallas_call(conv_kernel, out_shape=(pltpu.VMEM((ZOUT, slots, early, ti...]
    pallas_call x1, Pallas kernels: 1.49 us -> 2.23 us  [shards(): pl.pallas_call(rest_kernel, out_shape=pltpu.VMEM((ZOUT, slots, channels -...]
  transfers between devices with their start and end apart: 5 -> 5, of which waited for: 1 -> 1; matrix products, arithmetic and copies ran while one was open for 0% -> 0% of each run, Pallas kernels for 28% -> 29%
where the time goes in v16:
time: 17.8 us; the launch traced here: 17.6 us
  Pallas kernels  8.95 us (50%)
  starting transfers between devices  8.35 us (47%)
    ppermute x1, starting transfers between devices, shards(): first = lax.ppermute(first, 'gy', [(i, (i + 1) % ny) for i in range(ny)])  2.99 us
    pallas_call x1, Pallas kernels, shards(): pl.pallas_call(pack_kernel, out_shape=(cells_shape, strip, strip, pltpu.V...  2.75 us
    ppermute x2, starting transfers between devices, swapped(): return lax.ppermute(array, axis, pairs)  2.34 us
    pallas_call x1, Pallas kernels, shards(): pl.pallas_call(rest_kernel, out_shape=pltpu.VMEM((ZOUT, slots, channels -...  2.23 us
    ppermute x1, starting transfers between devices, shards(): lax.ppermute(own_block, 'gy', [(i, (i + 2) % 4) for i in range(4)])  2 us
    pallas_call x1, Pallas kernels, shards(): pl.pallas_call(finish_kernel, out_shape=(shape((ZOUT, channels, slots, ti...  1.14 us
    pallas_call x1, Pallas kernels, shards(): pl.pallas_call(functools.partial(mix_kernel, gathered), out_shape=(value_...  1.14 us
    pallas_call x1, Pallas kernels, shards(): pl.pallas_call(conv_kernel, out_shape=(pltpu.VMEM((ZOUT, slots, early, ti...  1.02 us
  transfers between devices with their start and end apart: 5, of which 1 were waited for; matrix products, arithmetic and copies ran while one was open for 0% of the time, Pallas kernels for 29%

profile of v16, /device:TPU:0, one launch (start us, length us, event | category | flops | bytes accessed | tf_op | source)
XLA Modules:
  0.0 17.6 jit_solution(12158611246896535091)
XLA Ops:
  0.0 2.8 %shard_map.82 = (f32[6,1536,128]{2,1,0:T(8,128)S(1)}, bf16[80,128]{1,0:T(8,128)(2,1)S(1)}, bf16[80,128]{1,0:T(8,128)(2,1)S(1)}, f32[32,64]{1,0:T(8,128)S(1)}, f32[3,2,32]{2,1,0:T(2,128)S(1)}, /*index=5*/s32[8]{0:T(128)S(4)}) custom-call(bf16[6,64,24,128]{3,2,1,0:T(8,128)(2,1)} %feature.1, s32[8]{0:T(128)} %widths_in.1, f32[27,64]{1,0:T(8,128)} %taps_in.1, ...), custom_call_target="tpu_custom_call" | custom-call | tf_op jit(solution)/shard_map/pallas_call | solution.py:437
  2.8 3.0 %collective-permute-start = (bf16[80,128]{1,0:T(8,128)(2,1)S(1)}, bf16[80,128]{1,0:T(8,128)(2,1)S(1)}, u32[]{:S(2)}, u32[]{:S(2)}) collective-permute-start(bf16[80,128]{1,0:T(8,128)(2,1)S(1)} %get-tuple-element.30), channel_id=1, source_target_pairs={{0,1},{1,2},{2,3},{3,0},{4,5},{5,6},{6,7},{7,4},{8,9},{9,10},{10,1... | collective-permute-start | bytes 61448 | tf_op jit(solution)/shard_map/ppermute | solution.py:464
  5.8 1.0 %collective-permute-start.1 = (bf16[80,128]{1,0:T(8,128)(2,1)S(1)}, bf16[80,128]{1,0:T(8,128)(2,1)S(1)}, u32[]{:S(2)}, u32[]{:S(2)}) collective-permute-start(bf16[80,128]{1,0:T(8,128)(2,1)S(1)} %get-tuple-element.31), channel_id=1, source_target_pairs={{1,0},{2,1},{3,2},{0,3},{5,4},{6,5},{7,6},{4,7},{9,8},{10,9},{11,1... | collective-permute-start | bytes 61448 | tf_op jit(solution)/shard_map/ppermute | solution.py:465
  6.8 0.5 %shard_map.83 = (f32[6,1536,128]{2,1,0:T(8,128)S(1)}, f32[32,64,128]{2,1,0:T(8,128)S(1)}, f32[3,2,32]{2,1,0:T(2,128)S(1)}) custom-call(s32[8]{0:T(128)S(4)} %get-tuple-element.23.widths, f32[32,64]{1,0:T(8,128)S(1)} %get-tuple-element.24.stacked, f32[3,2,32]{2,1,0:T(2,128)S(1)} %get-tuple-element.25.coarse, ...), custom_call_target="tpu_custom_call", output_to_operand_aliasing={{0}: (3, {})} | custom-call | flops 100000000 | bytes 1000000 | tf_op jit(solution)/shard_map/pallas_call | solution.py:467
  7.3 2.0 %collective-permute-start.2 = (f32[3,2,32]{2,1,0:T(2,128)S(1)}, f32[3,2,32]{2,1,0:T(2,128)S(1)}, u32[]{:S(2)}, u32[]{:S(2)}) collective-permute-start(f32[3,2,32]{2,1,0:T(2,128)S(1)} %get-tuple-element.34.refs_2_), channel_id=1, source_target_pairs={{0,2},{1,3},{2,0},{3,1},{4,6},{5,7},{6,4},{7,5},{8,10},{9,11},{10,... | collective-permute-start | bytes 2312 | tf_op jit(solution)/shard_map/ppermute | solution.py:477
  9.3 1.0 %shard_map.84 = (f32[2,24,16,128]{3,2,1,0:T(8,128)S(1)}, f32[2,4,64,128]{3,2,1,0:T(8,128)S(1)}) custom-call(s32[8]{0:T(128)S(4)} %get-tuple-element.23.widths, f32[6,1536,128]{2,1,0:T(8,128)S(1)} %get-tuple-element.28.cells, f32[32,64,128]{2,1,0:T(8,128)S(1)} %get-tuple-element.27.weights), custom_call_target="tpu_custom_call" | custom-call | flops 1000000000 | bytes 1000000 | tf_op jit(solution)/shard_map/pallas_call | solution.py:478
  10.3 0.0 collective-permute-done.first.refs_0_
  10.3 0.0 collective-permute-done.1.second.refs_1_
  10.3 0.2 %shard_map.85 = (f32[2,64,128]{2,1,0:T(8,128)S(1)}, bf16[256,128]{1,0:T(8,128)(2,1)S(1)}, bf16[256,128]{1,0:T(8,128)(2,1)S(1)}) custom-call(s32[8]{0:T(128)S(4)} %get-tuple-element.23.widths, bf16[80,128]{1,0:T(8,128)(2,1)S(1)} %collective-permute-done.first.refs_0_, bf16[80,128]{1,0:T(8,128)(2,1)S(1)} %collective-permute-done.1.second.refs_1_, ...), custom_call_target="tpu_custom_call" | custom-call | tf_op jit(solution)/shard_map/pallas_call | solution.py:489
  10.5 2.3 %collective-permute-start.3 = (bf16[256,128]{1,0:T(8,128)(2,1)S(1)}, bf16[256,128]{1,0:T(8,128)(2,1)S(1)}, u32[]{:S(2)}, u32[]{:S(2)}) collective-permute-start(bf16[256,128]{1,0:T(8,128)(2,1)S(1)} %get-tuple-element.37), channel_id=1, source_target_pairs={{4,8},{8,4},{12,16},{16,12},{20,24},{24,20},{28,0},{0,28},{5,9},{9... | collective-permute-start | bytes 196616 | tf_op jit(solution)/shard_map/ppermute | solution.py:422
  12.8 0.0 collective-permute-start.4
  12.8 0.0 copy-start
  12.8 2.2 %shard_map.86.rest = f32[2,24,48,128]{3,2,1,0:T(8,128)S(1)} custom-call(f32[2,64,128]{2,1,0:T(8,128)S(1)} %get-tuple-element.33.edge, f32[6,1536,128]{2,1,0:T(8,128)S(1)} %get-tuple-element.28.cells, f32[32,64,128]{2,1,0:T(8,128)S(1)} %get-tuple-element.27.weights), custom_call_target="tpu_custom_call" | custom-call | flops 1000000000 | bytes 1000000 | tf_op jit(solution)/shard_map/pallas_call | solution.py:499
  15.1 0.0 collective-permute-done.2.refs_3_
  15.1 0.0 copy-done
  15.1 1.1 %shard_map.87 = (f32[2,1536,128]{2,1,0:T(8,128)S(1)}, f32[2,4,64,128]{3,2,1,0:T(8,128)S(1)}, f32[2,4,64,128]{3,2,1,0:T(8,128)S(1)}) custom-call(s32[8]{0:T(128)S(4)} %get-tuple-element.23.widths, bf16[64,64]{1,0:T(8,128)(2,1)S(1)} %copy-done, f32[6,1536,128]{2,1,0:T(8,128)S(1)} %get-tuple-element.28.cells, f32[32,64,128]{2,1,0:T(8,128)S(1)} %get-tuple-element.27.weights, ...), custom_call_target="tpu_custom_call" | custom-call | flops 1000000000 | bytes 1000000 | tf_op jit(solution)/shard_map/pallas_call | solution.py:508
  16.2 0.2 collective-permute-done.3.far
  16.4 0.0 collective-permute-done.4.near
  16.4 1.1 %shard_map.88 = (bf16[2,64,24,128]{3,2,1,0:T(8,128)(2,1)}, f32[2,1536,128]{2,1,0:T(8,128)S(1)}) custom-call(s32[8]{0:T(128)S(4)} %get-tuple-element.23.widths, bf16[64,64]{1,0:T(8,128)(2,1)S(1)} %copy-done, f32[32,64,128]{2,1,0:T(8,128)S(1)} %get-tuple-element.27.weights, ...), custom_call_target="tpu_custom_call", output_to_operand_aliasing={{1}: (7, {})} | custom-call | tf_op jit(solution)/shard_map/pallas_call | solution.py:518
Async XLA Ops:
  2.8 7.5 %collective-permute-start = (bf16[80,128]{1,0:T(8,128)(2,1)S(1)}, bf16[80,128]{1,0:T(8,128)(2,1)S(1)}, u32[]{:S(2)}, u32[]{:S(2)}) collective-permute-start(bf16[80,128]{1,0:T(8,128)(2,1)S(1)} %get-tuple-element.30), channel_id=1, source_target_pairs={{0,1},{1,2},{2,3},{3,0},{4,5},{5,6},{6,7},{7,4},{8,9},{9,10},{10,1... | collective-permute-start | bytes 61448 | tf_op jit(solution)/shard_map/ppermute | solution.py:464
  5.8 4.5 %collective-permute-start.1 = (bf16[80,128]{1,0:T(8,128)(2,1)S(1)}, bf16[80,128]{1,0:T(8,128)(2,1)S(1)}, u32[]{:S(2)}, u32[]{:S(2)}) collective-permute-start(bf16[80,128]{1,0:T(8,128)(2,1)S(1)} %get-tuple-element.31), channel_id=1, source_target_pairs={{1,0},{2,1},{3,2},{0,3},{5,4},{6,5},{7,6},{4,7},{9,8},{10,9},{11,1... | collective-permute-start | bytes 61448 | tf_op jit(solution)/shard_map/ppermute | solution.py:465
  7.3 7.8 %collective-permute-start.2 = (f32[3,2,32]{2,1,0:T(2,128)S(1)}, f32[3,2,32]{2,1,0:T(2,128)S(1)}, u32[]{:S(2)}, u32[]{:S(2)}) collective-permute-start(f32[3,2,32]{2,1,0:T(2,128)S(1)} %get-tuple-element.34.refs_2_), channel_id=1, source_target_pairs={{0,2},{1,3},{2,0},{3,1},{4,6},{5,7},{6,4},{7,5},{8,10},{9,11},{10,... | collective-permute-start | bytes 2312 | tf_op jit(solution)/shard_map/ppermute | solution.py:477
  10.5 5.9 %collective-permute-start.3 = (bf16[256,128]{1,0:T(8,128)(2,1)S(1)}, bf16[256,128]{1,0:T(8,128)(2,1)S(1)}, u32[]{:S(2)}, u32[]{:S(2)}) collective-permute-start(bf16[256,128]{1,0:T(8,128)(2,1)S(1)} %get-tuple-element.37), channel_id=1, source_target_pairs={{4,8},{8,4},{12,16},{16,12},{20,24},{24,20},{28,0},{0,28},{5,9},{9... | collective-permute-start | bytes 196616 | tf_op jit(solution)/shard_map/ppermute | solution.py:422
  12.8 3.6 %collective-permute-start.4 = (bf16[256,128]{1,0:T(8,128)(2,1)S(1)}, bf16[256,128]{1,0:T(8,128)(2,1)S(1)}, u32[]{:S(2)}, u32[]{:S(2)}) collective-permute-start(bf16[256,128]{1,0:T(8,128)(2,1)S(1)} %get-tuple-element.38), channel_id=1, source_target_pairs={{0,4},{4,0},{8,12},{12,8},{16,20},{20,16},{24,28},{28,24},{1,5},{5... | collective-permute-start | bytes 196616 | tf_op jit(solution)/shard_map/ppermute | solution.py:422
  12.8 2.3 %copy-start = (bf16[64,64]{1,0:T(8,128)(2,1)S(1)}, bf16[64,64]{1,0:T(8,128)(2,1)}, u32[]{:S(2)}) copy-start(bf16[64,64]{1,0:T(8,128)(2,1)} %mix.3) | copy-start | bytes 24580

commit v17 on v16

--- a/solution.py
+++ b/solution.py
@@ -37,8 +37,8 @@
 
 def pack_kernel(
     feature, widths_in, taps_in, dw_bias_in, pw_bias_in, lift_in, coarse_in,
-    cells, first, second, stacked, own_block, widths,
-    planes, widths_here, taps, dw_bias, pw_bias, lift, coarse, tail, picked, sems, small_sems,
+    cells, weights, first, second, own_block, widths,
+    planes, widths_here, taps, dw_bias, pw_bias, lift, coarse, stacked, tail, picked, sems, small_sems,
 ):
     count, channels, slots, tile = feature.shape
 
@@ -75,6 +75,9 @@
         stacked[DW_BIAS : DW_BIAS + 1, :] = dw_bias[...]
         stacked[PW_BIAS : PW_BIAS + 1, :] = pw_bias[...]
         stacked[LIFT : LIFT + 3, :] = lift[...]
+        turned = jnp.transpose(stacked[...])
+        for t in range(stacked.shape[0]):
+            weights[t] = jnp.broadcast_to(turned[:, t : t + 1], (channels, tile))
 
         own_block[...] = coarse[...]
         parts, own_rows, ncy = coarse.shape
@@ -201,26 +204,11 @@
                         depth[z, out, to, :] = shifted_sum(*(sums.pop((out, dy)) for dy in (-1, 0, 1)))
 
 
-def spread_kernel(widths, stacked, coarse, cells_in, cells, weights, own_block):
+def outer_kernel(widths, weights, coarse, cells_in, cells, rims, own_block):
     width = widths[lax.axis_index("gx")]
     channels, tile = weights.shape[1:]
     slots = cells.shape[1] // channels
     own_block[...] = coarse[...]
-    turned = jnp.transpose(stacked[...])
-    for t in range(stacked.shape[0]):
-        weights[t] = jnp.broadcast_to(turned[:, t : t + 1], (channels, tile))
-    for r in range(2):
-
-        @pl.when(width + r < slots)
-        def _():
-            for z in range(cells.shape[0]):
-                cells[z, pl.ds(width + r, channels, stride=slots), :] = jnp.zeros((channels, tile), F32)
-
-
-def conv_kernel(widths, cells, weights, depth, rims):
-    width = widths[lax.axis_index("gx")]
-    channels, tile = weights.shape[1:]
-    slots = cells.shape[1] // channels
     for b in range(channels // ROWS):
         at = slice(b * ROWS, (b + 1) * ROWS)
         for side, dx in enumerate((1, -1)):
@@ -233,7 +221,15 @@
                     ]
                     parts = [sum(weight * row for weight, row in zip(weights_of, rows)) for weights_of in tap]
                     rims[z, 2 * side + r, at, :] = shifted_sum(*parts)
-
+    for r in range(2):
+
+        @pl.when(width + r < slots)
+        def _():
+            for z in range(cells.shape[0]):
+                cells[z, pl.ds(width + r, channels, stride=slots), :] = jnp.zeros((channels, tile), F32)
+
+
+def conv_kernel(cells, weights, depth):
     def convolve(b, carry):
         convolve_block(cells, weights, depth, b, 0)
         return carry
@@ -434,13 +430,13 @@
         lift_weight.T,
         coarse,
     )
-    cells, first, second, stacked, block, slab_widths = pl.pallas_call(
+    cells, weights, first, second, block, slab_widths = pl.pallas_call(
         pack_kernel,
         out_shape=(
             cells_shape,
+            pltpu.VMEM((32, channels, tile), F32),
             strip,
             strip,
-            pltpu.VMEM((32, channels), F32),
             pltpu.VMEM(coarse.shape, F32),
             pltpu.SMEM(widths.shape, jnp.int32),
         ),
@@ -454,6 +450,7 @@
             pltpu.VMEM((1, channels), F32),
             pltpu.VMEM((parts, channels), F32),
             pltpu.VMEM(coarse.shape, F32),
+            pltpu.VMEM((32, channels), F32),
             pltpu.VMEM((16, tile), F32),
             pltpu.VMEM((3, 2, channels, tile), F32),
             pltpu.SemaphoreType.DMA((3, 2)),
@@ -464,28 +461,29 @@
     first = lax.ppermute(first, "gy", [(i, (i + 1) % ny) for i in range(ny)])
     second = lax.ppermute(second, "gy", [((i + 1) % ny, i) for i in range(ny)])
     early = SPLIT * ROWS
-    cells, weights, own_block = pl.pallas_call(
-        spread_kernel,
-        out_shape=(cells_shape, pltpu.VMEM((32, channels, tile), F32), pltpu.VMEM(coarse.shape, F32)),
+    cells, rims, own_block = pl.pallas_call(
+        outer_kernel,
+        out_shape=(
+            cells_shape,
+            pltpu.VMEM((ZOUT, 4, channels, tile), F32),
+            pltpu.VMEM(coarse.shape, F32),
+        ),
         in_specs=[smem] + [vmem] * 3,
         out_specs=(vmem,) * 3,
         input_output_aliases={3: 0},
         compiler_params=params,
         cost_estimate=pl.CostEstimate(flops=10**8, bytes_accessed=10**6, transcendentals=0),
-    )(slab_widths, stacked, block, cells)
+    )(slab_widths, weights, block, cells)
     if not gathered:
         opposite = lax.ppermute(own_block, "gy", [(i, (i + 2) % 4) for i in range(4)])
-    depth, rims = pl.pallas_call(
+    depth = pl.pallas_call(
         conv_kernel,
-        out_shape=(
-            pltpu.VMEM((ZOUT, slots, early, tile), F32),
-            pltpu.VMEM((ZOUT, 4, channels, tile), F32),
-        ),
-        in_specs=[smem] + [vmem] * 2,
-        out_specs=(vmem,) * 2,
+        out_shape=pltpu.VMEM((ZOUT, slots, early, tile), F32),
+        in_specs=[vmem] * 2,
+        out_specs=vmem,
         compiler_params=params,
         cost_estimate=pl.CostEstimate(flops=10**9, bytes_accessed=10**6, transcendentals=0),
-    )(slab_widths, cells, weights)
+    )(cells, weights)
     edge, far, near = pl.pallas_call(
         rim_kernel,
         out_shape=(pltpu.VMEM((2, channels, tile), F32), message, message),

time: 17.8 us -> 17.6 us (0.989)
  waiting for transfers between devices: 0.17 us -> 0.41 us
  Pallas kernels: 8.95 us -> 8.77 us
    ppermute x2, waiting for transfers between devices: 0.16 us -> 0.41 us  [swapped(): return lax.ppermute(array, axis, pairs)]
  transfers between devices with their start and end apart: 5 -> 5, of which waited for: 1 -> 1; matrix products, arithmetic and copies ran while one was open for 0% -> 0% of each run, Pallas kernels for 29% -> 27%
where the time goes in v17:
time: 17.6 us; the launch traced here: 17.5 us
  Pallas kernels  8.77 us (50%)
  starting transfers between devices  8.19 us (47%)
  waiting for transfers between devices  0.41 us (2%)
    ppermute x1, starting transfers between devices, shards(): first = lax.ppermute(first, 'gy', [(i, (i + 1) % ny) for i in range(ny)])  2.99 us
    pallas_call x1, Pallas kernels, shards(): pl.pallas_call(pack_kernel, out_shape=(cells_shape, pltpu.VMEM((32, chann...  2.98 us
    pallas_call x1, Pallas kernels, shards(): pl.pallas_call(rest_kernel, out_shape=pltpu.VMEM((ZOUT, slots, channels -...  2.23 us
    ppermute x2, starting transfers between devices, swapped(): return lax.ppermute(array, axis, pairs)  2.18 us
    ppermute x1, starting transfers between devices, shards(): lax.ppermute(own_block, 'gy', [(i, (i + 2) % 4) for i in range(4)])  2 us
    pallas_call x1, Pallas kernels, shards(): pl.pallas_call(finish_kernel, out_shape=(shape((ZOUT, channels, slots, ti...  1.14 us
    pallas_call x1, Pallas kernels, shards(): pl.pallas_call(functools.partial(mix_kernel, gathered), out_shape=(value_...  1.13 us
    ppermute x1, starting transfers between devices, shards(): second = lax.ppermute(second, 'gy', [((i + 1) % ny, i) for i in range(ny)])  1.02 us
  transfers between devices with their start and end apart: 5, of which 1 were waited for; matrix products, arithmetic and copies ran while one was open for 0% of the time, Pallas kernels for 27%

profile of v17, /device:TPU:0, one launch (start us, length us, event | category | flops | bytes accessed | tf_op | source)
XLA Modules:
  0.0 17.5 jit_solution(12299939789254204236)
XLA Ops:
  0.0 3.0 %shard_map.82 = (f32[6,1536,128]{2,1,0:T(8,128)S(1)}, f32[32,64,128]{2,1,0:T(8,128)S(1)}, bf16[80,128]{1,0:T(8,128)(2,1)S(1)}, bf16[80,128]{1,0:T(8,128)(2,1)S(1...) custom-call(bf16[6,64,24,128]{3,2,1,0:T(8,128)(2,1)} %feature.1, s32[8]{0:T(128)} %widths_in.1, f32[27,64]{1,0:T(8,128)} %taps_in.1, ...), custom_call_target="tpu_custom_call" | custom-call | tf_op jit(solution)/shard_map/pallas_call | solution.py:433
  3.0 3.0 %collective-permute-start = (bf16[80,128]{1,0:T(8,128)(2,1)S(1)}, bf16[80,128]{1,0:T(8,128)(2,1)S(1)}, u32[]{:S(2)}, u32[]{:S(2)}) collective-permute-start(bf16[80,128]{1,0:T(8,128)(2,1)S(1)} %get-tuple-element.26), channel_id=1, source_target_pairs={{0,1},{1,2},{2,3},{3,0},{4,5},{5,6},{6,7},{7,4},{8,9},{9,10},{10,1... | collective-permute-start | bytes 61448 | tf_op jit(solution)/shard_map/ppermute | solution.py:461
  6.0 1.0 %collective-permute-start.1 = (bf16[80,128]{1,0:T(8,128)(2,1)S(1)}, bf16[80,128]{1,0:T(8,128)(2,1)S(1)}, u32[]{:S(2)}, u32[]{:S(2)}) collective-permute-start(bf16[80,128]{1,0:T(8,128)(2,1)S(1)} %get-tuple-element.27), channel_id=1, source_target_pairs={{1,0},{2,1},{3,2},{0,3},{5,4},{6,5},{7,6},{4,7},{9,8},{10,9},{11,1... | collective-permute-start | bytes 61448 | tf_op jit(solution)/shard_map/ppermute | solution.py:462
  7.0 0.4 %shard_map.83 = (f32[6,1536,128]{2,1,0:T(8,128)S(1)}, f32[2,4,64,128]{3,2,1,0:T(8,128)S(1)}, f32[3,2,32]{2,1,0:T(2,128)S(1)}) custom-call(s32[8]{0:T(128)S(4)} %get-tuple-element.21.widths, f32[32,64,128]{2,1,0:T(8,128)S(1)} %get-tuple-element.22.weights, f32[3,2,32]{2,1,0:T(2,128)S(1)} %get-tuple-element.23.coarse, ...), custom_call_target="tpu_custom_call", output_to_operand_aliasing={{0}: (3, {})} | custom-call | flops 100000000 | bytes 1000000 | tf_op jit(solution)/shard_map/pallas_call | solution.py:464
  7.4 2.0 %collective-permute-start.2 = (f32[3,2,32]{2,1,0:T(2,128)S(1)}, f32[3,2,32]{2,1,0:T(2,128)S(1)}, u32[]{:S(2)}, u32[]{:S(2)}) collective-permute-start(f32[3,2,32]{2,1,0:T(2,128)S(1)} %get-tuple-element.30.refs_2_), channel_id=1, source_target_pairs={{0,2},{1,3},{2,0},{3,1},{4,6},{5,7},{6,4},{7,5},{8,10},{9,11},{10,... | collective-permute-start | bytes 2312 | tf_op jit(solution)/shard_map/ppermute | solution.py:478
  9.4 0.7 %shard_map.84.depth = f32[2,24,16,128]{3,2,1,0:T(8,128)S(1)} custom-call(f32[6,1536,128]{2,1,0:T(8,128)S(1)} %get-tuple-element.25.cells, f32[32,64,128]{2,1,0:T(8,128)S(1)} %get-tuple-element.22.weights), custom_call_target="tpu_custom_call" | custom-call | flops 1000000000 | bytes 1000000 | tf_op jit(solution)/shard_map/pallas_call | solution.py:479
  10.1 0.0 collective-permute-done.first.refs_0_
  10.1 0.0 collective-permute-done.1.second.refs_1_
  10.1 0.2 %shard_map.85 = (f32[2,64,128]{2,1,0:T(8,128)S(1)}, bf16[256,128]{1,0:T(8,128)(2,1)S(1)}, bf16[256,128]{1,0:T(8,128)(2,1)S(1)}) custom-call(s32[8]{0:T(128)S(4)} %get-tuple-element.21.widths, bf16[80,128]{1,0:T(8,128)(2,1)S(1)} %collective-permute-done.first.refs_0_, bf16[80,128]{1,0:T(8,128)(2,1)S(1)} %collective-permute-done.1.second.refs_1_, ...), custom_call_target="tpu_custom_call" | custom-call | tf_op jit(solution)/shard_map/pallas_call | solution.py:487
  10.3 2.2 %collective-permute-start.3 = (bf16[256,128]{1,0:T(8,128)(2,1)S(1)}, bf16[256,128]{1,0:T(8,128)(2,1)S(1)}, u32[]{:S(2)}, u32[]{:S(2)}) collective-permute-start(bf16[256,128]{1,0:T(8,128)(2,1)S(1)} %get-tuple-element.33), channel_id=1, source_target_pairs={{4,8},{8,4},{12,16},{16,12},{20,24},{24,20},{28,0},{0,28},{5,9},{9... | collective-permute-start | bytes 196616 | tf_op jit(solution)/shard_map/ppermute | solution.py:418
  12.5 0.0 collective-permute-start.4
  12.5 0.0 copy-start
  12.5 2.2 %shard_map.86.rest = f32[2,24,48,128]{3,2,1,0:T(8,128)S(1)} custom-call(f32[2,64,128]{2,1,0:T(8,128)S(1)} %get-tuple-element.29.edge, f32[6,1536,128]{2,1,0:T(8,128)S(1)} %get-tuple-element.25.cells, f32[32,64,128]{2,1,0:T(8,128)S(1)} %get-tuple-element.22.weights), custom_call_target="tpu_custom_call" | custom-call | flops 1000000000 | bytes 1000000 | tf_op jit(solution)/shard_map/pallas_call | solution.py:497
  14.8 0.0 collective-permute-done.2.refs_3_
  14.8 0.0 copy-done
  14.8 1.1 %shard_map.87 = (f32[2,1536,128]{2,1,0:T(8,128)S(1)}, f32[2,4,64,128]{3,2,1,0:T(8,128)S(1)}, f32[2,4,64,128]{3,2,1,0:T(8,128)S(1)}) custom-call(s32[8]{0:T(128)S(4)} %get-tuple-element.21.widths, bf16[64,64]{1,0:T(8,128)(2,1)S(1)} %copy-done, f32[6,1536,128]{2,1,0:T(8,128)S(1)} %get-tuple-element.25.cells, f32[32,64,128]{2,1,0:T(8,128)S(1)} %get-tuple-element.22.weights, ...), custom_call_target="tpu_custom_call" | custom-call | flops 1000000000 | bytes 1000000 | tf_op jit(solution)/shard_map/pallas_call | solution.py:506
  15.9 0.4 %collective-permute-done.3.far = bf16[256,128]{1,0:T(8,128)(2,1)S(1)} collective-permute-done((bf16[256,128]{1,0:T(8,128)(2,1)S(1)}, bf16[256,128]{1,0:T(8,128)(2,1)S(1)}, u32[]{:S(2)}, u32[]{:S(2)}) %collective-permute-start.3) | collective-permute-done | bytes 65568 | tf_op jit(solution)/shard_map/ppermute | solution.py:418
  16.3 0.0 collective-permute-done.4.near
  16.3 1.1 %shard_map.88 = (bf16[2,64,24,128]{3,2,1,0:T(8,128)(2,1)}, f32[2,1536,128]{2,1,0:T(8,128)S(1)}) custom-call(s32[8]{0:T(128)S(4)} %get-tuple-element.21.widths, bf16[64,64]{1,0:T(8,128)(2,1)S(1)} %copy-done, f32[32,64,128]{2,1,0:T(8,128)S(1)} %get-tuple-element.22.weights, ...), custom_call_target="tpu_custom_call", output_to_operand_aliasing={{1}: (7, {})} | custom-call | tf_op jit(solution)/shard_map/pallas_call | solution.py:516
Async XLA Ops:
  3.0 7.1 %collective-permute-start = (bf16[80,128]{1,0:T(8,128)(2,1)S(1)}, bf16[80,128]{1,0:T(8,128)(2,1)S(1)}, u32[]{:S(2)}, u32[]{:S(2)}) collective-permute-start(bf16[80,128]{1,0:T(8,128)(2,1)S(1)} %get-tuple-element.26), channel_id=1, source_target_pairs={{0,1},{1,2},{2,3},{3,0},{4,5},{5,6},{6,7},{7,4},{8,9},{9,10},{10,1... | collective-permute-start | bytes 61448 | tf_op jit(solution)/shard_map/ppermute | solution.py:461
  6.0 4.2 %collective-permute-start.1 = (bf16[80,128]{1,0:T(8,128)(2,1)S(1)}, bf16[80,128]{1,0:T(8,128)(2,1)S(1)}, u32[]{:S(2)}, u32[]{:S(2)}) collective-permute-start(bf16[80,128]{1,0:T(8,128)(2,1)S(1)} %get-tuple-element.27), channel_id=1, source_target_pairs={{1,0},{2,1},{3,2},{0,3},{5,4},{6,5},{7,6},{4,7},{9,8},{10,9},{11,1... | collective-permute-start | bytes 61448 | tf_op jit(solution)/shard_map/ppermute | solution.py:462
  7.4 7.4 %collective-permute-start.2 = (f32[3,2,32]{2,1,0:T(2,128)S(1)}, f32[3,2,32]{2,1,0:T(2,128)S(1)}, u32[]{:S(2)}, u32[]{:S(2)}) collective-permute-start(f32[3,2,32]{2,1,0:T(2,128)S(1)} %get-tuple-element.30.refs_2_), channel_id=1, source_target_pairs={{0,2},{1,3},{2,0},{3,1},{4,6},{5,7},{6,4},{7,5},{8,10},{9,11},{10,... | collective-permute-start | bytes 2312 | tf_op jit(solution)/shard_map/ppermute | solution.py:478
  10.3 6.0 %collective-permute-start.3 = (bf16[256,128]{1,0:T(8,128)(2,1)S(1)}, bf16[256,128]{1,0:T(8,128)(2,1)S(1)}, u32[]{:S(2)}, u32[]{:S(2)}) collective-permute-start(bf16[256,128]{1,0:T(8,128)(2,1)S(1)} %get-tuple-element.33), channel_id=1, source_target_pairs={{4,8},{8,4},{12,16},{16,12},{20,24},{24,20},{28,0},{0,28},{5,9},{9... | collective-permute-start | bytes 196616 | tf_op jit(solution)/shard_map/ppermute | solution.py:418
  12.5 3.8 %collective-permute-start.4 = (bf16[256,128]{1,0:T(8,128)(2,1)S(1)}, bf16[256,128]{1,0:T(8,128)(2,1)S(1)}, u32[]{:S(2)}, u32[]{:S(2)}) collective-permute-start(bf16[256,128]{1,0:T(8,128)(2,1)S(1)} %get-tuple-element.34), channel_id=1, source_target_pairs={{0,4},{4,0},{8,12},{12,8},{16,20},{20,16},{24,28},{28,24},{1,5},{5... | collective-permute-start | bytes 196616 | tf_op jit(solution)/shard_map/ppermute | solution.py:418
  12.5 2.3 %copy-start = (bf16[64,64]{1,0:T(8,128)(2,1)S(1)}, bf16[64,64]{1,0:T(8,128)(2,1)}, u32[]{:S(2)}) copy-start(bf16[64,64]{1,0:T(8,128)(2,1)} %mix.3) | copy-start | bytes 24580

commit v18 on v17

--- a/solution.py
+++ b/solution.py
@@ -11,7 +11,7 @@
 ZOUT = 2
 CF = 16
 ROWS = 8
-SPLIT = 2
+SPLIT = 1
 CHUNK = 16
 DW_BIAS, PW_BIAS, LIFT = 27, 28, 29
 F32 = jnp.float32
@@ -105,32 +105,18 @@
             total = part if total is None else total + part
         return total
 
-    lane, row = lane_iota((slots, tile)), row_iota((slots, tile))
-    mine = (lane >> 3) == (row & 15)
-    in_even, in_odd = mine & ((lane & 4) == 0), mine & ((lane & 4) != 0)
+    shape = (ZOUT * tile, tile)
+    row, lane = row_iota(shape), lane_iota(shape)
+    column = jnp.where((lane & 3) < 2, tile - 2 + (lane & 3), (lane & 3) - 2)
+    picks = (row == jnp.where((lane & 4) != 0, tile + column, column)).astype(BF16)
+    mine = (lane_iota((slots, tile)) >> 3) == (row_iota((slots, tile)) & 15)
     sublane = row_iota((ROWS, tile))
 
-    def placed(m, k):
-        both = []
-        for z in range(ZOUT):
-            plane = planes[ZOUT * m + z, k].astype(F32)
-            cells[ZOUT * m + z, k * slots : (k + 1) * slots, :] = plane
-            both.append(
-                jnp.concatenate(
-                    [
-                        pltpu.roll(plane[x : x + ROWS], (2 + 4 * z + 8 * x) % tile, 1, stride=8, stride_axis=0)
-                        for x in range(0, slots, ROWS)
-                    ],
-                    axis=0,
-                )
-            )
-        rows = jnp.where(in_even, both[0], jnp.where(in_odd, both[1], 0.0))
-        return rows[0:ROWS] + rows[ROWS : 2 * ROWS], rows[2 * ROWS :]
-
-    def summed(m, k, step):
+    def summed(placed, step):
         if step == 0:
-            return placed(m, k)
-        one, two = summed(m, k, step // 2), summed(m, k + step, step // 2)
+            rows = jnp.where(mine, placed, 0.0)
+            return rows[0:ROWS] + rows[ROWS : 2 * ROWS], rows[2 * ROWS :]
+        one, two = summed(placed[: step * slots], step // 2), summed(placed[step * slots :], step // 2)
         turn = (sublane & step) != 0
         return tuple(
             jnp.where(turn, b, a) + pltpu.roll(jnp.where(turn, a, b), step, 0) for a, b in zip(one, two)
@@ -139,9 +125,14 @@
     for m in range(3):
         for part in range(2):
             copy_of(m, part).wait()
-            for c in range(part * half_of, (part + 1) * half_of, ROWS):
-                for half, total in enumerate(summed(m, c, ROWS // 2)):
-                    picked[m, half, c : c + ROWS, :] = total
+            for c in range(part * half_of, (part + 1) * half_of, CHUNK):
+                rows = [planes[ZOUT * m + z, c : c + CHUNK].reshape(CHUNK * slots, tile) for z in range(ZOUT)]
+                for z in range(ZOUT):
+                    cells[ZOUT * m + z, c * slots : (c + CHUNK) * slots, :] = rows[z].astype(F32)
+                placed = jnp.dot(jnp.concatenate(rows, axis=1), picks, preferred_element_type=F32)
+                for k in range(0, CHUNK, ROWS):
+                    for half, total in enumerate(summed(placed[k * slots : (k + ROWS) * slots], ROWS // 2)):
+                        picked[m, half, c + k : c + k + ROWS, :] = total
         if m == 0:
             scale = weights_by_lane()
     width = widths_here[lax.axis_index("gx")]

time: 17.6 us -> 17.9 us (1.017)
  Pallas kernels: 8.77 us -> 9.3 us
  waiting for transfers between devices: 0.41 us -> 0.01 us
    pallas_call x1, Pallas kernels: 2.98 us -> 3.49 us  [shards(): pl.pallas_call(pack_kernel, out_shape=(cells_shape, pltpu.VMEM((32, chann...]
    ppermute x2, waiting for transfers between devices: 0.41 us -> 0.01 us  [swapped(): return lax.ppermute(array, axis, pairs)]
    pallas_call x1, Pallas kernels: 0.74 us -> 0.37 us  [shards(): pl.pallas_call(conv_kernel, out_shape=pltpu.VMEM((ZOUT, slots, early, til...]
    pallas_call x1, Pallas kernels: 2.23 us -> 2.59 us  [shards(): pl.pallas_call(rest_kernel, out_shape=pltpu.VMEM((ZOUT, slots, channels -...]
  transfers between devices with their start and end apart: 5 -> 5, of which waited for: 1 -> 0; matrix products, arithmetic and copies ran while one was open for 0% -> 0% of each run, Pallas kernels for 27% -> 26%
where the time goes in v18:
time: 17.9 us; the launch traced here: 17.7 us
  Pallas kernels  9.3 us (52%)
  starting transfers between devices  8.28 us (46%)
    pallas_call x1, Pallas kernels, shards(): pl.pallas_call(pack_kernel, out_shape=(cells_shape, pltpu.VMEM((32, chann...  3.49 us
    ppermute x1, starting transfers between devices, shards(): first = lax.ppermute(first, 'gy', [(i, (i + 1) % ny) for i in range(ny)])  2.99 us
    pallas_call x1, Pallas kernels, shards(): pl.pallas_call(rest_kernel, out_shape=pltpu.VMEM((ZOUT, slots, channels -...  2.59 us
    ppermute x2, starting transfers between devices, swapped(): return lax.ppermute(array, axis, pairs)  2.27 us
    ppermute x1, starting transfers between devices, shards(): lax.ppermute(own_block, 'gy', [(i, (i + 2) % 4) for i in range(4)])  2 us
    pallas_call x1, Pallas kernels, shards(): pl.pallas_call(finish_kernel, out_shape=(shape((ZOUT, channels, slots, ti...  1.15 us
    pallas_call x1, Pallas kernels, shards(): pl.pallas_call(functools.partial(mix_kernel, gathered), out_shape=(value_...  1.13 us
    ppermute x1, starting transfers between devices, shards(): second = lax.ppermute(second, 'gy', [((i + 1) % ny, i) for i in range(ny)])  1.02 us
  transfers between devices with their start and end apart: 5, of which 0 were waited for; matrix products, arithmetic and copies ran while one was open for 0% of the time, Pallas kernels for 26%

profile of v18, /device:TPU:0, one launch (start us, length us, event | category | flops | bytes accessed | tf_op | source)
XLA Modules:
  0.0 17.7 jit_solution(8920384835475719338)
XLA Ops:
  0.0 3.5 %shard_map.82 = (f32[6,1536,128]{2,1,0:T(8,128)S(1)}, f32[32,64,128]{2,1,0:T(8,128)S(1)}, bf16[80,128]{1,0:T(8,128)(2,1)S(1)}, bf16[80,128]{1,0:T(8,128)(2,1)S(1...) custom-call(bf16[6,64,24,128]{3,2,1,0:T(8,128)(2,1)} %feature.1, s32[8]{0:T(128)} %widths_in.1, f32[27,64]{1,0:T(8,128)} %taps_in.1, ...), custom_call_target="tpu_custom_call" | custom-call | tf_op jit(solution)/shard_map/pallas_call | solution.py:424
  3.5 3.0 %collective-permute-start = (bf16[80,128]{1,0:T(8,128)(2,1)S(1)}, bf16[80,128]{1,0:T(8,128)(2,1)S(1)}, u32[]{:S(2)}, u32[]{:S(2)}) collective-permute-start(bf16[80,128]{1,0:T(8,128)(2,1)S(1)} %get-tuple-element.26), channel_id=1, source_target_pairs={{0,1},{1,2},{2,3},{3,0},{4,5},{5,6},{6,7},{7,4},{8,9},{9,10},{10,1... | collective-permute-start | bytes 61448 | tf_op jit(solution)/shard_map/ppermute | solution.py:452
  6.5 1.0 %collective-permute-start.1 = (bf16[80,128]{1,0:T(8,128)(2,1)S(1)}, bf16[80,128]{1,0:T(8,128)(2,1)S(1)}, u32[]{:S(2)}, u32[]{:S(2)}) collective-permute-start(bf16[80,128]{1,0:T(8,128)(2,1)S(1)} %get-tuple-element.27), channel_id=1, source_target_pairs={{1,0},{2,1},{3,2},{0,3},{5,4},{6,5},{7,6},{4,7},{9,8},{10,9},{11,1... | collective-permute-start | bytes 61448 | tf_op jit(solution)/shard_map/ppermute | solution.py:453
  7.5 0.4 %shard_map.83 = (f32[6,1536,128]{2,1,0:T(8,128)S(1)}, f32[2,4,64,128]{3,2,1,0:T(8,128)S(1)}, f32[3,2,32]{2,1,0:T(2,128)S(1)}) custom-call(s32[8]{0:T(128)S(4)} %get-tuple-element.21.widths, f32[32,64,128]{2,1,0:T(8,128)S(1)} %get-tuple-element.22.weights, f32[3,2,32]{2,1,0:T(2,128)S(1)} %get-tuple-element.23.coarse, ...), custom_call_target="tpu_custom_call", output_to_operand_aliasing={{0}: (3, {})} | custom-call | flops 100000000 | bytes 1000000 | tf_op jit(solution)/shard_map/pallas_call | solution.py:455
  7.9 2.0 %collective-permute-start.2 = (f32[3,2,32]{2,1,0:T(2,128)S(1)}, f32[3,2,32]{2,1,0:T(2,128)S(1)}, u32[]{:S(2)}, u32[]{:S(2)}) collective-permute-start(f32[3,2,32]{2,1,0:T(2,128)S(1)} %get-tuple-element.30.refs_2_), channel_id=1, source_target_pairs={{0,2},{1,3},{2,0},{3,1},{4,6},{5,7},{6,4},{7,5},{8,10},{9,11},{10,... | collective-permute-start | bytes 2312 | tf_op jit(solution)/shard_map/ppermute | solution.py:469
  9.9 0.4 %shard_map.84.depth = f32[2,24,8,128]{3,2,1,0:T(8,128)S(1)} custom-call(f32[6,1536,128]{2,1,0:T(8,128)S(1)} %get-tuple-element.25.cells, f32[32,64,128]{2,1,0:T(8,128)S(1)} %get-tuple-element.22.weights), custom_call_target="tpu_custom_call" | custom-call | flops 1000000000 | bytes 1000000 | tf_op jit(solution)/shard_map/pallas_call | solution.py:470
  10.3 0.0 collective-permute-done.first.refs_0_
  10.3 0.0 collective-permute-done.1.second.refs_1_
  10.3 0.2 %shard_map.85 = (f32[2,64,128]{2,1,0:T(8,128)S(1)}, bf16[256,128]{1,0:T(8,128)(2,1)S(1)}, bf16[256,128]{1,0:T(8,128)(2,1)S(1)}) custom-call(s32[8]{0:T(128)S(4)} %get-tuple-element.21.widths, bf16[80,128]{1,0:T(8,128)(2,1)S(1)} %collective-permute-done.first.refs_0_, bf16[80,128]{1,0:T(8,128)(2,1)S(1)} %collective-permute-done.1.second.refs_1_, ...), custom_call_target="tpu_custom_call" | custom-call | tf_op jit(solution)/shard_map/pallas_call | solution.py:478
  10.5 2.3 %collective-permute-start.3 = (bf16[256,128]{1,0:T(8,128)(2,1)S(1)}, bf16[256,128]{1,0:T(8,128)(2,1)S(1)}, u32[]{:S(2)}, u32[]{:S(2)}) collective-permute-start(bf16[256,128]{1,0:T(8,128)(2,1)S(1)} %get-tuple-element.33), channel_id=1, source_target_pairs={{4,8},{8,4},{12,16},{16,12},{20,24},{24,20},{28,0},{0,28},{5,9},{9... | collective-permute-start | bytes 196616 | tf_op jit(solution)/shard_map/ppermute | solution.py:409
  12.7 0.0 collective-permute-start.4
  12.8 0.0 copy-start
  12.8 2.6 %shard_map.86.rest = f32[2,24,56,128]{3,2,1,0:T(8,128)S(1)} custom-call(f32[2,64,128]{2,1,0:T(8,128)S(1)} %get-tuple-element.29.edge, f32[6,1536,128]{2,1,0:T(8,128)S(1)} %get-tuple-element.25.cells, f32[32,64,128]{2,1,0:T(8,128)S(1)} %get-tuple-element.22.weights), custom_call_target="tpu_custom_call" | custom-call | flops 1000000000 | bytes 1000000 | tf_op jit(solution)/shard_map/pallas_call | solution.py:488
  15.4 0.0 collective-permute-done.2.refs_3_
  15.4 0.0 copy-done
  15.4 1.1 %shard_map.87 = (f32[2,1536,128]{2,1,0:T(8,128)S(1)}, f32[2,4,64,128]{3,2,1,0:T(8,128)S(1)}, f32[2,4,64,128]{3,2,1,0:T(8,128)S(1)}) custom-call(s32[8]{0:T(128)S(4)} %get-tuple-element.21.widths, bf16[64,64]{1,0:T(8,128)(2,1)S(1)} %copy-done, f32[6,1536,128]{2,1,0:T(8,128)S(1)} %get-tuple-element.25.cells, f32[32,64,128]{2,1,0:T(8,128)S(1)} %get-tuple-element.22.weights, ...), custom_call_target="tpu_custom_call" | custom-call | flops 1000000000 | bytes 1000000 | tf_op jit(solution)/shard_map/pallas_call | solution.py:497
  16.5 0.0 collective-permute-done.3.far
  16.5 0.0 collective-permute-done.4.near
  16.5 1.2 %shard_map.88 = (bf16[2,64,24,128]{3,2,1,0:T(8,128)(2,1)}, f32[2,1536,128]{2,1,0:T(8,128)S(1)}) custom-call(s32[8]{0:T(128)S(4)} %get-tuple-element.21.widths, bf16[64,64]{1,0:T(8,128)(2,1)S(1)} %copy-done, f32[32,64,128]{2,1,0:T(8,128)S(1)} %get-tuple-element.22.weights, ...), custom_call_target="tpu_custom_call", output_to_operand_aliasing={{1}: (7, {})} | custom-call | tf_op jit(solution)/shard_map/pallas_call | solution.py:507
Async XLA Ops:
  3.5 6.8 %collective-permute-start = (bf16[80,128]{1,0:T(8,128)(2,1)S(1)}, bf16[80,128]{1,0:T(8,128)(2,1)S(1)}, u32[]{:S(2)}, u32[]{:S(2)}) collective-permute-start(bf16[80,128]{1,0:T(8,128)(2,1)S(1)} %get-tuple-element.26), channel_id=1, source_target_pairs={{0,1},{1,2},{2,3},{3,0},{4,5},{5,6},{6,7},{7,4},{8,9},{9,10},{10,1... | collective-permute-start | bytes 61448 | tf_op jit(solution)/shard_map/ppermute | solution.py:452
  6.5 3.8 %collective-permute-start.1 = (bf16[80,128]{1,0:T(8,128)(2,1)S(1)}, bf16[80,128]{1,0:T(8,128)(2,1)S(1)}, u32[]{:S(2)}, u32[]{:S(2)}) collective-permute-start(bf16[80,128]{1,0:T(8,128)(2,1)S(1)} %get-tuple-element.27), channel_id=1, source_target_pairs={{1,0},{2,1},{3,2},{0,3},{5,4},{6,5},{7,6},{4,7},{9,8},{10,9},{11,1... | collective-permute-start | bytes 61448 | tf_op jit(solution)/shard_map/ppermute | solution.py:453
  7.9 7.5 %collective-permute-start.2 = (f32[3,2,32]{2,1,0:T(2,128)S(1)}, f32[3,2,32]{2,1,0:T(2,128)S(1)}, u32[]{:S(2)}, u32[]{:S(2)}) collective-permute-start(f32[3,2,32]{2,1,0:T(2,128)S(1)} %get-tuple-element.30.refs_2_), channel_id=1, source_target_pairs={{0,2},{1,3},{2,0},{3,1},{4,6},{5,7},{6,4},{7,5},{8,10},{9,11},{10,... | collective-permute-start | bytes 2312 | tf_op jit(solution)/shard_map/ppermute | solution.py:469
  10.5 6.0 %collective-permute-start.3 = (bf16[256,128]{1,0:T(8,128)(2,1)S(1)}, bf16[256,128]{1,0:T(8,128)(2,1)S(1)}, u32[]{:S(2)}, u32[]{:S(2)}) collective-permute-start(bf16[256,128]{1,0:T(8,128)(2,1)S(1)} %get-tuple-element.33), channel_id=1, source_target_pairs={{4,8},{8,4},{12,16},{16,12},{20,24},{24,20},{28,0},{0,28},{5,9},{9... | collective-permute-start | bytes 196616 | tf_op jit(solution)/shard_map/ppermute | solution.py:409
  12.7 3.8 %collective-permute-start.4 = (bf16[256,128]{1,0:T(8,128)(2,1)S(1)}, bf16[256,128]{1,0:T(8,128)(2,1)S(1)}, u32[]{:S(2)}, u32[]{:S(2)}) collective-permute-start(bf16[256,128]{1,0:T(8,128)(2,1)S(1)} %get-tuple-element.34), channel_id=1, source_target_pairs={{0,4},{4,0},{8,12},{12,8},{16,20},{20,16},{24,28},{28,24},{1,5},{5... | collective-permute-start | bytes 196616 | tf_op jit(solution)/shard_map/ppermute | solution.py:409
  12.8 2.6 %copy-start = (bf16[64,64]{1,0:T(8,128)(2,1)S(1)}, bf16[64,64]{1,0:T(8,128)(2,1)}, u32[]{:S(2)}) copy-start(bf16[64,64]{1,0:T(8,128)(2,1)} %mix.3) | copy-start | bytes 24580

commit v19 on v17

--- a/solution.py
+++ b/solution.py
@@ -11,7 +11,7 @@
 ZOUT = 2
 CF = 16
 ROWS = 8
-SPLIT = 2
+SPLIT = 1
 CHUNK = 16
 DW_BIAS, PW_BIAS, LIFT = 27, 28, 29
 F32 = jnp.float32
@@ -66,7 +66,7 @@
     for m in range(3):
         for part in range(2):
             copy_of(m, part).start()
-    def weights_by_lane():
+    def take_small():
         for copy in small:
             copy.wait()
         for d in range(widths.shape[0]):
@@ -91,19 +91,6 @@
                     tail[k * own_rows : (k + 1) * own_rows, p * ncy : (p + 1) * ncy] = term
         for message in (first, second):
             message[channels:, :] = tail[...].astype(BF16)
-
-        row, along = row_iota((taps.shape[0], tile)), lane_iota((taps.shape[0], tile))
-        by_side = jnp.where((along & 2) != 0, 2, 0)
-        chosen = jnp.concatenate(
-            [(row == tap_of(m, dx, -1) + by_side).astype(BF16) for m in range(3) for dx in (-1, 0, 1)], axis=1
-        )
-        total, rest = None, taps[...]
-        for _ in range(3):
-            term = rest.astype(BF16)
-            rest = rest - term.astype(F32)
-            part = lax.dot_general(term, chosen, (((0,), (0,)), ((), ())), preferred_element_type=F32)
-            total = part if total is None else total + part
-        return total
 
     lane, row = lane_iota((slots, tile)), row_iota((slots, tile))
     mine = (lane >> 3) == (row & 15)
@@ -143,7 +130,7 @@
                 for half, total in enumerate(summed(m, c, ROWS // 2)):
                     picked[m, half, c : c + ROWS, :] = total
         if m == 0:
-            scale = weights_by_lane()
+            take_small()
     width = widths_here[lax.axis_index("gx")]
 
     shape = (channels, tile)
@@ -162,9 +149,9 @@
             ),
         }
         for dx in (-1, 0, 1):
-            begin = (3 * m + dx + 1) * tile
+            weight = jnp.where(on_left, weights[tap_of(m, dx, 1)], weights[tap_of(m, dx, -1)])
             for half in range(2):
-                term = scale[:, begin : begin + tile] * moved[dx][half]
+                term = weight * moved[dx][half]
                 packed[half] = term if packed[half] is None else packed[half] + term
     left = jnp.where(on_left, packed[0], pltpu.roll(packed[1], tile - 2, 1))
     right = jnp.where(on_left, pltpu.roll(packed[1], 2, 1), packed[0])

time: 17.6 us -> 17.3 us (0.983)
  waiting for transfers between devices: 0.41 us -> 0.01 us
    ppermute x2, waiting for transfers between devices: 0.41 us -> 0.01 us  [swapped(): return lax.ppermute(array, axis, pairs)]
    pallas_call x1, Pallas kernels: 0.74 us -> 0.37 us  [shards(): pl.pallas_call(conv_kernel, out_shape=pltpu.VMEM((ZOUT, slots, early, til...]
    pallas_call x1, Pallas kernels: 2.23 us -> 2.59 us  [shards(): pl.pallas_call(rest_kernel, out_shape=pltpu.VMEM((ZOUT, slots, channels -...]
  transfers between devices with their start and end apart: 5 -> 5, of which waited for: 1 -> 0; matrix products, arithmetic and copies ran while one was open for 0% -> 0% of each run, Pallas kernels for 27% -> 27%
where the time goes in v19:
time: 17.3 us; the launch traced here: 17.1 us
  Pallas kernels  8.75 us (51%)
  starting transfers between devices  8.28 us (48%)
    ppermute x1, starting transfers between devices, shards(): first = lax.ppermute(first, 'gy', [(i, (i + 1) % ny) for i in range(ny)])  2.99 us
    pallas_call x1, Pallas kernels, shards(): pl.pallas_call(pack_kernel, out_shape=(cells_shape, pltpu.VMEM((32, chann...  2.94 us
    pallas_call x1, Pallas kernels, shards(): pl.pallas_call(rest_kernel, out_shape=pltpu.VMEM((ZOUT, slots, channels -...  2.59 us
    ppermute x2, starting transfers between devices, swapped(): return lax.ppermute(array, axis, pairs)  2.27 us
    ppermute x1, starting transfers between devices, shards(): lax.ppermute(own_block, 'gy', [(i, (i + 2) % 4) for i in range(4)])  2 us
    pallas_call x1, Pallas kernels, shards(): pl.pallas_call(finish_kernel, out_shape=(shape((ZOUT, channels, slots, ti...  1.15 us
    pallas_call x1, Pallas kernels, shards(): pl.pallas_call(functools.partial(mix_kernel, gathered), out_shape=(value_...  1.13 us
    ppermute x1, starting transfers between devices, shards(): second = lax.ppermute(second, 'gy', [((i + 1) % ny, i) for i in range(ny)])  1.02 us
  transfers between devices with their start and end apart: 5, of which 0 were waited for; matrix products, arithmetic and copies ran while one was open for 0% of the time, Pallas kernels for 27%

profile of v19, /device:TPU:0, one launch (start us, length us, event | category | flops | bytes accessed | tf_op | source)
XLA Modules:
  0.0 17.1 jit_solution(10257329931947032832)
XLA Ops:
  0.0 2.9 %shard_map.82 = (f32[6,1536,128]{2,1,0:T(8,128)S(1)}, f32[32,64,128]{2,1,0:T(8,128)S(1)}, bf16[80,128]{1,0:T(8,128)(2,1)S(1)}, bf16[80,128]{1,0:T(8,128)(2,1)S(1...) custom-call(bf16[6,64,24,128]{3,2,1,0:T(8,128)(2,1)} %feature.1, s32[8]{0:T(128)} %widths_in.1, f32[27,64]{1,0:T(8,128)} %taps_in.1, ...), custom_call_target="tpu_custom_call" | custom-call | tf_op jit(solution)/shard_map/pallas_call | solution.py:420
  3.0 3.0 %collective-permute-start = (bf16[80,128]{1,0:T(8,128)(2,1)S(1)}, bf16[80,128]{1,0:T(8,128)(2,1)S(1)}, u32[]{:S(2)}, u32[]{:S(2)}) collective-permute-start(bf16[80,128]{1,0:T(8,128)(2,1)S(1)} %get-tuple-element.26), channel_id=1, source_target_pairs={{0,1},{1,2},{2,3},{3,0},{4,5},{5,6},{6,7},{7,4},{8,9},{9,10},{10,1... | collective-permute-start | bytes 61448 | tf_op jit(solution)/shard_map/ppermute | solution.py:448
  5.9 1.0 %collective-permute-start.1 = (bf16[80,128]{1,0:T(8,128)(2,1)S(1)}, bf16[80,128]{1,0:T(8,128)(2,1)S(1)}, u32[]{:S(2)}, u32[]{:S(2)}) collective-permute-start(bf16[80,128]{1,0:T(8,128)(2,1)S(1)} %get-tuple-element.27), channel_id=1, source_target_pairs={{1,0},{2,1},{3,2},{0,3},{5,4},{6,5},{7,6},{4,7},{9,8},{10,9},{11,1... | collective-permute-start | bytes 61448 | tf_op jit(solution)/shard_map/ppermute | solution.py:449
  7.0 0.4 %shard_map.83 = (f32[6,1536,128]{2,1,0:T(8,128)S(1)}, f32[2,4,64,128]{3,2,1,0:T(8,128)S(1)}, f32[3,2,32]{2,1,0:T(2,128)S(1)}) custom-call(s32[8]{0:T(128)S(4)} %get-tuple-element.21.widths, f32[32,64,128]{2,1,0:T(8,128)S(1)} %get-tuple-element.22.weights, f32[3,2,32]{2,1,0:T(2,128)S(1)} %get-tuple-element.23.coarse, ...), custom_call_target="tpu_custom_call", output_to_operand_aliasing={{0}: (3, {})} | custom-call | flops 100000000 | bytes 1000000 | tf_op jit(solution)/shard_map/pallas_call | solution.py:451
  7.3 2.0 %collective-permute-start.2 = (f32[3,2,32]{2,1,0:T(2,128)S(1)}, f32[3,2,32]{2,1,0:T(2,128)S(1)}, u32[]{:S(2)}, u32[]{:S(2)}) collective-permute-start(f32[3,2,32]{2,1,0:T(2,128)S(1)} %get-tuple-element.30.refs_2_), channel_id=1, source_target_pairs={{0,2},{1,3},{2,0},{3,1},{4,6},{5,7},{6,4},{7,5},{8,10},{9,11},{10,... | collective-permute-start | bytes 2312 | tf_op jit(solution)/shard_map/ppermute | solution.py:465
  9.3 0.4 %shard_map.84.depth = f32[2,24,8,128]{3,2,1,0:T(8,128)S(1)} custom-call(f32[6,1536,128]{2,1,0:T(8,128)S(1)} %get-tuple-element.25.cells, f32[32,64,128]{2,1,0:T(8,128)S(1)} %get-tuple-element.22.weights), custom_call_target="tpu_custom_call" | custom-call | flops 1000000000 | bytes 1000000 | tf_op jit(solution)/shard_map/pallas_call | solution.py:466
  9.7 0.0 collective-permute-done.first.refs_0_
  9.7 0.0 collective-permute-done.1.second.refs_1_
  9.7 0.2 %shard_map.85 = (f32[2,64,128]{2,1,0:T(8,128)S(1)}, bf16[256,128]{1,0:T(8,128)(2,1)S(1)}, bf16[256,128]{1,0:T(8,128)(2,1)S(1)}) custom-call(s32[8]{0:T(128)S(4)} %get-tuple-element.21.widths, bf16[80,128]{1,0:T(8,128)(2,1)S(1)} %collective-permute-done.first.refs_0_, bf16[80,128]{1,0:T(8,128)(2,1)S(1)} %collective-permute-done.1.second.refs_1_, ...), custom_call_target="tpu_custom_call" | custom-call | tf_op jit(solution)/shard_map/pallas_call | solution.py:474
  9.9 2.3 %collective-permute-start.3 = (bf16[256,128]{1,0:T(8,128)(2,1)S(1)}, bf16[256,128]{1,0:T(8,128)(2,1)S(1)}, u32[]{:S(2)}, u32[]{:S(2)}) collective-permute-start(bf16[256,128]{1,0:T(8,128)(2,1)S(1)} %get-tuple-element.33), channel_id=1, source_target_pairs={{4,8},{8,4},{12,16},{16,12},{20,24},{24,20},{28,0},{0,28},{5,9},{9... | collective-permute-start | bytes 196616 | tf_op jit(solution)/shard_map/ppermute | solution.py:405
  12.2 0.0 collective-permute-start.4
  12.2 0.0 copy-start
  12.2 2.6 %shard_map.86.rest = f32[2,24,56,128]{3,2,1,0:T(8,128)S(1)} custom-call(f32[2,64,128]{2,1,0:T(8,128)S(1)} %get-tuple-element.29.edge, f32[6,1536,128]{2,1,0:T(8,128)S(1)} %get-tuple-element.25.cells, f32[32,64,128]{2,1,0:T(8,128)S(1)} %get-tuple-element.22.weights), custom_call_target="tpu_custom_call" | custom-call | flops 1000000000 | bytes 1000000 | tf_op jit(solution)/shard_map/pallas_call | solution.py:484
  14.8 0.0 collective-permute-done.2.refs_3_
  14.8 0.0 copy-done
  14.8 1.1 %shard_map.87 = (f32[2,1536,128]{2,1,0:T(8,128)S(1)}, f32[2,4,64,128]{3,2,1,0:T(8,128)S(1)}, f32[2,4,64,128]{3,2,1,0:T(8,128)S(1)}) custom-call(s32[8]{0:T(128)S(4)} %get-tuple-element.21.widths, bf16[64,64]{1,0:T(8,128)(2,1)S(1)} %copy-done, f32[6,1536,128]{2,1,0:T(8,128)S(1)} %get-tuple-element.25.cells, f32[32,64,128]{2,1,0:T(8,128)S(1)} %get-tuple-element.22.weights, ...), custom_call_target="tpu_custom_call" | custom-call | flops 1000000000 | bytes 1000000 | tf_op jit(solution)/shard_map/pallas_call | solution.py:493
  16.0 0.0 collective-permute-done.3.far
  16.0 0.0 collective-permute-done.4.near
  16.0 1.2 %shard_map.88 = (bf16[2,64,24,128]{3,2,1,0:T(8,128)(2,1)}, f32[2,1536,128]{2,1,0:T(8,128)S(1)}) custom-call(s32[8]{0:T(128)S(4)} %get-tuple-element.21.widths, bf16[64,64]{1,0:T(8,128)(2,1)S(1)} %copy-done, f32[32,64,128]{2,1,0:T(8,128)S(1)} %get-tuple-element.22.weights, ...), custom_call_target="tpu_custom_call", output_to_operand_aliasing={{1}: (7, {})} | custom-call | tf_op jit(solution)/shard_map/pallas_call | solution.py:503
Async XLA Ops:
  3.0 6.8 %collective-permute-start = (bf16[80,128]{1,0:T(8,128)(2,1)S(1)}, bf16[80,128]{1,0:T(8,128)(2,1)S(1)}, u32[]{:S(2)}, u32[]{:S(2)}) collective-permute-start(bf16[80,128]{1,0:T(8,128)(2,1)S(1)} %get-tuple-element.26), channel_id=1, source_target_pairs={{0,1},{1,2},{2,3},{3,0},{4,5},{5,6},{6,7},{7,4},{8,9},{9,10},{10,1... | collective-permute-start | bytes 61448 | tf_op jit(solution)/shard_map/ppermute | solution.py:448
  5.9 3.8 %collective-permute-start.1 = (bf16[80,128]{1,0:T(8,128)(2,1)S(1)}, bf16[80,128]{1,0:T(8,128)(2,1)S(1)}, u32[]{:S(2)}, u32[]{:S(2)}) collective-permute-start(bf16[80,128]{1,0:T(8,128)(2,1)S(1)} %get-tuple-element.27), channel_id=1, source_target_pairs={{1,0},{2,1},{3,2},{0,3},{5,4},{6,5},{7,6},{4,7},{9,8},{10,9},{11,1... | collective-permute-start | bytes 61448 | tf_op jit(solution)/shard_map/ppermute | solution.py:449
  7.3 7.5 %collective-permute-start.2 = (f32[3,2,32]{2,1,0:T(2,128)S(1)}, f32[3,2,32]{2,1,0:T(2,128)S(1)}, u32[]{:S(2)}, u32[]{:S(2)}) collective-permute-start(f32[3,2,32]{2,1,0:T(2,128)S(1)} %get-tuple-element.30.refs_2_), channel_id=1, source_target_pairs={{0,2},{1,3},{2,0},{3,1},{4,6},{5,7},{6,4},{7,5},{8,10},{9,11},{10,... | collective-permute-start | bytes 2312 | tf_op jit(solution)/shard_map/ppermute | solution.py:465
  9.9 6.0 %collective-permute-start.3 = (bf16[256,128]{1,0:T(8,128)(2,1)S(1)}, bf16[256,128]{1,0:T(8,128)(2,1)S(1)}, u32[]{:S(2)}, u32[]{:S(2)}) collective-permute-start(bf16[256,128]{1,0:T(8,128)(2,1)S(1)} %get-tuple-element.33), channel_id=1, source_target_pairs={{4,8},{8,4},{12,16},{16,12},{20,24},{24,20},{28,0},{0,28},{5,9},{9... | collective-permute-start | bytes 196616 | tf_op jit(solution)/shard_map/ppermute | solution.py:405
  12.2 3.8 %collective-permute-start.4 = (bf16[256,128]{1,0:T(8,128)(2,1)S(1)}, bf16[256,128]{1,0:T(8,128)(2,1)S(1)}, u32[]{:S(2)}, u32[]{:S(2)}) collective-permute-start(bf16[256,128]{1,0:T(8,128)(2,1)S(1)} %get-tuple-element.34), channel_id=1, source_target_pairs={{0,4},{4,0},{8,12},{12,8},{16,20},{20,16},{24,28},{28,24},{1,5},{5... | collective-permute-start | bytes 196616 | tf_op jit(solution)/shard_map/ppermute | solution.py:405
  12.2 2.6 %copy-start = (bf16[64,64]{1,0:T(8,128)(2,1)S(1)}, bf16[64,64]{1,0:T(8,128)(2,1)}, u32[]{:S(2)}) copy-start(bf16[64,64]{1,0:T(8,128)(2,1)} %mix.3) | copy-start | bytes 24580
